TPU v7x, 32 devices: a whole 2x2x4 slice. The times are simulated.
32 devices in a mesh: lon: 8 (over z, core), lev: 4 (over y, x).
Axes of the slice: x: 2, y: 2, z: 4, core: 2. Of those that a mesh axis runs over, the one named last changes fastest.
Arguments:
- inputs: bfloat16 [2, 8, 48, 96, 192], P(None, 'lev', None, 'lon'), may hold values from -6 to 6
- cotangent: bfloat16 [2, 8, 48, 96, 192], P(None, 'lev', None, 'lon'), may hold values from -6 to 6
- grid_sizes: int32 [2, 2], replicated, may hold values from 43 to 96, as said below
- offsets: int32 [2], replicated, may hold values from 1 to 6, as said below
- gain_one: float32 [192], replicated, may hold values from 0.25 to 1.75
- shift_one: float32 [192], replicated, may hold values from -1 to 1
- qkv_window: bfloat16 [192, 576], replicated, may hold values from -0.4375 to 0.4375
- out_window: bfloat16 [192, 192], replicated, may hold values from -1.25 to 1.25
- bias_table: float32 [8, 6, 6, 6, 23], replicated, may hold values from -3 to 3
- gain_two: float32 [192], replicated, may hold values from 0.25 to 1.75
- shift_two: float32 [192], replicated, may hold values from -1 to 1
- qkv_column: bfloat16 [192, 576], replicated, may hold values from -0.4375 to 0.4375
- out_column: bfloat16 [192, 192], replicated, may hold values from -0.75 to 0.75
- gain_three: float32 [192], replicated, may hold values from 0.25 to 1.75
- shift_three: float32 [192], replicated, may hold values from -1 to 1
- w_up: bfloat16 [192, 768], replicated, may hold values from -0.4375 to 0.4375
- w_down: bfloat16 [768, 192], replicated, may hold values from -0.21875 to 0.21875
Outputs:
- result: bfloat16 [2, 8, 48, 96, 192], P(None, 'lev', None, 'lon')
- input_grad: bfloat16 [2, 8, 48, 96, 192], P(None, 'lev', None, 'lon')
- grad_gain_one: float32 [192], replicated
- grad_shift_one: float32 [192], replicated
- grad_qkv_window: float32 [192, 576], replicated
- grad_out_window: float32 [192, 192], replicated
- grad_bias_table: float32 [8, 6, 6, 6, 23], replicated
- grad_gain_two: float32 [192], replicated
- grad_shift_two: float32 [192], replicated
- grad_qkv_column: float32 [192, 576], replicated
- grad_out_column: float32 [192, 192], replicated
- grad_gain_three: float32 [192], replicated
- grad_shift_three: float32 [192], replicated
- grad_w_up: float32 [192, 768], replicated
- grad_w_down: float32 [768, 192], replicated
Inputs may be any that keep to these rules, and one draw needn't show every extreme that they name: grid_sizes[b, 0] is from 43 to 48 and grid_sizes[b, 1] from 90 to 96; one sample holds the largest value of the array and another one the smallest. `offsets`: every offset is 1 to 6; sample 0's is 6.
All inputs are finite; a program needn't handle non-finite values.
Results may differ from a plain program's by a relative error of at most 0.018.
Values may be sent and summed in bfloat16 or wider, within the bound.
No kernel may reach another device: no remote copies, remote signals or barrier semaphores. Data moves between devices by JAX's collectives and lax.ppermute only.
A program may use at most 256 MiB of HBM per device.

v0:
```python
import jax
import jax.numpy as jnp
from jax import lax
from jax.sharding import PartitionSpec as P

WLAT = 6
WLON = 12


EPSILON = 1e-05
NEGATIVE = -1000000000.0


def shifted(block, axis, distance):
    devices = range(lax.axis_size(axis))
    route = [((i - distance) % len(devices), i) for i in devices]
    return lax.ppermute(block, axis, route)


def layer_norm(values, gain, shift):
    center = values - jnp.mean(values, axis=-1, keepdims=True)
    spread = jnp.mean(center * center, axis=-1, keepdims=True)
    return center * lax.rsqrt(spread + EPSILON) * gain + shift


def norm_backward(values, gain, shift, grad_normed):
    _, pullback = jax.vjp(layer_norm, values, gain, shift)
    return pullback(grad_normed)


def gelu_exact(values):
    return jax.nn.gelu(values, approximate=False)


def flat_product(left, right):
    return jnp.einsum(
        "td,te->de",
        left.reshape(-1, left.shape[-1]),
        right.reshape(-1, right.shape[-1]),
        preferred_element_type=jnp.float32,
    )


def lon_table():
    relative = jnp.arange(2 * WLON - 1, dtype=jnp.int32)[:, None, None]
    query_col = jnp.arange(WLON, dtype=jnp.int32)[None, :, None]
    key_col = jnp.arange(WLON, dtype=jnp.int32)[None, None, :]
    return (query_col - key_col + WLON - 1 == relative).astype(jnp.float32)


def to_windows(grid_cells):
    leading = grid_cells.shape[:-3]
    lat_rows, lon_cols, feature_count = grid_cells.shape[-3:]
    pieces = grid_cells.reshape(
        leading + (lat_rows // WLAT, WLAT, lon_cols // WLON, WLON, feature_count)
    )
    depth_count = len(leading)
    axes_order = tuple(range(depth_count)) + (
        depth_count,
        depth_count + 2,
        depth_count + 1,
        depth_count + 3,
        depth_count + 4,
    )
    return pieces.transpose(axes_order).reshape(
        leading + (lat_rows // WLAT, lon_cols // WLON, WLAT * WLON, feature_count)
    )


def from_windows(windows):
    leading = windows.shape[:-4]
    band_count, window_count, _, feature_count = windows.shape[-4:]
    pieces = windows.reshape(leading + (band_count, window_count, WLAT, WLON, feature_count))
    depth_count = len(leading)
    axes_order = tuple(range(depth_count)) + (
        depth_count,
        depth_count + 2,
        depth_count + 1,
        depth_count + 3,
        depth_count + 4,
    )
    return pieces.transpose(axes_order).reshape(
        leading + (band_count * WLAT, window_count * WLON, feature_count)
    )


def slide_columns(extended, starts, slab_cols):

    def one_sample(sample_slab, start_col):
        return lax.dynamic_slice_in_dim(sample_slab, start_col, slab_cols, axis=2)

    return jax.vmap(one_sample)(extended, starts)


def window_scores(queries, keyset, earth_bias, valid, scale):
    raw_scores = (
        jnp.einsum("slbwqhe,slbwkhe->slbwhqk", queries, keyset, preferred_element_type=jnp.float32)
        * scale
    )
    raw_scores = raw_scores + earth_bias[None, None, :, None]
    return jnp.where(valid[:, None, :, :, None, None, :], raw_scores, NEGATIVE)


def column_scores(queries, keyset, scale):
    return (
        jnp.einsum("slache,smache->sachlm", queries, keyset, preferred_element_type=jnp.float32)
        * scale
    )


def column_forward(queries, keyset, values, scale):
    scores = column_scores(queries, keyset, scale)
    row_peak = jnp.max(scores, axis=-1, keepdims=True)
    exps = jnp.exp(scores - row_peak)
    row_total = jnp.sum(exps, axis=-1, keepdims=True)
    attn_probs = exps / row_total
    log_total = row_peak + jnp.log(row_total)
    column_out = jnp.einsum(
        "sachlm,smache->slache",
        attn_probs.astype(jnp.bfloat16),
        values,
        preferred_element_type=jnp.float32,
    )
    return (column_out.astype(jnp.bfloat16), log_total)


def column_backward(queries, keyset, values, log_total, grad_out, scale):
    attn_probs = jnp.exp(column_scores(queries, keyset, scale) - log_total)
    grad_probs = jnp.einsum(
        "slache,smache->sachlm", grad_out, values, preferred_element_type=jnp.float32
    )
    row_inner = jnp.sum(grad_probs * attn_probs, axis=-1, keepdims=True)
    grad_scores = (attn_probs * (grad_probs - row_inner)).astype(jnp.bfloat16)
    grad_queries = (
        jnp.einsum("sachlm,smache->slache", grad_scores, keyset, preferred_element_type=jnp.float32)
        * scale
    )
    grad_keys = (
        jnp.einsum(
            "sachlm,slache->smache", grad_scores, queries, preferred_element_type=jnp.float32
        )
        * scale
    )
    grad_values = jnp.einsum(
        "sachlm,slache->smache",
        attn_probs.astype(jnp.bfloat16),
        grad_out,
        preferred_element_type=jnp.float32,
    )
    return (grad_queries, grad_keys, grad_values)


def on_device(
    inputs,
    cotangent,
    grid_sizes,
    offsets,
    gain_one,
    shift_one,
    qkv_window,
    out_window,
    bias_table,
    gain_two,
    shift_two,
    qkv_column,
    out_column,
    gain_three,
    shift_three,
    w_up,
    w_down,
):
    tokens_in, cot_in = (inputs, cotangent)
    samples, levels, lat_rows, slab_cols, feature_count = tokens_in.shape
    head_count = bias_table.shape[1]
    head_size = feature_count // head_count
    scale = head_size ** (-0.5)
    half_window = WLON // 2
    tokens_win = WLAT * WLON
    residual = tokens_in.astype(jnp.float32)
    local_bands = lat_rows // WLAT
    earth_bias = jnp.einsum(
        "khijr,rab->khiajb", bias_table, lon_table(), precision=lax.Precision.HIGHEST
    )
    earth_bias = earth_bias.reshape(local_bands, head_count, tokens_win, tokens_win)
    cycle_cols = slab_cols * lax.axis_size("lon")
    orig_cols = (
        lax.axis_index("lon") * slab_cols
        + offsets[:, None]
        + jnp.arange(slab_cols, dtype=jnp.int32)[None, :]
    ) % cycle_cols
    col_ok = orig_cols < grid_sizes[:, 1:2]
    row_ok = jnp.arange(lat_rows, dtype=jnp.int32)[None, :] < grid_sizes[:, 0:1]
    valid_grid = (row_ok[:, :, None] & col_ok[:, None, :]).astype(jnp.float32)
    valid = to_windows(valid_grid[..., None])[..., 0] > 0.5
    normed_one = layer_norm(residual, gain_one, shift_one).astype(jnp.bfloat16)
    ahead = shifted(normed_one[:, :, :, :half_window], "lon", -1)
    rolled = slide_columns(jnp.concatenate([normed_one, ahead], axis=3), offsets, slab_cols)
    qkv_grid = jnp.dot(rolled, qkv_window, preferred_element_type=jnp.float32).astype(jnp.bfloat16)
    qkv_win = to_windows(qkv_grid)
    win_shape = qkv_win.shape[:-1] + (head_count, head_size)
    win_queries = qkv_win[..., :feature_count].reshape(win_shape)
    win_keys = qkv_win[..., feature_count : 2 * feature_count].reshape(win_shape)
    win_values = qkv_win[..., 2 * feature_count :].reshape(win_shape)
    scores = window_scores(win_queries, win_keys, earth_bias, valid, scale)
    row_peak = jnp.max(scores, axis=-1, keepdims=True)
    exps = jnp.exp(scores - row_peak)
    row_total = jnp.sum(exps, axis=-1, keepdims=True)
    win_log_total = row_peak + jnp.log(row_total)
    attn_probs = exps / row_total
    attended = jnp.einsum(
        "slbwhqk,slbwkhe->slbwqhe",
        attn_probs.astype(jnp.bfloat16),
        win_values,
        preferred_element_type=jnp.float32,
    )
    attended = from_windows(
        attended.astype(jnp.bfloat16).reshape(qkv_win.shape[:-1] + (feature_count,))
    )
    behind = shifted(attended[:, :, :, slab_cols - half_window :], "lon", 1)
    unrolled = slide_columns(
        jnp.concatenate([behind, attended], axis=3), half_window - offsets, slab_cols
    )
    after_window = residual + jnp.dot(unrolled, out_window, preferred_element_type=jnp.float32)
    normed_two = layer_norm(after_window, gain_two, shift_two).astype(jnp.bfloat16)
    qkv_two = jnp.dot(normed_two, qkv_column, preferred_element_type=jnp.float32).astype(
        jnp.bfloat16
    )
    local_pairs = qkv_two[..., feature_count:]
    all_pairs = lax.all_gather(local_pairs, "lev", axis=1, tiled=True)
    col_queries = qkv_two[..., :feature_count].reshape(qkv_two.shape[:-1] + (head_count, head_size))
    pair_shape = all_pairs.shape[:-1] + (head_count, head_size)
    col_keys = all_pairs[..., :feature_count].reshape(pair_shape)
    col_values = all_pairs[..., feature_count:].reshape(pair_shape)
    col_out, col_log_total = column_forward(col_queries, col_keys, col_values, scale)
    column_out = col_out.reshape(normed_two.shape)
    after_column = after_window + jnp.dot(
        column_out, out_column, preferred_element_type=jnp.float32
    )
    normed_three = layer_norm(after_column, gain_three, shift_three).astype(jnp.bfloat16)
    hidden = jnp.dot(normed_three, w_up, preferred_element_type=jnp.float32)
    activated = gelu_exact(hidden).astype(jnp.bfloat16)
    result = (after_column + jnp.dot(activated, w_down, preferred_element_type=jnp.float32)).astype(
        jnp.bfloat16
    )
    grad_w_down = flat_product(activated, cot_in)
    grad_activated = jnp.dot(cot_in, w_down.T, preferred_element_type=jnp.float32)
    _, gelu_pull = jax.vjp(gelu_exact, hidden)
    grad_hidden = gelu_pull(grad_activated)[0].astype(jnp.bfloat16)
    grad_w_up = flat_product(normed_three, grad_hidden)
    grad_normed_three = jnp.dot(grad_hidden, w_up.T, preferred_element_type=jnp.float32)
    grad_col_norm, grad_gain_three, grad_shift_three = norm_backward(
        after_column, gain_three, shift_three, grad_normed_three
    )
    grad_after_column = cot_in.astype(jnp.float32) + grad_col_norm
    grad_branch_two = grad_after_column.astype(jnp.bfloat16)
    grad_out_column = flat_product(column_out, grad_branch_two)
    grad_column_out = jnp.dot(
        grad_branch_two, out_column.T, preferred_element_type=jnp.float32
    ).astype(jnp.bfloat16)
    grad_queries, grad_keys, grad_values = column_backward(
        col_queries,
        col_keys,
        col_values,
        col_log_total,
        grad_column_out.reshape(col_queries.shape),
        scale,
    )
    pair_terms = jnp.concatenate(
        [
            grad_keys.reshape(all_pairs.shape[:-1] + (feature_count,)),
            grad_values.reshape(all_pairs.shape[:-1] + (feature_count,)),
        ],
        axis=-1,
    )
    pair_grads = lax.psum_scatter(
        pair_terms.astype(jnp.bfloat16), "lev", scatter_dimension=1, tiled=True
    )
    grad_qkv_two = jnp.concatenate(
        [grad_queries.reshape(normed_two.shape).astype(jnp.bfloat16), pair_grads], axis=-1
    )
    grad_qkv_column = flat_product(normed_two, grad_qkv_two)
    grad_normed_two = jnp.dot(grad_qkv_two, qkv_column.T, preferred_element_type=jnp.float32)
    grad_win_norm, grad_gain_two, grad_shift_two = norm_backward(
        after_window, gain_two, shift_two, grad_normed_two
    )
    grad_after_window = grad_after_column + grad_win_norm
    grad_branch_one = grad_after_window.astype(jnp.bfloat16)
    grad_out_window = flat_product(unrolled, grad_branch_one)
    grad_unrolled = jnp.dot(
        grad_branch_one, out_window.T, preferred_element_type=jnp.float32
    ).astype(jnp.bfloat16)
    ahead_grad = shifted(grad_unrolled[:, :, :, :half_window], "lon", -1)
    grad_attended = slide_columns(
        jnp.concatenate([grad_unrolled, ahead_grad], axis=3), offsets, slab_cols
    )
    grad_att_win = to_windows(grad_attended).reshape(win_shape)
    attn_again = jnp.exp(
        window_scores(win_queries, win_keys, earth_bias, valid, scale) - win_log_total
    )
    grad_probs = jnp.einsum(
        "slbwqhe,slbwkhe->slbwhqk", grad_att_win, win_values, preferred_element_type=jnp.float32
    )
    row_inner = jnp.sum(grad_probs * attn_again, axis=-1, keepdims=True)
    grad_scores = (attn_again * (grad_probs - row_inner)).astype(jnp.bfloat16)
    grad_bias_full = jnp.sum(grad_scores.astype(jnp.float32), axis=(0, 1, 3))
    grad_bias_local = jnp.einsum(
        "khiajb,rab->khijr",
        grad_bias_full.reshape(local_bands, head_count, WLAT, WLON, WLAT, WLON),
        lon_table(),
        precision=lax.Precision.HIGHEST,
    )
    grad_win_q = (
        jnp.einsum(
            "slbwhqk,slbwkhe->slbwqhe", grad_scores, win_keys, preferred_element_type=jnp.float32
        )
        * scale
    )
    grad_win_k = (
        jnp.einsum(
            "slbwhqk,slbwqhe->slbwkhe", grad_scores, win_queries, preferred_element_type=jnp.float32
        )
        * scale
    )
    grad_win_v = jnp.einsum(
        "slbwhqk,slbwqhe->slbwkhe",
        attn_again.astype(jnp.bfloat16),
        grad_att_win,
        preferred_element_type=jnp.float32,
    )
    flat_shape = qkv_win.shape[:-1] + (feature_count,)
    grad_qkv_win = jnp.concatenate(
        [
            grad_win_q.reshape(flat_shape).astype(jnp.bfloat16),
            grad_win_k.reshape(flat_shape).astype(jnp.bfloat16),
            grad_win_v.reshape(flat_shape).astype(jnp.bfloat16),
        ],
        axis=-1,
    )
    grad_qkv_one = from_windows(grad_qkv_win)
    grad_qkv_window = flat_product(rolled, grad_qkv_one)
    grad_rolled = jnp.dot(grad_qkv_one, qkv_window.T, preferred_element_type=jnp.float32)
    behind_grad = shifted(
        grad_rolled[:, :, :, slab_cols - half_window :].astype(jnp.bfloat16), "lon", 1
    ).astype(jnp.float32)
    grad_normed_one = slide_columns(
        jnp.concatenate([behind_grad, grad_rolled], axis=3), half_window - offsets, slab_cols
    )
    grad_input_norm, grad_gain_one, grad_shift_one = norm_backward(
        residual, gain_one, shift_one, grad_normed_one
    )
    input_grad = (grad_after_window + grad_input_norm).astype(jnp.bfloat16)
    summed = lax.psum(
        (
            grad_gain_one,
            grad_shift_one,
            grad_qkv_window,
            grad_out_window,
            grad_bias_local,
            grad_gain_two,
            grad_shift_two,
            grad_qkv_column,
            grad_out_column,
            grad_gain_three,
            grad_shift_three,
            grad_w_up,
            grad_w_down,
        ),
        ("lon", "lev"),
    )
    return (
        result,
        input_grad,
        summed[0],
        summed[1],
        summed[2],
        summed[3],
        summed[4],
        summed[5],
        summed[6],
        summed[7],
        summed[8],
        summed[9],
        summed[10],
        summed[11],
        summed[12],
    )


def solution(mesh):
    return jax.shard_map(
        on_device,
        mesh=mesh,
        in_specs=(
            P(None, "lev", None, "lon", None),
            P(None, "lev", None, "lon", None),
            P(),
            P(),
            P(),
            P(),
            P(),
            P(),
            P(),
            P(),
            P(),
            P(),
            P(),
            P(),
            P(),
            P(),
            P(),
        ),
        out_specs=(
            P(None, "lev", None, "lon", None),
            P(None, "lev", None, "lon", None),
            P(),
            P(),
            P(),
            P(),
            P(),
            P(),
            P(),
            P(),
            P(),
            P(),
            P(),
            P(),
            P(),
        ),
        check_vma=False,
    )
```

profile of v0, /device:TPU:0, one launch (start us, length us, event | category | flops | bytes accessed | tf_op | source)
XLA Modules:
  0.0 991.3 jit_solution(14046505055564555147)
XLA Ops:
  14.5 4.5 collective-permute-start
  19.4 7.0 convolution_bitcast_fusion
  26.6 18.3 %copy.242 = f32[8,6,6,12,6,12]{3,2,5,4,1,0:T(8,128)} copy(f32[8,6,6,12,6,12]{5,0,4,2,1,3:T(8,128)} %convolution_bitcast_fusion) | data formatting | bytes 1990656 | tf_op jit(solution)/shard_map/add | solution.py:100
  44.9 8.2 reshape.470
  64.6 4.5 fusion.106
  69.1 3.9 copy.171
  73.0 3.9 copy.170
  76.9 4.0 copy.169
  80.9 4.6 fusion.107
  89.9 4.6 copy.175
  94.5 6.2 reshape_transpose_reshape_reshape.3
  101.0 11.1 %collective-permute-done.1 = bf16[2,2,48,6,192]{4,2,1,0,3:T(8,128)(2,1)S(1)} collective-permute-done((bf16[2,2,48,6,192]{4,2,1,0,3:T(8,128)(2,1)S(1)}, bf16[2,2,48,6,192]{4,2,1,0,3:T(8,128)(2,1)S(1)}, u32[]{:S(2)}, u32[]{:S(2)}) %collective-permute-start.1) | collective-permute-done | bytes 442400 | tf_op jit(solution)/shard_map/ppermute | solution.py:17
  125.1 4.0 copy.180
  129.1 8.9 copy.182
  138.0 59.7 %all-gather.2.cloned.1.call-done = bf16[2,8,48,12,384]{4,2,3,1,0:T(8,128)(2,1)} async-done(((bf16[2,2,48,12,384]{4,2,3,1,0:T(8,128)(2,1)}), bf16[2,8,48,12,384]{4,2,3,1,0:T(8,128)(2,1)}) %all-gather.2.cloned.1.call-update) | async-done | bytes 7077904 | tf_op jit(solution)/shard_map/all_gather | solution.py:229
  197.7 10.3 %fusion.105 = (bf16[2,8,48,12,192]{4,2,3,1,0:T(8,128)(2,1)}, bf16[2,8,48,12,192]{4,2,3,1,0:T(8,128)(2,1)}) fusion(bf16[2,8,48,12,384]{4,2,3,1,0:T(8,128)(2,1)} %all-gather.2.cloned.1.call-done), kind=kLoop, calls=%fused_computation.198 | loop fusion | bytes 14155776 | tf_op jit(solution)/shard_map/slice | solution.py:232
  208.1 10.9 %copy.181 = bf16[2,8,48,12,192]{2,4,3,1,0:T(8,128)(2,1)} copy(bf16[2,8,48,12,192]{4,2,3,1,0:T(8,128)(2,1)} %get-tuple-element.77) | data formatting | bytes 7077888 | tf_op jit(solution)/shard_map/slice | solution.py:232
  219.0 16.2 %copy.183 = bf16[2,8,48,12,6,32]{5,1,4,3,2,0:T(8,128)(2,1)} copy(bf16[2,8,48,12,6,32]{2,5,4,3,1,0:T(8,128)(2,1)} %bitcast.208) | data formatting | bytes 7077888 | tf_op jit(solution)/shard_map/reshape | solution.py:232
  235.2 10.9 %copy.179 = bf16[2,8,48,12,192]{2,4,3,1,0:T(8,128)(2,1)} copy(bf16[2,8,48,12,192]{4,2,3,1,0:T(8,128)(2,1)} %get-tuple-element.78) | data formatting | bytes 7077888 | tf_op jit(solution)/shard_map/slice | solution.py:233
  246.1 16.3 %copy.184 = bf16[2,8,48,12,6,32]{5,1,4,3,2,0:T(8,128)(2,1)} copy(bf16[2,8,48,12,6,32]{2,5,4,3,1,0:T(8,128)(2,1)} %bitcast.209) | data formatting | bytes 7077888 | tf_op jit(solution)/shard_map/reshape | solution.py:233
  262.3 16.6 %fusion.109 = (f32[2,48,12,6,2]{4,3,2,1,0:T(8,128)}, f32[2,48,12,6,2,8]{5,4,3,2,1,0:T(2,128)}) fusion(bf16[2,2,48,12,6,32]{5,1,4,3,2,0:T(2,128)(2,1)} %copy.182, bf16[2,8,48,12,6,32]{5,1,4,3,2,0:T(8,128)(2,1)} %copy.183), kind=kOutput, calls=%fused_computation.202 | convolution fusion | flops 7285248 | bytes 4921344 | tf_op jit(solution)/shard_map/slache,smache->sachlm/dot_general | solution.py:106
  278.9 21.1 %fusion.12 = f32[2,48,12,6,2]{4,3,2,1,0:T(8,128)} fusion(f32[2,48,12,6,2,8]{5,4,3,2,1,0:T(2,128)} %get-tuple-element.89, f32[2,48,12,6,2]{4,3,2,1,0:T(8,128)} %get-tuple-element.88), kind=kLoop, calls=%fused_computation.51 | loop fusion | flops 207360 | bytes 552960 | tf_op jit(solution)/shard_map/reduce_sum | solution.py:115
  300.0 6.0 log_add_fusion
  307.5 21.0 %fusion.9 = bf16[2,2,48,12,6,32]{5,1,4,3,2,0:T(2,128)(2,1)} fusion(bf16[2,8,48,12,6,32]{5,1,4,3,2,0:T(8,128)(2,1)} %copy.184, f32[2,48,12,6,2,8]{5,4,3,2,1,0:T(2,128)S(1)} %copy-done.8, f32[2,48,12,6,2]{4,3,2,1,0:T(8,128)S(1)} %copy-done.13, f32[2,48,12,6,2]{4,3,2,1,0:T(8,128)S(1)} %copy-done.12), kind=kOutput, calls=%fused_computation.46 | convolution fusion | flops 7852032 | bytes 4976640 | tf_op jit(solution)/shard_map/sachlm,smache->slache/dot_general | solution.py:118
  328.6 9.2 copy.185
  344.4 16.6 %multiply_convert_fusion.3 = (bf16[2,2,48,12,768]{4,2,3,1,0:T(8,128)(2,1)}, f32[2,2,48,12,768]{4,2,3,1,0:T(8,128)S(1)}) fusion(f32[2,2,48,12,768]{4,2,3,1,0:T(8,128)S(1)} %get-tuple-element.92, u16[2,2,48,768]{3,2,1,0:T(8,128)(2,1)S(1)} %get-tuple-element.46, u16[2,2,48,768]{3,2,1,0:T(8,128)(2,1)S(1)} %get-tuple-element.45), kind=kLoop, calls=%fused_computation.25 | loop fusion | flops 123863040 | bytes 18284544 | tf_op jit(solution)/shard_map/convert_element_type | solution.py:241
  372.9 8.8 copy.188
  381.7 24.4 %multiply_reduce_fusion.1 = (f32[2,48,12,6,2]{4,3,2,1,0:T(8,128)}, f32[2,48,12,6,2,8]{5,4,3,2,1,0:T(2,128)}) fusion(f32[2,48,12,6,2,8]{5,4,3,2,1,0:T(2,128)} %get-tuple-element.89, f32[2,48,12,6,2]{4,3,2,1,0:T(8,128)} %log_add_fusion, bf16[2,2,48,12,6,32]{5,1,4,3,2,0:T(2,128)(2,1)} %copy.188, bf16[2,8,48,12,6,32]{5,1,4,3,2,0:T(8,128)(2,1)} %copy.184), kind=kOutput, calls=%fused_computation.22 | convolution fusion | flops 7395840 | bytes 5419008 | tf_op jit(solution)/shard_map/slache,smache->sachlm/dot_general | solution.py:129
  406.1 19.5 %convert_bitcast_fusion = bf16[2,8,48,12,6,32]{5,1,4,3,2,0:T(8,128)(2,1)} fusion(bf16[2,2,48,12,6,32]{5,1,4,3,2,0:T(2,128)(2,1)S(1)} %copy-done.37, f32[2,48,12,6,2,8]{5,4,3,2,1,0:T(2,128)} %get-tuple-element.89, f32[2,48,12,6,2]{4,3,2,1,0:T(8,128)S(1)} %bitcast.213), kind=kOutput, calls=%fused_computation.5 | convolution fusion | flops 9068544 | bytes 4921344 | tf_op jit(solution)/shard_map/sachlm,slache->smache/dot_general | solution.py:144
  425.6 17.1 %copy.195 = bf16[2,8,48,12,6,32]{2,5,4,3,1,0:T(8,128)(2,1)} copy(bf16[2,8,48,12,6,32]{5,1,4,3,2,0:T(8,128)(2,1)} %convert_bitcast_fusion) | data formatting | bytes 7077888 | tf_op jit(solution)/shard_map/sachlm,slache->smache/transpose | solution.py:144
  442.7 11.2 %copy.197 = bf16[2,8,48,12,192]{4,2,3,1,0:T(8,128)(2,1)} copy(bf16[2,8,48,12,192]{2,4,3,1,0:T(8,128)(2,1)} %bitcast.210) | data formatting | bytes 7077888 | tf_op jit(solution)/shard_map/reshape | solution.py:271
  453.9 21.1 %multiply_convert_fusion.2 = bf16[2,48,12,6,2,8]{5,4,3,2,1,0:T(2,128)(2,1)S(1)} fusion(f32[2,48,12,6,2,8]{5,4,3,2,1,0:T(2,128)} %get-tuple-element.95, f32[2,48,12,6,2]{4,3,2,1,0:T(8,128)} %get-tuple-element.94, f32[2,48,12,6,2,8]{5,4,3,2,1,0:T(2,128)} %get-tuple-element.89, f32[2,48,12,6,2]{4,3,2,1,0:T(8,128)} %log_add_fusion), kind=kLoop, calls=%fused_computation.21 | loop fusion | flops 442368 | bytes 1216512 | tf_op jit(solution)/shard_map/convert_element_type | solution.py:133
  476.8 10.9 %fusion = bf16[2,8,48,12,6,32]{5,1,4,3,2,0:T(8,128)(2,1)} fusion(bf16[2,2,48,12,6,32]{5,1,4,3,2,0:T(2,128)(2,1)S(1)} %copy-done.36, bf16[2,48,12,6,2,8]{5,4,3,2,1,0:T(2,128)(2,1)S(1)} %multiply_convert_fusion.2), kind=kOutput, calls=%fused_computation.6 | convolution fusion | flops 10616832 | bytes 4644864 | tf_op jit(solution)/shard_map/sachlm,slache->smache/dot_general | solution.py:139
  487.7 17.1 %copy.193 = bf16[2,8,48,12,6,32]{2,5,4,3,1,0:T(8,128)(2,1)} copy(bf16[2,8,48,12,6,32]{5,1,4,3,2,0:T(8,128)(2,1)} %fusion) | data formatting | bytes 7077888 | tf_op jit(solution)/shard_map/mul | solution.py:139
  504.7 11.2 %copy.196 = bf16[2,8,48,12,192]{4,2,3,1,0:T(8,128)(2,1)} copy(bf16[2,8,48,12,192]{2,4,3,1,0:T(8,128)(2,1)} %bitcast.211) | data formatting | bytes 7077888 | tf_op jit(solution)/shard_map/reshape | solution.py:270
  515.9 9.4 pad_maximum_fusion
  529.0 3.9 reshape.420
  533.0 4.9 copy.221
  539.4 6.5 reshape_reshape.3
  547.5 12.6 %fusion.10 = bf16[2,2,48,12,6,32]{5,1,4,3,2,0:T(2,128)(2,1)} fusion(bf16[2,8,48,12,6,32]{5,1,4,3,2,0:T(8,128)(2,1)} %copy.183, bf16[2,48,12,6,2,8]{5,4,3,2,1,0:T(2,128)(2,1)} %copy-done.33), kind=kOutput, calls=%fused_computation.47 | convolution fusion | flops 7962624 | bytes 4644864 | tf_op jit(solution)/shard_map/sachlm,smache->slache/dot_general | solution.py:135
  560.1 7.5 copy.191
  572.8 4.2 convolution_bitcast_fusion.3
  582.9 94.0 %all-reduce.6.cloned.1.call-done = bf16[2,8,48,12,384]{4,2,3,1,0:T(8,128)(2,1)} async-done(((bf16[2,8,48,12,384]{4,2,3,1,0:T(8,128)(2,1)}), bf16[2,8,48,12,384]{4,2,3,1,0:T(8,128)(2,1)}) %all-reduce.6.cloned.1.call-update) | async-done | bytes 7077904
  692.1 4.6 collective-permute-done.2
  701.5 3.8 reshape.419
  705.3 4.0 copy.201
  709.4 6.3 fusion.53
  715.6 5.4 multiply_reduce_fusion
  721.1 4.2 convert_reduce_fusion
  730.8 4.5 copy.208
  735.3 7.0 convert_element_type.214
  747.5 5.9 copy.205
  753.4 7.4 convert_element_type.209
  763.3 5.9 copy.203
  769.2 7.0 convert_element_type.205
  782.9 8.5 reshape.421
  791.3 20.2 %convolution_bitcast_fusion.1 = f32[8,6,6,6,23]{4,3,2,1,0:T(8,128)} fusion(f32[8,6,6,12,6,12]{5,4,3,2,1,0:T(8,128)} %reshape.421, s32[12,12]{1,0:T(8,128)S(1)} %copy-done.69), kind=kOutput, calls=%fused_computation.123 | convolution fusion | flops 68680944 | bytes 1154880 | tf_op jit(solution)/shard_map/khiajb,rab->khijr/dot_general | solution.py:306
  820.9 3.4 convert_element_type.217
  824.3 3.6 convert_element_type.218
  827.9 3.5 fusion.34
  841.0 3.3 fusion.42
  844.3 40.0 %all-reduce.1 = (f32[192]{0:T(256)}, f32[192]{0:T(256)}, f32[192]{0:T(256)}, f32[192]{0:T(256)}, f32[192]{0:T(256)}, /*index=5*/f32[192]{0:T(256)}) all-reduce(f32[192]{0:T(256)S(1)} %get-tuple-element.51, f32[192]{0:T(256)S(1)} %reduce_sum.231, f32[192]{0:T(256)S(1)} %get-tuple-element.47, ...), channel_id=1, replica_groups=mesh['lon'=8,'lev'=4] {'lon','lev'}, use_global_device_ids=true, to_apply=%region_20.21 | all-reduce | flops 1152 | bytes 9216 | tf_op jit(solution)/shard_map/psum | solution.py:352
  884.3 4.4 add_convert_fusion.1
  888.6 87.4 %all-reduce.8.cloned.1.call-done = (f32[192,576]{1,0:T(8,128)}, f32[192,192]{1,0:T(8,128)}, f32[8,6,6,6,23]{4,3,2,1,0:T(8,128)}, f32[192,576]{1,0:T(8,128)}, f32...) async-done(((f32[192,576]{1,0:T(8,128)}, f32[192,192]{1,0:T(8,128)}, f32[8,6,6,6,23]{4,3,2,1,0:T(8,128)}, f32[192,576]{1,0:T(8,128)}, f32[192,192]{1,0:T(8,128)}, ...) | async-done | bytes 2518288 | tf_op jit(solution)/shard_map/psum | solution.py:352
  (290 shorter events, 142.8 us)
Async XLA Ops:
  7.2 12.2 %copy-start = (f32[8,6,6,6,23]{4,0,3,2,1:T(8,128)S(1)}, f32[8,6,6,6,23]{4,0,3,2,1:T(8,128)}, u32[]{:S(2)}) copy-start(f32[8,6,6,6,23]{4,0,3,2,1:T(8,128)} %param.25) | copy-start | bytes 476932
  7.2 3.9 copy-start.7
  7.2 11.8 %copy-start.81 = (s32[2,2]{1,0:T(2,128)S(1)}, s32[2,2]{1,0:T(2,128)}, u32[]{:S(2)}) copy-start(s32[2,2]{1,0:T(2,128)} %param.19) | copy-start | bytes 52
  7.2 12.1 %copy-start.85 = (s32[2]{0:T(128)S(1)}, s32[2]{0:T(128)}, u32[]{:S(2)}) copy-start(s32[2]{0:T(128)} %param.20) | copy-start | bytes 28
  7.2 190.5 %all-gather.2.cloned.1.call-start = ((), (), s32[]{:S(2)}) async-start(), calls=%async_computation | async-start | bytes 8847360 | tf_op jit(solution)/shard_map/all_gather | solution.py:229
  9.1 5.4 copy-start.40
  11.1 7.9 copy-start.60
  11.1 7.9 copy-start.47
  14.5 38.6 %collective-permute-start = (bf16[2,2,48,6,192]{4,2,3,1,0:T(8,128)(2,1)}, bf16[2,2,48,6,192]{4,2,3,1,0:T(8,128)(2,1)S(1)}, u32[]{:S(2)}, u32[]{:S(2)}) collective-permute-start(bf16[2,2,48,6,192]{4,2,3,1,0:T(8,128)(2,1)} %slice.84), channel_id=1, source_target_pairs={{4,0},{8,4},{12,8},{16,12},{20,16},{24,20},{28,24},{0,28},{5,1},{9... | collective-permute-start | bytes 1327112 | tf_op jit(solution)/shard_map/ppermute | solution.py:17
  19.0 7.4 copy-start.68
  53.1 59.3 %copy-start.76 = (s32[2]{0:T(128)}, s32[2]{0:T(128)S(1)}, u32[]{:S(2)}) copy-start(s32[2]{0:T(128)S(1)} %get-tuple-element.82) | copy-start | bytes 28
  54.7 4.6 copy-start.64
  101.0 13.1 %copy-start.55 = (bf16[192,192]{1,0:T(8,128)(2,1)S(1)}, bf16[192,192]{1,0:T(8,128)(2,1)}, u32[]{:S(2)}) copy-start(bf16[192,192]{1,0:T(8,128)(2,1)} %param.24) | copy-start | bytes 221188
  101.0 11.2 %collective-permute-start.1 = (bf16[2,2,48,6,192]{4,2,1,0,3:T(8,128)(2,1)S(1)}, bf16[2,2,48,6,192]{4,2,1,0,3:T(8,128)(2,1)S(1)}, u32[]{:S(2)}, u32[]{:S(2)}) collective-permute-start(bf16[2,2,48,6,192]{4,2,1,0,3:T(8,128)(2,1)S(1)} %slice.88), channel_id=1, source_target_pairs={{28,0},{0,4},{4,8},{8,12},{12,16},{16,20},{20,24},{24,28},{29,1},{... | collective-permute-start | bytes 1327112 | tf_op jit(solution)/shard_map/ppermute | solution.py:17
  116.3 221.5 %copy-start.3 = (f32[2,2,48,12,192]{4,2,3,1,0:T(8,128)}, f32[2,2,48,12,192]{4,2,3,1,0:T(8,128)S(1)}, u32[]{:S(2)}) copy-start(f32[2,2,48,12,192]{4,2,3,1,0:T(8,128)S(1)} %get-tuple-element.87) | copy-start | bytes 5308420
  117.1 5.6 copy-start.57
  117.1 5.5 copy-start.49
  122.6 554.2 %all-reduce.6.cloned.1.call-start = ((), (), s32[]{:S(2)}) async-start(), calls=%async_computation.1 | async-start | bytes 14155776
  278.9 21.2 %copy-start.12 = (f32[2,48,12,6,2]{4,3,2,1,0:T(8,128)S(1)}, f32[2,48,12,6,2]{4,3,2,1,0:T(8,128)}, u32[]{:S(2)}) copy-start(f32[2,48,12,6,2]{4,3,2,1,0:T(8,128)} %get-tuple-element.88) | copy-start | bytes 165892
  300.0 6.0 copy-start.8
  300.0 7.5 copy-start.13
  328.6 9.2 copy-start.54
  337.8 3.7 copy-start.73
  337.8 3.7 copy-start.78
  337.8 3.7 copy-start.84
  340.7 25.7 %copy-start.5 = (f32[2,2,48,12,192]{4,2,3,1,0:T(8,128)}, f32[2,2,48,12,192]{4,2,3,1,0:T(8,128)S(1)}, u32[]{:S(2)}) copy-start(f32[2,2,48,12,192]{4,2,3,1,0:T(8,128)S(1)} %get-tuple-element.91) | copy-start | bytes 5308420
  344.4 16.6 %copy-start.29 = (bf16[2,2,48,12,192]{4,2,3,1,0:T(8,128)(2,1)S(1)}, bf16[2,2,48,12,192]{4,2,3,1,0:T(8,128)(2,1)}, u32[]{:S(2)}) copy-start(bf16[2,2,48,12,192]{4,2,3,1,0:T(8,128)(2,1)} %param.18) | copy-start | bytes 2654212
  344.4 16.6 %copy-start.59 = (bf16[768,192]{0,1:T(8,128)(2,1)S(1)}, bf16[768,192]{0,1:T(8,128)(2,1)}, u32[]{:S(2)}) copy-start(bf16[768,192]{0,1:T(8,128)(2,1)} %param.33) | copy-start | bytes 884740
  372.9 33.3 %slice-start.2 = ((s8[4718592]{0:T(1024)(128)(4,1)}), s8[524288]{0:T(1024)(128)(4,1)S(1)}, s32[]{:S(2)}) async-start(s8[4718592]{0:T(1024)(128)(4,1)} %bitcast.212), calls=%async_computation.5 | async-start | bytes 1048576
  381.7 24.5 %slice-start.3 = ((s8[4718592]{0:T(1024)(128)(4,1)}), s8[4194304]{0:T(1024)(128)(4,1)S(1)}, s32[]{:S(2)}) async-start(s8[4718592]{0:T(1024)(128)(4,1)} %bitcast.212), calls=%async_computation.6 | async-start | bytes 8388608
  381.7 24.5 %copy-start.37 = (bf16[2,2,48,12,6,32]{5,1,4,3,2,0:T(2,128)(2,1)S(1)}, bf16[2,2,48,12,6,32]{5,1,4,3,2,0:T(2,128)(2,1)}, u32[]{:S(2)}) copy-start(bf16[2,2,48,12,6,32]{5,1,4,3,2,0:T(2,128)(2,1)} %copy.188) | copy-start | bytes 2654212
  453.9 22.9 %copy-start.36 = (bf16[2,2,48,12,6,32]{5,1,4,3,2,0:T(2,128)(2,1)S(1)}, bf16[2,2,48,12,6,32]{5,1,4,3,2,0:T(2,128)(2,1)}, u32[]{:S(2)}) copy-start(bf16[2,2,48,12,6,32]{5,1,4,3,2,0:T(2,128)(2,1)} %copy.182) | copy-start | bytes 2654212
  525.3 7.6 copy-start.39
  525.3 7.6 copy-start.52
  525.3 450.7 %all-reduce.8.cloned.1.call-start = ((), (), s32[]{:S(2)}) async-start(), calls=%async_computation.2 | async-start | bytes 7471104 | tf_op jit(solution)/shard_map/psum | solution.py:352
  539.4 6.5 copy-start.28
  569.8 7.2 copy-start.17
  572.8 4.2 copy-start.6
  577.0 3.3 copy-start.35
  580.3 98.4 %copy-start.44 = (f32[2,2,48,12]{2,3,1,0:T(8,128)S(1)}, f32[2,2,48,12]{2,3,1,0:T(8,128)}, u32[]{:S(2)}) copy-start(f32[2,2,48,12]{2,3,1,0:T(8,128)} %copy-done.43) | copy-start | bytes 27652
  580.3 98.4 %copy-start.63 = (bf16[192,576]{1,0:T(8,128)(2,1)S(1)}, bf16[192,576]{1,0:T(8,128)(2,1)}, u32[]{:S(2)}) copy-start(bf16[192,576]{1,0:T(8,128)(2,1)} %param.28) | copy-start | bytes 663556
  580.3 98.4 %copy-start.71 = (f32[192]{0:T(256)S(1)}, f32[192]{0:T(256)}, u32[]{:S(2)}) copy-start(f32[192]{0:T(256)} %param.26) | copy-start | bytes 2308
  582.9 95.8 %copy-start.4 = (f32[2,2,48,12,192]{4,2,3,1,0:T(8,128)S(1)}, f32[2,2,48,12,192]{4,2,3,1,0:T(8,128)}, u32[]{:S(2)}) copy-start(f32[2,2,48,12,192]{4,2,3,1,0:T(8,128)} %copy-done.3) | copy-start | bytes 5308420
  686.0 3.4 copy-start.80
  686.5 10.2 %collective-permute-start.2 = (bf16[2,2,48,6,192]{4,2,3,1,0:T(8,128)(2,1)S(1)}, bf16[2,2,48,6,192]{4,2,3,1,0:T(8,128)(2,1)S(1)}, u32[]{:S(2)}, u32[]{:S(2)}) collective-permute-start(bf16[2,2,48,6,192]{4,2,3,1,0:T(8,128)(2,1)S(1)} %slice.93), channel_id=1, source_target_pairs={{4,0},{8,4},{12,8},{16,12},{20,16},{24,20},{28,24},{0,28},{5,1},{9... | collective-permute-start | bytes 1327112 | tf_op jit(solution)/shard_map/ppermute | solution.py:17
  692.1 6.4 copy-start.75
  709.3 6.3 copy-start.25
  709.4 11.7 %slice-start = ((s8[7077888]{0:T(1024)(128)(4,1)}), s8[4194304]{0:T(1024)(128)(4,1)S(1)}, s32[]{:S(2)}) async-start(s8[7077888]{0:T(1024)(128)(4,1)} %bitcast.206), calls=%async_computation.3 | async-start | bytes 8388608
  715.6 5.4 slice-start.1
  721.1 4.2 copy-start.19
  769.2 8.5 copy-start.65
  782.8 8.5 copy-start.69
  782.8 48.7 %collective-permute-start.3 = (bf16[2,2,48,6,192]{4,2,3,1,0:T(8,128)(2,1)}, bf16[2,2,48,6,192]{4,2,3,1,0:T(8,128)(2,1)}, u32[]{:S(2)}, u32[]{:S(2)}) collective-permute-start(bf16[2,2,48,6,192]{4,2,3,1,0:T(8,128)(2,1)} %slice.98), channel_id=1, source_target_pairs={{28,0},{0,4},{4,8},{8,12},{12,16},{16,20},{20,24},{24,28},{29,1},{... | collective-permute-start | bytes 1327112 | tf_op jit(solution)/shard_map/ppermute | solution.py:17
  811.5 4.4 copy-start.15
  813.7 4.4 copy-start.26
  820.9 3.4 copy-start.27
  840.6 3.7 copy-start.82
  840.6 3.7 copy-start.83
  976.0 4.7 copy-start.67
  976.0 5.4 copy-start.53
  976.0 6.2 copy-start.66
  976.0 6.9 copy-start.46
  976.0 7.7 copy-start.45
  976.0 8.5 copy-start.1
  (34 other events, 74.4 us)
Sparse Core Ops, SparseCore 0:
  122.8 74.9 all-gather.1
  525.4 151.4 all-reduce.5
  831.6 144.3 all-reduce.7
where the time goes:
time: 1010 us; the launch traced here: 991 us
  local copies, waits for them, and re-layouts  366 us (36%)
  waiting for transfers between devices  257 us (25%)
  matrix products  198 us (20%)
  other arithmetic  107 us (11%)
  blocking collectives  40 us (4%)
  between operations  15.9 us (2%)
    unnamed x4, waiting for transfers between devices  94 us
    psum x1, waiting for transfers between devices, on_device(): lax.psum((grad_gain_one, grad_shift_one, grad_qkv_window, grad_out_window...  87.4 us
    all_gather x1, waiting for transfers between devices, on_device(): all_pairs = lax.all_gather(local_pairs, 'lev', axis=1, tiled=True)  59.7 us
    psum x1, blocking collectives, on_device(): lax.psum((grad_gain_one, grad_shift_one, grad_qkv_window, grad_out_window...  40 us
    add x2, local copies, waits for them, and re-layouts, window_scores(): raw_scores = raw_scores + earth_bias[None, None, :, None]  26.5 us
    dot_general x1, matrix products, column_backward(): jnp.einsum('slache,smache->sachlm', grad_out, values, preferred_element_t...  24.4 us
    unnamed x191, local copies, waits for them, and re-layouts  23.1 us
    convert_element_type x5, local copies, waits for them, and re-layouts, on_device(): grad_win_k.reshape(flat_shape).astype(jnp.bfloat16)  21.6 us
  transfers between devices with their start and end apart: 7, of which 5 were waited for; matrix products, arithmetic and copies ran while one was open for 17% of the time, Pallas kernels for 0%

commit v1 on v0

v1 whole, which is shorter than its diff:
```python
import functools

import jax
import jax.numpy as jnp
import numpy as np
from jax import lax
from jax.experimental import pallas as pl
from jax.experimental.pallas import tpu as pltpu
from jax.sharding import PartitionSpec as P

WLAT = 6
WLON = 12
TOK = WLAT * WLON
HALF = TOK // 2
HALO0 = 32
HALO = TOK - HALO0
GROUP = 8
EPSILON = 1e-05
NEGATIVE = -1000000000.0
F32 = jnp.float32
BF16 = jnp.bfloat16
LANES = 128
UNIT = 16


def up16(n):
    return (n + 15) // 16 * 16


def nn(a, b, **kw):
    return lax.dot_general(a, b, (((1,), (0,)), ((), ())), preferred_element_type=F32, **kw)


def nt(a, b):
    return lax.dot_general(a, b, (((1,), (1,)), ((), ())), preferred_element_type=F32)


def tn(a, b):
    return lax.dot_general(a, b, (((0,), (0,)), ((), ())), preferred_element_type=F32)


class Sizes:
    def __init__(self, lev, lon, shape, heads, hidden):
        self.lev, self.lon = lev, lon
        self.s, self.l, self.rows, self.cells, self.d = shape
        self.heads, self.ff = heads, hidden
        self.bands = self.rows // WLAT
        self.nb = self.bands // lev
        self.lt = self.l * lev
        self.n = self.lt * TOK
        self.ro = up16(self.nb * TOK)
        self.rh = up16(self.nb * HALO)
        self.nblk = self.l + (self.l + 1) // 2
        self.tokens = self.cells * self.rows
        self.np = 2 * lev
        self.blocks = 2 * (2 * hidden // 2 + 3 * self.d + self.d) // LANES * (self.d // 96)
        self.hb = self.blocks // self.np
        self.units = self.bands * 4 + 2
        self.upp = -(-self.units // self.np)
        self.pr = self.hb * 96 + self.upp * UNIT


def slot_rows(z):
    own = np.full((z.ro,), -(10**6), np.int32)
    halo = np.full((z.rh,), -(10**6), np.int32)
    for b in range(z.nb):
        for t in range(TOK):
            own[b * TOK + t] = (t // WLAT) * z.rows + b * WLAT + t % WLAT
            if t >= HALF:
                halo[b * HALO + t - HALO0] = own[b * TOK + t] - z.tokens
    return own, halo


def pack_kernel(z, scal, own_base, halo_base, x_ref, *rest):
    own_refs, halo_refs, onehot = rest[: z.lev], rest[z.lev : 2 * z.lev], rest[2 * z.lev]
    p = scal[0]
    off = scal[1 + pl.program_id(0)]
    span = z.ro + z.rh
    for k in range(z.lev):
        add = off * z.rows + (p ^ k) * (z.nb * WLAT)
        for base, at, size in ((own_base, 0, z.ro), (halo_base, z.ro, z.rh)):
            hit = lax.broadcasted_iota(jnp.int32, (size, z.tokens), 1) == base[...] + add
            onehot[k * span + at : k * span + at + size] = jnp.where(hit, 1.0, 0.0).astype(BF16)
    parts, high = [], []
    for l in range(z.l):
        x = x_ref[0, l].reshape(z.tokens, z.d)
        parts.append(x[:, :LANES])
        high.append(x[:, LANES:])
    if z.l % 2:
        high.append(jnp.zeros_like(high[0]))
    for l in range(0, len(high), 2):
        parts.append(jnp.concatenate([high[l], high[l + 1]], axis=1))
    moved = nn(onehot[...], jnp.concatenate(parts, axis=1)).astype(BF16)
    for k in range(z.lev):
        for j in range(z.nblk):
            piece = moved[k * span : (k + 1) * span, j * LANES : (j + 1) * LANES]
            own_refs[k][0, j] = piece[: z.ro]
            halo_refs[k][0, j] = piece[z.ro :]


def pack(z, x, scal, interpret=False):
    own, halo = slot_rows(z)
    shapes = [jax.ShapeDtypeStruct((z.s, z.nblk, z.ro, LANES), BF16)] * z.lev
    shapes += [jax.ShapeDtypeStruct((z.s, z.nblk, z.rh, LANES), BF16)] * z.lev
    spec = lambda r: pl.BlockSpec((1, z.nblk, r, LANES), lambda s, _: (s, 0, 0, 0))
    whole = lambda r: pl.BlockSpec((r, 1), lambda s, _: (0, 0))
    out = pl.pallas_call(
        functools.partial(pack_kernel, z),
        grid_spec=pltpu.PrefetchScalarGridSpec(
            num_scalar_prefetch=1,
            grid=(z.s,),
            in_specs=[
                whole(z.ro),
                whole(z.rh),
                pl.BlockSpec((1, z.l, z.cells, z.rows, z.d), lambda s, _: (s, 0, 0, 0, 0)),
            ],
            out_specs=[spec(z.ro)] * z.lev + [spec(z.rh)] * z.lev,
            scratch_shapes=[pltpu.VMEM((z.lev * (z.ro + z.rh), z.tokens), BF16)],
        ),
        out_shape=shapes,
        compiler_params=pltpu.CompilerParams(vmem_limit_bytes=60 * 2**20),
        name="pack",
    )(scal, jnp.asarray(own)[:, None], jnp.asarray(halo)[:, None], x)
    return out[: z.lev], out[z.lev :]


def unpack_kernel(z, scal, base, *rest):
    pieces, out_ref, onehot = rest[: 2 * z.lev], rest[2 * z.lev], rest[2 * z.lev + 1]
    p = scal[0]
    off = scal[1 + pl.program_id(0)]
    span = z.ro + z.rh
    for k in range(z.lev):
        add = off * z.rows + (p ^ k) * (z.nb * WLAT)
        row = lax.broadcasted_iota(jnp.int32, (z.tokens, span), 0)
        hit = row == base[...] + add
        onehot[:, k * span : (k + 1) * span] = jnp.where(hit, 1.0, 0.0).astype(BF16)
    columns = []
    for j in range(z.nblk):
        rows = []
        for k in range(z.lev):
            rows += [pieces[k][0, j], pieces[z.lev + k][0, j]]
        columns.append(jnp.concatenate(rows, axis=0))
    moved = nn(onehot[...], jnp.concatenate(columns, axis=1))
    half = z.d - LANES
    for l in range(z.l):
        low = moved[:, l * LANES : (l + 1) * LANES]
        at = (z.l + l // 2) * LANES + (l % 2) * half
        tokens = jnp.concatenate([low, moved[:, at : at + half]], axis=1)
        out_ref[0, l] = tokens.reshape(z.cells, z.rows, z.d).astype(BF16)


def unpack(z, own, halo, scal):
    own_rows, halo_rows = slot_rows(z)
    base = jnp.asarray(np.concatenate([own_rows, halo_rows]))[None]
    spec = lambda r: pl.BlockSpec((1, z.nblk, r, LANES), lambda s, _: (s, 0, 0, 0))
    span = z.ro + z.rh
    return pl.pallas_call(
        functools.partial(unpack_kernel, z),
        grid_spec=pltpu.PrefetchScalarGridSpec(
            num_scalar_prefetch=1,
            grid=(z.s,),
            in_specs=[pl.BlockSpec((1, span), lambda s, _: (0, 0))]
            + [spec(z.ro)] * z.lev
            + [spec(z.rh)] * z.lev,
            out_specs=pl.BlockSpec((1, z.l, z.cells, z.rows, z.d), lambda s, _: (s, 0, 0, 0, 0)),
            scratch_shapes=[pltpu.VMEM((z.tokens, z.lev * span), BF16)],
        ),
        out_shape=jax.ShapeDtypeStruct((z.s, z.l, z.cells, z.rows, z.d), BF16),
        compiler_params=pltpu.CompilerParams(vmem_limit_bytes=60 * 2**20),
        name="unpack",
    )(scal, base, *own, *halo)


def loop(n, body):
    lax.fori_loop(0, n, lambda i, c: (body(i), c)[1], 0)


def head_masks(z):
    lane = lax.broadcasted_iota(jnp.int32, (1, z.d), 1)
    size = z.d // z.heads
    return [(lane >= h * size) & (lane < (h + 1) * size) for h in range(z.heads)]


def spread(values, masks):
    return jnp.concatenate([jnp.where(m, values, 0.0) for m in masks], axis=0).astype(BF16)


def gather_heads(stacked, masks):
    n = stacked.shape[0] // len(masks)
    total = jnp.where(masks[0], stacked[:n], 0.0)
    for h in range(1, len(masks)):
        total = jnp.where(masks[h], stacked[h * n : (h + 1) * n], total)
    return total


def attend(q, k, v, bias, masks, scale):
    scores = nt(k.astype(BF16), spread(q, masks)) * scale + bias
    exps = jnp.exp(scores - jnp.max(scores, axis=0, keepdims=True))
    probs = (exps * (1.0 / jnp.sum(exps, axis=0, keepdims=True))).astype(BF16)
    return probs, gather_heads(tn(probs, v.astype(BF16)), masks)


def attend_back(q, k, v, probs, grad_out, masks, scale):
    q_rows, g_rows = spread(q, masks), spread(grad_out, masks)
    wide = probs.astype(F32)
    grad_probs = nt(v.astype(BF16), g_rows)
    inner = jnp.sum(grad_probs * wide, axis=0, keepdims=True)
    grad_scores = (wide * (grad_probs - inner)).astype(BF16)
    grad_v = nn(probs, g_rows)
    grad_k = nn(grad_scores, q_rows) * scale
    grad_q = gather_heads(tn(grad_scores, k.astype(BF16)), masks) * scale
    return grad_q, grad_k, grad_v, grad_scores


def normalized(values):
    center = values - jnp.mean(values, axis=-1, keepdims=True)
    rstd = lax.rsqrt(jnp.mean(center * center, axis=-1, keepdims=True) + EPSILON)
    return center * rstd, rstd


def norm_back(normed, rstd, grad, gain):
    gained = grad * gain
    return rstd * (
        gained
        - jnp.mean(gained, axis=-1, keepdims=True)
        - normed * jnp.mean(gained * normed, axis=-1, keepdims=True)
    )


def fold_rows(values):
    return jnp.sum(values.reshape(values.shape[0] // 8, 8, values.shape[1]), axis=0)


def load_wire(z, own_refs, halo_refs, own_s, halo_s):
    for k in range(z.lev):
        own_s[k] = own_refs[k][0].astype(F32)
        halo_s[k] = halo_refs[k][0].astype(F32)


def wire_level(z, own_s, halo_s, k, l, b):
    half = z.d - LANES
    at = (l % 2) * half

    def rows(ref, size):
        start = pl.multiple_of(b * size, 8)
        low = ref[k, l, pl.ds(start, size), :]
        high = ref[k, z.l + l // 2, pl.ds(start, size), :]
        return jnp.concatenate([low, high[:, at : at + half]], axis=1)

    own, halo = rows(own_s, TOK), rows(halo_s, HALO)
    return jnp.concatenate([own[:HALO0], own[HALO0:] + halo], axis=0)


def store_wire_level(z, own_s, halo_s, k, b, tokens):
    parts = [t[:, :LANES] for t in tokens]
    high = [t[:, LANES:] for t in tokens]
    if z.l % 2:
        high.append(jnp.zeros_like(high[0]))
    for l in range(0, len(high), 2):
        parts.append(jnp.concatenate([high[l], high[l + 1]], axis=1))
    for j, part in enumerate(parts):
        own_s[k, j, pl.ds(pl.multiple_of(b * TOK, 8), TOK), :] = part
        halo_s[k, j, pl.ds(pl.multiple_of(b * HALO, 8), HALO), :] = part[HALO0:]


def clear_pad(z, own_s, halo_s):
    if z.ro > z.nb * TOK:
        own_s[:, :, z.nb * TOK :, :] = jnp.zeros_like(own_s[:, :, z.nb * TOK :, :])
    if z.rh > z.nb * HALO:
        halo_s[:, :, z.nb * HALO :, :] = jnp.zeros_like(halo_s[:, :, z.nb * HALO :, :])


def flush_wire(z, own_s, halo_s, own_refs, halo_refs):
    for k in range(z.lev):
        own_refs[k][0] = own_s[k].astype(BF16)
        halo_refs[k][0] = halo_s[k].astype(BF16)


def bf16_rows(z, ref):
    return ref[...].reshape(z.n, z.d).astype(BF16)


def put_rows(z, ref, values):
    ref[...] = values.reshape(z.lt, TOK, z.d)


def forward_kernel(z, *refs):
    it = iter(refs)
    take = lambda n: [next(it) for _ in range(n)]
    own_in, halo_in = take(z.lev), take(z.lev)
    bias_ref, mask_ref, column_mask = take(3)
    gain1, shift1, gain2, shift2, gain3, shift3 = take(6)
    wq1, wk1, wv1, wo1, wq2, wk2, wv2, wo2, w_up, w_down_t = take(10)
    own_out, halo_out = take(z.lev), take(z.lev)
    aw_ref, ac_ref, att_ref, co_ref, act_ref, slope_ref, probs_ref, probs2_ref = take(8)
    own_s, halo_s, x_s, n_s, q_s, k_s, v_s, o_s, bias_s, h_s = take(10)
    scale = (z.d // z.heads) ** (-0.5)
    masks = head_masks(z)
    b = pl.program_id(1)

    @pl.when(b == 0)
    def _():
        load_wire(z, own_in, halo_in, own_s, halo_s)

    bias_s[...] = bias_ref[0] + mask_ref[0, 0]

    def first(k):
        for l in range(z.l):
            x = wire_level(z, own_s, halo_s, k, l, b)
            x_s[k * z.l + l] = x
            n_s[k * z.l + l] = normalized(x)[0] * gain1[...] + shift1[...]

    loop(z.lev, first)
    tokens = bf16_rows(z, n_s)
    for w, out in ((wq1, q_s), (wk1, k_s), (wv1, v_s)):
        put_rows(z, out, nn(tokens, w[...]))

    def window(lv):
        probs, out = attend(
            q_s[lv], k_s[lv], v_s[lv], bias_s[...], masks, scale
        )
        probs_ref[0, 0, lv] = probs
        o_s[lv] = out

    loop(z.lt, window)
    att = bf16_rows(z, o_s)
    att_ref[0, 0] = att
    put_rows(z, o_s, nn(att, wo1[...]))

    def second(lv):
        after = x_s[lv] + o_s[lv]
        aw_ref[0, 0, lv] = after
        n_s[lv] = normalized(after)[0] * gain2[...] + shift2[...]

    loop(z.lt, second)
    tokens = bf16_rows(z, n_s)
    for w, out in ((wq2, q_s), (wk2, k_s), (wv2, v_s)):
        put_rows(z, out, nn(tokens, w[...]))

    def column(g):
        at = pl.ds(pl.multiple_of(g * GROUP, GROUP), GROUP)
        flat = lambda ref: ref[:, at, :].reshape(z.lt * GROUP, z.d)
        probs, out = attend(
            flat(q_s), flat(k_s), flat(v_s), column_mask[...], masks, scale
        )
        probs2_ref[0, 0, g] = probs
        o_s[:, at, :] = out.reshape(z.lt, GROUP, z.d)

    loop(TOK // GROUP, column)
    co = bf16_rows(z, o_s)
    co_ref[0, 0] = co
    put_rows(z, o_s, nn(co, wo2[...]))

    def third(lv):
        after = aw_ref[0, 0, lv] + o_s[lv]
        ac_ref[0, 0, lv] = after
        n_s[lv] = normalized(after)[0] * gain3[...] + shift3[...]

    loop(z.lt, third)
    h_s[...] = nn(bf16_rows(z, n_s), w_up[...])

    def gelu(i):
        at = pl.ds(pl.multiple_of(i * 16, 16), 16)
        hidden = h_s[at, :]
        share = 0.5 + 0.5 * lax.erf(hidden * (0.5**0.5))
        density = jnp.exp(hidden * hidden * -0.5) * ((2.0 * np.pi) ** -0.5)
        act_ref[0, 0, at, :] = (hidden * share).astype(BF16)
        slope_ref[0, 0, at, :] = (share + hidden * density).astype(BF16)

    loop(z.n // 16, gelu)
    put_rows(z, o_s, nt(act_ref[0, 0], w_down_t[...]))

    def last(k):
        store_wire_level(
            z, own_s, halo_s, k, b,
            [ac_ref[0, 0, k * z.l + l] + o_s[k * z.l + l] for l in range(z.l)],
        )

    loop(z.lev, last)

    @pl.when(b == z.nb - 1)
    def _():
        clear_pad(z, own_s, halo_s)
        flush_wire(z, own_s, halo_s, own_out, halo_out)


def wire_specs(z):
    spec = lambda r: pl.BlockSpec((1, z.nblk, r, LANES), lambda s, b: (s, 0, 0, 0))
    return [spec(z.ro)] * z.lev + [spec(z.rh)] * z.lev


def wire_shapes(z):
    return [jax.ShapeDtypeStruct((z.s, z.nblk, r, LANES), BF16) for r in [z.ro] * z.lev + [z.rh] * z.lev]


def unit_spec(shape):
    return pl.BlockSpec((1, 1) + shape, lambda s, b: (s, b) + (0,) * len(shape))


def whole_spec(array):
    return pl.BlockSpec(array.shape, lambda s, b: (0,) * array.ndim)


def residual_shapes(z):
    return [
        ((z.lt, TOK, z.d), F32),
        ((z.lt, TOK, z.d), F32),
        ((z.n, z.d), BF16),
        ((z.n, z.d), BF16),
        ((z.n, z.ff), BF16),
        ((z.n, z.ff), BF16),
        ((z.lt, TOK, z.heads * TOK), BF16),
        ((TOK // GROUP, z.lt * GROUP, z.heads * z.lt * GROUP), BF16),
    ]


def forward(z, own, halo, bias, mask, column_mask, norms, weights):
    res = residual_shapes(z)
    rows3 = (z.lt, TOK, z.d)
    out = pl.pallas_call(
        functools.partial(forward_kernel, z),
        grid=(z.s, z.nb),
        in_specs=wire_specs(z)
        + [
            pl.BlockSpec((1, TOK, z.heads * TOK), lambda s, b: (b, 0, 0)),
            pl.BlockSpec((1, 1, TOK, 1), lambda s, b: (s, b, 0, 0)),
            whole_spec(column_mask),
        ]
        + [whole_spec(a) for a in norms]
        + [whole_spec(a) for a in weights],
        out_specs=wire_specs(z) + [unit_spec(shape) for shape, _ in res],
        out_shape=wire_shapes(z) + [jax.ShapeDtypeStruct((z.s, z.nb) + shape, t) for shape, t in res],
        scratch_shapes=[
            pltpu.VMEM((z.lev, z.nblk, z.ro, LANES), F32),
            pltpu.VMEM((z.lev, z.nblk, z.rh, LANES), F32),
        ]
        + [pltpu.VMEM(rows3, F32)] * 6
        + [pltpu.VMEM((TOK, z.heads * TOK), F32), pltpu.VMEM((z.n, z.ff), F32)],
        compiler_params=pltpu.CompilerParams(vmem_limit_bytes=60 * 2**20),
        name="forward",
    )(*own, *halo, bias, mask, column_mask, *norms, *weights)
    return out[: z.lev], out[z.lev : 2 * z.lev], out[2 * z.lev :]


def grad_list(z):
    return [
        ("up", z.ff), ("down_t", z.ff),
        ("q1", z.d), ("k1", z.d), ("v1", z.d),
        ("q2", z.d), ("k2", z.d), ("v2", z.d),
        ("o1", z.d), ("o2", z.d),
    ]


def half_blocks(z):
    full, rest = [], []
    for name, columns in grad_list(z):
        for row in range(0, z.d, 96):
            for col in range(0, columns, LANES):
                width = min(LANES, columns - col)
                (full if width == LANES else rest).append((name, row, col, width))
    out = [[piece + (0,)] for piece in full]
    for i in range(0, len(rest), 2):
        out.append([rest[i] + (0,), rest[i + 1] + (rest[i][3],)])
    return out


def bias_rows(z):
    pick = np.zeros((WLON * 8, TOK), np.float32)
    for a in range(WLON):
        for i in range(WLAT):
            pick[a * 8 + i, a * WLAT + i] = 1.0
    return pick


def backward_kernel(z, scal, *refs):
    it = iter(refs)
    take = lambda n: [next(it) for _ in range(n)]
    own_x, halo_x = take(z.lev), take(z.lev)
    own_c, halo_c = take(z.lev), take(z.lev)
    aw_ref, ac_ref, att_ref, co_ref, act_ref, slope_ref, probs_ref, probs2_ref = take(8)
    (pick_ref,) = take(1)
    gain1, shift1, gain2, shift2, gain3, shift3 = take(6)
    wq1, wk1, wv1, wo1, wq2, wk2, wv2, wo2, w_up, w_down_t = take(10)
    own_out, halo_out = take(z.lev), take(z.lev)
    (wire_ref,) = take(1)
    own_s, halo_s, owc_s, hac_s = take(4)
    x_s, g_s, n_s, q_s, k_s, v_s, dq_s, dk_s, dv_s, o_s, rstd_s = take(11)
    ga_s, gh_s, db_s, vec_s = take(4)
    grads = {name: ref for (name, _), ref in zip(grad_list(z), take(len(grad_list(z))))}
    scale = (z.d // z.heads) ** (-0.5)
    masks = head_masks(z)
    s, b = pl.program_id(0), pl.program_id(1)

    @pl.when((s == 0) & (b == 0))
    def _():
        for ref in list(grads.values()) + [db_s, vec_s]:
            ref[...] = jnp.zeros_like(ref)

    @pl.when(b == 0)
    def _():
        load_wire(z, own_x, halo_x, own_s, halo_s)
        load_wire(z, own_c, halo_c, owc_s, hac_s)

    def first(k):
        for l in range(z.l):
            g_s[k * z.l + l] = wire_level(z, owc_s, hac_s, k, l, b)
            x_s[k * z.l + l] = wire_level(z, own_s, halo_s, k, l, b)

    loop(z.lev, first)

    cot = bf16_rows(z, g_s)
    ga_s[...] = nn(cot, w_down_t[...])
    grads["down_t"][...] += tn(cot, act_ref[0, 0])

    def slope(i):
        at = pl.ds(pl.multiple_of(i * 16, 16), 16)
        gh_s[at, :] = (ga_s[at, :] * slope_ref[0, 0, at, :].astype(F32)).astype(BF16)

    loop(z.n // 16, slope)

    def renorm(source):
        def body(lv):
            normed, rstd = normalized(source(lv))
            n_s[lv] = normed
            rstd_s[lv] = rstd

        loop(z.lt, body)

    def normed_tokens(gain, shift):
        return (n_s[...] * gain[...] + shift[...]).reshape(z.n, z.d).astype(BF16)

    def norm_step(gain, at, target):
        def body(lv):
            grad, normed = o_s[lv], n_s[lv]
            vec_s[at] += fold_rows(grad * normed)
            vec_s[at + 1] += fold_rows(grad)
            target[lv] = target[lv] + norm_back(normed, rstd_s[lv], grad, gain[...])

        loop(z.lt, body)

    renorm(lambda lv: ac_ref[0, 0, lv])
    grads["up"][...] += tn(normed_tokens(gain3, shift3), gh_s[...])
    put_rows(z, o_s, nt(gh_s[...], w_up[...]))
    norm_step(gain3, 4, g_s)

    branch = bf16_rows(z, g_s)
    grads["o2"][...] += tn(co_ref[0, 0], branch)
    put_rows(z, o_s, nt(branch, wo2[...]))
    renorm(lambda lv: aw_ref[0, 0, lv])
    tokens = normed_tokens(gain2, shift2)
    for w, out in ((wq2, q_s), (wk2, k_s), (wv2, v_s)):
        put_rows(z, out, nn(tokens, w[...]))

    def column(g):
        at = pl.ds(pl.multiple_of(g * GROUP, GROUP), GROUP)
        flat = lambda ref: ref[:, at, :].reshape(z.lt * GROUP, z.d)
        dq, dk, dv, _ = attend_back(
            flat(q_s), flat(k_s), flat(v_s), probs2_ref[0, 0, g], flat(o_s), masks, scale
        )
        for ref, value in ((dq_s, dq), (dk_s, dk), (dv_s, dv)):
            ref[:, at, :] = value.reshape(z.lt, GROUP, z.d)

    loop(TOK // GROUP, column)

    def project_back(tokens, names, ws):
        total = None
        for name, w, ref in zip(names, ws, (dq_s, dk_s, dv_s)):
            grad = bf16_rows(z, ref)
            grads[name][...] += tn(tokens, grad)
            part = nt(grad, w[...])
            total = part if total is None else total + part
        put_rows(z, o_s, total)

    project_back(tokens, ("q2", "k2", "v2"), (wq2, wk2, wv2))
    norm_step(gain2, 2, g_s)

    branch = bf16_rows(z, g_s)
    grads["o1"][...] += tn(att_ref[0, 0], branch)
    put_rows(z, o_s, nt(branch, wo1[...]))
    renorm(lambda lv: x_s[lv])
    tokens = normed_tokens(gain1, shift1)
    for w, out in ((wq1, q_s), (wk1, k_s), (wv1, v_s)):
        put_rows(z, out, nn(tokens, w[...]))

    def window(lv):
        dq, dk, dv, ds = attend_back(
            q_s[lv], k_s[lv], v_s[lv], probs_ref[0, 0, lv], o_s[lv], masks, scale
        )
        dq_s[lv], dk_s[lv], dv_s[lv] = dq, dk, dv
        db_s[b] += ds.astype(F32)

    loop(z.lt, window)
    project_back(tokens, ("q1", "k1", "v1"), (wq1, wk1, wv1))
    norm_step(gain1, 0, g_s)

    def last(k):
        store_wire_level(z, owc_s, hac_s, k, b, [g_s[k * z.l + l] for l in range(z.l)])

    loop(z.lev, last)

    @pl.when(b == z.nb - 1)
    def _():
        clear_pad(z, owc_s, hac_s)
        flush_wire(z, owc_s, hac_s, own_out, halo_out)

    @pl.when((s == z.s - 1) & (b == z.nb - 1))
    def _():
        for at, pieces in enumerate(half_blocks(z)):
            values = [grads[n][r : r + 96, c : c + width] for n, r, c, width, _ in pieces]
            block = values[0] if len(values) == 1 else jnp.concatenate(values, axis=1)
            start = (at % z.hb) * 96
            wire_ref[at // z.hb, start : start + 96, :] = block.astype(BF16)
        extra = z.hb * 96
        wire_ref[:, extra:, :] = jnp.zeros_like(wire_ref[:, extra:, :])
        vectors = [jnp.sum(vec_s[i], axis=0, keepdims=True) for i in range(6)]
        vectors = jnp.concatenate(vectors + [jnp.zeros((UNIT - 6, z.d), F32)], axis=0)
        vectors = jnp.concatenate([vectors, jnp.zeros((UNIT, 2 * LANES - z.d), F32)], axis=1)

        def put_unit(u, value):
            start = extra + (u % z.upp) * UNIT
            if not isinstance(u, int):
                start = pl.multiple_of(start, UNIT)
            wire_ref[u // z.upp, pl.ds(start, UNIT), :] = value.astype(BF16)

        for j in range(2):
            put_unit(z.bands * 4 + j, vectors[:, j * LANES : (j + 1) * LANES])
        lane = lax.broadcasted_iota(jnp.int32, (1, z.heads * TOK), 1)
        odd = jnp.zeros(lane.shape, jnp.bool_)
        for h in range(1, z.heads, 2):
            odd = odd | ((lane >= h * TOK) & (lane < (h + 1) * TOK))
        width = -(-(z.heads * TOK) // LANES) * LANES
        for band in range(z.nb):
            rows = nn(pick_ref[...], db_s[band], precision=lax.Precision.HIGHEST)
            halves = []
            for parity in range(2):
                kept = jnp.where(odd if parity else ~odd, rows, 0.0)
                kept = jnp.concatenate(
                    [kept, jnp.zeros((rows.shape[0], width - z.heads * TOK), F32)], axis=1
                )
                total = None
                for a in range(WLON):
                    part = kept[a * 8 : (a + 1) * 8]
                    shift = (WLON - 1 - a) * WLAT
                    if shift:
                        part = pltpu.roll(part, shift, 1)
                    total = part if total is None else total + part
                halves.append(total)
            both = jnp.concatenate(halves, axis=0)
            for j in range(4):
                put_unit((scal[0] * z.nb + band) * 4 + j, both[:, j * LANES : (j + 1) * LANES])


def backward(z, scal, own_x, halo_x, own_c, halo_c, residuals, norms, weights):
    res = residual_shapes(z)
    rows3 = (z.lt, TOK, z.d)
    pick = jnp.asarray(bias_rows(z))
    drop = lambda spec: pl.BlockSpec(spec.block_shape, lambda s, b, _, m=spec.index_map: m(s, b))
    out = pl.pallas_call(
        functools.partial(backward_kernel, z),
        grid_spec=pltpu.PrefetchScalarGridSpec(
            num_scalar_prefetch=1,
            grid=(z.s, z.nb),
            in_specs=[
                drop(spec)
                for spec in wire_specs(z) * 2
                + [unit_spec(shape) for shape, _ in res]
                + [whole_spec(pick)]
                + [whole_spec(a) for a in norms]
                + [whole_spec(a) for a in weights]
            ],
            out_specs=[drop(spec) for spec in wire_specs(z)]
            + [pl.BlockSpec((z.np, z.pr, LANES), lambda s, b, _: (0, 0, 0))],
            scratch_shapes=[
                pltpu.VMEM((z.lev, z.nblk, z.ro, LANES), F32),
                pltpu.VMEM((z.lev, z.nblk, z.rh, LANES), F32),
            ]
            * 2
            + [pltpu.VMEM(rows3, F32)] * 10
            + [
                pltpu.VMEM((z.lt, TOK, 1), F32),
                pltpu.VMEM((z.n, z.ff), F32),
                pltpu.VMEM((z.n, z.ff), BF16),
                pltpu.VMEM((z.nb, TOK, z.heads * TOK), F32),
                pltpu.VMEM((6, 8, z.d), F32),
            ]
            + [pltpu.VMEM((z.d, columns), F32) for _, columns in grad_list(z)],
        ),
        out_shape=wire_shapes(z) + [jax.ShapeDtypeStruct((z.np, z.pr, LANES), BF16)],
        compiler_params=pltpu.CompilerParams(vmem_limit_bytes=62 * 2**20),
        name="backward",
    )(scal, *own_x, *halo_x, *own_c, *halo_c, *residuals, pick, *norms, *weights)
    return out[: z.lev], out[z.lev : 2 * z.lev], out[2 * z.lev]


def tree(parts):
    while len(parts) > 1:
        parts = [parts[i] + parts[i + 1] for i in range(0, len(parts), 2)]
    return parts[0]


def lev_swap(z, array, k):
    return lax.ppermute(array, "lev", [(i, i ^ k) for i in range(z.lev)])


def lon_swap(z, array, k):
    return lax.ppermute(array, "lon", [(i, i ^ k) for i in range(z.lon)])


def sum_wire(z, wire, p, w):
    core = w % 2
    mine = lax.dynamic_slice_in_dim(wire, core * z.lev, z.lev, axis=0)
    other = lax.dynamic_slice_in_dim(wire, (1 - core) * z.lev, z.lev, axis=0)
    half = (mine.astype(F32) + lon_swap(z, other, 1).astype(F32)).astype(BF16)
    piece = lambda k: lax.dynamic_index_in_dim(half, p ^ k, axis=0, keepdims=False)
    parts = [piece(0)] + [lev_swap(z, piece(k), k) for k in range(1, z.lev)]
    quarter = tree([v.astype(F32) for v in parts]).astype(BF16)
    parts = [quarter] + [lon_swap(z, quarter, 2 * k) for k in range(1, z.lon // 2)]
    done = tree([v.astype(F32) for v in parts]).astype(BF16)
    own = jnp.stack([done] + [lev_swap(z, done, k) for k in range(1, z.lev)])
    return own, lon_swap(z, own, 1)


def finish_kernel(z, scal, own, other, *outs):
    p, core = scal[0], scal[1]
    named = {name: ref for (name, _), ref in zip(grad_list(z), outs)}
    vec_ref, bias_ref = outs[len(named) :]

    def read(piece, start, size):
        half, j = piece // z.lev, piece % z.lev
        rows = slice(start, start + size)
        a = own[p ^ j, rows, :].astype(F32)
        c = other[p ^ j, rows, :].astype(F32)
        return jnp.where(core == half, a, c)

    for at, pieces in enumerate(half_blocks(z)):
        block = read(at // z.hb, (at % z.hb) * 96, 96)
        for n, r, c, width, lane in pieces:
            named[n][r : r + 96, c : c + width] = block[:, lane : lane + width]
    extra = z.hb * 96
    for u in range(z.units):
        value = read(u // z.upp, extra + (u % z.upp) * UNIT, UNIT)
        if u < z.bands * 4:
            bias_ref[u // 4, :, (u % 4) * LANES : (u % 4 + 1) * LANES] = value
        else:
            j = u - z.bands * 4
            vec_ref[:, j * LANES : (j + 1) * LANES] = value


def finish(z, scal, own, other):
    shapes = [jax.ShapeDtypeStruct((z.d, columns), F32) for _, columns in grad_list(z)]
    shapes += [
        jax.ShapeDtypeStruct((UNIT, 2 * LANES), F32),
        jax.ShapeDtypeStruct((z.bands, UNIT, 4 * LANES), F32),
    ]
    full = lambda a: pl.BlockSpec(a.shape, lambda _, n=len(a.shape): (0,) * n)
    full0 = lambda a: pl.BlockSpec(a.shape, lambda i, _, n=len(a.shape): (0,) * n)
    out = pl.pallas_call(
        functools.partial(finish_kernel, z),
        grid_spec=pltpu.PrefetchScalarGridSpec(
            num_scalar_prefetch=1,
            grid=(1,),
            in_specs=[full0(own), full0(other)],
            out_specs=[full0(a) for a in shapes],
        ),
        out_shape=shapes,
        compiler_params=pltpu.CompilerParams(vmem_limit_bytes=60 * 2**20),
        name="finish",
    )(scal, own, other)
    named = {name: value for (name, _), value in zip(grad_list(z), out)}
    return named, out[-2], out[-1]


def table_of(z, rows):
    rows = rows.reshape(z.bands, 2, 8, 4 * LANES)[:, :, :WLAT]
    distances = 2 * WLON - 1
    halves = []
    for parity in range(2):
        lanes = rows[:, parity, :, parity * TOK :]
        lanes = jnp.pad(lanes, ((0, 0), (0, 0), (0, TOK)))[..., : z.heads * TOK]
        lanes = lanes.reshape(z.bands, WLAT, z.heads // 2, 2 * TOK)[..., : distances * WLAT]
        halves.append(lanes.reshape(z.bands, WLAT, z.heads // 2, distances, WLAT))
    both = jnp.stack(halves, axis=3)
    return both.transpose(0, 2, 3, 5, 1, 4).reshape(z.bands, z.heads, WLAT, WLAT, distances)


def lon_table():
    relative = jnp.arange(2 * WLON - 1, dtype=jnp.int32)[:, None, None]
    query_col = jnp.arange(WLON, dtype=jnp.int32)[None, :, None]
    key_col = jnp.arange(WLON, dtype=jnp.int32)[None, None, :]
    return (query_col - key_col + WLON - 1 == relative).astype(F32)


def exchange(z, own, halo):
    own = [own[0]] + [lev_swap(z, own[k], k) for k in range(1, z.lev)]
    both = lambda a, k, d: lax.ppermute(
        a,
        ("lon", "lev"),
        [
            (w * z.lev + i, (w + d) % z.lon * z.lev + (i ^ k))
            for w in range(z.lon)
            for i in range(z.lev)
        ],
    )
    return own, both, halo


def send_west(z, own, halo):
    own, both, halo = exchange(z, own, halo)
    return own, [both(halo[k], k, -1) for k in range(z.lev)]


def send_east(z, own, halo):
    own, both, halo = exchange(z, own, halo)
    return own, [both(halo[k], k, 1) for k in range(z.lev)]


def on_device(
    inputs, cotangent, grid_sizes, offsets, gain_one, shift_one, qkv_window, out_window, bias_table,
    gain_two, shift_two, qkv_column, out_column, gain_three, shift_three, w_up, w_down,
):
    d = inputs.shape[-1]
    z = Sizes(lax.axis_size("lev"), lax.axis_size("lon"), inputs.shape, bias_table.shape[1], w_up.shape[1])
    p, w = lax.axis_index("lev"), lax.axis_index("lon")
    scal = jnp.concatenate([p[None].astype(jnp.int32), offsets.astype(jnp.int32)])
    swap = lambda a: a.transpose(0, 1, 3, 2, 4)

    own_x, halo_x = send_west(z, *pack(z, swap(inputs), scal))
    own_c, halo_c = send_west(z, *pack(z, swap(cotangent), scal))

    table = lax.dynamic_slice_in_dim(bias_table, p * z.nb, z.nb, axis=0)
    bias = jnp.einsum("khijr,rab->kbjhai", table, lon_table(), precision=lax.Precision.HIGHEST)
    bias = bias.reshape(z.nb, TOK, z.heads * TOK)
    cell = (w * z.cells + offsets[:, None] + jnp.arange(WLON)[None, :]) % (z.cells * z.lon)
    row = (p * z.nb + jnp.arange(z.nb))[:, None] * WLAT + jnp.arange(WLAT)[None, :]
    cell_ok = cell < grid_sizes[:, 1:2]
    row_ok = row[None] < grid_sizes[:, 0][:, None, None]
    valid = cell_ok[:, None, :, None] & row_ok[:, :, None, :]
    mask = jnp.where(valid, 0.0, NEGATIVE).astype(F32).reshape(z.s, z.nb, TOK, 1)
    of_key = np.arange(z.lt * GROUP) % GROUP
    of_query = np.tile(of_key, z.heads)
    column_mask = jnp.asarray(
        np.where(of_key[:, None] == of_query[None, :], 0.0, NEGATIVE).astype(np.float32)
    )

    norms = [v[None] for v in (gain_one, shift_one, gain_two, shift_two, gain_three, shift_three)]
    three = lambda a: [a[:, :d], a[:, d : 2 * d], a[:, 2 * d :]]
    weights = three(qkv_window) + [out_window] + three(qkv_column) + [out_column, w_up, w_down.T]

    own_r, halo_r, residuals = forward(z, own_x, halo_x, bias, mask, column_mask, norms, weights)
    own_r, halo_r = send_east(z, own_r, halo_r)
    own_g, halo_g, wire = backward(
        z, scal, own_x, halo_x, own_c, halo_c, residuals, norms, weights
    )
    own_g, halo_g = send_east(z, own_g, halo_g)
    result = unpack(z, own_r, halo_r, scal)
    input_grad = unpack(z, own_g, halo_g, scal)
    own, other = sum_wire(z, wire, p, w)
    named, vectors, rows = finish(z, jnp.stack([p, w % 2]).astype(jnp.int32), own, other)
    vec = [vectors[i, :d] for i in range(6)]
    qkv = lambda i: jnp.concatenate([named["q" + i], named["k" + i], named["v" + i]], axis=1)
    return (
        swap(result), swap(input_grad),
        vec[0], vec[1], qkv("1"), named["o1"], table_of(z, rows),
        vec[2], vec[3], qkv("2"), named["o2"],
        vec[4], vec[5], named["up"], named["down_t"].T,
    )


def solution(mesh):
    tokens = P(None, "lev", None, "lon", None)
    return jax.shard_map(
        on_device,
        mesh=mesh,
        in_specs=(tokens, tokens) + (P(),) * 15,
        out_specs=(tokens, tokens) + (P(),) * 13,
        check_vma=False,
    )
```

time: 1010 us -> 333 us (0.33); the launches traced: 991 us -> 333 us
  local copies, waits for them, and re-layouts: 366 us -> 34 us
  waiting for transfers between devices: 257 us -> 57.9 us
  matrix products: 198 us -> 3.42 us
  Pallas kernels: 0 us -> 185 us
  other arithmetic: 107 us -> 8.87 us
  blocking collectives: 40 us -> 0 us
  starting transfers between devices: 7.49 us -> 42.1 us
  between operations: 15.9 us -> 1.25 us
    dot_general x32 -> x1, matrix products: 198 us -> 3.42 us  [on_device(): jnp.einsum('khijr,rab->kbjhai', table, lon_table(), precision=lax.Precisi...]
    pallas_call x0 -> x7, Pallas kernels: none -> 185 us  [the longest x1 91.2 us: backward(): pl.pallas_call(functools.partial(backward_kernel, z), grid_spec=pltpu.Pre...]
    convert_element_type x23 -> x0, local copies, waits for them, and re-layouts: 96.1 us -> none  [the longest x5 21.6 us: on_device(): grad_win_k.reshape(flat_shape).astype(jnp.bfloat16)]
    unnamed x4 -> x0, waiting for transfers between devices: 94 us -> none
    psum x1 -> x0, waiting for transfers between devices: 87.4 us -> none  [on_device(): lax.psum((grad_gain_one, grad_shift_one, grad_qkv_window, grad_out_window...]
    reshape x9 -> x3, local copies, waits for them, and re-layouts: 86.4 us -> 6.13 us  [the longest x1 5.83 us: on_device(): bias = bias.reshape(z.nb, TOK, z.heads * TOK)]
    all_gather x1 -> x0, waiting for transfers between devices: 59.7 us -> none  [on_device(): all_pairs = lax.all_gather(local_pairs, 'lev', axis=1, tiled=True)]
    slice x15 -> x7, local copies, waits for them, and re-layouts: 58.8 us -> 4.56 us  [the longest x2 1.91 us: table_of(): lanes = rows[:, parity, :, parity * TOK:]]
  transfers between devices with their start and end apart: 7 -> 39, of which waited for: 5 -> 18; matrix products, arithmetic and copies ran while one was open for 17% -> 7% of each run, Pallas kernels for 0% -> 26%
where the time goes in v1:
time: 333 us
  Pallas kernels  185 us (56%)
  waiting for transfers between devices  57.9 us (17%)
  starting transfers between devices  42.1 us (13%)
  local copies, waits for them, and re-layouts  34 us (10%)
  other arithmetic  8.87 us (3%)
  matrix products  3.42 us (1%)
    pallas_call x1, Pallas kernels, backward(): pl.pallas_call(functools.partial(backward_kernel, z), grid_spec=pltpu.Pre...  91.2 us
    pallas_call x1, Pallas kernels, forward(): pl.pallas_call(functools.partial(forward_kernel, z), grid=(z.s, z.nb), in...  72.3 us
    ppermute x16, waiting for transfers between devices, exchange(): lax.ppermute(a, ('lon', 'lev'), [(w * z.lev + i, (w + d) % z.lon * z.lev...  26.7 us
    ppermute x18, starting transfers between devices, lev_swap(): return lax.ppermute(array, 'lev', [(i, i ^ k) for i in range(z.lev)])  22.8 us
    ppermute x18, waiting for transfers between devices, lev_swap(): return lax.ppermute(array, 'lev', [(i, i ^ k) for i in range(z.lev)])  15.8 us
    ppermute x5, waiting for transfers between devices, lon_swap(): return lax.ppermute(array, 'lon', [(i, i ^ k) for i in range(z.lon)])  15.4 us
    ppermute x16, starting transfers between devices, exchange(): lax.ppermute(a, ('lon', 'lev'), [(w * z.lev + i, (w + d) % z.lon * z.lev...  14.5 us
    transpose x1, local copies, waits for them, and re-layouts, on_device(): jnp.einsum('khijr,rab->kbjhai', table, lon_table(), precision=lax.Precisi...  11 us
  transfers between devices with their start and end apart: 39, of which 18 were waited for; matrix products, arithmetic and copies ran while one was open for 7% of the time, Pallas kernels for 26%

profile of v1, /device:TPU:0, one launch (start us, length us, event | category | flops | bytes accessed | tf_op | source)
XLA Modules:
  0.0 332.9 jit_solution(6368179010564391410)
XLA Ops:
  0.7 1.3 pad_add_fusion.scal
  2.0 4.5 %pack.2 = (bf16[2,3,144,128]{3,2,1,0:T(8,128)(2,1)}, bf16[2,3,144,128]{3,2,1,0:T(8,128)(2,1)}, bf16[2,3,144,128]{3,2,1,0:T(8,128)(2,1)}, bf16[2,3,144,128]{3,2,1...) custom-call(s32[3]{0:T(128)} %pad_add_fusion.scal, ...), custom_call_target="tpu_custom_call" | custom-call | tf_op jit(solution)/shard_map/pack/pallas_call | solution.py:107
  6.5 3.0 collective-permute-start
  9.5 2.8 collective-permute-start.3
  12.3 0.9 collective-permute-start.4
  13.2 1.1 collective-permute-start.5
  14.3 1.4 collective-permute-start.6
  15.9 3.4 %convolution_bitcast_fusion = f32[2,12,6,6,12,6]{1,2,5,3,0,4:T(8,128)} fusion(f32[2,6,6,6,23]{4,0,3,2,1:T(2,128)S(1)} %constant_dynamic-slice_fusion.1, s32[12,12]{1,0:T(8,128)S(1)} %subtract_add_fusion), kind=kOutput, calls=%fused_computation.1 | convolution fusion | flops 17172720 | bytes 289152 | tf_op jit(solution)/shard_map/khijr,rab->kbjhai/dot_general | solution.py:831
  19.3 11.0 %copy.68 = f32[2,12,6,6,12,6]{5,4,3,2,1,0:T(8,128)} copy(f32[2,12,6,6,12,6]{1,2,5,3,0,4:T(8,128)} %convolution_bitcast_fusion) | data formatting | bytes 497664 | tf_op jit(solution)/shard_map/khijr,rab->kbjhai/transpose | solution.py:831
  30.3 5.8 %reshape.152.refs_8_ = f32[2,72,432]{2,1,0:T(8,128)} reshape(f32[2,12,6,6,12,6]{5,4,3,2,1,0:T(8,128)} %copy.68) | data formatting | bytes 497664 | tf_op jit(solution)/shard_map/reshape | solution.py:832
  36.9 4.6 %pack.3 = (bf16[2,3,144,128]{3,2,1,0:T(8,128)(2,1)}, bf16[2,3,144,128]{3,2,1,0:T(8,128)(2,1)}, bf16[2,3,144,128]{3,2,1,0:T(8,128)(2,1)}, bf16[2,3,144,128]{3,2,1...) custom-call(s32[3]{0:T(128)} %pad_add_fusion.scal, ...), custom_call_target="tpu_custom_call" | custom-call | tf_op jit(solution)/shard_map/pack/pallas_call | solution.py:107
  41.5 1.6 collective-permute-start.1
  43.7 1.5 collective-permute-start.18
  45.1 0.9 fusion.6
  46.4 1.5 collective-permute-start.14
  47.9 5.2 %collective-permute-done.18.refs_13_ = bf16[2,3,80,128]{3,2,1,0:T(8,128)(2,1)S(1)} collective-permute-done((bf16[2,3,80,128]{3,2,1,0:T(8,128)(2,1)}, bf16[2,3,80,128]{3,2,1,0:T(8,128)(2,1)S(1)}, u32[]{:S(2)}, u32[]{:S(2)}) %collective-permute-start.18) | collective-permute-done | bytes 122912 | tf_op jit(solution)/shard_map/ppermute | solution.py:795
  53.1 0.7 copy-done.30
  53.8 1.5 collective-permute-start.15
  55.8 2.5 collective-permute-start.20
  58.4 0.7 and_select_fusion.refs_9_
  59.2 72.3 %forward.1 = (bf16[2,3,144,128]{3,2,1,0:T(8,128)(2,1)}, bf16[2,3,144,128]{3,2,1,0:T(8,128)(2,1)}, bf16[2,3,144,128]{3,2,1,0:T(8,128)(2,1)}, bf16[2,3,144,128]{3,...) custom-call(bf16[2,3,144,128]{3,2,1,0:T(8,128)(2,1)} %get-tuple-elem, ...), custom_call_target="tpu_custom_call" | custom-call | tf_op jit(solution)/shard_map/forward/pallas_call | solution.py:420
  132.8 91.2 %backward.1 = (bf16[2,3,144,128]{3,2,1,0:T(8,128)(2,1)}, bf16[2,3,144,128]{3,2,1,0:T(8,128)(2,1)}, bf16[2,3,144,128]{3,2,1,0:T(8,128)(2,1)}, bf16[2,3,144,128]{3...) custom-call(s32[3]{0:T(128)} %pad_add_fusion.scal, ...), custom_call_target="tpu_custom_call" | custom-call | tf_op jit(solution)/shard_map/backward/pallas_call | solution.py:658
  224.0 1.2 constant_dynamic-slice_fusion
  225.6 1.9 collective-permute-done.28
  227.8 1.6 collective-permute-start.31
  229.9 1.5 collective-permute-start.29
  231.3 4.6 %collective-permute-done.31 = bf16[656,128]{1,0:T(8,128)(2,1)S(1)} collective-permute-done((bf16[656,128]{1,0:T(8,128)(2,1)S(1)}, bf16[656,128]{1,0:T(8,128)(2,1)S(1)}, u32[]{:S(2)}, u32[]{:S(2)}) %collective-permute-start.31) | collective-permute-done | bytes 167968 | tf_op jit(solution)/shard_map/ppermute | solution.py:702
  235.9 2.9 collective-permute-done.30
  239.4 2.6 collective-permute-start.33
  242.0 1.4 collective-permute-start.32
  243.4 4.7 %collective-permute-done.34 = bf16[656,128]{1,0:T(8,128)(2,1)S(1)} collective-permute-done((bf16[656,128]{1,0:T(8,128)(2,1)S(1)}, bf16[656,128]{1,0:T(8,128)(2,1)S(1)}, u32[]{:S(2)}, u32[]{:S(2)}) %collective-permute-start.34) | collective-permute-done | bytes 167968 | tf_op jit(solution)/shard_map/ppermute | solution.py:706
  248.1 8.8 %collective-permute-done.33 = bf16[656,128]{1,0:T(8,128)(2,1)S(1)} collective-permute-done((bf16[656,128]{1,0:T(8,128)(2,1)S(1)}, bf16[656,128]{1,0:T(8,128)(2,1)S(1)}, u32[]{:S(2)}, u32[]{:S(2)}) %collective-permute-start.33) | collective-permute-done | bytes 167968 | tf_op jit(solution)/shard_map/ppermute | solution.py:706
  257.0 1.6 collective-permute-start.37
  259.0 1.5 collective-permute-start.35
  260.5 4.5 %collective-permute-done.37 = bf16[656,128]{1,0:T(8,128)(2,1)S(1)} collective-permute-done((bf16[656,128]{1,0:T(8,128)(2,1)S(1)}, bf16[656,128]{1,0:T(8,128)(2,1)S(1)}, u32[]{:S(2)}, u32[]{:S(2)}) %collective-permute-start.37) | collective-permute-done | bytes 167968 | tf_op jit(solution)/shard_map/ppermute | solution.py:702
  265.0 1.8 collective-permute-done.36
  267.9 1.6 collective-permute-start.13
  269.5 3.6 %collective-permute-done.10.rest_4_ = bf16[2,3,80,128]{3,2,1,0:T(8,128)(2,1)S(1)} collective-permute-done((bf16[2,3,80,128]{3,2,1,0:T(8,128)(2,1)S(1)}, bf16[2,3,80,128]{3,2,1,0:T(8,128)(2,1)S(1)}, u32[]{:S(2)}, u32[]{:S(2)}) %collective-permute-start.10) | collective-permute-done | bytes 122912 | tf_op jit(solution)/shard_map/ppermute | solution.py:795
  273.2 1.5 collective-permute-done.11.rest_5_
  274.7 1.3 collective-permute-done.12.rest_6_
  276.0 1.5 collective-permute-start.7
  277.5 0.9 collective-permute-done.13.rest_7_
  278.8 0.7 collective-permute-done.24.rest_4_
  279.5 2.5 collective-permute-done.25.rest_5_
  282.0 1.6 collective-permute-start.9
  283.6 6.2 %collective-permute-done.26.rest_6_ = bf16[2,3,80,128]{3,2,1,0:T(8,128)(2,1)S(1)} collective-permute-done((bf16[2,3,80,128]{3,2,1,0:T(8,128)(2,1)}, bf16[2,3,80,128]{3,2,1,0:T(8,128)(2,1)S(1)}, u32[]{:S(2)}, u32[]{:S(2)}) %collective-permute-start.26) | collective-permute-done | bytes 122912 | tf_op jit(solution)/shard_map/ppermute | solution.py:795
  289.8 1.3 collective-permute-start.21
  291.1 0.7 collective-permute-start.22
  291.9 1.5 collective-permute-start.23
  293.3 1.7 collective-permute-start.27
  295.7 4.5 %unpack.2 = bf16[2,2,12,48,192]{4,3,2,1,0:T(8,128)(2,1)} custom-call(s32[3]{0:T(128)} %pad_add_fusion.scal, s32[1,224]{1,0:T(1,128)} %constant.83.base, bf16[2,3,144,128]{3,2,1,0:T(8,128)(2,1)} %get-tuple-element.76.rest_0_, bf16[2,3,144,128]{3,2,1,0:T(8,128)(2,1)} %copy-done.17, bf16[2,3,144,128]{3,2,1,0:T(8,128)(2,1)} %copy-done.19, ...), custom_call_target="tpu_custom_call" | custom-call | tf_op jit(solution)/shard_map/unpack/pallas_call | solution.py:157
  300.2 4.3 %collective-permute-done.27.rest_7_ = bf16[2,3,80,128]{3,2,1,0:T(8,128)(2,1)S(1)} collective-permute-done((bf16[2,3,80,128]{3,2,1,0:T(8,128)(2,1)}, bf16[2,3,80,128]{3,2,1,0:T(8,128)(2,1)S(1)}, u32[]{:S(2)}, u32[]{:S(2)}) %collective-permute-start.27) | collective-permute-done | bytes 122912 | tf_op jit(solution)/shard_map/ppermute | solution.py:795
  304.6 2.0 collective-permute-done.22.rest_2_
  307.4 4.5 %unpack.3 = bf16[2,2,12,48,192]{4,3,2,1,0:T(8,128)(2,1)} custom-call(s32[3]{0:T(128)} %pad_add_fusion.scal, s32[1,224]{1,0:T(1,128)} %constant.83.base, bf16[2,3,144,128]{3,2,1,0:T(8,128)(2,1)} %get-tuple-element.100.rest_0_, bf16[2,3,144,128]{3,2,1,0:T(8,128)(2,1)} %copy-done.18, bf16[2,3,144,128]{3,2,1,0:T(8,128)(2,1)} %copy-done.20, ...), custom_call_target="tpu_custom_call" | custom-call | tf_op jit(solution)/shard_map/unpack/pallas_call | solution.py:157
  311.9 0.8 copy-done.7
  312.8 3.7 %finish.1 = (f32[192,768]{1,0:T(8,128)}, f32[192,768]{1,0:T(8,128)}, f32[192,192]{1,0:T(8,128)}, f32[192,192]{1,0:T(8,128)}, f32[192,192]{1,0:T(8,128)}, /*index...) custom-call(s32[2]{0:T(128)} %pad_add_fusion.1.scal, ...), custom_call_target="tpu_custom_call" | custom-call | tf_op jit(solution)/shard_map/finish/pallas_call | solution.py:757
  316.5 1.0 slice.88
  317.5 0.9 slice.85
  318.4 1.5 fusion.8
  321.0 1.8 stack_reshape.6
  322.8 3.7 %maximum_bitcast_fusion = f32[8,3,2,6,6,23]{3,5,0,1,4,2:T(8,128)} fusion(f32[8,6,3,1,23,6]{5,4,0,2,1,3:T(8,128)S(1)} %stack_reshape.7, f32[8,6,3,1,23,6]{5,4,0,2,1,3:T(8,128)} %stack_reshape.6), kind=kLoop, calls=%fused_computation | loop fusion | flops 39744 | bytes 317952 | tf_op jit(solution)/shard_map/transpose | solution.py:783
  326.5 4.5 %copy.74 = f32[8,3,2,6,6,23]{5,0,4,3,2,1:T(8,128)} copy(f32[8,3,2,6,6,23]{3,5,0,1,4,2:T(8,128)} %maximum_bitcast_fusion) | data formatting | bytes 317952 | tf_op jit(solution)/shard_map/transpose | solution.py:783
  331.0 0.9 pad_maximum_fusion.1
  331.9 0.9 pad_maximum_fusion.2
  (165 shorter events, 9.8 us)
Async XLA Ops:
  0.6 15.1 %copy-start = (f32[8,6,6,6,23]{4,0,3,2,1:T(8,128)S(1)}, f32[8,6,6,6,23]{4,0,3,2,1:T(8,128)}, u32[]{:S(2)}) copy-start(f32[8,6,6,6,23]{4,0,3,2,1:T(8,128)} %param.33) | copy-start | bytes 476932
  6.5 48.8 %collective-permute-start = (bf16[2,3,144,128]{3,2,1,0:T(8,128)(2,1)}, bf16[2,3,144,128]{3,2,1,0:T(8,128)(2,1)S(1)}, u32[]{:S(2)}, u32[]{:S(2)}) collective-permute-start(bf16[2,3,144,128]{3,2,1,0:T(8,128)(2,1)} %get-tuple-element.69), channel_id=1, source_target_pairs={{0,1},{1,0},{2,3},{3,2},{4,5},{5,4},{6,7},{7,6},{8,9},{9,8},{10,11... | collective-permute-start | bytes 663560 | tf_op jit(solution)/shard_map/ppermute | solution.py:702
  9.5 32.0 %collective-permute-start.3 = (bf16[2,3,80,128]{3,2,1,0:T(8,128)(2,1)}, bf16[2,3,80,128]{3,2,1,0:T(8,128)(2,1)S(1)}, u32[]{:S(2)}, u32[]{:S(2)}) collective-permute-start(bf16[2,3,80,128]{3,2,1,0:T(8,128)(2,1)} %get-tuple-element.72), channel_id=1, source_target_pairs={{0,28},{1,29},{2,30},{3,31},{4,0},{5,1},{6,2},{7,3},{8,4},{9,5},{1... | collective-permute-start | bytes 368648 | tf_op jit(solution)/shard_map/ppermute | solution.py:795
  12.3 30.8 %collective-permute-start.4 = (bf16[2,3,80,128]{3,2,1,0:T(8,128)(2,1)}, bf16[2,3,80,128]{3,2,1,0:T(8,128)(2,1)S(1)}, u32[]{:S(2)}, u32[]{:S(2)}) collective-permute-start(bf16[2,3,80,128]{3,2,1,0:T(8,128)(2,1)} %get-tuple-element.73), channel_id=1, source_target_pairs={{0,29},{1,28},{2,31},{3,30},{4,1},{5,0},{6,3},{7,2},{8,5},{9,4},{1... | collective-permute-start | bytes 368648 | tf_op jit(solution)/shard_map/ppermute | solution.py:795
  13.2 30.4 %collective-permute-start.5 = (bf16[2,3,80,128]{3,2,1,0:T(8,128)(2,1)}, bf16[2,3,80,128]{3,2,1,0:T(8,128)(2,1)S(1)}, u32[]{:S(2)}, u32[]{:S(2)}) collective-permute-start(bf16[2,3,80,128]{3,2,1,0:T(8,128)(2,1)} %get-tuple-element.74), channel_id=1, source_target_pairs={{0,30},{1,31},{2,28},{3,29},{4,2},{5,3},{6,0},{7,1},{8,6},{9,7},{1... | collective-permute-start | bytes 368648 | tf_op jit(solution)/shard_map/ppermute | solution.py:795
  14.3 29.3 %collective-permute-start.6 = (bf16[2,3,80,128]{3,2,1,0:T(8,128)(2,1)}, bf16[2,3,80,128]{3,2,1,0:T(8,128)(2,1)S(1)}, u32[]{:S(2)}, u32[]{:S(2)}) collective-permute-start(bf16[2,3,80,128]{3,2,1,0:T(8,128)(2,1)} %get-tuple-element.75), channel_id=1, source_target_pairs={{0,31},{1,30},{2,29},{3,28},{4,3},{5,2},{6,1},{7,0},{8,7},{9,6},{1... | collective-permute-start | bytes 368648 | tf_op jit(solution)/shard_map/ppermute | solution.py:795
  30.3 11.2 %copy-start.46 = (bf16[2,3,144,128]{3,2,1,0:T(8,128)(2,1)S(1)}, bf16[2,3,144,128]{3,2,1,0:T(8,128)(2,1)}, u32[]{:S(2)}) copy-start(bf16[2,3,144,128]{3,2,1,0:T(8,128)(2,1)} %get-tuple-element.70) | copy-start | bytes 663556
  30.3 12.8 %copy-start.45 = (bf16[2,3,144,128]{3,2,1,0:T(8,128)(2,1)S(1)}, bf16[2,3,144,128]{3,2,1,0:T(8,128)(2,1)}, u32[]{:S(2)}) copy-start(bf16[2,3,144,128]{3,2,1,0:T(8,128)(2,1)} %get-tuple-element.71) | copy-start | bytes 663556
  30.3 14.8 %copy-start.12 = (bf16[192,576]{1,0:T(8,128)(2,1)S(1)}, bf16[192,576]{1,0:T(8,128)(2,1)}, u32[]{:S(2)}) copy-start(bf16[192,576]{1,0:T(8,128)(2,1)} %param.36) | copy-start | bytes 663556
  30.3 14.8 %copy-start.13 = (bf16[192,576]{1,0:T(8,128)(2,1)S(1)}, bf16[192,576]{1,0:T(8,128)(2,1)}, u32[]{:S(2)}) copy-start(bf16[192,576]{1,0:T(8,128)(2,1)} %param.31) | copy-start | bytes 663556
  41.5 17.7 %copy-start.8 = (bf16[2,3,80,128]{3,2,1,0:T(8,128)(2,1)}, bf16[2,3,80,128]{3,2,1,0:T(8,128)(2,1)S(1)}, u32[]{:S(2)}) copy-start(bf16[2,3,80,128]{3,2,1,0:T(8,128)(2,1)S(1)} %collective-permute-done.3.refs_4_) | copy-start | bytes 368644
  41.5 14.3 %collective-permute-start.1 = (bf16[2,3,144,128]{3,2,1,0:T(8,128)(2,1)S(1)}, bf16[2,3,144,128]{3,2,1,0:T(8,128)(2,1)S(1)}, u32[]{:S(2)}, u32[]{:S(2)}) collective-permute-start(bf16[2,3,144,128]{3,2,1,0:T(8,128)(2,1)S(1)} %copy-done.46), channel_id=1, source_target_pairs={{0,2},{1,3},{2,0},{3,1},{4,6},{5,7},{6,4},{7,5},{8,10},{9,11},{10,... | collective-permute-start | bytes 663560 | tf_op jit(solution)/shard_map/ppermute | solution.py:702
  43.1 16.1 %copy-start.9 = (bf16[2,3,80,128]{3,2,1,0:T(8,128)(2,1)}, bf16[2,3,80,128]{3,2,1,0:T(8,128)(2,1)S(1)}, u32[]{:S(2)}) copy-start(bf16[2,3,80,128]{3,2,1,0:T(8,128)(2,1)S(1)} %collective-permute-done.4.refs_5_) | copy-start | bytes 368644
  43.1 12.7 %collective-permute-start.2 = (bf16[2,3,144,128]{3,2,1,0:T(8,128)(2,1)S(1)}, bf16[2,3,144,128]{3,2,1,0:T(8,128)(2,1)S(1)}, u32[]{:S(2)}, u32[]{:S(2)}) collective-permute-start(bf16[2,3,144,128]{3,2,1,0:T(8,128)(2,1)S(1)} %copy-done.45), channel_id=1, source_target_pairs={{0,3},{1,2},{2,1},{3,0},{4,7},{5,6},{6,5},{7,4},{8,11},{9,10},{10,... | collective-permute-start | bytes 663560 | tf_op jit(solution)/shard_map/ppermute | solution.py:702
  43.6 15.5 %copy-start.10 = (bf16[2,3,80,128]{3,2,1,0:T(8,128)(2,1)}, bf16[2,3,80,128]{3,2,1,0:T(8,128)(2,1)S(1)}, u32[]{:S(2)}) copy-start(bf16[2,3,80,128]{3,2,1,0:T(8,128)(2,1)S(1)} %collective-permute-done.5.refs_6_) | copy-start | bytes 368644
  43.6 2.8 collective-permute-start.17
  43.6 15.5 %copy-start.11 = (bf16[2,3,80,128]{3,2,1,0:T(8,128)(2,1)}, bf16[2,3,80,128]{3,2,1,0:T(8,128)(2,1)S(1)}, u32[]{:S(2)}) copy-start(bf16[2,3,80,128]{3,2,1,0:T(8,128)(2,1)S(1)} %collective-permute-done.6.refs_7_) | copy-start | bytes 368644
  43.7 9.5 %collective-permute-start.18 = (bf16[2,3,80,128]{3,2,1,0:T(8,128)(2,1)}, bf16[2,3,80,128]{3,2,1,0:T(8,128)(2,1)S(1)}, u32[]{:S(2)}, u32[]{:S(2)}) collective-permute-start(bf16[2,3,80,128]{3,2,1,0:T(8,128)(2,1)} %get-tuple-element.89), channel_id=1, source_target_pairs={{0,29},{1,28},{2,31},{3,30},{4,1},{5,0},{6,3},{7,2},{8,5},{9,4},{1... | collective-permute-start | bytes 368648 | tf_op jit(solution)/shard_map/ppermute | solution.py:795
  46.4 85.8 %copy-start.29 = (bf16[2,3,80,128]{3,2,1,0:T(8,128)(2,1)}, bf16[2,3,80,128]{3,2,1,0:T(8,128)(2,1)S(1)}, u32[]{:S(2)}) copy-start(bf16[2,3,80,128]{3,2,1,0:T(8,128)(2,1)S(1)} %collective-permute-done.17.refs_12_) | copy-start | bytes 368644
  46.4 85.1 %collective-permute-start.14 = (bf16[2,3,144,128]{3,2,1,0:T(8,128)(2,1)}, bf16[2,3,144,128]{3,2,1,0:T(8,128)(2,1)S(1)}, u32[]{:S(2)}, u32[]{:S(2)}) collective-permute-start(bf16[2,3,144,128]{3,2,1,0:T(8,128)(2,1)} %get-tuple-element.85), channel_id=1, source_target_pairs={{0,1},{1,0},{2,3},{3,2},{4,5},{5,4},{6,7},{7,6},{8,9},{9,8},{10,11... | collective-permute-start | bytes 663560 | tf_op jit(solution)/shard_map/ppermute | solution.py:702
  53.8 77.8 %collective-permute-start.15 = (bf16[2,3,144,128]{3,2,1,0:T(8,128)(2,1)}, bf16[2,3,144,128]{3,2,1,0:T(8,128)(2,1)S(1)}, u32[]{:S(2)}, u32[]{:S(2)}) collective-permute-start(bf16[2,3,144,128]{3,2,1,0:T(8,128)(2,1)} %get-tuple-element.86), channel_id=1, source_target_pairs={{0,2},{1,3},{2,0},{3,1},{4,6},{5,7},{6,4},{7,5},{8,10},{9,11},{10,... | collective-permute-start | bytes 663560 | tf_op jit(solution)/shard_map/ppermute | solution.py:702
  55.3 76.3 %collective-permute-start.16 = (bf16[2,3,144,128]{3,2,1,0:T(8,128)(2,1)}, bf16[2,3,144,128]{3,2,1,0:T(8,128)(2,1)S(1)}, u32[]{:S(2)}, u32[]{:S(2)}) collective-permute-start(bf16[2,3,144,128]{3,2,1,0:T(8,128)(2,1)} %get-tuple-element.87), channel_id=1, source_target_pairs={{0,3},{1,2},{2,1},{3,0},{4,7},{5,6},{6,5},{7,4},{8,11},{9,10},{10,... | collective-permute-start | bytes 663560 | tf_op jit(solution)/shard_map/ppermute | solution.py:702
  55.8 75.7 %collective-permute-start.19 = (bf16[2,3,80,128]{3,2,1,0:T(8,128)(2,1)}, bf16[2,3,80,128]{3,2,1,0:T(8,128)(2,1)S(1)}, u32[]{:S(2)}, u32[]{:S(2)}) collective-permute-start(bf16[2,3,80,128]{3,2,1,0:T(8,128)(2,1)} %get-tuple-element.90), channel_id=1, source_target_pairs={{0,30},{1,31},{2,28},{3,29},{4,2},{5,3},{6,0},{7,1},{8,6},{9,7},{1... | collective-permute-start | bytes 368648 | tf_op jit(solution)/shard_map/ppermute | solution.py:795
  55.8 75.7 %collective-permute-start.20 = (bf16[2,3,80,128]{3,2,1,0:T(8,128)(2,1)}, bf16[2,3,80,128]{3,2,1,0:T(8,128)(2,1)S(1)}, u32[]{:S(2)}, u32[]{:S(2)}) collective-permute-start(bf16[2,3,80,128]{3,2,1,0:T(8,128)(2,1)} %get-tuple-element.91), channel_id=1, source_target_pairs={{0,31},{1,30},{2,29},{3,28},{4,3},{5,2},{6,1},{7,0},{8,7},{9,6},{1... | collective-permute-start | bytes 368648 | tf_op jit(solution)/shard_map/ppermute | solution.py:795
  225.3 2.2 collective-permute-start.28
  227.7 39.3 %copy-start.50 = (bf16[2,3,80,128]{3,2,1,0:T(8,128)(2,1)S(1)}, bf16[2,3,80,128]{3,2,1,0:T(8,128)(2,1)}, u32[]{:S(2)}) copy-start(bf16[2,3,80,128]{3,2,1,0:T(8,128)(2,1)} %get-tuple-element.80) | copy-start | bytes 368644
  227.7 39.8 %copy-start.49 = (bf16[2,3,80,128]{3,2,1,0:T(8,128)(2,1)S(1)}, bf16[2,3,80,128]{3,2,1,0:T(8,128)(2,1)}, u32[]{:S(2)}) copy-start(bf16[2,3,80,128]{3,2,1,0:T(8,128)(2,1)} %get-tuple-element.81) | copy-start | bytes 368644
  227.7 40.2 %copy-start.48 = (bf16[2,3,80,128]{3,2,1,0:T(8,128)(2,1)S(1)}, bf16[2,3,80,128]{3,2,1,0:T(8,128)(2,1)}, u32[]{:S(2)}) copy-start(bf16[2,3,80,128]{3,2,1,0:T(8,128)(2,1)} %get-tuple-element.82) | copy-start | bytes 368644
  227.7 40.2 %copy-start.47 = (bf16[2,3,80,128]{3,2,1,0:T(8,128)(2,1)S(1)}, bf16[2,3,80,128]{3,2,1,0:T(8,128)(2,1)}, u32[]{:S(2)}) copy-start(bf16[2,3,80,128]{3,2,1,0:T(8,128)(2,1)} %get-tuple-element.83) | copy-start | bytes 368644
  227.8 50.6 %copy-start.44 = (bf16[2,3,144,128]{3,2,1,0:T(8,128)(2,1)S(1)}, bf16[2,3,144,128]{3,2,1,0:T(8,128)(2,1)}, u32[]{:S(2)}) copy-start(bf16[2,3,144,128]{3,2,1,0:T(8,128)(2,1)} %get-tuple-element.78) | copy-start | bytes 663556
  227.8 54.2 %copy-start.42 = (bf16[2,3,144,128]{3,2,1,0:T(8,128)(2,1)S(1)}, bf16[2,3,144,128]{3,2,1,0:T(8,128)(2,1)}, u32[]{:S(2)}) copy-start(bf16[2,3,144,128]{3,2,1,0:T(8,128)(2,1)} %get-tuple-element.79) | copy-start | bytes 663556
  227.8 64.1 %copy-start.43 = (bf16[2,3,144,128]{3,2,1,0:T(8,128)(2,1)S(1)}, bf16[2,3,144,128]{3,2,1,0:T(8,128)(2,1)}, u32[]{:S(2)}) copy-start(bf16[2,3,144,128]{3,2,1,0:T(8,128)(2,1)} %get-tuple-element.103) | copy-start | bytes 663556
  227.8 8.1 %collective-permute-start.31 = (bf16[656,128]{1,0:T(8,128)(2,1)S(1)}, bf16[656,128]{1,0:T(8,128)(2,1)S(1)}, u32[]{:S(2)}, u32[]{:S(2)}) collective-permute-start(bf16[656,128]{1,0:T(8,128)(2,1)S(1)} %get-tuple-element.124), channel_id=1, source_target_pairs={{0,3},{1,2},{2,1},{3,0},{4,7},{5,6},{6,5},{7,4},{8,11},{9,10},{10,... | collective-permute-start | bytes 503816 | tf_op jit(solution)/shard_map/ppermute | solution.py:702
  229.4 9.4 %collective-permute-start.30 = (bf16[656,128]{1,0:T(8,128)(2,1)S(1)}, bf16[656,128]{1,0:T(8,128)(2,1)S(1)}, u32[]{:S(2)}, u32[]{:S(2)}) collective-permute-start(bf16[656,128]{1,0:T(8,128)(2,1)S(1)} %get-tuple-element.125), channel_id=1, source_target_pairs={{0,2},{1,3},{2,0},{3,1},{4,6},{5,7},{6,4},{7,5},{8,10},{9,11},{10,... | collective-permute-start | bytes 503816 | tf_op jit(solution)/shard_map/ppermute | solution.py:702
  229.9 8.9 %collective-permute-start.29 = (bf16[656,128]{1,0:T(8,128)(2,1)S(1)}, bf16[656,128]{1,0:T(8,128)(2,1)S(1)}, u32[]{:S(2)}, u32[]{:S(2)}) collective-permute-start(bf16[656,128]{1,0:T(8,128)(2,1)S(1)} %get-tuple-element.123), channel_id=1, source_target_pairs={{0,1},{1,0},{2,3},{3,2},{4,5},{5,4},{6,7},{7,6},{8,9},{9,8},{10,11... | collective-permute-start | bytes 503816 | tf_op jit(solution)/shard_map/ppermute | solution.py:702
  238.9 9.2 %collective-permute-start.34 = (bf16[656,128]{1,0:T(8,128)(2,1)S(1)}, bf16[656,128]{1,0:T(8,128)(2,1)S(1)}, u32[]{:S(2)}, u32[]{:S(2)}) collective-permute-start(bf16[656,128]{1,0:T(8,128)(2,1)S(1)} %fusion.1), channel_id=1, source_target_pairs={{0,24},{4,28},{8,16},{12,20},{16,8},{20,12},{24,0},{28,4},{1,25},{... | collective-permute-start | bytes 503816 | tf_op jit(solution)/shard_map/ppermute | solution.py:706
  239.4 17.5 %collective-permute-start.33 = (bf16[656,128]{1,0:T(8,128)(2,1)S(1)}, bf16[656,128]{1,0:T(8,128)(2,1)S(1)}, u32[]{:S(2)}, u32[]{:S(2)}) collective-permute-start(bf16[656,128]{1,0:T(8,128)(2,1)S(1)} %fusion.1), channel_id=1, source_target_pairs={{0,16},{4,20},{8,24},{12,28},{16,0},{20,4},{24,8},{28,12},{1,17},{... | collective-permute-start | bytes 503816 | tf_op jit(solution)/shard_map/ppermute | solution.py:706
  242.0 14.9 %collective-permute-start.32 = (bf16[656,128]{1,0:T(8,128)(2,1)S(1)}, bf16[656,128]{1,0:T(8,128)(2,1)S(1)}, u32[]{:S(2)}, u32[]{:S(2)}) collective-permute-start(bf16[656,128]{1,0:T(8,128)(2,1)S(1)} %fusion.1), channel_id=1, source_target_pairs={{0,8},{4,12},{8,0},{12,4},{16,24},{20,28},{24,16},{28,20},{1,9},{5... | collective-permute-start | bytes 503816 | tf_op jit(solution)/shard_map/ppermute | solution.py:706
  257.0 8.1 %collective-permute-start.37 = (bf16[656,128]{1,0:T(8,128)(2,1)S(1)}, bf16[656,128]{1,0:T(8,128)(2,1)S(1)}, u32[]{:S(2)}, u32[]{:S(2)}) collective-permute-start(bf16[656,128]{1,0:T(8,128)(2,1)S(1)} %add_convert_fusion.1), channel_id=1, source_target_pairs={{0,3},{1,2},{2,1},{3,0},{4,7},{5,6},{6,5},{7,4},{8,11},{9,10},{10,... | collective-permute-start | bytes 503816 | tf_op jit(solution)/shard_map/ppermute | solution.py:702
  258.5 8.3 %collective-permute-start.36 = (bf16[656,128]{1,0:T(8,128)(2,1)S(1)}, bf16[656,128]{1,0:T(8,128)(2,1)S(1)}, u32[]{:S(2)}, u32[]{:S(2)}) collective-permute-start(bf16[656,128]{1,0:T(8,128)(2,1)S(1)} %add_convert_fusion.1), channel_id=1, source_target_pairs={{0,2},{1,3},{2,0},{3,1},{4,6},{5,7},{6,4},{7,5},{8,10},{9,11},{10,... | collective-permute-start | bytes 503816 | tf_op jit(solution)/shard_map/ppermute | solution.py:702
  259.0 7.8 %collective-permute-start.35 = (bf16[656,128]{1,0:T(8,128)(2,1)S(1)}, bf16[656,128]{1,0:T(8,128)(2,1)S(1)}, u32[]{:S(2)}, u32[]{:S(2)}) collective-permute-start(bf16[656,128]{1,0:T(8,128)(2,1)S(1)} %add_convert_fusion.1), channel_id=1, source_target_pairs={{0,1},{1,0},{2,3},{3,2},{4,5},{5,4},{6,7},{7,6},{8,9},{9,8},{10,11... | collective-permute-start | bytes 503816 | tf_op jit(solution)/shard_map/ppermute | solution.py:702
  266.9 45.0 %copy-start.2 = (bf16[4,656,128]{2,1,0:T(8,128)(2,1)}, bf16[4,656,128]{2,1,0:T(8,128)(2,1)S(1)}, u32[]{:S(2)}) copy-start(bf16[4,656,128]{2,1,0:T(8,128)(2,1)S(1)} %pad_maximum_fusion.own) | copy-start | bytes 2015236
  266.9 45.0 %collective-permute-start.38 = (bf16[4,656,128]{2,1,0:T(8,128)(2,1)S(1)}, bf16[4,656,128]{2,1,0:T(8,128)(2,1)S(1)}, u32[]{:S(2)}, u32[]{:S(2)}) collective-permute-start(bf16[4,656,128]{2,1,0:T(8,128)(2,1)S(1)} %pad_maximum_fusion.own), channel_id=1, source_target_pairs={{0,4},{4,0},{8,12},{12,8},{16,20},{20,16},{24,28},{28,24},{1,5},{5... | collective-permute-start | bytes 2015240 | tf_op jit(solution)/shard_map/ppermute | solution.py:706
  267.0 6.2 %collective-permute-start.10 = (bf16[2,3,80,128]{3,2,1,0:T(8,128)(2,1)S(1)}, bf16[2,3,80,128]{3,2,1,0:T(8,128)(2,1)S(1)}, u32[]{:S(2)}, u32[]{:S(2)}) collective-permute-start(bf16[2,3,80,128]{3,2,1,0:T(8,128)(2,1)S(1)} %copy-done.50), channel_id=1, source_target_pairs={{0,4},{1,5},{2,6},{3,7},{4,8},{5,9},{6,10},{7,11},{8,12},{9,13},{1... | collective-permute-start | bytes 368648 | tf_op jit(solution)/shard_map/ppermute | solution.py:795
  267.5 7.2 %collective-permute-start.11 = (bf16[2,3,80,128]{3,2,1,0:T(8,128)(2,1)S(1)}, bf16[2,3,80,128]{3,2,1,0:T(8,128)(2,1)S(1)}, u32[]{:S(2)}, u32[]{:S(2)}) collective-permute-start(bf16[2,3,80,128]{3,2,1,0:T(8,128)(2,1)S(1)} %copy-done.49), channel_id=1, source_target_pairs={{0,5},{1,4},{2,7},{3,6},{4,9},{5,8},{6,11},{7,10},{8,13},{9,12},{1... | collective-permute-start | bytes 368648 | tf_op jit(solution)/shard_map/ppermute | solution.py:795
  267.9 8.1 %collective-permute-start.12 = (bf16[2,3,80,128]{3,2,1,0:T(8,128)(2,1)S(1)}, bf16[2,3,80,128]{3,2,1,0:T(8,128)(2,1)S(1)}, u32[]{:S(2)}, u32[]{:S(2)}) collective-permute-start(bf16[2,3,80,128]{3,2,1,0:T(8,128)(2,1)S(1)} %copy-done.48), channel_id=1, source_target_pairs={{0,6},{1,7},{2,4},{3,5},{4,10},{5,11},{6,8},{7,9},{8,14},{9,15},{1... | collective-permute-start | bytes 368648 | tf_op jit(solution)/shard_map/ppermute | solution.py:795
  267.9 10.4 %collective-permute-start.13 = (bf16[2,3,80,128]{3,2,1,0:T(8,128)(2,1)S(1)}, bf16[2,3,80,128]{3,2,1,0:T(8,128)(2,1)S(1)}, u32[]{:S(2)}, u32[]{:S(2)}) collective-permute-start(bf16[2,3,80,128]{3,2,1,0:T(8,128)(2,1)S(1)} %copy-done.47), channel_id=1, source_target_pairs={{0,7},{1,6},{2,5},{3,4},{4,11},{5,10},{6,9},{7,8},{8,15},{9,14},{1... | collective-permute-start | bytes 368648 | tf_op jit(solution)/shard_map/ppermute | solution.py:795
  273.2 22.5 %copy-start.35 = (bf16[2,3,80,128]{3,2,1,0:T(8,128)(2,1)}, bf16[2,3,80,128]{3,2,1,0:T(8,128)(2,1)S(1)}, u32[]{:S(2)}) copy-start(bf16[2,3,80,128]{3,2,1,0:T(8,128)(2,1)S(1)} %collective-permute-done.10.rest_4_) | copy-start | bytes 368644
  273.2 6.3 %collective-permute-start.24 = (bf16[2,3,80,128]{3,2,1,0:T(8,128)(2,1)}, bf16[2,3,80,128]{3,2,1,0:T(8,128)(2,1)S(1)}, u32[]{:S(2)}, u32[]{:S(2)}) collective-permute-start(bf16[2,3,80,128]{3,2,1,0:T(8,128)(2,1)} %get-tuple-element.104), channel_id=1, source_target_pairs={{0,4},{1,5},{2,6},{3,7},{4,8},{5,9},{6,10},{7,11},{8,12},{9,13},{1... | collective-permute-start | bytes 368648 | tf_op jit(solution)/shard_map/ppermute | solution.py:795
  274.7 21.0 %copy-start.36 = (bf16[2,3,80,128]{3,2,1,0:T(8,128)(2,1)}, bf16[2,3,80,128]{3,2,1,0:T(8,128)(2,1)S(1)}, u32[]{:S(2)}) copy-start(bf16[2,3,80,128]{3,2,1,0:T(8,128)(2,1)S(1)} %collective-permute-done.11.rest_5_) | copy-start | bytes 368644
  274.7 7.3 %collective-permute-start.25 = (bf16[2,3,80,128]{3,2,1,0:T(8,128)(2,1)}, bf16[2,3,80,128]{3,2,1,0:T(8,128)(2,1)S(1)}, u32[]{:S(2)}, u32[]{:S(2)}) collective-permute-start(bf16[2,3,80,128]{3,2,1,0:T(8,128)(2,1)} %get-tuple-element.105), channel_id=1, source_target_pairs={{0,5},{1,4},{2,7},{3,6},{4,9},{5,8},{6,11},{7,10},{8,13},{9,12},{1... | collective-permute-start | bytes 368648 | tf_op jit(solution)/shard_map/ppermute | solution.py:795
  276.0 19.6 %copy-start.37 = (bf16[2,3,80,128]{3,2,1,0:T(8,128)(2,1)}, bf16[2,3,80,128]{3,2,1,0:T(8,128)(2,1)S(1)}, u32[]{:S(2)}) copy-start(bf16[2,3,80,128]{3,2,1,0:T(8,128)(2,1)S(1)} %collective-permute-done.12.rest_6_) | copy-start | bytes 368644
  276.0 15.1 %collective-permute-start.7 = (bf16[2,3,144,128]{3,2,1,0:T(8,128)(2,1)}, bf16[2,3,144,128]{3,2,1,0:T(8,128)(2,1)S(1)}, u32[]{:S(2)}, u32[]{:S(2)}) collective-permute-start(bf16[2,3,144,128]{3,2,1,0:T(8,128)(2,1)} %get-tuple-element.77), channel_id=1, source_target_pairs={{0,1},{1,0},{2,3},{3,2},{4,5},{5,4},{6,7},{7,6},{8,9},{9,8},{10,11... | collective-permute-start | bytes 663560 | tf_op jit(solution)/shard_map/ppermute | solution.py:702
  278.4 17.3 %copy-start.38 = (bf16[2,3,80,128]{3,2,1,0:T(8,128)(2,1)}, bf16[2,3,80,128]{3,2,1,0:T(8,128)(2,1)S(1)}, u32[]{:S(2)}) copy-start(bf16[2,3,80,128]{3,2,1,0:T(8,128)(2,1)S(1)} %collective-permute-done.13.rest_7_) | copy-start | bytes 368644
  278.4 13.5 %collective-permute-start.8 = (bf16[2,3,144,128]{3,2,1,0:T(8,128)(2,1)S(1)}, bf16[2,3,144,128]{3,2,1,0:T(8,128)(2,1)S(1)}, u32[]{:S(2)}, u32[]{:S(2)}) collective-permute-start(bf16[2,3,144,128]{3,2,1,0:T(8,128)(2,1)S(1)} %copy-done.44), channel_id=1, source_target_pairs={{0,2},{1,3},{2,0},{3,1},{4,6},{5,7},{6,4},{7,5},{8,10},{9,11},{10,... | collective-permute-start | bytes 663560 | tf_op jit(solution)/shard_map/ppermute | solution.py:702
  279.5 27.1 %copy-start.33 = (bf16[2,3,80,128]{3,2,1,0:T(8,128)(2,1)}, bf16[2,3,80,128]{3,2,1,0:T(8,128)(2,1)S(1)}, u32[]{:S(2)}) copy-start(bf16[2,3,80,128]{3,2,1,0:T(8,128)(2,1)S(1)} %collective-permute-done.24.rest_4_) | copy-start | bytes 368644
  279.5 10.3 %collective-permute-start.26 = (bf16[2,3,80,128]{3,2,1,0:T(8,128)(2,1)}, bf16[2,3,80,128]{3,2,1,0:T(8,128)(2,1)S(1)}, u32[]{:S(2)}, u32[]{:S(2)}) collective-permute-start(bf16[2,3,80,128]{3,2,1,0:T(8,128)(2,1)} %get-tuple-element.106), channel_id=1, source_target_pairs={{0,6},{1,7},{2,4},{3,5},{4,10},{5,11},{6,8},{7,9},{8,14},{9,15},{1... | collective-permute-start | bytes 368648 | tf_op jit(solution)/shard_map/ppermute | solution.py:795
  282.0 24.6 %copy-start.34 = (bf16[2,3,80,128]{3,2,1,0:T(8,128)(2,1)}, bf16[2,3,80,128]{3,2,1,0:T(8,128)(2,1)S(1)}, u32[]{:S(2)}) copy-start(bf16[2,3,80,128]{3,2,1,0:T(8,128)(2,1)S(1)} %collective-permute-done.25.rest_5_) | copy-start | bytes 368644
  282.0 11.3 %collective-permute-start.9 = (bf16[2,3,144,128]{3,2,1,0:T(8,128)(2,1)S(1)}, bf16[2,3,144,128]{3,2,1,0:T(8,128)(2,1)S(1)}, u32[]{:S(2)}, u32[]{:S(2)}) collective-permute-start(bf16[2,3,144,128]{3,2,1,0:T(8,128)(2,1)S(1)} %copy-done.42), channel_id=1, source_target_pairs={{0,3},{1,2},{2,1},{3,0},{4,7},{5,6},{6,5},{7,4},{8,11},{9,10},{10,... | collective-permute-start | bytes 663560 | tf_op jit(solution)/shard_map/ppermute | solution.py:702
  289.8 16.9 %copy-start.39 = (bf16[2,3,80,128]{3,2,1,0:T(8,128)(2,1)}, bf16[2,3,80,128]{3,2,1,0:T(8,128)(2,1)S(1)}, u32[]{:S(2)}) copy-start(bf16[2,3,80,128]{3,2,1,0:T(8,128)(2,1)S(1)} %collective-permute-done.26.rest_6_) | copy-start | bytes 368644
  289.8 14.8 %collective-permute-start.21 = (bf16[2,3,144,128]{3,2,1,0:T(8,128)(2,1)}, bf16[2,3,144,128]{3,2,1,0:T(8,128)(2,1)S(1)}, u32[]{:S(2)}, u32[]{:S(2)}) collective-permute-start(bf16[2,3,144,128]{3,2,1,0:T(8,128)(2,1)} %get-tuple-element.101), channel_id=1, source_target_pairs={{0,1},{1,0},{2,3},{3,2},{4,5},{5,4},{6,7},{7,6},{8,9},{9,8},{10,11... | collective-permute-start | bytes 663560 | tf_op jit(solution)/shard_map/ppermute | solution.py:702
  291.1 15.5 %collective-permute-start.22 = (bf16[2,3,144,128]{3,2,1,0:T(8,128)(2,1)}, bf16[2,3,144,128]{3,2,1,0:T(8,128)(2,1)S(1)}, u32[]{:S(2)}, u32[]{:S(2)}) collective-permute-start(bf16[2,3,144,128]{3,2,1,0:T(8,128)(2,1)} %get-tuple-element.102), channel_id=1, source_target_pairs={{0,2},{1,3},{2,0},{3,1},{4,6},{5,7},{6,4},{7,5},{8,10},{9,11},{10,... | collective-permute-start | bytes 663560 | tf_op jit(solution)/shard_map/ppermute | solution.py:702
  291.9 14.8 %collective-permute-start.23 = (bf16[2,3,144,128]{3,2,1,0:T(8,128)(2,1)S(1)}, bf16[2,3,144,128]{3,2,1,0:T(8,128)(2,1)S(1)}, u32[]{:S(2)}, u32[]{:S(2)}) collective-permute-start(bf16[2,3,144,128]{3,2,1,0:T(8,128)(2,1)S(1)} %copy-done.43), channel_id=1, source_target_pairs={{0,3},{1,2},{2,1},{3,0},{4,7},{5,6},{6,5},{7,4},{8,11},{9,10},{10,... | collective-permute-start | bytes 663560 | tf_op jit(solution)/shard_map/ppermute | solution.py:702
  293.3 11.2 %collective-permute-start.27 = (bf16[2,3,80,128]{3,2,1,0:T(8,128)(2,1)}, bf16[2,3,80,128]{3,2,1,0:T(8,128)(2,1)S(1)}, u32[]{:S(2)}, u32[]{:S(2)}) collective-permute-start(bf16[2,3,80,128]{3,2,1,0:T(8,128)(2,1)} %get-tuple-element.107), channel_id=1, source_target_pairs={{0,7},{1,6},{2,5},{3,4},{4,11},{5,10},{6,9},{7,8},{8,15},{9,14},{1... | collective-permute-start | bytes 368648 | tf_op jit(solution)/shard_map/ppermute | solution.py:795
  (27 other events, 84.1 us)

commit v2 on v1

v2 whole, which is shorter than its diff:
```python
import functools

import jax
import jax.numpy as jnp
import numpy as np
from jax import lax
from jax.experimental import pallas as pl
from jax.experimental.pallas import tpu as pltpu
from jax.sharding import PartitionSpec as P

WLAT = 6
WLON = 12
TOK = WLAT * WLON
HALF = TOK // 2
HALO0 = 32
HALO = TOK - HALO0
GROUP = 8
CHUNK = 2
EPSILON = 1e-05
NEGATIVE = -1000000000.0
F32 = jnp.float32
BF16 = jnp.bfloat16
LANES = 128
UNIT = 16


def up16(n):
    return (n + 15) // 16 * 16


def nn(a, b, **kw):
    return lax.dot_general(a, b, (((1,), (0,)), ((), ())), preferred_element_type=F32, **kw)


def nt(a, b):
    return lax.dot_general(a, b, (((1,), (1,)), ((), ())), preferred_element_type=F32)


def tn(a, b):
    return lax.dot_general(a, b, (((0,), (0,)), ((), ())), preferred_element_type=F32)


class Sizes:
    def __init__(self, lev, lon, shape, heads, hidden):
        self.lev, self.lon = lev, lon
        self.s, self.l, self.rows, self.cells, self.d = shape
        self.heads, self.ff = heads, hidden
        self.bands = self.rows // WLAT
        self.nb = self.bands // lev
        self.lt = self.l * lev
        self.n = self.lt * TOK
        self.ro = up16(self.nb * TOK)
        self.rh = self.nb * HALO
        self.nblk = self.l + (self.l + 1) // 2
        self.tokens = self.cells * self.rows
        self.np = 2 * lev
        self.blocks = 2 * (2 * hidden // 2 + 3 * self.d + self.d) // LANES * (self.d // 96)
        self.hb = self.blocks // self.np
        self.units = self.bands * 4 + 2
        self.upp = -(-self.units // self.np)
        self.pr = self.hb * 96 + self.upp * UNIT


def slot_rows(z):
    own = np.full((z.ro,), -(10**6), np.int32)
    halo = np.full((z.rh,), -(10**6), np.int32)
    for b in range(z.nb):
        for t in range(TOK):
            own[b * TOK + t] = (t // WLAT) * z.rows + b * WLAT + t % WLAT
            if t >= HALF:
                halo[b * HALO + t - HALO0] = own[b * TOK + t] - z.tokens
    return own, halo


def lane_parts(z, levels):
    parts = [v[:, :LANES] for v in levels]
    high = [v[:, LANES:] for v in levels]
    if z.l % 2:
        high.append(jnp.zeros_like(high[0]))
    for l in range(0, len(high), 2):
        parts.append(jnp.concatenate([high[l], high[l + 1]], axis=1))
    return parts


def pack_kernel(z, scal, base, x_ref, halo_ref, *rest):
    outs, onehot = rest[: z.lev], rest[z.lev]
    p = scal[0]
    off = scal[1 + pl.program_id(0)]
    rows = z.tokens + halo_ref.shape[2] * z.rows
    column = lax.broadcasted_iota(jnp.int32, (z.ro, rows), 1)
    for k in range(z.lev):
        hit = column == base[...] + (off * z.rows + (p ^ k) * (z.nb * WLAT))
        onehot[k * z.ro : (k + 1) * z.ro] = jnp.where(hit, 1.0, 0.0).astype(BF16)
    levels = []
    for l in range(z.l):
        cells = [r[0, l].reshape(r.shape[2] * z.rows, z.d) for r in (x_ref, halo_ref)]
        levels.append(jnp.concatenate(cells, axis=0))
    moved = nn(onehot[...], jnp.concatenate(lane_parts(z, levels), axis=1)).astype(BF16)
    for k in range(z.lev):
        for j in range(z.nblk):
            outs[k][0, j] = moved[k * z.ro : (k + 1) * z.ro, j * LANES : (j + 1) * LANES]


def pack(z, x, halo, scal):
    own, _ = slot_rows(z)
    tokens = lambda a: pl.BlockSpec((1,) + a.shape[1:], lambda s, _: (s, 0, 0, 0, 0))
    spec = pl.BlockSpec((1, z.nblk, z.ro, LANES), lambda s, _: (s, 0, 0, 0))
    return pl.pallas_call(
        functools.partial(pack_kernel, z),
        grid_spec=pltpu.PrefetchScalarGridSpec(
            num_scalar_prefetch=1,
            grid=(x.shape[0],),
            in_specs=[pl.BlockSpec((z.ro, 1), lambda s, _: (0, 0)), tokens(x), tokens(halo)],
            out_specs=[spec] * z.lev,
            scratch_shapes=[
                pltpu.VMEM((z.lev * z.ro, z.tokens + halo.shape[2] * z.rows), BF16)
            ],
        ),
        out_shape=[jax.ShapeDtypeStruct((x.shape[0], z.nblk, z.ro, LANES), BF16)] * z.lev,
        compiler_params=pltpu.CompilerParams(vmem_limit_bytes=60 * 2**20),
        cost_estimate=cost(4),
        name="pack",
    )(scal, jnp.asarray(own)[:, None], x, halo)


def unpack_kernel(z, scal, own_base, halo_base, *rest):
    pieces, halo_ref, out_ref, onehot = rest[: z.lev], rest[z.lev], rest[z.lev + 1], rest[z.lev + 2]
    p = scal[0]
    off = scal[1 + pl.program_id(0)]
    at = 0
    for base, size in ((own_base, z.ro), (halo_base, z.rh)):
        row = lax.broadcasted_iota(jnp.int32, (z.tokens, size), 0)
        for k in range(z.lev):
            hit = row == base[...] + (off * z.rows + (p ^ k) * (z.nb * WLAT))
            onehot[:, at : at + size] = jnp.where(hit, 1.0, 0.0).astype(BF16)
            at += size
    columns = []
    for j in range(z.nblk):
        rows = [r[0, j] for r in pieces] + [halo_ref[k, 0, j] for k in range(z.lev)]
        columns.append(jnp.concatenate(rows, axis=0))
    moved = nn(onehot[...], jnp.concatenate(columns, axis=1))
    half = z.d - LANES
    for l in range(z.l):
        low = moved[:, l * LANES : (l + 1) * LANES]
        at = (z.l + l // 2) * LANES + (l % 2) * half
        tokens = jnp.concatenate([low, moved[:, at : at + half]], axis=1)
        out_ref[0, l] = tokens.reshape(z.cells, z.rows, z.d).astype(BF16)


def unpack(z, own, halo, scal):
    bases = [jnp.asarray(v)[None] for v in slot_rows(z)]
    spec = pl.BlockSpec((1, z.nblk, z.ro, LANES), lambda s, _: (s, 0, 0, 0))
    return pl.pallas_call(
        functools.partial(unpack_kernel, z),
        grid_spec=pltpu.PrefetchScalarGridSpec(
            num_scalar_prefetch=1,
            grid=(z.s,),
            in_specs=[pl.BlockSpec((1, v.shape[1]), lambda s, _: (0, 0)) for v in bases]
            + [spec] * z.lev
            + [pl.BlockSpec((z.lev, 1, z.nblk, z.rh, LANES), lambda s, _: (0, s, 0, 0, 0))],
            out_specs=pl.BlockSpec((1, z.l, z.cells, z.rows, z.d), lambda s, _: (s, 0, 0, 0, 0)),
            scratch_shapes=[pltpu.VMEM((z.tokens, z.lev * (z.ro + z.rh)), BF16)],
        ),
        out_shape=jax.ShapeDtypeStruct((z.s, z.l, z.cells, z.rows, z.d), BF16),
        compiler_params=pltpu.CompilerParams(vmem_limit_bytes=60 * 2**20),
        cost_estimate=cost(4),
        name="unpack",
    )(scal, *bases, *own, halo)


def cost(microseconds):
    return pl.CostEstimate(
        flops=int(microseconds * 5e8), transcendentals=0, bytes_accessed=int(microseconds * 3e6)
    )


def loop(n, body, unroll=None):
    unroll = n if unroll is None else unroll

    def some(i, c):
        for j in range(unroll):
            body(i * unroll + j)
        return c

    if n == unroll:
        some(0, 0)
    else:
        lax.fori_loop(0, n // unroll, some, 0)


def head_masks(z, weight=1.0):
    lane = lax.broadcasted_iota(jnp.int32, (1, LANES), 1)
    size = z.d // z.heads
    inside = [(lane >= h * size) & (lane < (h + 1) * size) for h in range(z.heads // 2)]
    return [jnp.where(m, weight, 0.0) for m in inside]


def spread(values, factors):
    return jnp.concatenate([values * f for f in factors], axis=0).astype(BF16)


def gather_heads(stacked, factors):
    n = stacked.shape[0] // len(factors)
    total = stacked[:n] * factors[0]
    for h in range(1, len(factors)):
        total = total + stacked[h * n : (h + 1) * n] * factors[h]
    return total


def pipelined(n, first, second, third):
    one, two = {}, {}
    for i in range(n + 2):
        if i < n:
            one[i] = first(i)
        if 0 <= i - 1 < n:
            two[i - 1] = second(i - 1, one.pop(i - 1))
        if i >= 2:
            third(i - 2, two.pop(i - 2))


def score(q, k, ones):
    return nt(k.astype(BF16), spread(q, ones))


def soften(scores):
    exps = jnp.exp2(scores - jnp.max(scores, axis=0, keepdims=True))
    return (exps * (1.0 / jnp.sum(exps, axis=0, keepdims=True))).astype(BF16)


def mix(probs, v, ones):
    return gather_heads(tn(probs, v.astype(BF16)), ones)


def grad_scores_of(probs, grad_probs):
    wide = probs.astype(F32)
    inner = jnp.sum(grad_probs * wide, axis=0, keepdims=True)
    return (wide * (grad_probs - inner)).astype(BF16)


def centered(values):
    return values - jnp.mean(values, axis=-1, keepdims=True)


def rstd_of(center):
    return lax.rsqrt(jnp.mean(center * center, axis=-1, keepdims=True) + EPSILON)


def norm_levels(n, load, store):
    def first(i):
        values = load(i)
        return values, centered(values)

    def second(i, got):
        return got + (rstd_of(got[1]),)

    def third(i, got):
        values, center, rstd = got
        store(i, values, center * rstd, rstd)

    pipelined(n, first, second, third)


def fold_rows(values):
    return jnp.sum(values.reshape(values.shape[0] // 8, 8, values.shape[1]), axis=0)


def load_wire(z, refs, wire_s):
    for k in range(z.lev):
        wire_s[k] = refs[k][0].astype(F32)


def wire_level(z, wire_s, k, l, b):
    half = z.d - LANES
    at = (l % 2) * half
    rows = pl.ds(pl.multiple_of(b * TOK, 8), TOK)
    low, high = wire_s[k, l, rows, :], wire_s[k, z.l + l // 2, rows, :]
    return jnp.concatenate([low, high[:, at : at + half]], axis=1)


def store_wire_levels(z, wire_s, b, level):
    for k in range(z.lev):
        parts = lane_parts(z, [level(k * z.l + l) for l in range(z.l)])
        for j, part in enumerate(parts):
            wire_s[k, j, pl.ds(pl.multiple_of(b * TOK, 8), TOK), :] = part


def flush_wire(z, wire_s, refs):
    if z.ro > z.nb * TOK:
        wire_s[:, :, z.nb * TOK :, :] = jnp.zeros_like(wire_s[:, :, z.nb * TOK :, :])
    for k in range(z.lev):
        refs[k][0] = wire_s[k].astype(BF16)


def bf16_rows(z, ref):
    return ref[...].reshape(z.n, ref.shape[-1]).astype(BF16)


def put_rows(z, ref, values):
    ref[...] = values.reshape(z.lt, TOK, values.shape[-1])


def some_rows(z, ref, i):
    rows = ref[i * CHUNK : (i + 1) * CHUNK]
    return rows.reshape(CHUNK * TOK, ref.shape[-1]).astype(BF16)


def tile(j, t):
    return slice((2 * j + t) * LANES, (2 * j + t + 1) * LANES)


def put(ref, at, value):
    ref[at] = value


def group(g):
    return slice(g * GROUP, (g + 1) * GROUP)


def attention(n, qkv, bias, probs_at, store, ones, factor):
    def first(i):
        return [
            (score(qkv(i, 0, t), qkv(i, 1, t), ones) * factor + bias(t), qkv(i, 2, t)) for t in range(2)
        ]

    def second(i, got):
        return [(soften(scores), v) for scores, v in got]

    def third(i, got):
        outs = [mix(probs, v, ones) for probs, v in got]
        for t in range(2):
            probs_at(i, t)[...] = got[t][0]
            store(i, t, outs[t])

    pipelined(n, first, second, third)


def attention_back(n, qkv, grad, probs_at, store, ones, scales, scale):
    def first(i):
        out = []
        for t in range(2):
            q, k, v = (qkv(i, j, t) for j in range(3))
            g_rows = spread(grad(i, t), ones)
            out.append(
                (probs_at(i, t)[...], nt(v.astype(BF16), g_rows), g_rows, spread(q, ones), k.astype(BF16))
            )
        return out

    def second(i, got):
        return [(item[0], grad_scores_of(item[0], item[1])) + item[2:] for item in got]

    def third(i, got):
        outs = []
        for probs, grad_scores, g_rows, q_rows, k in got:
            outs.append(
                (
                    gather_heads(tn(grad_scores, k), scales),
                    nn(grad_scores, q_rows) * scale,
                    nn(probs, g_rows),
                    grad_scores,
                )
            )
        for t in range(2):
            store(i, t, outs[t])

    pipelined(n, first, second, third)


def score_factor(z):
    return np.float32((z.d // z.heads) ** (-0.5) * np.log2(np.e))


def forward_kernel(z, *refs):
    it = iter(refs)
    take = lambda n: [next(it) for _ in range(n)]
    wire_in = take(z.lev)
    bias_ref, mask_ref, column_mask = take(3)
    gain1, shift1, gain2, shift2, gain3, shift3 = take(6)
    w_qkv1, wo1, w_qkv2, wo2, w_up, w_down_t = take(6)
    wire_out = take(z.lev)
    norm1_ref, norm2_ref, norm3_ref, att_ref, co_ref, act_ref, slope_ref, probs_ref, probs2_ref = take(9)
    wire_s, x_s, n_s, o_s, a_s, qkv_s, bias_s = take(7)
    ones = head_masks(z)
    b = pl.program_id(1)

    @pl.when(b == 0)
    def _():
        load_wire(z, wire_in, wire_s)

    bias_s[...] = bias_ref[0] + mask_ref[0, 0]

    def keep(ref, gain, shift):
        def store(lv, values, normed, rstd):
            x_s[lv] = values
            n_s[lv] = normed * gain[...] + shift[...]
            room = jnp.broadcast_to(rstd, (TOK, 2 * LANES - z.d))
            ref[0, 0, lv] = jnp.concatenate([normed, room], axis=1)

        return store

    norm_levels(
        z.lt, lambda lv: wire_level(z, wire_s, lv // z.l, lv % z.l, b), keep(norm1_ref, gain1, shift1)
    )
    put_rows(z, qkv_s, nn(bf16_rows(z, n_s), w_qkv1[...]))

    attention(
        z.lt,
        lambda lv, j, t: qkv_s[lv, :, tile(j, t)],
        lambda t: bias_s[t],
        lambda lv, t: probs_ref.at[0, 0, lv, t],
        lambda lv, t, out: put(a_s, (lv, slice(None), tile(0, t)), out),
        ones,
        score_factor(z),
    )
    att = bf16_rows(z, a_s)
    att_ref[0, 0] = att
    put_rows(z, o_s, nn(att, wo1[...]))

    norm_levels(z.lt, lambda lv: x_s[lv] + o_s[lv], keep(norm2_ref, gain2, shift2))
    put_rows(z, qkv_s, nn(bf16_rows(z, n_s), w_qkv2[...]))

    attention(
        TOK // GROUP,
        lambda g, j, t: qkv_s[:, group(g), tile(j, t)].reshape(z.lt * GROUP, LANES),
        lambda t: column_mask[...],
        lambda g, t: probs2_ref.at[0, 0, g, t],
        lambda g, t, out: put(a_s, (slice(None), group(g), tile(0, t)), out.reshape(z.lt, GROUP, LANES)),
        ones,
        score_factor(z),
    )
    co = bf16_rows(z, a_s)
    co_ref[0, 0] = co
    put_rows(z, o_s, nn(co, wo2[...]))

    norm_levels(z.lt, lambda lv: x_s[lv] + o_s[lv], keep(norm3_ref, gain3, shift3))

    def up(i):
        return nn(some_rows(z, n_s, i), w_up[...])

    def gelu(i, hidden):
        share = 0.5 + 0.5 * lax.erf(hidden * (0.5**0.5))
        density = jnp.exp(hidden * hidden * -0.5) * ((2.0 * np.pi) ** -0.5)
        return (hidden * share).astype(BF16), (share + hidden * density).astype(BF16)

    def down(i, got):
        act, slope = got
        out = nt(act, w_down_t[...])
        rows = slice(i * CHUNK * TOK, (i + 1) * CHUNK * TOK)
        act_ref[0, 0, rows], slope_ref[0, 0, rows] = act, slope
        o_s[i * CHUNK : (i + 1) * CHUNK] = out.reshape(CHUNK, TOK, z.d)

    pipelined(z.lt // CHUNK, up, gelu, down)

    store_wire_levels(z, wire_s, b, lambda lv: x_s[lv] + o_s[lv])

    @pl.when(b == z.nb - 1)
    def _():
        flush_wire(z, wire_s, wire_out)


def wire_specs(z):
    return [pl.BlockSpec((1, z.nblk, z.ro, LANES), lambda s, b: (s, 0, 0, 0))] * z.lev


def wire_shapes(z):
    return [jax.ShapeDtypeStruct((z.s, z.nblk, z.ro, LANES), BF16)] * z.lev


def unit_spec(shape):
    return pl.BlockSpec((1, 1) + shape, lambda s, b: (s, b) + (0,) * len(shape))


def whole_spec(array):
    return pl.BlockSpec(array.shape, lambda s, b: (0,) * array.ndim)


def residual_shapes(z):
    return [
        ((z.lt, TOK, 2 * LANES), F32),
        ((z.lt, TOK, 2 * LANES), F32),
        ((z.lt, TOK, 2 * LANES), F32),
        ((z.n, 2 * LANES), BF16),
        ((z.n, 2 * LANES), BF16),
        ((z.n, z.ff), BF16),
        ((z.n, z.ff), BF16),
        ((z.lt, 2, TOK, z.heads // 2 * TOK), BF16),
        ((TOK // GROUP, 2, z.lt * GROUP, z.heads // 2 * z.lt * GROUP), BF16),
    ]


def forward(z, wire, bias, mask, column_mask, norms, weights):
    res = residual_shapes(z)
    rows3 = (z.lt, TOK, z.d)
    out = pl.pallas_call(
        functools.partial(forward_kernel, z),
        grid=(z.s, z.nb),
        in_specs=wire_specs(z)
        + [
            pl.BlockSpec((1, 2, TOK, z.heads // 2 * TOK), lambda s, b: (b, 0, 0, 0)),
            pl.BlockSpec((1, 1, TOK, 1), lambda s, b: (s, b, 0, 0)),
            whole_spec(column_mask),
        ]
        + [whole_spec(a) for a in norms]
        + [whole_spec(a) for a in weights],
        out_specs=wire_specs(z) + [unit_spec(shape) for shape, _ in res],
        out_shape=wire_shapes(z) + [jax.ShapeDtypeStruct((z.s, z.nb) + shape, t) for shape, t in res],
        scratch_shapes=[pltpu.VMEM((z.lev, z.nblk, z.ro, LANES), F32)]
        + [pltpu.VMEM(rows3, F32)] * 3
        + [
            pltpu.VMEM((z.lt, TOK, 2 * LANES), F32),
            pltpu.VMEM((z.lt, TOK, 6 * LANES), F32),
            pltpu.VMEM((2, TOK, z.heads // 2 * TOK), F32),
        ],
        compiler_params=pltpu.CompilerParams(vmem_limit_bytes=60 * 2**20),
        cost_estimate=cost(30),
        name="forward",
    )(*wire, bias, mask, column_mask, *norms, *weights)
    return out[: z.lev], out[z.lev :]


def grad_list(z):
    return [
        ("up", z.ff), ("down_t", z.ff),
        ("qkv1", 3 * z.d), ("qkv2", 3 * z.d),
        ("o1", z.d), ("o2", z.d),
    ]


def half_blocks(z):
    full, rest = [], []
    for name, columns in grad_list(z):
        for row in range(0, z.d, 96):
            for col in range(0, columns, LANES):
                width = min(LANES, columns - col)
                (full if width == LANES else rest).append((name, row, col, width))
    out = [[piece + (0,)] for piece in full]
    for i in range(0, len(rest), 2):
        out.append([rest[i] + (0,), rest[i + 1] + (rest[i][3],)])
    return out


def grad_buffer(z, name, columns):
    if name[:3] == "qkv":
        return (z.d, 6 * LANES)
    if name[0] == "o":
        return (2 * LANES, columns)
    return (z.d, columns)


def grad_block(z, name, ref, row, col, width):
    half = z.d // 2
    if name[0] == "o":
        start = row // half * LANES
        return ref[start : start + 96, col : col + width]
    if name[:3] != "qkv":
        return ref[row : row + 96, col : col + width]
    pieces = []
    while width:
        t, lane = col // half, col % half
        count = min(width, half - lane)
        pieces.append(ref[row : row + 96, t * LANES + lane : t * LANES + lane + count])
        col, width = col + count, width - count
    return pieces[0] if len(pieces) == 1 else jnp.concatenate(pieces, axis=1)


def bias_rows(z):
    pick = np.zeros((WLON * 8, TOK), np.float32)
    for a in range(WLON):
        for i in range(WLAT):
            pick[a * 8 + i, a * WLAT + i] = 1.0
    return pick


def backward_kernel(z, scal, *refs):
    it = iter(refs)
    take = lambda n: [next(it) for _ in range(n)]
    wire_in = take(z.lev)
    norm1_ref, norm2_ref, norm3_ref, att_ref, co_ref, act_ref, slope_ref, probs_ref, probs2_ref = take(9)
    (pick_ref,) = take(1)
    gain1, shift1, gain2, shift2, gain3, shift3 = take(6)
    w_qkv1, wo1, w_qkv2, wo2, w_up, w_down_t = take(6)
    wire_out = take(z.lev)
    mine_ref, other_ref = take(2)
    wire_s, g_s, o_s, a_s, qkv_s, grad_s, gh_s, db_s, vec_s, sums_s = take(10)
    grads = {name: ref for (name, _), ref in zip(grad_list(z), take(len(grad_list(z))))}
    scale = np.float32((z.d // z.heads) ** (-0.5))
    ones, scales = head_masks(z), head_masks(z, scale)
    s, b = pl.program_id(0), pl.program_id(1)

    @pl.when((s == 0) & (b == 0))
    def _():
        for ref in list(grads.values()) + [db_s, vec_s]:
            ref[...] = jnp.zeros_like(ref)

    @pl.when(b == 0)
    def _():
        load_wire(z, wire_in, wire_s)

    for k in range(z.lev):
        got = [wire_level(z, wire_s, k, l, b) for l in range(z.l)]
        for l in range(z.l):
            g_s[k * z.l + l] = got[l]

    def normed_tokens(ref, gain, shift):
        normed = ref[0, 0][:, :, : z.d] * gain[...] + shift[...]
        return normed.reshape(z.n, z.d).astype(BF16)

    def back_down(i):
        rows = slice(i * CHUNK * TOK, (i + 1) * CHUNK * TOK)
        return nn(some_rows(z, g_s, i), w_down_t[...]), slope_ref[0, 0, rows, :].astype(F32)

    def back_gelu(i, got):
        return (got[0] * got[1]).astype(BF16)

    def back_up(i, grad):
        out = nt(grad, w_up[...])
        gh_s[i * CHUNK * TOK : (i + 1) * CHUNK * TOK] = grad
        o_s[i * CHUNK : (i + 1) * CHUNK] = out.reshape(CHUNK, TOK, z.d)

    pipelined(z.lt // CHUNK, back_down, back_gelu, back_up)
    grads["down_t"][...] += tn(bf16_rows(z, g_s), act_ref[0, 0])
    grads["up"][...] += tn(normed_tokens(norm3_ref, gain3, shift3), gh_s[...])

    def norm_step(ref, gain, at, target):
        sums = [vec_s[at], vec_s[at + 1]]

        def first(lv):
            grad, normed, rstd = o_s[lv], ref[0, 0, lv, :, : z.d], ref[0, 0, lv, :, z.d : z.d + 1]
            sums[0] += fold_rows(grad * normed)
            sums[1] += fold_rows(grad)
            return target[lv], normed, rstd, grad * gain[...]

        def second(lv, got):
            old, normed, rstd, gained = got
            one = jnp.mean(gained, axis=-1, keepdims=True)
            two = jnp.mean(gained * normed, axis=-1, keepdims=True)
            return old, normed, rstd, gained, one, two

        def third(lv, got):
            old, normed, rstd, gained, one, two = got
            target[lv] = old + rstd * (gained - one - normed * two)

        pipelined(z.lt, first, second, third)
        vec_s[at], vec_s[at + 1] = sums

    norm_step(norm3_ref, gain3, 4, g_s)

    branch = bf16_rows(z, g_s)
    grads["o2"][...] += tn(co_ref[0, 0], branch)
    put_rows(z, a_s, nt(branch, wo2[...]))
    tokens = normed_tokens(norm2_ref, gain2, shift2)
    put_rows(z, qkv_s, nn(tokens, w_qkv2[...]))

    def keep_column(g, t, got):
        for j in range(3):
            grad_s[:, group(g), tile(j, t)] = got[j].reshape(z.lt, GROUP, LANES)

    attention_back(
        TOK // GROUP,
        lambda g, j, t: qkv_s[:, group(g), tile(j, t)].reshape(z.lt * GROUP, LANES),
        lambda g, t: a_s[:, group(g), tile(0, t)].reshape(z.lt * GROUP, LANES),
        lambda g, t: probs2_ref.at[0, 0, g, t],
        keep_column,
        ones,
        scales,
        scale,
    )

    def project_back(tokens, name, w):
        grad = bf16_rows(z, grad_s)
        grads[name][...] += tn(tokens, grad)
        put_rows(z, o_s, nt(grad, w[...]))

    project_back(tokens, "qkv2", w_qkv2)
    norm_step(norm2_ref, gain2, 2, g_s)

    branch = bf16_rows(z, g_s)
    grads["o1"][...] += tn(att_ref[0, 0], branch)
    put_rows(z, a_s, nt(branch, wo1[...]))
    tokens = normed_tokens(norm1_ref, gain1, shift1)
    put_rows(z, qkv_s, nn(tokens, w_qkv1[...]))

    def keep_window(lv, t, got):
        for j in range(3):
            grad_s[lv, :, tile(j, t)] = got[j]
        db_s[b, t] += got[3].astype(F32)

    attention_back(
        z.lt,
        lambda lv, j, t: qkv_s[lv, :, tile(j, t)],
        lambda lv, t: a_s[lv, :, tile(0, t)],
        lambda lv, t: probs_ref.at[0, 0, lv, t],
        keep_window,
        ones,
        scales,
        scale,
    )
    project_back(tokens, "qkv1", w_qkv1)
    norm_step(norm1_ref, gain1, 0, g_s)

    store_wire_levels(z, wire_s, b, lambda lv: g_s[lv])

    @pl.when(b == z.nb - 1)
    def _():
        flush_wire(z, wire_s, wire_out)

    @pl.when((s == z.s - 1) & (b == z.nb - 1))
    def _():
        p, core = scal[0], scal[1]

        def place(i):
            return ((i // z.lev) ^ core) * z.lev + ((i % z.lev) ^ p)

        for at, pieces in enumerate(half_blocks(z)):
            values = [grad_block(z, n, grads[n], r, c, width) for n, r, c, width, _ in pieces]
            block = values[0] if len(values) == 1 else jnp.concatenate(values, axis=1)
            start = (at % z.hb) * 96
            sums_s[place(at // z.hb), start : start + 96, :] = block.astype(BF16)
        extra = z.hb * 96
        sums_s[:, extra:, :] = jnp.zeros_like(sums_s[:, extra:, :])
        vectors = [jnp.sum(vec_s[i], axis=0, keepdims=True) for i in range(6)]
        vectors = jnp.concatenate(vectors + [jnp.zeros((UNIT - 6, z.d), F32)], axis=0)
        vectors = jnp.concatenate([vectors, jnp.zeros((UNIT, 2 * LANES - z.d), F32)], axis=1)

        def put_unit(u, value):
            start = extra + (u % z.upp) * UNIT
            if not isinstance(u, int):
                start = pl.multiple_of(start, UNIT)
            sums_s[place(u // z.upp), pl.ds(start, UNIT), :] = value.astype(BF16)

        for j in range(2):
            put_unit(z.bands * 4 + j, vectors[:, j * LANES : (j + 1) * LANES])
        lane = lax.broadcasted_iota(jnp.int32, (1, z.heads * TOK), 1)
        odd = jnp.zeros(lane.shape, jnp.bool_)
        for h in range(1, z.heads, 2):
            odd = odd | ((lane >= h * TOK) & (lane < (h + 1) * TOK))
        width = -(-(z.heads * TOK) // LANES) * LANES
        for band in range(z.nb):
            rows = [nn(pick_ref[...], db_s[band, t], precision=lax.Precision.HIGHEST) for t in range(2)]
            rows = jnp.concatenate(rows, axis=1)
            halves = []
            for parity in range(2):
                kept = jnp.where(odd if parity else ~odd, rows, 0.0)
                kept = jnp.concatenate(
                    [kept, jnp.zeros((rows.shape[0], width - z.heads * TOK), F32)], axis=1
                )
                total = None
                for a in range(WLON):
                    part = kept[a * 8 : (a + 1) * 8]
                    shift = (WLON - 1 - a) * WLAT
                    if shift:
                        part = pltpu.roll(part, shift, 1)
                    total = part if total is None else total + part
                halves.append(total)
            both = jnp.concatenate(halves, axis=0)
            for j in range(4):
                put_unit((scal[0] * z.nb + band) * 4 + j, both[:, j * LANES : (j + 1) * LANES])
        mine_ref[...] = sums_s[: z.lev]
        other_ref[...] = sums_s[z.lev :]


def backward(z, scal, wire, residuals, norms, weights):
    res = residual_shapes(z)
    rows3 = (z.lt, TOK, z.d)
    pick = jnp.asarray(bias_rows(z))
    drop = lambda spec: pl.BlockSpec(spec.block_shape, lambda s, b, _, m=spec.index_map: m(s, b))
    half = (z.lev, z.pr, LANES)
    out = pl.pallas_call(
        functools.partial(backward_kernel, z),
        grid_spec=pltpu.PrefetchScalarGridSpec(
            num_scalar_prefetch=1,
            grid=(z.s, z.nb),
            in_specs=[
                drop(spec)
                for spec in wire_specs(z)
                + [unit_spec(shape) for shape, _ in res]
                + [whole_spec(pick)]
                + [whole_spec(a) for a in norms]
                + [whole_spec(a) for a in weights]
            ],
            out_specs=[drop(spec) for spec in wire_specs(z)]
            + [pl.BlockSpec(half, lambda s, b, _: (0, 0, 0))] * 2,
            scratch_shapes=[pltpu.VMEM((z.lev, z.nblk, z.ro, LANES), F32)]
            + [pltpu.VMEM(rows3, F32)] * 2
            + [
                pltpu.VMEM((z.lt, TOK, 2 * LANES), F32),
                pltpu.VMEM((z.lt, TOK, 6 * LANES), F32),
                pltpu.VMEM((z.lt, TOK, 6 * LANES), F32),
                pltpu.VMEM((z.n, z.ff), BF16),
                pltpu.VMEM((z.nb, 2, TOK, z.heads // 2 * TOK), F32),
                pltpu.VMEM((6, 8, z.d), F32),
                pltpu.VMEM((z.np, z.pr, LANES), BF16),
            ]
            + [pltpu.VMEM(grad_buffer(z, *item), F32) for item in grad_list(z)],
        ),
        out_shape=wire_shapes(z) + [jax.ShapeDtypeStruct(half, BF16)] * 2,
        compiler_params=pltpu.CompilerParams(vmem_limit_bytes=62 * 2**20),
        cost_estimate=cost(40),
        name="backward",
    )(scal, *wire, *residuals, pick, *norms, *weights)
    return out[: z.lev], out[z.lev], out[z.lev + 1]


def tree(parts):
    while len(parts) > 1:
        parts = [parts[i] + parts[i + 1] for i in range(0, len(parts), 2)]
    return parts[0]


def lev_swap(z, array, k):
    return lax.ppermute(array, "lev", [(i, i ^ k) for i in range(z.lev)])


def lon_swap(z, array, k):
    return lax.ppermute(array, "lon", [(i, i ^ k) for i in range(z.lon)])


def sum_wire(z, mine, other):
    got = lon_swap(z, other, 1)
    half = [(mine[k].astype(F32) + got[k].astype(F32)).astype(BF16) for k in range(z.lev)]
    parts = [half[0]] + [lev_swap(z, half[k], k) for k in range(1, z.lev)]
    quarter = tree([v.astype(F32) for v in parts]).astype(BF16)
    parts = [quarter] + [lon_swap(z, quarter, 2 * k) for k in range(1, z.lon // 2)]
    done = tree([v.astype(F32) for v in parts]).astype(BF16)
    own = jnp.stack([done] + [lev_swap(z, done, k) for k in range(1, z.lev)])
    return own, lon_swap(z, own, 1)


def table_lanes(z, h):
    lanes = np.full((WLAT, 32), -1, np.int32)
    for i in range(WLAT):
        lanes[i, : 2 * WLON - 1] = h * TOK + np.arange(2 * WLON - 1) * WLAT + i
    return lanes.reshape(1, WLAT * 32)


def finish_kernel(z, scal, lanes, order, own, other, *outs):
    p, core = scal[0], scal[1]
    named = {name: ref for (name, _), ref in zip(grad_list(z), outs)}
    vec_refs, bias_ref = outs[len(named) : len(named) + 6], outs[len(named) + 6]

    def read(piece, start, size):
        half, j = piece // z.lev, piece % z.lev
        rows = slice(start, start + size)
        return jnp.where(core == half, own[p ^ j, rows, :], other[p ^ j, rows, :])

    for at, pieces in enumerate(half_blocks(z)):
        block = read(at // z.hb, (at % z.hb) * 96, 96).astype(F32)
        for n, r, c, width, lane in pieces:
            named[n][r : r + 96, c : c + width] = block[:, lane : lane + width]
    extra = z.hb * 96
    units = [read(u // z.upp, extra + (u % z.upp) * UNIT, UNIT) for u in range(z.units)]
    vectors = jnp.concatenate(units[z.bands * 4 :], axis=1).astype(F32)
    for i in range(6):
        vec_refs[i][...] = vectors[i : i + 1, : z.d]
    table = [jnp.concatenate(units[4 * k : 4 * k + 4], axis=1) for k in range(z.bands)]
    table = nn(order[...], jnp.concatenate(table, axis=0)).astype(BF16)
    half = table.shape[0] // 2
    for h in range(z.heads):
        at = lax.broadcasted_iota(jnp.int32, (4 * LANES, WLAT * 32), 0)
        pick = jnp.where(at == lanes[h : h + 1, :], 1.0, 0.0).astype(BF16)
        rows = table[(h % 2) * half : (h % 2) * half + half]
        got = nn(rows, pick)
        for i in range(WLAT):
            values = got[: WLAT * z.bands, i * 32 : i * 32 + 2 * WLON - 1]
            bias_ref[h, i] = values.reshape(WLAT, z.bands, 2 * WLON - 1)


def finish(z, scal, own, other):
    shapes = [jax.ShapeDtypeStruct((z.d, columns), F32) for _, columns in grad_list(z)]
    shapes += [jax.ShapeDtypeStruct((1, z.d), F32)] * 6
    shapes += [jax.ShapeDtypeStruct((z.heads, WLAT, WLAT, z.bands, 2 * WLON - 1), F32)]
    lanes = jnp.asarray(np.concatenate([table_lanes(z, h) for h in range(z.heads)]))
    order = np.zeros((2 * 8 * z.bands, z.bands * UNIT), np.float32)
    for parity in range(2):
        for i in range(8):
            for k in range(z.bands):
                order[parity * 8 * z.bands + i * z.bands + k, k * UNIT + parity * 8 + i] = 1.0
    order = jnp.asarray(order, BF16)
    full = lambda a: pl.BlockSpec(a.shape, lambda i, _, n=len(a.shape): (0,) * n)
    out = pl.pallas_call(
        functools.partial(finish_kernel, z),
        grid_spec=pltpu.PrefetchScalarGridSpec(
            num_scalar_prefetch=1,
            grid=(1,),
            in_specs=[full(a) for a in (lanes, order, own, other)],
            out_specs=[full(a) for a in shapes],
        ),
        out_shape=shapes,
        compiler_params=pltpu.CompilerParams(vmem_limit_bytes=60 * 2**20),
        cost_estimate=cost(4),
        name="finish",
    )(scal, lanes, order, own, other)
    named = {name: value for (name, _), value in zip(grad_list(z), out)}
    vectors = [v.reshape(z.d) for v in out[len(named) : len(named) + 6]]
    return named, vectors, out[-1].transpose(3, 0, 1, 2, 4)


def bias_kernel(z, table_ref, pick_ref, out_ref, even_s, odd_s):
    width = 4 * LANES
    lane = lax.broadcasted_iota(jnp.int32, (2 * WLON - 1, width), 1)
    step = lax.broadcasted_iota(jnp.int32, (2 * WLON - 1, width), 0) * WLAT
    for parity, ref in ((0, even_s), (1, odd_s)):
        total = None
        for h in range(parity, z.heads, 2):
            for i in range(WLAT):
                place = jnp.where(lane == step + (h * TOK + i), 1.0, 0.0).astype(BF16)
                values = table_ref[h, i]
                high = values.astype(BF16)
                low = (values - high.astype(F32)).astype(BF16)
                part = nn(jnp.concatenate([high, low], axis=0), place)
                total = part if total is None else total + part
        rows = z.nb * 8
        ref[...] = total[:rows] + total[rows:]
    head = lax.broadcasted_iota(jnp.int32, (1, width), 1)
    odd = jnp.zeros(head.shape, jnp.bool_)
    for h in range(1, z.heads, 2):
        odd = odd | ((head >= h * TOK) & (head < (h + 1) * TOK))
    side = z.heads // 2 * TOK
    for b in range(z.nb):
        even, uneven = even_s[b * 8 : (b + 1) * 8], odd_s[b * 8 : (b + 1) * 8]
        rows = []
        for a in range(WLON):
            shift = (width - (WLON - 1 - a) * WLAT) % width
            turned = [pltpu.roll(v, shift, 1) if shift else v for v in (even, uneven)]
            rows.append(jnp.where(odd, turned[1], turned[0]))
        rows = jnp.concatenate(rows, axis=0)
        full = lax.dot_general(
            pick_ref[...], rows, (((0,), (0,)), ((), ())),
            precision=lax.Precision.HIGHEST, preferred_element_type=F32,
        ) * np.float32(np.log2(np.e))
        out_ref[b, 0] = full[:, :side]
        out_ref[b, 1] = full[:, side : 2 * side]


def bias_of(z, bias_table, p):
    table = lax.dynamic_slice_in_dim(bias_table, p * z.nb, z.nb, axis=0)
    table = jnp.pad(table.transpose(1, 2, 0, 3, 4), ((0, 0),) * 3 + ((0, 2), (0, 0)))
    table = table.reshape(z.heads, WLAT, z.nb * 8, 2 * WLON - 1)
    return pl.pallas_call(
        functools.partial(bias_kernel, z),
        out_shape=jax.ShapeDtypeStruct((z.nb, 2, TOK, z.heads // 2 * TOK), F32),
        scratch_shapes=[pltpu.VMEM((z.nb * 8, 4 * LANES), F32)] * 2,
        compiler_params=pltpu.CompilerParams(vmem_limit_bytes=60 * 2**20),
        cost_estimate=cost(4),
        name="bias",
    )(table, jnp.asarray(bias_rows(z)))


def lev_exchange(z, wire):
    return [wire[0]] + [lev_swap(z, wire[k], k) for k in range(1, z.lev)]


def lon_shift(z, array, distance):
    return lax.ppermute(array, "lon", [(w, (w + distance) % z.lon) for w in range(z.lon)])


def last_cells(z, wire):
    rows = [a[:, :, : z.nb * TOK].reshape(z.s, z.nblk, z.nb, TOK, LANES)[:, :, :, HALO0:] for a in wire]
    return jnp.stack(rows).reshape(z.lev, z.s, z.nblk, z.rh, LANES)


def on_device(
    inputs, cotangent, grid_sizes, offsets, gain_one, shift_one, qkv_window, out_window, bias_table,
    gain_two, shift_two, qkv_column, out_column, gain_three, shift_three, w_up, w_down,
):
    d = inputs.shape[-1]
    z = Sizes(lax.axis_size("lev"), lax.axis_size("lon"), inputs.shape, bias_table.shape[1], w_up.shape[1])
    p, w = lax.axis_index("lev"), lax.axis_index("lon")
    scal = jnp.concatenate([p[None].astype(jnp.int32), offsets.astype(jnp.int32)])
    swap = lambda a: a.transpose(0, 1, 3, 2, 4)

    half = WLON // 2
    x, c = swap(inputs), swap(cotangent)
    halo_x = lon_shift(z, x[:, :, :half], -1)
    halo_c = lon_shift(z, c[:, :, :half], -1)
    bias = bias_of(z, bias_table, p)
    wire_x = lev_exchange(z, pack(z, x, halo_x, scal))
    wire_c = lev_exchange(z, pack(z, c, halo_c, scal))
    cell = (w * z.cells + offsets[:, None] + jnp.arange(WLON)[None, :]) % (z.cells * z.lon)
    row = (p * z.nb + jnp.arange(z.nb))[:, None] * WLAT + jnp.arange(WLAT)[None, :]
    cell_ok = cell < grid_sizes[:, 1:2]
    row_ok = row[None] < grid_sizes[:, 0][:, None, None]
    valid = cell_ok[:, None, :, None] & row_ok[:, :, None, :]
    mask = jnp.where(valid, 0.0, NEGATIVE).astype(F32).reshape(z.s, z.nb, TOK, 1)
    of_key = np.arange(z.lt * GROUP) % GROUP
    of_query = np.tile(of_key, z.heads // 2)
    column_mask = jnp.asarray(
        np.where(of_key[:, None] == of_query[None, :], 0.0, NEGATIVE).astype(np.float32)
    )

    norms = [v[None] for v in (gain_one, shift_one, gain_two, shift_two, gain_three, shift_three)]
    room = ((0, 0), (0, 0), (0, LANES - d // 2))
    wide = lambda a: jnp.pad(a.reshape(d, 6, d // 2), room).reshape(d, 6 * LANES)
    tall = lambda a: jnp.pad(a.reshape(2, d // 2, d), (room[0], room[2], room[0])).reshape(2 * LANES, d)
    weights = [wide(qkv_window), tall(out_window), wide(qkv_column), tall(out_column), w_up, w_down.T]

    places = jnp.stack([p, w % 2]).astype(jnp.int32)
    wire_r, residuals = forward(z, wire_x, bias, mask, column_mask, norms, weights)
    wire_r = lev_exchange(z, wire_r)
    wire_g, mine, other = backward(z, places, wire_c, residuals, norms, weights)
    wire_g = lev_exchange(z, wire_g)
    result = unpack(z, wire_r, lon_shift(z, last_cells(z, wire_r), 1), scal)
    input_grad = unpack(z, wire_g, lon_shift(z, last_cells(z, wire_g), 1), scal)
    own, other = sum_wire(z, mine, other)
    named, vec, table = finish(z, places, own, other)
    return (
        swap(result), swap(input_grad),
        vec[0], vec[1], named["qkv1"], named["o1"], table,
        vec[2], vec[3], named["qkv2"], named["o2"],
        vec[4], vec[5], named["up"], named["down_t"].T,
    )


def solution(mesh):
    tokens = P(None, "lev", None, "lon", None)
    return jax.shard_map(
        on_device,
        mesh=mesh,
        in_specs=(tokens, tokens) + (P(),) * 15,
        out_specs=(tokens, tokens) + (P(),) * 13,
        check_vma=False,
    )
```

time: 333 us -> 164 us (0.49)
  Pallas kernels: 185 us -> 89.5 us
  waiting for transfers between devices: 57.9 us -> 26.3 us
  local copies, waits for them, and re-layouts: 34 us -> 8.92 us
  starting transfers between devices: 42.1 us -> 32.4 us
  other arithmetic: 8.87 us -> 4.74 us
  matrix products: 3.42 us -> 0 us
    pallas_call x1, Pallas kernels: 91.2 us -> 35.9 us  [backward(): pl.pallas_call(functools.partial(backward_kernel, z), grid_spec=pltpu.Pre...]
    pallas_call x1, Pallas kernels: 72.3 us -> 27.6 us  [forward(): pl.pallas_call(functools.partial(forward_kernel, z), grid=(z.s, z.nb), in...]
    ppermute x16 -> x4, waiting for transfers between devices: 26.7 us -> 6.25 us  [lon_shift(): lax.ppermute(array, 'lon', [(w, (w + distance) % z.lon) for w in range(z....]
    transpose x2 -> x1, local copies, waits for them, and re-layouts: 15.5 us -> 0.08 us  [bias_of(): table.transpose(1, 2, 0, 3, 4)]
    ppermute x5, waiting for transfers between devices: 15.4 us -> 5.69 us  [lon_swap(): return lax.ppermute(array, 'lon', [(i, i ^ k) for i in range(z.lon)])]
    ppermute x16 -> x4, starting transfers between devices: 14.5 us -> 5.33 us  [lon_shift(): lax.ppermute(array, 'lon', [(w, (w + distance) % z.lon) for w in range(z....]
    transpose x1 -> x0, other arithmetic: 3.68 us -> none  [table_of(): both.transpose(0, 2, 3, 5, 1, 4)]
    reshape x3, local copies, waits for them, and re-layouts: 6.13 us -> 2.49 us  [the longest x2 1.74 us: on_device(): jnp.pad(a.reshape(d, 6, d // 2), room).reshape(d, 6 * LANES)]
  transfers between devices with their start and end apart: 39 -> 27, of which waited for: 18 -> 12; matrix products, arithmetic and copies ran while one was open for 7% -> 6% of each run, Pallas kernels for 26% -> 30%
where the time goes in v2:
time: 164 us; the launch traced here: 163 us
  Pallas kernels  89.5 us (55%)
  starting transfers between devices  32.4 us (20%)
  waiting for transfers between devices  26.3 us (16%)
  local copies, waits for them, and re-layouts  8.92 us (5%)
  other arithmetic  4.74 us (3%)
    pallas_call x1, Pallas kernels, backward(): pl.pallas_call(functools.partial(backward_kernel, z), grid_spec=pltpu.Pre...  35.9 us
    pallas_call x1, Pallas kernels, forward(): pl.pallas_call(functools.partial(forward_kernel, z), grid=(z.s, z.nb), in...  27.6 us
    ppermute x18, starting transfers between devices, lev_swap(): return lax.ppermute(array, 'lev', [(i, i ^ k) for i in range(z.lev)])  22.5 us
    ppermute x18, waiting for transfers between devices, lev_swap(): return lax.ppermute(array, 'lev', [(i, i ^ k) for i in range(z.lev)])  14.3 us
    pallas_call x2, Pallas kernels, unpack(): pl.pallas_call(functools.partial(unpack_kernel, z), grid_spec=pltpu.Prefe...  9.67 us
    pallas_call x2, Pallas kernels, pack(): pl.pallas_call(functools.partial(pack_kernel, z), grid_spec=pltpu.Prefetc...  8.88 us
    ppermute x4, waiting for transfers between devices, lon_shift(): lax.ppermute(array, 'lon', [(w, (w + distance) % z.lon) for w in range(z....  6.25 us
    ppermute x5, waiting for transfers between devices, lon_swap(): return lax.ppermute(array, 'lon', [(i, i ^ k) for i in range(z.lon)])  5.69 us
  transfers between devices with their start and end apart: 27, of which 12 were waited for; matrix products, arithmetic and copies ran while one was open for 6% of the time, Pallas kernels for 30%

profile of v2, /device:TPU:0, one launch (start us, length us, event | category | flops | bytes accessed | tf_op | source)
XLA Modules:
  0.0 163.0 jit_solution(1998193520100330411)
XLA Ops:
  0.7 1.2 slice.80
  1.9 4.5 %collective-permute-start = (bf16[2,2,6,48,192]{4,3,2,1,0:T(8,128)(2,1)S(1)}, bf16[2,2,6,48,192]{4,3,2,1,0:T(8,128)(2,1)}, u32[]{:S(2)}, u32[]{:S(2)}) collective-permute-start(bf16[2,2,6,48,192]{4,3,2,1,0:T(8,128)(2,1)S(1)} %slice.80), channel_id=1, source_target_pairs={{0,28},{4,0},{8,4},{12,8},{16,12},{20,16},{24,20},{28,24},{1,29},{... | collective-permute-start | bytes 1327112 | tf_op jit(solution)/shard_map/ppermute | solution.py:953
  6.4 1.1 slice.85
  7.5 0.7 collective-permute-start.8
  8.3 0.2 slice_reduce_fusion.1
  8.6 0.1 and.49
  8.7 0.1 fusion.6
  8.9 0.1 and.43
  9.0 0.8 and_select_fusion.refs_5_
  9.8 0.1 dynamic-slice_bitcast_fusion
  9.9 0.7 pad_bitcast_fusion.table_ref
  10.6 2.9 %bias.1.refs_4_ = f32[2,2,72,216]{3,2,1,0:T(8,128)} custom-call(f32[6,6,16,23]{3,2,1,0:T(8,128)} %pad_bitcast_fusion.table_ref, f32[96,72]{1,0:T(8,128)} %constant.59.clone.pick_ref.refs_13_), custom_call_target="tpu_custom_call" | custom-call | flops 2000000000 | bytes 12000000 | tf_op jit(solution)/shard_map/bias/pallas_call | solution.py:938
  13.6 0.6 pad_add_fusion.scal
  14.1 4.5 %pack.2 = (bf16[2,3,144,128]{3,2,1,0:T(8,128)(2,1)}, bf16[2,3,144,128]{3,2,1,0:T(8,128)(2,1)}, bf16[2,3,144,128]{3,2,1,0:T(8,128)(2,1)}, bf16[2,3,144,128]{3,2,1,0:T(8,128)(2,1)}) custom-call(s32[3]{0:T(128)} %pad_add_fusion.scal, s32[144,1]{1,0:T(8,128)} %constant.79.base, bf16[2,2,12,48,192]{4,3,2,1,0:T(8,128)(2,1)} %bitcast.78, ...), custom_call_target="tpu_custom_call" | custom-call | flops 2000000000 | bytes 12000000 | tf_op jit(solution)/shard_map/pack/pallas_call | solution.py:108
  18.7 1.6 collective-permute-start.1
  20.2 1.5 collective-permute-start.2
  21.7 0.5 collective-permute-start.3
  22.2 0.6 pad_add_fusion.1.scal
  22.8 0.2 copy.46
  23.0 0.9 copy.50.refs_13_.refs_20_
  23.9 0.2 copy.48
  24.1 0.9 copy.51.refs_15_.refs_22_
  25.0 0.7 pad.20
  25.7 0.7 pad.22
  26.3 0.8 copy-done.15
  27.2 4.4 %pack.3 = (bf16[2,3,144,128]{3,2,1,0:T(8,128)(2,1)}, bf16[2,3,144,128]{3,2,1,0:T(8,128)(2,1)}, bf16[2,3,144,128]{3,2,1,0:T(8,128)(2,1)}, bf16[2,3,144,128]{3,2,1,0:T(8,128)(2,1)}) custom-call(s32[3]{0:T(128)} %pad_add_fusion.scal, s32[144,1]{1,0:T(8,128)} %constant.79.base, bf16[2,2,12,48,192]{4,3,2,1,0:T(8,128)(2,1)} %bitcast.80, ...), custom_call_target="tpu_custom_call" | custom-call | flops 2000000000 | bytes 12000000 | tf_op jit(solution)/shard_map/pack/pallas_call | solution.py:108
  31.6 1.5 collective-permute-start.10
  33.1 1.4 collective-permute-start.11
  34.5 0.5 collective-permute-start.9
  35.1 27.6 %forward.1 = (bf16[2,3,144,128]{3,2,1,0:T(8,128)(2,1)}, bf16[2,3,144,128]{3,2,1,0:T(8,128)(2,1)}, bf16[2,3,144,128]{3,2,1,0:T(8,128)(2,1)}, bf16[2,3,144,128]{3,...) custom-call(bf16[2,3,144,128]{3,2,1,0:T(8,128)(2,1)} %get-tuple-elem, ...), custom_call_target="tpu_custom_call" | custom-call | flops 15000000512 | bytes 90000000 | tf_op jit(solution)/shard_map/forward/pallas_call | solution.py:493
  62.7 0.6 copy-done.19
  63.4 0.1 copy-done.20
  63.5 35.9 %backward.1 = (bf16[2,3,144,128]{3,2,1,0:T(8,128)(2,1)}, bf16[2,3,144,128]{3,2,1,0:T(8,128)(2,1)}, bf16[2,3,144,128]{3,2,1,0:T(8,128)(2,1)}, bf16[2,3,144,128]{3...) custom-call(s32[2]{0:T(128)} %pad_add_fusion.1.scal, ...), custom_call_target="tpu_custom_call" | custom-call | flops 20000000000 | bytes 120000000 | tf_op jit(solution)/shard_map/backward/pallas_call | solution.py:767
  99.6 2.3 %collective-permute-done.16 = bf16[4,656,128]{2,1,0:T(8,128)(2,1)S(1)} collective-permute-done((bf16[4,656,128]{2,1,0:T(8,128)(2,1)}, bf16[4,656,128]{2,1,0:T(8,128)(2,1)S(1)}, u32[]{:S(2)}, u32[]{:S(2)}) %collective-permute-start.16) | collective-permute-done | bytes 671776 | tf_op jit(solution)/shard_map/ppermute | solution.py:814
  101.9 1.2 fusion.3
  103.1 1.6 collective-permute-start.17
  104.7 1.5 collective-permute-start.18
  106.2 0.5 collective-permute-start.19
  106.7 1.5 collective-permute-start.12
  108.2 1.5 collective-permute-start.13
  109.7 0.6 collective-permute-done.17
  110.3 2.5 %collective-permute-start.14 = (bf16[2,3,144,128]{3,2,1,0:T(8,128)(2,1)}, bf16[2,3,144,128]{3,2,1,0:T(8,128)(2,1)S(1)}, u32[]{:S(2)}, u32[]{:S(2)}) collective-permute-start(bf16[2,3,144,128]{3,2,1,0:T(8,128)(2,1)} %get-tuple-element.79), channel_id=1, source_target_pairs={{0,3},{1,2},{2,1},{3,0},{4,7},{5,6},{6,5},{7,4},{8,11},{9,10},{10,... | collective-permute-start | bytes 663560 | tf_op jit(solution)/shard_map/ppermute | solution.py:810
  112.8 2.4 %collective-permute-done.18 = bf16[656,128]{1,0:T(8,128)(2,1)S(1)} collective-permute-done((bf16[656,128]{1,0:T(8,128)(2,1)S(1)}, bf16[656,128]{1,0:T(8,128)(2,1)S(1)}, u32[]{:S(2)}, u32[]{:S(2)}) %collective-permute-start.18) | collective-permute-done | bytes 167968 | tf_op jit(solution)/shard_map/ppermute | solution.py:810
  115.2 1.0 fusion.1
  116.3 2.4 %collective-permute-start.21 = (bf16[656,128]{1,0:T(8,128)(2,1)S(1)}, bf16[656,128]{1,0:T(8,128)(2,1)S(1)}, u32[]{:S(2)}, u32[]{:S(2)}) collective-permute-start(bf16[656,128]{1,0:T(8,128)(2,1)S(1)} %fusion.1), channel_id=1, source_target_pairs={{0,16},{4,20},{8,24},{12,28},{16,0},{20,4},{24,8},{28,12},{1,17},{... | collective-permute-start | bytes 503816 | tf_op jit(solution)/shard_map/ppermute | solution.py:814
  118.7 1.9 %collective-permute-start.22 = (bf16[656,128]{1,0:T(8,128)(2,1)S(1)}, bf16[656,128]{1,0:T(8,128)(2,1)S(1)}, u32[]{:S(2)}, u32[]{:S(2)}) collective-permute-start(bf16[656,128]{1,0:T(8,128)(2,1)S(1)} %fusion.1), channel_id=1, source_target_pairs={{0,24},{4,28},{8,16},{12,20},{16,8},{20,12},{24,0},{28,4},{1,25},{... | collective-permute-start | bytes 503816 | tf_op jit(solution)/shard_map/ppermute | solution.py:814
  120.7 2.4 %collective-permute-done.13.rest_2_ = bf16[2,3,144,128]{3,2,1,0:T(8,128)(2,1)S(1)} collective-permute-done((bf16[2,3,144,128]{3,2,1,0:T(8,128)(2,1)}, bf16[2,3,144,128]{3,2,1,0:T(8,128)(2,1)S(1)}, u32[]{:S(2)}, u32[]{:S(2)}) %collective-permute-start.13) | collective-permute-done | bytes 221216 | tf_op jit(solution)/shard_map/ppermute | solution.py:810
  123.2 1.2 collective-permute-done.14.rest_3_
  124.5 1.0 collective-permute-start.5
  125.5 1.9 %collective-permute-start.6 = (bf16[2,3,144,128]{3,2,1,0:T(8,128)(2,1)S(1)}, bf16[2,3,144,128]{3,2,1,0:T(8,128)(2,1)S(1)}, u32[]{:S(2)}, u32[]{:S(2)}) collective-permute-start(bf16[2,3,144,128]{3,2,1,0:T(8,128)(2,1)S(1)} %copy-done.16), channel_id=1, source_target_pairs={{0,3},{1,2},{2,1},{3,0},{4,7},{5,6},{6,5},{7,4},{8,11},{9,10},{10,... | collective-permute-start | bytes 663560 | tf_op jit(solution)/shard_map/ppermute | solution.py:810
  127.4 3.4 %collective-permute-done.21 = bf16[656,128]{1,0:T(8,128)(2,1)S(1)} collective-permute-done((bf16[656,128]{1,0:T(8,128)(2,1)S(1)}, bf16[656,128]{1,0:T(8,128)(2,1)S(1)}, u32[]{:S(2)}, u32[]{:S(2)}) %collective-permute-start.21) | collective-permute-done | bytes 167968 | tf_op jit(solution)/shard_map/ppermute | solution.py:814
  130.8 0.1 add_convert_fusion
  130.9 1.6 collective-permute-start.23
  132.4 0.5 collective-permute-start.24
  132.9 1.5 collective-permute-start.25
  134.5 3.7 %collective-permute-done.5.rest_2_ = bf16[2,3,144,128]{3,2,1,0:T(8,128)(2,1)S(1)} collective-permute-done((bf16[2,3,144,128]{3,2,1,0:T(8,128)(2,1)S(1)}, bf16[2,3,144,128]{3,2,1,0:T(8,128)(2,1)S(1)}, u32[]{:S(2)}, u32[]{:S(2)}) %collective-permute-start.5) | collective-permute-done | bytes 221216 | tf_op jit(solution)/shard_map/ppermute | solution.py:810
  138.4 0.8 collective-permute-done.23
  139.3 3.0 %collective-permute-done.24 = bf16[656,128]{1,0:T(8,128)(2,1)S(1)} collective-permute-done((bf16[656,128]{1,0:T(8,128)(2,1)S(1)}, bf16[656,128]{1,0:T(8,128)(2,1)S(1)}, u32[]{:S(2)}, u32[]{:S(2)}) %collective-permute-start.24) | collective-permute-done | bytes 167968 | tf_op jit(solution)/shard_map/ppermute | solution.py:810
  142.2 0.1 pad_maximum_fusion.own
  142.4 5.9 %collective-permute-done.15.rest_4_ = bf16[4,2,3,80,128]{4,3,2,1,0:T(8,128)(2,1)} collective-permute-done((bf16[4,2,3,80,128]{4,3,2,1,0:T(8,128)(2,1)S(1)}, bf16[4,2,3,80,128]{4,3,2,1,0:T(8,128)(2,1)}, u32[]{:S(2)}, u32[]{:S(2)}) %collective-permute-start.15) | collective-permute-done | bytes 491552 | tf_op jit(solution)/shard_map/ppermute | solution.py:953
  148.4 4.9 %unpack.3 = bf16[2,2,12,48,192]{4,3,2,1,0:T(8,128)(2,1)} custom-call(s32[3]{0:T(128)} %pad_add_fusion.scal, s32[1,144]{1,0:T(1,128)} %constant.77.own_base, s32[1,80]{1,0:T(1,128)} %constant.78.halo_base, bf16[2,3,144,128]{3,2,1,0:T(8,128)(2,1)} %get-tuple-element.76.rest_0_, bf16[2,3,144,128]{3,2,1,0:T(8,128)(2,1)} %copy-done.8, ...), custom_call_target="tpu_custom_call" | custom-call | flops 2000000000 | bytes 12000000 | tf_op jit(solution)/shard_map/unpack/pallas_call | solution.py:153
  153.4 0.3 collective-permute-done.7.rest_4_
  153.7 4.7 %unpack.2 = bf16[2,2,12,48,192]{4,3,2,1,0:T(8,128)(2,1)} custom-call(s32[3]{0:T(128)} %pad_add_fusion.scal, s32[1,144]{1,0:T(1,128)} %constant.77.own_base, s32[1,80]{1,0:T(1,128)} %constant.78.halo_base, bf16[2,3,144,128]{3,2,1,0:T(8,128)(2,1)} %get-tuple-element.59.rest_0_, bf16[2,3,144,128]{3,2,1,0:T(8,128)(2,1)} %copy-done.11, ...), custom_call_target="tpu_custom_call" | custom-call | flops 2000000000 | bytes 12000000 | tf_op jit(solution)/shard_map/unpack/pallas_call | solution.py:153
  158.4 4.4 %finish.1 = (f32[192,768]{1,0:T(8,128)}, f32[192,768]{1,0:T(8,128)}, f32[192,576]{1,0:T(8,128)}, f32[192,576]{1,0:T(8,128)}, f32[192,192]{1,0:T(8,128)}, /*index...) custom-call(s32[2]{0:T(128)} %pad_add_fusion.1.scal, ...), custom_call_target="tpu_custom_call" | custom-call | flops 2000000000 | bytes 12000000 | tf_op jit(solution)/shard_map/finish/pallas_call | solution.py:879
  (84 shorter events, 1.2 us)
Async XLA Ops:
  0.6 9.1 %copy-start = (f32[8,6,6,6,23]{4,0,3,2,1:T(8,128)S(1)}, f32[8,6,6,6,23]{4,0,3,2,1:T(8,128)}, u32[]{:S(2)}) copy-start(f32[8,6,6,6,23]{4,0,3,2,1:T(8,128)} %param.36) | copy-start | bytes 476932
  0.7 7.7 %copy-start.14 = (s32[2,2]{1,0:T(2,128)S(1)}, s32[2,2]{1,0:T(2,128)}, u32[]{:S(2)}) copy-start(s32[2,2]{1,0:T(2,128)} %param.30) | copy-start | bytes 52
  0.7 8.1 %copy-start.22 = (s32[2]{0:T(128)S(1)}, s32[2]{0:T(128)}, u32[]{:S(2)}) copy-start(s32[2]{0:T(128)} %param.31) | copy-start | bytes 28
  1.9 12.3 %collective-permute-start = (bf16[2,2,6,48,192]{4,3,2,1,0:T(8,128)(2,1)S(1)}, bf16[2,2,6,48,192]{4,3,2,1,0:T(8,128)(2,1)}, u32[]{:S(2)}, u32[]{:S(2)}) collective-permute-start(bf16[2,2,6,48,192]{4,3,2,1,0:T(8,128)(2,1)S(1)} %slice.80), channel_id=1, source_target_pairs={{0,28},{4,0},{8,4},{12,8},{16,12},{20,16},{24,20},{28,24},{1,29},{... | collective-permute-start | bytes 1327112 | tf_op jit(solution)/shard_map/ppermute | solution.py:953
  7.5 18.8 %collective-permute-start.8 = (bf16[2,2,6,48,192]{4,3,2,1,0:T(8,128)(2,1)S(1)}, bf16[2,2,6,48,192]{4,3,2,1,0:T(8,128)(2,1)S(1)}, u32[]{:S(2)}, u32[]{:S(2)}) collective-permute-start(bf16[2,2,6,48,192]{4,3,2,1,0:T(8,128)(2,1)S(1)} %slice.85), channel_id=1, source_target_pairs={{0,28},{4,0},{8,4},{12,8},{16,12},{20,16},{24,20},{28,24},{1,29},{... | collective-permute-start | bytes 1327112 | tf_op jit(solution)/shard_map/ppermute | solution.py:953
  14.1 8.7 %copy-start.2 = (bf16[192,576]{1,0:T(8,128)(2,1)S(1)}, bf16[192,576]{1,0:T(8,128)(2,1)}, u32[]{:S(2)}) copy-start(bf16[192,576]{1,0:T(8,128)(2,1)} %param.34) | copy-start | bytes 663556
  14.1 9.8 %copy-start.3 = (bf16[192,576]{1,0:T(8,128)(2,1)S(1)}, bf16[192,576]{1,0:T(8,128)(2,1)}, u32[]{:S(2)}) copy-start(bf16[192,576]{1,0:T(8,128)(2,1)} %param.39) | copy-start | bytes 663556
  18.6 6.4 %copy-start.4 = (bf16[192,192]{1,0:T(8,128)(2,1)S(1)}, bf16[192,192]{1,0:T(8,128)(2,1)}, u32[]{:S(2)}) copy-start(bf16[192,192]{1,0:T(8,128)(2,1)} %param.35) | copy-start | bytes 221188
  18.6 7.0 %copy-start.5 = (bf16[192,192]{1,0:T(8,128)(2,1)S(1)}, bf16[192,192]{1,0:T(8,128)(2,1)}, u32[]{:S(2)}) copy-start(bf16[192,192]{1,0:T(8,128)(2,1)} %param.40) | copy-start | bytes 221188
  18.7 15.9 %collective-permute-start.1 = (bf16[2,3,144,128]{3,2,1,0:T(8,128)(2,1)}, bf16[2,3,144,128]{3,2,1,0:T(8,128)(2,1)}, u32[]{:S(2)}, u32[]{:S(2)}) collective-permute-start(bf16[2,3,144,128]{3,2,1,0:T(8,128)(2,1)} %get-tuple-element.56), channel_id=1, source_target_pairs={{0,1},{1,0},{2,3},{3,2},{4,5},{5,4},{6,7},{7,6},{8,9},{9,8},{10,11... | collective-permute-start | bytes 663560 | tf_op jit(solution)/shard_map/ppermute | solution.py:810
  20.2 14.8 %collective-permute-start.2 = (bf16[2,3,144,128]{3,2,1,0:T(8,128)(2,1)}, bf16[2,3,144,128]{3,2,1,0:T(8,128)(2,1)}, u32[]{:S(2)}, u32[]{:S(2)}) collective-permute-start(bf16[2,3,144,128]{3,2,1,0:T(8,128)(2,1)} %get-tuple-element.57), channel_id=1, source_target_pairs={{0,2},{1,3},{2,0},{3,1},{4,6},{5,7},{6,4},{7,5},{8,10},{9,11},{10,... | collective-permute-start | bytes 663560 | tf_op jit(solution)/shard_map/ppermute | solution.py:810
  21.7 13.3 %collective-permute-start.3 = (bf16[2,3,144,128]{3,2,1,0:T(8,128)(2,1)}, bf16[2,3,144,128]{3,2,1,0:T(8,128)(2,1)}, u32[]{:S(2)}, u32[]{:S(2)}) collective-permute-start(bf16[2,3,144,128]{3,2,1,0:T(8,128)(2,1)} %get-tuple-element.58), channel_id=1, source_target_pairs={{0,3},{1,2},{2,1},{3,0},{4,7},{5,6},{6,5},{7,4},{8,11},{9,10},{10,... | collective-permute-start | bytes 663560 | tf_op jit(solution)/shard_map/ppermute | solution.py:810
  26.3 0.8 copy-start.15
  31.6 31.1 %collective-permute-start.10 = (bf16[2,3,144,128]{3,2,1,0:T(8,128)(2,1)}, bf16[2,3,144,128]{3,2,1,0:T(8,128)(2,1)S(1)}, u32[]{:S(2)}, u32[]{:S(2)}) collective-permute-start(bf16[2,3,144,128]{3,2,1,0:T(8,128)(2,1)} %get-tuple-element.65), channel_id=1, source_target_pairs={{0,2},{1,3},{2,0},{3,1},{4,6},{5,7},{6,4},{7,5},{8,10},{9,11},{10,... | collective-permute-start | bytes 663560 | tf_op jit(solution)/shard_map/ppermute | solution.py:810
  33.1 29.6 %collective-permute-start.11 = (bf16[2,3,144,128]{3,2,1,0:T(8,128)(2,1)}, bf16[2,3,144,128]{3,2,1,0:T(8,128)(2,1)S(1)}, u32[]{:S(2)}, u32[]{:S(2)}) collective-permute-start(bf16[2,3,144,128]{3,2,1,0:T(8,128)(2,1)} %get-tuple-element.66), channel_id=1, source_target_pairs={{0,3},{1,2},{2,1},{3,0},{4,7},{5,6},{6,5},{7,4},{8,11},{9,10},{10,... | collective-permute-start | bytes 663560 | tf_op jit(solution)/shard_map/ppermute | solution.py:810
  34.5 28.2 %collective-permute-start.9 = (bf16[2,3,144,128]{3,2,1,0:T(8,128)(2,1)}, bf16[2,3,144,128]{3,2,1,0:T(8,128)(2,1)S(1)}, u32[]{:S(2)}, u32[]{:S(2)}) collective-permute-start(bf16[2,3,144,128]{3,2,1,0:T(8,128)(2,1)} %get-tuple-element.64), channel_id=1, source_target_pairs={{0,1},{1,0},{2,3},{3,2},{4,5},{5,4},{6,7},{7,6},{8,9},{9,8},{10,11... | collective-permute-start | bytes 663560 | tf_op jit(solution)/shard_map/ppermute | solution.py:810
  62.7 0.7 copy-start.19
  62.7 0.8 copy-start.20
  62.7 0.8 copy-start.21
  99.5 21.2 %copy-start.7 = (bf16[2,3,144,128]{3,2,1,0:T(8,128)(2,1)S(1)}, bf16[2,3,144,128]{3,2,1,0:T(8,128)(2,1)}, u32[]{:S(2)}) copy-start(bf16[2,3,144,128]{3,2,1,0:T(8,128)(2,1)} %get-tuple-element.76.rest_0_) | copy-start | bytes 663556
  99.5 21.2 %copy-start.6 = (bf16[2,3,144,128]{3,2,1,0:T(8,128)(2,1)S(1)}, bf16[2,3,144,128]{3,2,1,0:T(8,128)(2,1)}, u32[]{:S(2)}) copy-start(bf16[2,3,144,128]{3,2,1,0:T(8,128)(2,1)} %get-tuple-element.59.rest_0_) | copy-start | bytes 663556
  99.5 23.7 %copy-start.18 = (bf16[2,3,144,128]{3,2,1,0:T(8,128)(2,1)S(1)}, bf16[2,3,144,128]{3,2,1,0:T(8,128)(2,1)}, u32[]{:S(2)}) copy-start(bf16[2,3,144,128]{3,2,1,0:T(8,128)(2,1)} %get-tuple-element.60) | copy-start | bytes 663556
  99.5 25.0 %copy-start.17 = (bf16[2,3,144,128]{3,2,1,0:T(8,128)(2,1)S(1)}, bf16[2,3,144,128]{3,2,1,0:T(8,128)(2,1)}, u32[]{:S(2)}) copy-start(bf16[2,3,144,128]{3,2,1,0:T(8,128)(2,1)} %get-tuple-element.61) | copy-start | bytes 663556
  99.5 26.0 %copy-start.16 = (bf16[2,3,144,128]{3,2,1,0:T(8,128)(2,1)S(1)}, bf16[2,3,144,128]{3,2,1,0:T(8,128)(2,1)}, u32[]{:S(2)}) copy-start(bf16[2,3,144,128]{3,2,1,0:T(8,128)(2,1)} %get-tuple-element.62) | copy-start | bytes 663556
  99.5 2.4 %collective-permute-start.16 = (bf16[4,656,128]{2,1,0:T(8,128)(2,1)}, bf16[4,656,128]{2,1,0:T(8,128)(2,1)S(1)}, u32[]{:S(2)}, u32[]{:S(2)}) collective-permute-start(bf16[4,656,128]{2,1,0:T(8,128)(2,1)} %get-tuple-element.81), channel_id=1, source_target_pairs={{0,4},{4,0},{8,12},{12,8},{16,20},{20,16},{24,28},{28,24},{1,5},{5... | collective-permute-start | bytes 2015240 | tf_op jit(solution)/shard_map/ppermute | solution.py:814
  103.1 7.2 %collective-permute-start.17 = (bf16[656,128]{1,0:T(8,128)(2,1)S(1)}, bf16[656,128]{1,0:T(8,128)(2,1)S(1)}, u32[]{:S(2)}, u32[]{:S(2)}) collective-permute-start(bf16[656,128]{1,0:T(8,128)(2,1)S(1)} %get-tuple-element.97), channel_id=1, source_target_pairs={{0,1},{1,0},{2,3},{3,2},{4,5},{5,4},{6,7},{7,6},{8,9},{9,8},{10,11... | collective-permute-start | bytes 503816 | tf_op jit(solution)/shard_map/ppermute | solution.py:810
  104.7 10.5 %collective-permute-start.18 = (bf16[656,128]{1,0:T(8,128)(2,1)S(1)}, bf16[656,128]{1,0:T(8,128)(2,1)S(1)}, u32[]{:S(2)}, u32[]{:S(2)}) collective-permute-start(bf16[656,128]{1,0:T(8,128)(2,1)S(1)} %get-tuple-element.99), channel_id=1, source_target_pairs={{0,2},{1,3},{2,0},{3,1},{4,6},{5,7},{6,4},{7,5},{8,10},{9,11},{10,... | collective-permute-start | bytes 503816 | tf_op jit(solution)/shard_map/ppermute | solution.py:810
  106.2 9.0 %collective-permute-start.19 = (bf16[656,128]{1,0:T(8,128)(2,1)S(1)}, bf16[656,128]{1,0:T(8,128)(2,1)S(1)}, u32[]{:S(2)}, u32[]{:S(2)}) collective-permute-start(bf16[656,128]{1,0:T(8,128)(2,1)S(1)} %get-tuple-element.98), channel_id=1, source_target_pairs={{0,3},{1,2},{2,1},{3,0},{4,7},{5,6},{6,5},{7,4},{8,11},{9,10},{10,... | collective-permute-start | bytes 503816 | tf_op jit(solution)/shard_map/ppermute | solution.py:810
  106.7 12.0 %collective-permute-start.12 = (bf16[2,3,144,128]{3,2,1,0:T(8,128)(2,1)}, bf16[2,3,144,128]{3,2,1,0:T(8,128)(2,1)S(1)}, u32[]{:S(2)}, u32[]{:S(2)}) collective-permute-start(bf16[2,3,144,128]{3,2,1,0:T(8,128)(2,1)} %get-tuple-element.77), channel_id=1, source_target_pairs={{0,1},{1,0},{2,3},{3,2},{4,5},{5,4},{6,7},{7,6},{8,9},{9,8},{10,11... | collective-permute-start | bytes 663560 | tf_op jit(solution)/shard_map/ppermute | solution.py:810
  108.2 15.0 %collective-permute-start.13 = (bf16[2,3,144,128]{3,2,1,0:T(8,128)(2,1)}, bf16[2,3,144,128]{3,2,1,0:T(8,128)(2,1)S(1)}, u32[]{:S(2)}, u32[]{:S(2)}) collective-permute-start(bf16[2,3,144,128]{3,2,1,0:T(8,128)(2,1)} %get-tuple-element.78), channel_id=1, source_target_pairs={{0,2},{1,3},{2,0},{3,1},{4,6},{5,7},{6,4},{7,5},{8,10},{9,11},{10,... | collective-permute-start | bytes 663560 | tf_op jit(solution)/shard_map/ppermute | solution.py:810
  110.3 14.1 %collective-permute-start.14 = (bf16[2,3,144,128]{3,2,1,0:T(8,128)(2,1)}, bf16[2,3,144,128]{3,2,1,0:T(8,128)(2,1)S(1)}, u32[]{:S(2)}, u32[]{:S(2)}) collective-permute-start(bf16[2,3,144,128]{3,2,1,0:T(8,128)(2,1)} %get-tuple-element.79), channel_id=1, source_target_pairs={{0,3},{1,2},{2,1},{3,0},{4,7},{5,6},{6,5},{7,4},{8,11},{9,10},{10,... | collective-permute-start | bytes 663560 | tf_op jit(solution)/shard_map/ppermute | solution.py:810
  116.2 9.3 %collective-permute-start.20 = (bf16[656,128]{1,0:T(8,128)(2,1)S(1)}, bf16[656,128]{1,0:T(8,128)(2,1)S(1)}, u32[]{:S(2)}, u32[]{:S(2)}) collective-permute-start(bf16[656,128]{1,0:T(8,128)(2,1)S(1)} %fusion.1), channel_id=1, source_target_pairs={{0,8},{4,12},{8,0},{12,4},{16,24},{20,28},{24,16},{28,20},{1,9},{5... | collective-permute-start | bytes 503816 | tf_op jit(solution)/shard_map/ppermute | solution.py:814
  116.3 14.5 %collective-permute-start.21 = (bf16[656,128]{1,0:T(8,128)(2,1)S(1)}, bf16[656,128]{1,0:T(8,128)(2,1)S(1)}, u32[]{:S(2)}, u32[]{:S(2)}) collective-permute-start(bf16[656,128]{1,0:T(8,128)(2,1)S(1)} %fusion.1), channel_id=1, source_target_pairs={{0,16},{4,20},{8,24},{12,28},{16,0},{20,4},{24,8},{28,12},{1,17},{... | collective-permute-start | bytes 503816 | tf_op jit(solution)/shard_map/ppermute | solution.py:814
  118.7 19.7 %copy-start.8 = (bf16[2,3,144,128]{3,2,1,0:T(8,128)(2,1)}, bf16[2,3,144,128]{3,2,1,0:T(8,128)(2,1)S(1)}, u32[]{:S(2)}) copy-start(bf16[2,3,144,128]{3,2,1,0:T(8,128)(2,1)S(1)} %collective-permute-done.12.rest_1_) | copy-start | bytes 663556
  118.7 12.0 %collective-permute-start.22 = (bf16[656,128]{1,0:T(8,128)(2,1)S(1)}, bf16[656,128]{1,0:T(8,128)(2,1)S(1)}, u32[]{:S(2)}, u32[]{:S(2)}) collective-permute-start(bf16[656,128]{1,0:T(8,128)(2,1)S(1)} %fusion.1), channel_id=1, source_target_pairs={{0,24},{4,28},{8,16},{12,20},{16,8},{20,12},{24,0},{28,4},{1,25},{... | collective-permute-start | bytes 503816 | tf_op jit(solution)/shard_map/ppermute | solution.py:814
  123.2 19.2 %copy-start.9 = (bf16[2,3,144,128]{3,2,1,0:T(8,128)(2,1)}, bf16[2,3,144,128]{3,2,1,0:T(8,128)(2,1)S(1)}, u32[]{:S(2)}) copy-start(bf16[2,3,144,128]{3,2,1,0:T(8,128)(2,1)S(1)} %collective-permute-done.13.rest_2_) | copy-start | bytes 663556
  123.2 9.7 %collective-permute-start.4 = (bf16[2,3,144,128]{3,2,1,0:T(8,128)(2,1)S(1)}, bf16[2,3,144,128]{3,2,1,0:T(8,128)(2,1)S(1)}, u32[]{:S(2)}, u32[]{:S(2)}) collective-permute-start(bf16[2,3,144,128]{3,2,1,0:T(8,128)(2,1)S(1)} %copy-done.18), channel_id=1, source_target_pairs={{0,1},{1,0},{2,3},{3,2},{4,5},{5,4},{6,7},{7,6},{8,9},{9,8},{10,11... | collective-permute-start | bytes 663560 | tf_op jit(solution)/shard_map/ppermute | solution.py:810
  124.5 17.9 %copy-start.10 = (bf16[2,3,144,128]{3,2,1,0:T(8,128)(2,1)}, bf16[2,3,144,128]{3,2,1,0:T(8,128)(2,1)S(1)}, u32[]{:S(2)}) copy-start(bf16[2,3,144,128]{3,2,1,0:T(8,128)(2,1)S(1)} %collective-permute-done.14.rest_3_) | copy-start | bytes 663556
  124.5 13.8 %collective-permute-start.5 = (bf16[2,3,144,128]{3,2,1,0:T(8,128)(2,1)S(1)}, bf16[2,3,144,128]{3,2,1,0:T(8,128)(2,1)S(1)}, u32[]{:S(2)}, u32[]{:S(2)}) collective-permute-start(bf16[2,3,144,128]{3,2,1,0:T(8,128)(2,1)S(1)} %copy-done.17), channel_id=1, source_target_pairs={{0,2},{1,3},{2,0},{3,1},{4,6},{5,7},{6,4},{7,5},{8,10},{9,11},{10,... | collective-permute-start | bytes 663560 | tf_op jit(solution)/shard_map/ppermute | solution.py:810
  125.5 12.7 %collective-permute-start.6 = (bf16[2,3,144,128]{3,2,1,0:T(8,128)(2,1)S(1)}, bf16[2,3,144,128]{3,2,1,0:T(8,128)(2,1)S(1)}, u32[]{:S(2)}, u32[]{:S(2)}) collective-permute-start(bf16[2,3,144,128]{3,2,1,0:T(8,128)(2,1)S(1)} %copy-done.16), channel_id=1, source_target_pairs={{0,3},{1,2},{2,1},{3,0},{4,7},{5,6},{6,5},{7,4},{8,11},{9,10},{10,... | collective-permute-start | bytes 663560 | tf_op jit(solution)/shard_map/ppermute | solution.py:810
  130.9 8.4 %collective-permute-start.23 = (bf16[656,128]{1,0:T(8,128)(2,1)S(1)}, bf16[656,128]{1,0:T(8,128)(2,1)S(1)}, u32[]{:S(2)}, u32[]{:S(2)}) collective-permute-start(bf16[656,128]{1,0:T(8,128)(2,1)S(1)} %add_convert_fusion), channel_id=1, source_target_pairs={{0,1},{1,0},{2,3},{3,2},{4,5},{5,4},{6,7},{7,6},{8,9},{9,8},{10,11... | collective-permute-start | bytes 503816 | tf_op jit(solution)/shard_map/ppermute | solution.py:810
  132.4 9.8 %collective-permute-start.24 = (bf16[656,128]{1,0:T(8,128)(2,1)S(1)}, bf16[656,128]{1,0:T(8,128)(2,1)S(1)}, u32[]{:S(2)}, u32[]{:S(2)}) collective-permute-start(bf16[656,128]{1,0:T(8,128)(2,1)S(1)} %add_convert_fusion), channel_id=1, source_target_pairs={{0,2},{1,3},{2,0},{3,1},{4,6},{5,7},{6,4},{7,5},{8,10},{9,11},{10,... | collective-permute-start | bytes 503816 | tf_op jit(solution)/shard_map/ppermute | solution.py:810
  132.9 20.4 %copy-start.11 = (bf16[2,3,144,128]{3,2,1,0:T(8,128)(2,1)}, bf16[2,3,144,128]{3,2,1,0:T(8,128)(2,1)S(1)}, u32[]{:S(2)}) copy-start(bf16[2,3,144,128]{3,2,1,0:T(8,128)(2,1)S(1)} %collective-permute-done.4.rest_1_) | copy-start | bytes 663556
  132.9 9.3 %collective-permute-start.25 = (bf16[656,128]{1,0:T(8,128)(2,1)S(1)}, bf16[656,128]{1,0:T(8,128)(2,1)S(1)}, u32[]{:S(2)}, u32[]{:S(2)}) collective-permute-start(bf16[656,128]{1,0:T(8,128)(2,1)S(1)} %add_convert_fusion), channel_id=1, source_target_pairs={{0,3},{1,2},{2,1},{3,0},{4,7},{5,6},{6,5},{7,4},{8,11},{9,10},{10,... | collective-permute-start | bytes 503816 | tf_op jit(solution)/shard_map/ppermute | solution.py:810
  138.2 15.1 %copy-start.12 = (bf16[2,3,144,128]{3,2,1,0:T(8,128)(2,1)}, bf16[2,3,144,128]{3,2,1,0:T(8,128)(2,1)S(1)}, u32[]{:S(2)}) copy-start(bf16[2,3,144,128]{3,2,1,0:T(8,128)(2,1)S(1)} %collective-permute-done.5.rest_2_) | copy-start | bytes 663556
  138.2 10.2 %collective-permute-start.15 = (bf16[4,2,3,80,128]{4,3,2,1,0:T(8,128)(2,1)S(1)}, bf16[4,2,3,80,128]{4,3,2,1,0:T(8,128)(2,1)}, u32[]{:S(2)}, u32[]{:S(2)}) collective-permute-start(bf16[4,2,3,80,128]{4,3,2,1,0:T(8,128)(2,1)S(1)} %pad_maximum_fusion.2), channel_id=1, source_target_pairs={{0,4},{4,8},{8,12},{12,16},{16,20},{20,24},{24,28},{28,0},{1,5},{5... | collective-permute-start | bytes 1474568 | tf_op jit(solution)/shard_map/ppermute | solution.py:953
  138.3 4.0 %copy-start.13 = (bf16[2,3,144,128]{3,2,1,0:T(8,128)(2,1)}, bf16[2,3,144,128]{3,2,1,0:T(8,128)(2,1)S(1)}, u32[]{:S(2)}) copy-start(bf16[2,3,144,128]{3,2,1,0:T(8,128)(2,1)S(1)} %collective-permute-done.6.rest_3_) | copy-start | bytes 663556
  138.4 15.3 %collective-permute-start.7 = (bf16[4,2,3,80,128]{4,3,2,1,0:T(8,128)(2,1)S(1)}, bf16[4,2,3,80,128]{4,3,2,1,0:T(8,128)(2,1)}, u32[]{:S(2)}, u32[]{:S(2)}) collective-permute-start(bf16[4,2,3,80,128]{4,3,2,1,0:T(8,128)(2,1)S(1)} %pad_maximum_fusion.1), channel_id=1, source_target_pairs={{0,4},{4,8},{8,12},{12,16},{16,20},{20,24},{24,28},{28,0},{1,5},{5... | collective-permute-start | bytes 1474568 | tf_op jit(solution)/shard_map/ppermute | solution.py:953
  142.4 11.0 %copy-start.1 = (bf16[4,656,128]{2,1,0:T(8,128)(2,1)}, bf16[4,656,128]{2,1,0:T(8,128)(2,1)S(1)}, u32[]{:S(2)}) copy-start(bf16[4,656,128]{2,1,0:T(8,128)(2,1)S(1)} %pad_maximum_fusion.own) | copy-start | bytes 2015236
  142.4 16.0 %collective-permute-start.26 = (bf16[4,656,128]{2,1,0:T(8,128)(2,1)S(1)}, bf16[4,656,128]{2,1,0:T(8,128)(2,1)}, u32[]{:S(2)}, u32[]{:S(2)}) collective-permute-start(bf16[4,656,128]{2,1,0:T(8,128)(2,1)S(1)} %pad_maximum_fusion.own), channel_id=1, source_target_pairs={{0,4},{4,0},{8,12},{12,8},{16,20},{20,16},{24,28},{28,24},{1,5},{5... | collective-permute-start | bytes 2015240 | tf_op jit(solution)/shard_map/ppermute | solution.py:814

commit v3 on v2

--- a/solution.py
+++ b/solution.py
@@ -82,90 +82,93 @@
     return parts
 
 
-def pack_kernel(z, scal, base, x_ref, halo_ref, *rest):
+def pack_kernel(z, offsets, base, x_ref, halo_ref, *rest):
     outs, onehot = rest[: z.lev], rest[z.lev]
-    p = scal[0]
-    off = scal[1 + pl.program_id(0)]
+    p = lax.axis_index("lev")
     rows = z.tokens + halo_ref.shape[2] * z.rows
     column = lax.broadcasted_iota(jnp.int32, (z.ro, rows), 1)
-    for k in range(z.lev):
-        hit = column == base[...] + (off * z.rows + (p ^ k) * (z.nb * WLAT))
-        onehot[k * z.ro : (k + 1) * z.ro] = jnp.where(hit, 1.0, 0.0).astype(BF16)
-    levels = []
-    for l in range(z.l):
-        cells = [r[0, l].reshape(r.shape[2] * z.rows, z.d) for r in (x_ref, halo_ref)]
-        levels.append(jnp.concatenate(cells, axis=0))
-    moved = nn(onehot[...], jnp.concatenate(lane_parts(z, levels), axis=1)).astype(BF16)
-    for k in range(z.lev):
-        for j in range(z.nblk):
-            outs[k][0, j] = moved[k * z.ro : (k + 1) * z.ro, j * LANES : (j + 1) * LANES]
-
-
-def pack(z, x, halo, scal):
+    for s in range(z.s):
+        for k in range(z.lev):
+            hit = column == base[...] + (offsets[s] * z.rows + (p ^ k) * (z.nb * WLAT))
+            onehot[s, k * z.ro : (k + 1) * z.ro] = jnp.where(hit, 1.0, 0.0).astype(BF16)
+        levels = []
+        for l in range(z.l):
+            cells = [r[s, l].reshape(r.shape[2] * z.rows, z.d) for r in (x_ref, halo_ref)]
+            levels.append(jnp.concatenate(cells, axis=0))
+        moved = nn(onehot[s], jnp.concatenate(lane_parts(z, levels), axis=1)).astype(BF16)
+        for k in range(z.lev):
+            for j in range(z.nblk):
+                outs[k][s, j] = moved[k * z.ro : (k + 1) * z.ro, j * LANES : (j + 1) * LANES]
+
+
+def in_vmem(count):
+    return [pl.BlockSpec(memory_space=pltpu.VMEM)] * count
+
+
+def in_smem(count):
+    return [pl.BlockSpec(memory_space=pltpu.SMEM)] * count
+
+
+def pack(z, x, halo, offsets):
     own, _ = slot_rows(z)
-    tokens = lambda a: pl.BlockSpec((1,) + a.shape[1:], lambda s, _: (s, 0, 0, 0, 0))
-    spec = pl.BlockSpec((1, z.nblk, z.ro, LANES), lambda s, _: (s, 0, 0, 0))
+    rows = z.tokens + halo.shape[2] * z.rows
     return pl.pallas_call(
         functools.partial(pack_kernel, z),
-        grid_spec=pltpu.PrefetchScalarGridSpec(
-            num_scalar_prefetch=1,
-            grid=(x.shape[0],),
-            in_specs=[pl.BlockSpec((z.ro, 1), lambda s, _: (0, 0)), tokens(x), tokens(halo)],
-            out_specs=[spec] * z.lev,
-            scratch_shapes=[
-                pltpu.VMEM((z.lev * z.ro, z.tokens + halo.shape[2] * z.rows), BF16)
-            ],
-        ),
-        out_shape=[jax.ShapeDtypeStruct((x.shape[0], z.nblk, z.ro, LANES), BF16)] * z.lev,
-        compiler_params=pltpu.CompilerParams(vmem_limit_bytes=60 * 2**20),
+        in_specs=in_smem(1) + in_vmem(3),
+        out_specs=in_vmem(z.lev),
+        scratch_shapes=[pltpu.VMEM((z.s, z.lev * z.ro, rows), BF16)],
+        out_shape=[jax.ShapeDtypeStruct((z.s, z.nblk, z.ro, LANES), BF16)] * z.lev,
+        compiler_params=pltpu.CompilerParams(vmem_limit_bytes=40 * 2**20),
         cost_estimate=cost(4),
         name="pack",
-    )(scal, jnp.asarray(own)[:, None], x, halo)
-
-
-def unpack_kernel(z, scal, own_base, halo_base, *rest):
-    pieces, halo_ref, out_ref, onehot = rest[: z.lev], rest[z.lev], rest[z.lev + 1], rest[z.lev + 2]
-    p = scal[0]
-    off = scal[1 + pl.program_id(0)]
-    at = 0
-    for base, size in ((own_base, z.ro), (halo_base, z.rh)):
-        row = lax.broadcasted_iota(jnp.int32, (z.tokens, size), 0)
-        for k in range(z.lev):
-            hit = row == base[...] + (off * z.rows + (p ^ k) * (z.nb * WLAT))
-            onehot[:, at : at + size] = jnp.where(hit, 1.0, 0.0).astype(BF16)
-            at += size
-    columns = []
-    for j in range(z.nblk):
-        rows = [r[0, j] for r in pieces] + [halo_ref[k, 0, j] for k in range(z.lev)]
-        columns.append(jnp.concatenate(rows, axis=0))
-    moved = nn(onehot[...], jnp.concatenate(columns, axis=1))
-    half = z.d - LANES
-    for l in range(z.l):
-        low = moved[:, l * LANES : (l + 1) * LANES]
-        at = (z.l + l // 2) * LANES + (l % 2) * half
-        tokens = jnp.concatenate([low, moved[:, at : at + half]], axis=1)
-        out_ref[0, l] = tokens.reshape(z.cells, z.rows, z.d).astype(BF16)
-
-
-def unpack(z, own, halo, scal):
-    bases = [jnp.asarray(v)[None] for v in slot_rows(z)]
-    spec = pl.BlockSpec((1, z.nblk, z.ro, LANES), lambda s, _: (s, 0, 0, 0))
+    )(offsets, jnp.asarray(own)[:, None], x, halo)
+
+
+def unpack_kernel(z, merged, offsets, *rest):
+    count = 1 if merged else 2
+    bases, pieces = rest[:count], rest[count : count + z.lev]
+    halo_ref, out_ref, onehot = rest[-3], rest[-2], rest[-1]
+    p = lax.axis_index("lev")
+    for s in range(z.s):
+        at = 0
+        for base, size in zip(bases, (z.ro, z.rh)):
+            row = lax.broadcasted_iota(jnp.int32, (z.tokens, size), 0)
+            for k in range(z.lev):
+                place = base[...] + (offsets[s] * z.rows + (p ^ k) * (z.nb * WLAT))
+                if merged:
+                    place = jnp.where(place >= z.tokens, place - z.tokens, place)
+                onehot[s, :, at : at + size] = jnp.where(row == place, 1.0, 0.0).astype(BF16)
+                at += size
+        columns = []
+        for j in range(z.nblk):
+            rows = [r[s, j] for r in pieces]
+            if not merged:
+                rows += [halo_ref[k, s, j] for k in range(z.lev)]
+            columns.append(jnp.concatenate(rows, axis=0))
+        moved = nn(onehot[s], jnp.concatenate(columns, axis=1))
+        half = z.d - LANES
+        for l in range(z.l):
+            low = moved[:, l * LANES : (l + 1) * LANES]
+            at = (z.l + l // 2) * LANES + (l % 2) * half
+            tokens = jnp.concatenate([low, moved[:, at : at + half]], axis=1)
+            out_ref[s, l] = tokens.reshape(z.cells, z.rows, z.d).astype(BF16)
+
+
+def unpack(z, own, halo, offsets):
+    merged = halo is None
+    bases = [jnp.asarray(v)[None] for v in slot_rows(z)][: 1 if merged else 2]
+    slots = z.ro if merged else z.ro + z.rh
+    arrays = bases + list(own) + ([] if merged else [halo])
     return pl.pallas_call(
-        functools.partial(unpack_kernel, z),
-        grid_spec=pltpu.PrefetchScalarGridSpec(
-            num_scalar_prefetch=1,
-            grid=(z.s,),
-            in_specs=[pl.BlockSpec((1, v.shape[1]), lambda s, _: (0, 0)) for v in bases]
-            + [spec] * z.lev
-            + [pl.BlockSpec((z.lev, 1, z.nblk, z.rh, LANES), lambda s, _: (0, s, 0, 0, 0))],
-            out_specs=pl.BlockSpec((1, z.l, z.cells, z.rows, z.d), lambda s, _: (s, 0, 0, 0, 0)),
-            scratch_shapes=[pltpu.VMEM((z.tokens, z.lev * (z.ro + z.rh)), BF16)],
-        ),
+        functools.partial(unpack_kernel, z, merged),
+        in_specs=in_smem(1) + in_vmem(len(arrays)),
+        out_specs=pl.BlockSpec(memory_space=pltpu.VMEM),
+        scratch_shapes=[pltpu.VMEM((z.s, z.tokens, z.lev * slots), BF16)],
         out_shape=jax.ShapeDtypeStruct((z.s, z.l, z.cells, z.rows, z.d), BF16),
-        compiler_params=pltpu.CompilerParams(vmem_limit_bytes=60 * 2**20),
+        compiler_params=pltpu.CompilerParams(vmem_limit_bytes=40 * 2**20),
         cost_estimate=cost(4),
         name="unpack",
-    )(scal, *bases, *own, halo)
+    )(offsets, *arrays)
 
 
 def cost(microseconds):
@@ -373,7 +376,7 @@
     it = iter(refs)
     take = lambda n: [next(it) for _ in range(n)]
     wire_in = take(z.lev)
-    bias_ref, mask_ref, column_mask = take(3)
+    offsets, sizes, bias_ref, column_mask = take(4)
     gain1, shift1, gain2, shift2, gain3, shift3 = take(6)
     w_qkv1, wo1, w_qkv2, wo2, w_up, w_down_t = take(6)
     wire_out = take(z.lev)
@@ -386,7 +389,14 @@
     def _():
         load_wire(z, wire_in, wire_s)
 
-    bias_s[...] = bias_ref[0] + mask_ref[0, 0]
+    s = pl.program_id(0)
+    token = lax.broadcasted_iota(jnp.int32, (TOK, 1), 0)
+    cell = (token * 43) >> 8
+    row = token - cell * WLAT + (lax.axis_index("lev") * z.nb + b) * WLAT
+    cell = cell + (lax.axis_index("lon") * z.cells + offsets[s])
+    cell = jnp.where(cell >= z.cells * z.lon, cell - z.cells * z.lon, cell)
+    valid = (row < sizes[s, 0]) & (cell < sizes[s, 1])
+    bias_s[...] = bias_ref[0] + jnp.where(valid, 0.0, NEGATIVE)
 
     def keep(ref, gain, shift):
         def store(lv, values, normed, rstd):
@@ -487,7 +497,7 @@
     ]
 
 
-def forward(z, wire, bias, mask, column_mask, norms, weights):
+def forward(z, wire, offsets, sizes, bias, column_mask, norms, weights):
     res = residual_shapes(z)
     rows3 = (z.lt, TOK, z.d)
     out = pl.pallas_call(
@@ -495,8 +505,8 @@
         grid=(z.s, z.nb),
         in_specs=wire_specs(z)
         + [
+            *in_smem(2),
             pl.BlockSpec((1, 2, TOK, z.heads // 2 * TOK), lambda s, b: (b, 0, 0, 0)),
-            pl.BlockSpec((1, 1, TOK, 1), lambda s, b: (s, b, 0, 0)),
             whole_spec(column_mask),
         ]
         + [whole_spec(a) for a in norms]
@@ -513,7 +523,7 @@
         compiler_params=pltpu.CompilerParams(vmem_limit_bytes=60 * 2**20),
         cost_estimate=cost(30),
         name="forward",
-    )(*wire, bias, mask, column_mask, *norms, *weights)
+    )(*wire, offsets, sizes, bias, column_mask, *norms, *weights)
     return out[: z.lev], out[z.lev :]
 
 
@@ -570,7 +580,7 @@
     return pick
 
 
-def backward_kernel(z, scal, *refs):
+def backward_kernel(z, *refs):
     it = iter(refs)
     take = lambda n: [next(it) for _ in range(n)]
     wire_in = take(z.lev)
@@ -579,8 +589,8 @@
     gain1, shift1, gain2, shift2, gain3, shift3 = take(6)
     w_qkv1, wo1, w_qkv2, wo2, w_up, w_down_t = take(6)
     wire_out = take(z.lev)
-    mine_ref, other_ref = take(2)
-    wire_s, g_s, o_s, a_s, qkv_s, grad_s, gh_s, db_s, vec_s, sums_s = take(10)
+    late_ref, mine_ref, other_ref = take(3)
+    wire_s, late_s, g_s, o_s, a_s, qkv_s, grad_s, gh_s, db_s, vec_s, sums_s = take(11)
     grads = {name: ref for (name, _), ref in zip(grad_list(z), take(len(grad_list(z))))}
     scale = np.float32((z.d // z.heads) ** (-0.5))
     ones, scales = head_masks(z), head_masks(z, scale)
@@ -702,10 +712,14 @@
     @pl.when(b == z.nb - 1)
     def _():
         flush_wire(z, wire_s, wire_out)
+        for band in range(z.nb):
+            rows = wire_s[:, :, band * TOK + HALO0 : (band + 1) * TOK, :]
+            late_s[:, :, band * HALO : (band + 1) * HALO, :] = rows
+        late_ref[:, 0] = late_s[...].astype(BF16)
 
     @pl.when((s == z.s - 1) & (b == z.nb - 1))
     def _():
-        p, core = scal[0], scal[1]
+        p, core = lax.axis_index("lev"), lax.axis_index("lon") % 2
 
         def place(i):
             return ((i // z.lev) ^ core) * z.lev + ((i % z.lev) ^ p)
@@ -753,33 +767,35 @@
                 halves.append(total)
             both = jnp.concatenate(halves, axis=0)
             for j in range(4):
-                put_unit((scal[0] * z.nb + band) * 4 + j, both[:, j * LANES : (j + 1) * LANES])
+                put_unit((p * z.nb + band) * 4 + j, both[:, j * LANES : (j + 1) * LANES])
         mine_ref[...] = sums_s[: z.lev]
         other_ref[...] = sums_s[z.lev :]
 
 
-def backward(z, scal, wire, residuals, norms, weights):
+def backward(z, wire, residuals, norms, weights):
     res = residual_shapes(z)
     rows3 = (z.lt, TOK, z.d)
     pick = jnp.asarray(bias_rows(z))
-    drop = lambda spec: pl.BlockSpec(spec.block_shape, lambda s, b, _, m=spec.index_map: m(s, b))
     half = (z.lev, z.pr, LANES)
     out = pl.pallas_call(
         functools.partial(backward_kernel, z),
-        grid_spec=pltpu.PrefetchScalarGridSpec(
-            num_scalar_prefetch=1,
+        **dict(
             grid=(z.s, z.nb),
             in_specs=[
-                drop(spec)
+                spec
                 for spec in wire_specs(z)
                 + [unit_spec(shape) for shape, _ in res]
                 + [whole_spec(pick)]
                 + [whole_spec(a) for a in norms]
                 + [whole_spec(a) for a in weights]
             ],
-            out_specs=[drop(spec) for spec in wire_specs(z)]
-            + [pl.BlockSpec(half, lambda s, b, _: (0, 0, 0))] * 2,
-            scratch_shapes=[pltpu.VMEM((z.lev, z.nblk, z.ro, LANES), F32)]
+            out_specs=[spec for spec in wire_specs(z)]
+            + [pl.BlockSpec((z.lev, 1, z.nblk, z.rh, LANES), lambda s, b: (0, s, 0, 0, 0))]
+            + [pl.BlockSpec(half, lambda s, b: (0, 0, 0))] * 2,
+            scratch_shapes=[
+                pltpu.VMEM((z.lev, z.nblk, z.ro, LANES), F32),
+                pltpu.VMEM((z.lev, z.nblk, z.rh, LANES), F32),
+            ]
             + [pltpu.VMEM(rows3, F32)] * 2
             + [
                 pltpu.VMEM((z.lt, TOK, 2 * LANES), F32),
@@ -792,12 +808,14 @@
             ]
             + [pltpu.VMEM(grad_buffer(z, *item), F32) for item in grad_list(z)],
         ),
-        out_shape=wire_shapes(z) + [jax.ShapeDtypeStruct(half, BF16)] * 2,
+        out_shape=wire_shapes(z)
+        + [jax.ShapeDtypeStruct((z.lev, z.s, z.nblk, z.rh, LANES), BF16)]
+        + [jax.ShapeDtypeStruct(half, BF16)] * 2,
         compiler_params=pltpu.CompilerParams(vmem_limit_bytes=62 * 2**20),
         cost_estimate=cost(40),
         name="backward",
-    )(scal, *wire, *residuals, pick, *norms, *weights)
-    return out[: z.lev], out[z.lev], out[z.lev + 1]
+    )(*wire, *residuals, pick, *norms, *weights)
+    return out[: z.lev], out[z.lev], out[z.lev + 1], out[z.lev + 2]
 
 
 def tree(parts):
@@ -814,15 +832,57 @@
     return lax.ppermute(array, "lon", [(i, i ^ k) for i in range(z.lon)])
 
 
-def sum_wire(z, mine, other):
+def merge_kernel(z, offsets, *refs):
+    wire, late_ref, outs = refs[: z.lev], refs[z.lev], refs[z.lev + 1 :]
+    row = lax.broadcasted_iota(jnp.int32, (HALO, LANES), 0) + HALO0
+    for s in range(z.s):
+        moved = row >= (z.cells - offsets[s]) * WLAT
+        for k in range(z.lev):
+            for j in range(z.nblk):
+                rows, late = wire[k][s, j].astype(F32), late_ref[k, s, j].astype(F32)
+                parts = []
+                for b in range(z.nb):
+                    own = rows[b * TOK : (b + 1) * TOK]
+                    got = late[b * HALO : (b + 1) * HALO]
+                    parts += [own[:HALO0], jnp.where(moved, got, own[HALO0:])]
+                if z.ro > z.nb * TOK:
+                    parts.append(rows[z.nb * TOK :])
+                outs[k][s, j] = jnp.concatenate(parts, axis=0).astype(BF16)
+
+
+def merge_cells(z, wire, late, offsets):
+    return pl.pallas_call(
+        functools.partial(merge_kernel, z),
+        in_specs=in_smem(1) + in_vmem(z.lev + 1),
+        out_specs=in_vmem(z.lev),
+        out_shape=[jax.ShapeDtypeStruct((z.s, z.nblk, z.ro, LANES), BF16)] * z.lev,
+        compiler_params=pltpu.CompilerParams(vmem_limit_bytes=40 * 2**20),
+        cost_estimate=cost(3),
+        name="merge",
+    )(offsets, *wire, late)
+
+
+def tie(values, *others):
+    return lax.optimization_barrier((values,) + others)[0]
+
+
+def sum_cores(z, mine, other):
     got = lon_swap(z, other, 1)
-    half = [(mine[k].astype(F32) + got[k].astype(F32)).astype(BF16) for k in range(z.lev)]
+    return [(mine[k].astype(F32) + got[k].astype(F32)).astype(BF16) for k in range(z.lev)]
+
+
+def sum_levels(z, half):
     parts = [half[0]] + [lev_swap(z, half[k], k) for k in range(1, z.lev)]
-    quarter = tree([v.astype(F32) for v in parts]).astype(BF16)
+    return tree([v.astype(F32) for v in parts]).astype(BF16)
+
+
+def sum_slabs(z, quarter):
     parts = [quarter] + [lon_swap(z, quarter, 2 * k) for k in range(1, z.lon // 2)]
-    done = tree([v.astype(F32) for v in parts]).astype(BF16)
-    own = jnp.stack([done] + [lev_swap(z, done, k) for k in range(1, z.lev)])
-    return own, lon_swap(z, own, 1)
+    return tree([v.astype(F32) for v in parts]).astype(BF16)
+
+
+def share_levels(z, done):
+    return [done] + [lev_swap(z, done, k) for k in range(1, z.lev)]
 
 
 def table_lanes(z, h):
@@ -832,8 +892,8 @@
     return lanes.reshape(1, WLAT * 32)
 
 
-def finish_kernel(z, scal, lanes, order, own, other, *outs):
-    p, core = scal[0], scal[1]
+def finish_kernel(z, lanes, order, own, other, *outs):
+    p, core = lax.axis_index("lev"), lax.axis_index("lon") % 2
     named = {name: ref for (name, _), ref in zip(grad_list(z), outs)}
     vec_refs, bias_ref = outs[len(named) : len(named) + 6], outs[len(named) + 6]
 
@@ -864,7 +924,7 @@
             bias_ref[h, i] = values.reshape(WLAT, z.bands, 2 * WLON - 1)
 
 
-def finish(z, scal, own, other):
+def finish(z, own, other):
     shapes = [jax.ShapeDtypeStruct((z.d, columns), F32) for _, columns in grad_list(z)]
     shapes += [jax.ShapeDtypeStruct((1, z.d), F32)] * 6
     shapes += [jax.ShapeDtypeStruct((z.heads, WLAT, WLAT, z.bands, 2 * WLON - 1), F32)]
@@ -875,26 +935,32 @@
             for k in range(z.bands):
                 order[parity * 8 * z.bands + i * z.bands + k, k * UNIT + parity * 8 + i] = 1.0
     order = jnp.asarray(order, BF16)
-    full = lambda a: pl.BlockSpec(a.shape, lambda i, _, n=len(a.shape): (0,) * n)
     out = pl.pallas_call(
         functools.partial(finish_kernel, z),
-        grid_spec=pltpu.PrefetchScalarGridSpec(
-            num_scalar_prefetch=1,
-            grid=(1,),
-            in_specs=[full(a) for a in (lanes, order, own, other)],
-            out_specs=[full(a) for a in shapes],
-        ),
+        in_specs=in_vmem(4),
+        out_specs=in_vmem(len(shapes)),
         out_shape=shapes,
-        compiler_params=pltpu.CompilerParams(vmem_limit_bytes=60 * 2**20),
+        compiler_params=pltpu.CompilerParams(vmem_limit_bytes=40 * 2**20),
         cost_estimate=cost(4),
         name="finish",
-    )(scal, lanes, order, own, other)
+    )(lanes, order, own, other)
     named = {name: value for (name, _), value in zip(grad_list(z), out)}
     vectors = [v.reshape(z.d) for v in out[len(named) : len(named) + 6]]
     return named, vectors, out[-1].transpose(3, 0, 1, 2, 4)
 
 
-def bias_kernel(z, table_ref, pick_ref, out_ref, even_s, odd_s):
+def bias_kernel(z, table_ref, pick_ref, qkv1, out1, qkv2, out2, out_ref, *rest):
+    even_s, odd_s = rest[4:]
+    side = z.d // 2
+    for source, target in ((qkv1, rest[0]), (qkv2, rest[2])):
+        room = jnp.zeros((z.d, LANES - side), BF16)
+        for t in range(6):
+            part = source[:, t * side : (t + 1) * side]
+            target[:, t * LANES : (t + 1) * LANES] = jnp.concatenate([part, room], axis=1)
+    for source, target in ((out1, rest[1]), (out2, rest[3])):
+        for t in range(2):
+            target[t * LANES : t * LANES + side] = source[t * side : (t + 1) * side]
+            target[t * LANES + side : (t + 1) * LANES] = jnp.zeros((LANES - side, z.d), BF16)
     width = 4 * LANES
     lane = lax.broadcasted_iota(jnp.int32, (2 * WLON - 1, width), 1)
     step = lax.broadcasted_iota(jnp.int32, (2 * WLON - 1, width), 0) * WLAT
@@ -931,18 +997,22 @@
         out_ref[b, 1] = full[:, side : 2 * side]
 
 
-def bias_of(z, bias_table, p):
+def bias_of(z, bias_table, p, weights):
     table = lax.dynamic_slice_in_dim(bias_table, p * z.nb, z.nb, axis=0)
     table = jnp.pad(table.transpose(1, 2, 0, 3, 4), ((0, 0),) * 3 + ((0, 2), (0, 0)))
     table = table.reshape(z.heads, WLAT, z.nb * 8, 2 * WLON - 1)
-    return pl.pallas_call(
+    wide = jax.ShapeDtypeStruct((z.d, 6 * LANES), BF16)
+    tall = jax.ShapeDtypeStruct((2 * LANES, z.d), BF16)
+    bias = jax.ShapeDtypeStruct((z.nb, 2, TOK, z.heads // 2 * TOK), F32)
+    out = pl.pallas_call(
         functools.partial(bias_kernel, z),
-        out_shape=jax.ShapeDtypeStruct((z.nb, 2, TOK, z.heads // 2 * TOK), F32),
+        out_shape=[bias, wide, tall, wide, tall],
         scratch_shapes=[pltpu.VMEM((z.nb * 8, 4 * LANES), F32)] * 2,
-        compiler_params=pltpu.CompilerParams(vmem_limit_bytes=60 * 2**20),
+        compiler_params=pltpu.CompilerParams(vmem_limit_bytes=40 * 2**20),
         cost_estimate=cost(4),
         name="bias",
-    )(table, jnp.asarray(bias_rows(z)))
+    )(table, jnp.asarray(bias_rows(z)), *weights)
+    return out[0], list(out[1:])
 
 
 def lev_exchange(z, wire):
@@ -964,23 +1034,21 @@
 ):
     d = inputs.shape[-1]
     z = Sizes(lax.axis_size("lev"), lax.axis_size("lon"), inputs.shape, bias_table.shape[1], w_up.shape[1])
-    p, w = lax.axis_index("lev"), lax.axis_index("lon")
-    scal = jnp.concatenate([p[None].astype(jnp.int32), offsets.astype(jnp.int32)])
+    p = lax.axis_index("lev")
     swap = lambda a: a.transpose(0, 1, 3, 2, 4)
 
     half = WLON // 2
     x, c = swap(inputs), swap(cotangent)
     halo_x = lon_shift(z, x[:, :, :half], -1)
-    halo_c = lon_shift(z, c[:, :, :half], -1)
-    bias = bias_of(z, bias_table, p)
-    wire_x = lev_exchange(z, pack(z, x, halo_x, scal))
-    wire_c = lev_exchange(z, pack(z, c, halo_c, scal))
-    cell = (w * z.cells + offsets[:, None] + jnp.arange(WLON)[None, :]) % (z.cells * z.lon)
-    row = (p * z.nb + jnp.arange(z.nb))[:, None] * WLAT + jnp.arange(WLAT)[None, :]
-    cell_ok = cell < grid_sizes[:, 1:2]
-    row_ok = row[None] < grid_sizes[:, 0][:, None, None]
-    valid = cell_ok[:, None, :, None] & row_ok[:, :, None, :]
-    mask = jnp.where(valid, 0.0, NEGATIVE).astype(F32).reshape(z.s, z.nb, TOK, 1)
+    raw = (qkv_window, out_window, qkv_column, out_column)
+    bias, weights = bias_of(z, bias_table, p, raw)
+    weights = weights + [w_up, w_down.T]
+    halo_x, bias = lax.optimization_barrier((halo_x, bias))
+    halo_c = lon_shift(z, tie(c[:, :, :half], halo_x), -1)
+    wire_x = pack(z, x, halo_x, offsets)
+    halo_c = tie(halo_c, *wire_x)
+    wire_x = lev_exchange(z, wire_x)
+    wire_c = lev_exchange(z, pack(z, c, halo_c, offsets))
     of_key = np.arange(z.lt * GROUP) % GROUP
     of_query = np.tile(of_key, z.heads // 2)
     column_mask = jnp.asarray(
@@ -988,20 +1056,22 @@
     )
 
     norms = [v[None] for v in (gain_one, shift_one, gain_two, shift_two, gain_three, shift_three)]
-    room = ((0, 0), (0, 0), (0, LANES - d // 2))
-    wide = lambda a: jnp.pad(a.reshape(d, 6, d // 2), room).reshape(d, 6 * LANES)
-    tall = lambda a: jnp.pad(a.reshape(2, d // 2, d), (room[0], room[2], room[0])).reshape(2 * LANES, d)
-    weights = [wide(qkv_window), tall(out_window), wide(qkv_column), tall(out_column), w_up, w_down.T]
-
-    places = jnp.stack([p, w % 2]).astype(jnp.int32)
-    wire_r, residuals = forward(z, wire_x, bias, mask, column_mask, norms, weights)
+    wire_r, residuals = forward(z, wire_x, offsets, grid_sizes, bias, column_mask, norms, weights)
     wire_r = lev_exchange(z, wire_r)
-    wire_g, mine, other = backward(z, places, wire_c, residuals, norms, weights)
-    wire_g = lev_exchange(z, wire_g)
-    result = unpack(z, wire_r, lon_shift(z, last_cells(z, wire_r), 1), scal)
-    input_grad = unpack(z, wire_g, lon_shift(z, last_cells(z, wire_g), 1), scal)
-    own, other = sum_wire(z, mine, other)
-    named, vec, table = finish(z, places, own, other)
+    grads = backward(z, wire_c, residuals, norms, weights)
+    (wire_g, late, mine, other), wire_r = lax.optimization_barrier((grads, wire_r))
+    halo_r = lon_shift(z, last_cells(z, wire_r), 1)
+    late = lon_shift(z, late, 1)
+    sums = sum_cores(z, mine, other)
+    sums = sum_levels(z, sums)
+    wire_g = lev_exchange(z, merge_cells(z, wire_g, late, offsets))
+    result = unpack(z, wire_r, halo_r, offsets)
+    sums = sum_slabs(z, tie(sums, halo_r, late))
+    sums = share_levels(z, tie(sums, result))
+    input_grad = unpack(z, wire_g, None, offsets)
+    own = jnp.stack(tie(sums, input_grad))
+    other = lon_swap(z, own, 1)
+    named, vec, table = finish(z, own, other)
     return (
         swap(result), swap(input_grad),
         vec[0], vec[1], named["qkv1"], named["o1"], table,

time: 164 us -> 148 us (0.902)
  Pallas kernels: 89.5 us -> 77.8 us
  starting transfers between devices: 32.4 us -> 35.5 us
  local copies, waits for them, and re-layouts: 8.92 us -> 6.62 us
  other arithmetic: 4.74 us -> 2.49 us
  waiting for transfers between devices: 26.3 us -> 24.5 us
    pallas_call x7 -> x8, Pallas kernels: 61.8 us -> 50 us  [the longest x1 35.4 us: backward(): pl.pallas_call(functools.partial(backward_kernel, z), **dict(grid=(z.s, z...]
    ppermute x18, waiting for transfers between devices: 14.3 us -> 8.57 us  [lev_swap(): return lax.ppermute(array, 'lev', [(i, i ^ k) for i in range(z.lev)])]
    ppermute x4, starting transfers between devices: 5.33 us -> 8.86 us  [lon_shift(): lax.ppermute(array, 'lon', [(w, (w + distance) % z.lon) for w in range(z....]
    unnamed x49 -> x67, local copies, waits for them, and re-layouts: 2.05 us -> 4.35 us
    ppermute x4, waiting for transfers between devices: 6.25 us -> 8.35 us  [lon_shift(): lax.ppermute(array, 'lon', [(w, (w + distance) % z.lon) for w in range(z....]
    ppermute x5, waiting for transfers between devices: 5.69 us -> 7.56 us  [lon_swap(): return lax.ppermute(array, 'lon', [(i, i ^ k) for i in range(z.lon)])]
    reshape x2 -> x0, local copies, waits for them, and re-layouts: 1.74 us -> none  [on_device(): jnp.pad(a.reshape(d, 6, d // 2), room).reshape(d, 6 * LANES)]
  transfers between devices with their start and end apart: 27 -> 27, of which waited for: 12 -> 12; matrix products, arithmetic and copies ran while one was open for 6% -> 2% of each run, Pallas kernels for 30% -> 51%
where the time goes in v3:
time: 148 us
  Pallas kernels  77.8 us (53%)
  starting transfers between devices  35.5 us (24%)
  waiting for transfers between devices  24.5 us (17%)
  local copies, waits for them, and re-layouts  6.62 us (4%)
  other arithmetic  2.49 us (2%)
    pallas_call x1, Pallas kernels, backward(): pl.pallas_call(functools.partial(backward_kernel, z), **dict(grid=(z.s, z...  35.4 us
    pallas_call x1, Pallas kernels, forward(): pl.pallas_call(functools.partial(forward_kernel, z), grid=(z.s, z.nb), in...  27.8 us
    ppermute x18, starting transfers between devices, lev_swap(): return lax.ppermute(array, 'lev', [(i, i ^ k) for i in range(z.lev)])  22 us
    ppermute x4, starting transfers between devices, lon_shift(): lax.ppermute(array, 'lon', [(w, (w + distance) % z.lon) for w in range(z....  8.86 us
    ppermute x18, waiting for transfers between devices, lev_swap(): return lax.ppermute(array, 'lev', [(i, i ^ k) for i in range(z.lev)])  8.57 us
    ppermute x4, waiting for transfers between devices, lon_shift(): lax.ppermute(array, 'lon', [(w, (w + distance) % z.lon) for w in range(z....  8.35 us
    ppermute x5, waiting for transfers between devices, lon_swap(): return lax.ppermute(array, 'lon', [(i, i ^ k) for i in range(z.lon)])  7.56 us
    pallas_call x2, Pallas kernels, unpack(): pl.pallas_call(functools.partial(unpack_kernel, z, merged), in_specs=in_s...  6.01 us
  transfers between devices with their start and end apart: 27, of which 12 were waited for; matrix products, arithmetic and copies ran while one was open for 2% of the time, Pallas kernels for 51%

profile of v3, /device:TPU:0, one launch (start us, length us, event | category | flops | bytes accessed | tf_op | source)
XLA Modules:
  0.0 148.0 jit_solution(8995750554232034075)
XLA Ops:
  0.6 0.0 copy-start
  0.7 0.0 copy-start.11
  0.7 2.1 %slice.57 = bf16[2,2,6,48,192]{4,3,2,1,0:T(8,128)(2,1)} slice(bf16[2,2,12,48,192]{4,3,2,1,0:T(8,128)(2,1)} %bitcast.46), slice={[0:2], [0:2], [0:6], [0:48], [0:192]} | slice | bytes 884736 | tf_op jit(solution)/shard_map/slice | solution.py:1042
  2.8 4.5 %collective-permute-start = (bf16[2,2,6,48,192]{4,3,2,1,0:T(8,128)(2,1)}, bf16[2,2,6,48,192]{4,3,2,1,0:T(8,128)(2,1)S(1)}, u32[]{:S(2)}, u32[]{:S(2)}) collective-permute-start(bf16[2,2,6,48,192]{4,3,2,1,0:T(8,128)(2,1)} %slice.57), channel_id=1, source_target_pairs={{0,28},{4,0},{8,4},{12,8},{16,12},{20,16},{24,20},{28,24},{1,29},{... | collective-permute-start | bytes 1327112 | tf_op jit(solution)/shard_map/ppermute | solution.py:1023
  7.3 0.1 dynamic-slice_bitcast_fusion
  7.6 0.0 copy-start.10
  7.6 1.2 bias.1
  8.9 0.7 copy-done.21
  9.6 0.7 copy-done.22
  10.3 0.7 copy-done.26
  10.9 4.1 %collective-permute-done.halo_ref = bf16[2,2,6,48,192]{4,3,2,1,0:T(8,128)(2,1)S(1)} collective-permute-done((bf16[2,2,6,48,192]{4,3,2,1,0:T(8,128)(2,1)}, bf16[2,2,6,48,192]{4,3,2,1,0:T(8,128)(2,1)S(1)}, u32[]{:S(2)}, u32[]{:S(2)}) %collective-permute-start) | collective-permute-done | bytes 442400 | tf_op jit(solution)/shard_map/ppermute | solution.py:1023
  15.0 3.6 %collective-permute-start.1 = (bf16[2,2,6,48,192]{4,3,2,1,0:T(8,128)(2,1)S(1)}, bf16[2,2,6,48,192]{4,3,2,1,0:T(8,128)(2,1)S(1)}, u32[]{:S(2)}, u32[]{:S(2)}) collective-permute-start(bf16[2,2,6,48,192]{4,3,2,1,0:T(8,128)(2,1)S(1)} %slice.56), channel_id=1, source_target_pairs={{0,28},{4,0},{8,4},{12,8},{16,12},{20,16},{24,20},{28,24},{1,29},{... | collective-permute-start | bytes 1327112 | tf_op jit(solution)/shard_map/ppermute | solution.py:1023
  18.6 2.1 %pack.2 = (bf16[2,3,144,128]{3,2,1,0:T(8,128)(2,1)S(1)}, bf16[2,3,144,128]{3,2,1,0:T(8,128)(2,1)S(1)}, bf16[2,3,144,128]{3,2,1,0:T(8,128)(2,1)S(1)}, bf16[2,3,144,128]{3,2,1,0:T(8,128)(2,1)S(1)}) custom-call(s32[2]{0:T(128)S(1)} %copy-done.8, s32[144,1]{1,0:T(8,128)S(1)} %copy-done.10, bf16[2,2,12,48,192]{4,3,2,1,0:T(8,128)(2,1)S(1)} %bitcast.47, ...), custom_call_target="tpu_custom_call" | custom-call | flops 2000000000 | bytes 12000000 | tf_op jit(solution)/shard_map/pack/pallas_call | solution.py:115
  20.8 0.7 copy-done.24
  21.5 1.5 %collective-permute-start.5 = (bf16[2,3,144,128]{3,2,1,0:T(8,128)(2,1)S(1)}, bf16[2,3,144,128]{3,2,1,0:T(8,128)(2,1)S(1)}, u32[]{:S(2)}, u32[]{:S(2)}) collective-permute-start(bf16[2,3,144,128]{3,2,1,0:T(8,128)(2,1)S(1)} %get-tuple-element.90), channel_id=1, source_target_pairs={{0,1},{1,0},{2,3},{3,2},{4,5},{5,4},{6,7},{7,6},{8,9},{9,8},{10,11... | collective-permute-start | bytes 663560 | tf_op jit(solution)/shard_map/ppermute | solution.py:828
  22.9 1.5 %collective-permute-start.6 = (bf16[2,3,144,128]{3,2,1,0:T(8,128)(2,1)S(1)}, bf16[2,3,144,128]{3,2,1,0:T(8,128)(2,1)S(1)}, u32[]{:S(2)}, u32[]{:S(2)}) collective-permute-start(bf16[2,3,144,128]{3,2,1,0:T(8,128)(2,1)S(1)} %get-tuple-element.91), channel_id=1, source_target_pairs={{0,2},{1,3},{2,0},{3,1},{4,6},{5,7},{6,4},{7,5},{8,10},{9,11},{10,... | collective-permute-start | bytes 663560 | tf_op jit(solution)/shard_map/ppermute | solution.py:828
  24.5 0.5 collective-permute-start.7
  24.9 1.1 collective-permute-done.1.halo_ref
  26.0 2.1 %pack.3 = (bf16[2,3,144,128]{3,2,1,0:T(8,128)(2,1)S(1)}, bf16[2,3,144,128]{3,2,1,0:T(8,128)(2,1)S(1)}, bf16[2,3,144,128]{3,2,1,0:T(8,128)(2,1)S(1)}, bf16[2,3,144,128]{3,2,1,0:T(8,128)(2,1)S(1)}) custom-call(s32[2]{0:T(128)S(1)} %copy-done.8, s32[144,1]{1,0:T(8,128)S(1)} %copy-done.10, bf16[2,2,12,48,192]{4,3,2,1,0:T(8,128)(2,1)S(1)} %bitcast.49, ...), custom_call_target="tpu_custom_call" | custom-call | flops 2000000000 | bytes 12000000 | tf_op jit(solution)/shard_map/pack/pallas_call | solution.py:115
  28.1 1.6 %collective-permute-start.2 = (bf16[2,3,144,128]{3,2,1,0:T(8,128)(2,1)S(1)}, bf16[2,3,144,128]{3,2,1,0:T(8,128)(2,1)S(1)}, u32[]{:S(2)}, u32[]{:S(2)}) collective-permute-start(bf16[2,3,144,128]{3,2,1,0:T(8,128)(2,1)S(1)} %get-tuple-element.95), channel_id=1, source_target_pairs={{0,1},{1,0},{2,3},{3,2},{4,5},{5,4},{6,7},{7,6},{8,9},{9,8},{10,11... | collective-permute-start | bytes 663560 | tf_op jit(solution)/shard_map/ppermute | solution.py:828
  29.7 1.5 %collective-permute-start.3 = (bf16[2,3,144,128]{3,2,1,0:T(8,128)(2,1)S(1)}, bf16[2,3,144,128]{3,2,1,0:T(8,128)(2,1)S(1)}, u32[]{:S(2)}, u32[]{:S(2)}) collective-permute-start(bf16[2,3,144,128]{3,2,1,0:T(8,128)(2,1)S(1)} %get-tuple-element.96), channel_id=1, source_target_pairs={{0,2},{1,3},{2,0},{3,1},{4,6},{5,7},{6,4},{7,5},{8,10},{9,11},{10,... | collective-permute-start | bytes 663560 | tf_op jit(solution)/shard_map/ppermute | solution.py:828
  31.2 0.5 collective-permute-start.4
  31.7 2.5 %collective-permute-done.7.refs_3_ = bf16[2,3,144,128]{3,2,1,0:T(8,128)(2,1)S(1)} collective-permute-done((bf16[2,3,144,128]{3,2,1,0:T(8,128)(2,1)S(1)}, bf16[2,3,144,128]{3,2,1,0:T(8,128)(2,1)S(1)}, u32[]{:S(2)}, u32[]{:S(2)}) %collective-permute-start.7) | collective-permute-done | bytes 221216 | tf_op jit(solution)/shard_map/ppermute | solution.py:828
  34.2 0.7 copy-done.32
  34.9 27.8 %forward.1 = (bf16[2,3,144,128]{3,2,1,0:T(8,128)(2,1)}, bf16[2,3,144,128]{3,2,1,0:T(8,128)(2,1)}, bf16[2,3,144,128]{3,2,1,0:T(8,128)(2,1)}, bf16[2,3,144,128]{3,...) custom-call(bf16[2,3,144,128]{3,2,1,0:T(8,128)(2,1)} %copy-done.24, ...), custom_call_target="tpu_custom_call" | custom-call | flops 15000000512 | bytes 90000000 | tf_op jit(solution)/shard_map/forward/pallas_call | solution.py:503
  62.7 1.4 collective-permute-start.8
  64.1 0.6 collective-permute-start.9
  64.7 1.5 %collective-permute-start.10 = (bf16[2,3,144,128]{3,2,1,0:T(8,128)(2,1)}, bf16[2,3,144,128]{3,2,1,0:T(8,128)(2,1)S(1)}, u32[]{:S(2)}, u32[]{:S(2)}) collective-permute-start(bf16[2,3,144,128]{3,2,1,0:T(8,128)(2,1)} %get-tuple-element.122), channel_id=1, source_target_pairs={{0,3},{1,2},{2,1},{3,0},{4,7},{5,6},{6,5},{7,4},{8,11},{9,10},{10,... | collective-permute-start | bytes 663560 | tf_op jit(solution)/shard_map/ppermute | solution.py:828
  66.3 0.7 copy-done.28
  66.9 0.1 copy-done.29
  67.0 35.4 %backward.1 = (bf16[2,3,144,128]{3,2,1,0:T(8,128)(2,1)}, bf16[2,3,144,128]{3,2,1,0:T(8,128)(2,1)}, bf16[2,3,144,128]{3,2,1,0:T(8,128)(2,1)}, bf16[2,3,144,128]{3...) custom-call(bf16[2,3,144,128]{3,2,1,0:T(8,128)(2,1)} %copy-done.23, ...), custom_call_target="tpu_custom_call" | custom-call | flops 20000000000 | bytes 120000000 | tf_op jit(solution)/shard_map/backward/pallas_call | solution.py:780
  102.5 0.1 collective-permute-start.16
  102.6 0.5 collective-permute-start.12
  103.2 0.1 pad_maximum_fusion.1
  103.2 0.3 collective-permute-start.11
  103.5 1.4 collective-permute-done.16
  104.9 1.2 fusion.3
  106.1 1.4 collective-permute-start.17
  107.5 0.6 collective-permute-start.19
  108.2 1.5 %collective-permute-start.18 = (bf16[656,128]{1,0:T(8,128)(2,1)S(1)}, bf16[656,128]{1,0:T(8,128)(2,1)S(1)}, u32[]{:S(2)}, u32[]{:S(2)}) collective-permute-start(bf16[656,128]{1,0:T(8,128)(2,1)S(1)} %get-tuple-element.159), channel_id=1, source_target_pairs={{0,2},{1,3},{2,0},{3,1},{4,6},{5,7},{6,4},{7,5},{8,10},{9,11},{10,... | collective-permute-start | bytes 503816 | tf_op jit(solution)/shard_map/ppermute | solution.py:828
  109.7 3.2 %collective-permute-done.12.refs_4_ = bf16[4,2,3,80,128]{4,3,2,1,0:T(8,128)(2,1)S(1)} collective-permute-done((bf16[4,2,3,80,128]{4,3,2,1,0:T(8,128)(2,1)}, bf16[4,2,3,80,128]{4,3,2,1,0:T(8,128)(2,1)S(1)}, u32[]{:S(2)}, u32[]{:S(2)}) %collective-permute-start.12) | collective-permute-done | bytes 491552 | tf_op jit(solution)/shard_map/ppermute | solution.py:1023
  112.9 0.7 merge.1
  113.6 1.4 collective-permute-start.13
  115.0 0.6 collective-permute-start.14
  115.6 1.3 collective-permute-done.19
  116.9 1.9 %collective-permute-done.18 = bf16[656,128]{1,0:T(8,128)(2,1)S(1)} collective-permute-done((bf16[656,128]{1,0:T(8,128)(2,1)S(1)}, bf16[656,128]{1,0:T(8,128)(2,1)S(1)}, u32[]{:S(2)}, u32[]{:S(2)}) %collective-permute-start.18) | collective-permute-done | bytes 167968 | tf_op jit(solution)/shard_map/ppermute | solution.py:828
  118.8 1.0 fusion.1
  119.9 2.3 %collective-permute-start.22 = (bf16[656,128]{1,0:T(8,128)(2,1)S(1)}, bf16[656,128]{1,0:T(8,128)(2,1)S(1)}, u32[]{:S(2)}, u32[]{:S(2)}) collective-permute-start(bf16[656,128]{1,0:T(8,128)(2,1)S(1)} %fusion.1), channel_id=1, source_target_pairs={{0,24},{4,28},{8,16},{12,20},{16,8},{20,12},{24,0},{28,4},{1,25},{... | collective-permute-start | bytes 503816 | tf_op jit(solution)/shard_map/ppermute | solution.py:832
  122.2 2.2 %collective-permute-start.20 = (bf16[656,128]{1,0:T(8,128)(2,1)S(1)}, bf16[656,128]{1,0:T(8,128)(2,1)S(1)}, u32[]{:S(2)}, u32[]{:S(2)}) collective-permute-start(bf16[656,128]{1,0:T(8,128)(2,1)S(1)} %fusion.1), channel_id=1, source_target_pairs={{0,8},{4,12},{8,0},{12,4},{16,24},{20,28},{24,16},{28,20},{1,9},{5... | collective-permute-start | bytes 503816 | tf_op jit(solution)/shard_map/ppermute | solution.py:832
  124.3 3.2 %unpack.2 = bf16[2,2,12,48,192]{4,3,2,1,0:T(8,128)(2,1)} custom-call(s32[2]{0:T(128)S(1)} %copy-done.9, s32[1,144]{1,0:T(1,128)S(1)} %copy-done.14, s32[1,80]{1,0:T(1,128)S(1)} %copy-done.15, bf16[2,3,144,128]{3,2,1,0:T(8,128)(2,1)S(1)} %copy-done.3, bf16[2,3,144,128]{3,2,1,0:T(8,128)(2,1)S(1)} %collective-permute-done.8.rest_3_, ...), custom_call_target="tpu_custom_call" | custom-call | flops 2000000000 | bytes 12000000 | tf_op jit(solution)/shard_map/unpack/pallas_call | solution.py:162
  127.5 0.8 collective-permute-done.22
  128.3 2.3 %collective-permute-start.15 = (bf16[2,3,144,128]{3,2,1,0:T(8,128)(2,1)S(1)}, bf16[2,3,144,128]{3,2,1,0:T(8,128)(2,1)S(1)}, u32[]{:S(2)}, u32[]{:S(2)}) collective-permute-start(bf16[2,3,144,128]{3,2,1,0:T(8,128)(2,1)S(1)} %get-tuple-element.135), channel_id=1, source_target_pairs={{0,3},{1,2},{2,1},{3,0},{4,7},{5,6},{6,5},{7,4},{8,11},{9,10},{10,... | collective-permute-start | bytes 663560 | tf_op jit(solution)/shard_map/ppermute | solution.py:828
  130.6 3.3 %collective-permute-done.21 = bf16[656,128]{1,0:T(8,128)(2,1)S(1)} collective-permute-done((bf16[656,128]{1,0:T(8,128)(2,1)S(1)}, bf16[656,128]{1,0:T(8,128)(2,1)S(1)}, u32[]{:S(2)}, u32[]{:S(2)}) %collective-permute-start.21) | collective-permute-done | bytes 167968 | tf_op jit(solution)/shard_map/ppermute | solution.py:832
  133.9 0.1 add_convert_fusion
  134.0 2.0 %collective-permute-start.25 = (bf16[656,128]{1,0:T(8,128)(2,1)S(1)}, bf16[656,128]{1,0:T(8,128)(2,1)S(1)}, u32[]{:S(2)}, u32[]{:S(2)}) collective-permute-start(bf16[656,128]{1,0:T(8,128)(2,1)S(1)} %add_convert_fusion), channel_id=1, source_target_pairs={{0,3},{1,2},{2,1},{3,0},{4,7},{5,6},{6,5},{7,4},{8,11},{9,10},{10,... | collective-permute-start | bytes 503816 | tf_op jit(solution)/shard_map/ppermute | solution.py:828
  136.0 0.6 collective-permute-start.24
  136.6 1.0 collective-permute-start.23
  137.6 2.8 %unpack.3 = bf16[2,2,12,48,192]{4,3,2,1,0:T(8,128)(2,1)} custom-call(s32[2]{0:T(128)S(1)} %copy-done.9, s32[1,144]{1,0:T(1,128)S(1)} %copy-done.14, bf16[2,3,144,128]{3,2,1,0:T(8,128)(2,1)S(1)} %get-tuple-element.132.rest_1_, bf16[2,3,144,128]{3,2,1,0:T(8,128)(2,1)S(1)} %collective-permute-done.13.rest_2_, ...), custom_call_target="tpu_custom_call" | custom-call | flops 2000000000 | bytes 12000000 | tf_op jit(solution)/shard_map/unpack/pallas_call | solution.py:162
  140.4 1.1 collective-permute-done.25
  141.5 1.7 %collective-permute-done.24 = bf16[656,128]{1,0:T(8,128)(2,1)S(1)} collective-permute-done((bf16[656,128]{1,0:T(8,128)(2,1)S(1)}, bf16[656,128]{1,0:T(8,128)(2,1)S(1)}, u32[]{:S(2)}, u32[]{:S(2)}) %collective-permute-start.24) | collective-permute-done | bytes 167968 | tf_op jit(solution)/shard_map/ppermute | solution.py:828
  143.3 0.1 pad_maximum_fusion.own
  143.4 0.1 collective-permute-start.26
  143.5 2.1 %collective-permute-done.26.other = bf16[4,656,128]{2,1,0:T(8,128)(2,1)S(1)} collective-permute-done((bf16[4,656,128]{2,1,0:T(8,128)(2,1)S(1)}, bf16[4,656,128]{2,1,0:T(8,128)(2,1)S(1)}, u32[]{:S(2)}, u32[]{:S(2)}) %collective-permute-start.26) | collective-permute-done | bytes 671776 | tf_op jit(solution)/shard_map/ppermute | solution.py:832
  145.6 2.5 %finish.1 = (f32[192,768]{1,0:T(8,128)}, f32[192,768]{1,0:T(8,128)}, f32[192,576]{1,0:T(8,128)}, f32[192,576]{1,0:T(8,128)}, f32[192,192]{1,0:T(8,128)}, /*index...) custom-call(s32[6,192]{1,0:T(8,128)S(1)} %copy-done.13, ...), custom_call_target="tpu_custom_call" | custom-call | flops 2000000000 | bytes 12000000 | tf_op jit(solution)/shard_map/finish/pallas_call | solution.py:938
  (79 shorter events, 0.3 us)
Async XLA Ops:
  0.6 6.6 %copy-start = (f32[8,6,6,6,23]{4,0,3,2,1:T(8,128)S(1)}, f32[8,6,6,6,23]{4,0,3,2,1:T(8,128)}, u32[]{:S(2)}) copy-start(f32[8,6,6,6,23]{4,0,3,2,1:T(8,128)} %param.35) | copy-start | bytes 476932
  0.7 6.9 %copy-start.11 = (f32[96,72]{1,0:T(8,128)S(1)}, f32[96,72]{1,0:T(8,128)}, u32[]{:S(2)}) copy-start(f32[96,72]{1,0:T(8,128)} %constant.24.clone.pick_ref.refs_13_) | copy-start | bytes 82948
  0.7 6.7 %copy-start.2 = (bf16[2,2,48,12,192]{4,2,3,1,0:T(8,128)(2,1)S(1)}, bf16[2,2,48,12,192]{4,2,3,1,0:T(8,128)(2,1)}, u32[]{:S(2)}) copy-start(bf16[2,2,48,12,192]{4,2,3,1,0:T(8,128)(2,1)} %param.28) | copy-start | bytes 2654212
  0.7 6.8 %copy-start.7 = (bf16[192,192]{1,0:T(8,128)(2,1)S(1)}, bf16[192,192]{1,0:T(8,128)(2,1)}, u32[]{:S(2)}) copy-start(bf16[192,192]{1,0:T(8,128)(2,1)} %out2.1) | copy-start | bytes 221188
  0.7 6.8 %copy-start.5 = (bf16[192,576]{1,0:T(8,128)(2,1)S(1)}, bf16[192,576]{1,0:T(8,128)(2,1)}, u32[]{:S(2)}) copy-start(bf16[192,576]{1,0:T(8,128)(2,1)} %qkv2.1) | copy-start | bytes 663556
  0.7 6.8 %copy-start.6 = (bf16[192,192]{1,0:T(8,128)(2,1)S(1)}, bf16[192,192]{1,0:T(8,128)(2,1)}, u32[]{:S(2)}) copy-start(bf16[192,192]{1,0:T(8,128)(2,1)} %out1.1) | copy-start | bytes 221188
  0.7 6.8 %copy-start.4 = (bf16[192,576]{1,0:T(8,128)(2,1)S(1)}, bf16[192,576]{1,0:T(8,128)(2,1)}, u32[]{:S(2)}) copy-start(bf16[192,576]{1,0:T(8,128)(2,1)} %qkv1.1) | copy-start | bytes 663556
  2.8 12.2 %collective-permute-start = (bf16[2,2,6,48,192]{4,3,2,1,0:T(8,128)(2,1)}, bf16[2,2,6,48,192]{4,3,2,1,0:T(8,128)(2,1)S(1)}, u32[]{:S(2)}, u32[]{:S(2)}) collective-permute-start(bf16[2,2,6,48,192]{4,3,2,1,0:T(8,128)(2,1)} %slice.57), channel_id=1, source_target_pairs={{0,28},{4,0},{8,4},{12,8},{16,12},{20,16},{24,20},{28,24},{1,29},{... | collective-permute-start | bytes 1327112 | tf_op jit(solution)/shard_map/ppermute | solution.py:1023
  7.6 11.0 %copy-start.1 = (bf16[2,2,48,12,192]{4,2,3,1,0:T(8,128)(2,1)S(1)}, bf16[2,2,48,12,192]{4,2,3,1,0:T(8,128)(2,1)}, u32[]{:S(2)}) copy-start(bf16[2,2,48,12,192]{4,2,3,1,0:T(8,128)(2,1)} %param.27) | copy-start | bytes 2654212
  7.6 11.0 %copy-start.8 = (s32[2]{0:T(128)S(1)}, s32[2]{0:T(128)}, u32[]{:S(2)}) copy-start(s32[2]{0:T(128)} %offsets.9) | copy-start | bytes 28
  7.6 11.0 %copy-start.10 = (s32[144,1]{1,0:T(8,128)S(1)}, s32[144,1]{1,0:T(8,128)}, u32[]{:S(2)}) copy-start(s32[144,1]{1,0:T(8,128)} %constant.36.base) | copy-start | bytes 1732
  8.8 0.7 copy-start.21
  9.6 0.7 copy-start.22
  10.3 0.7 copy-start.26
  10.9 9.8 %copy-start.20 = (bf16[192,768]{1,0:T(8,128)(2,1)}, bf16[192,768]{1,0:T(8,128)(2,1)S(1)}, u32[]{:S(2)}) copy-start(bf16[192,768]{1,0:T(8,128)(2,1)S(1)} %get-tuple-element.99.refs_14_.refs_20_) | copy-start | bytes 884740
  10.9 9.8 %copy-start.25 = (bf16[256,192]{1,0:T(8,128)(2,1)}, bf16[256,192]{1,0:T(8,128)(2,1)S(1)}, u32[]{:S(2)}) copy-start(bf16[256,192]{1,0:T(8,128)(2,1)S(1)} %get-tuple-element.100.refs_15_.refs_21_) | copy-start | bytes 294916
  15.0 11.0 %collective-permute-start.1 = (bf16[2,2,6,48,192]{4,3,2,1,0:T(8,128)(2,1)S(1)}, bf16[2,2,6,48,192]{4,3,2,1,0:T(8,128)(2,1)S(1)}, u32[]{:S(2)}, u32[]{:S(2)}) collective-permute-start(bf16[2,2,6,48,192]{4,3,2,1,0:T(8,128)(2,1)S(1)} %slice.56), channel_id=1, source_target_pairs={{0,28},{4,0},{8,4},{12,8},{16,12},{20,16},{24,20},{28,24},{1,29},{... | collective-permute-start | bytes 1327112 | tf_op jit(solution)/shard_map/ppermute | solution.py:1023
  20.8 0.7 copy-start.24
  21.5 9.8 %collective-permute-start.5 = (bf16[2,3,144,128]{3,2,1,0:T(8,128)(2,1)S(1)}, bf16[2,3,144,128]{3,2,1,0:T(8,128)(2,1)S(1)}, u32[]{:S(2)}, u32[]{:S(2)}) collective-permute-start(bf16[2,3,144,128]{3,2,1,0:T(8,128)(2,1)S(1)} %get-tuple-element.90), channel_id=1, source_target_pairs={{0,1},{1,0},{2,3},{3,2},{4,5},{5,4},{6,7},{7,6},{8,9},{9,8},{10,11... | collective-permute-start | bytes 663560 | tf_op jit(solution)/shard_map/ppermute | solution.py:828
  22.9 8.8 %collective-permute-start.6 = (bf16[2,3,144,128]{3,2,1,0:T(8,128)(2,1)S(1)}, bf16[2,3,144,128]{3,2,1,0:T(8,128)(2,1)S(1)}, u32[]{:S(2)}, u32[]{:S(2)}) collective-permute-start(bf16[2,3,144,128]{3,2,1,0:T(8,128)(2,1)S(1)} %get-tuple-element.91), channel_id=1, source_target_pairs={{0,2},{1,3},{2,0},{3,1},{4,6},{5,7},{6,4},{7,5},{8,10},{9,11},{10,... | collective-permute-start | bytes 663560 | tf_op jit(solution)/shard_map/ppermute | solution.py:828
  24.5 9.7 %collective-permute-start.7 = (bf16[2,3,144,128]{3,2,1,0:T(8,128)(2,1)S(1)}, bf16[2,3,144,128]{3,2,1,0:T(8,128)(2,1)S(1)}, u32[]{:S(2)}, u32[]{:S(2)}) collective-permute-start(bf16[2,3,144,128]{3,2,1,0:T(8,128)(2,1)S(1)} %get-tuple-element.92), channel_id=1, source_target_pairs={{0,3},{1,2},{2,1},{3,0},{4,7},{5,6},{6,5},{7,4},{8,11},{9,10},{10,... | collective-permute-start | bytes 663560 | tf_op jit(solution)/shard_map/ppermute | solution.py:828
  28.1 34.5 %copy-start.23 = (bf16[2,3,144,128]{3,2,1,0:T(8,128)(2,1)}, bf16[2,3,144,128]{3,2,1,0:T(8,128)(2,1)S(1)}, u32[]{:S(2)}) copy-start(bf16[2,3,144,128]{3,2,1,0:T(8,128)(2,1)S(1)} %get-tuple-element.94.refs_0_) | copy-start | bytes 663556
  28.1 36.6 %collective-permute-start.2 = (bf16[2,3,144,128]{3,2,1,0:T(8,128)(2,1)S(1)}, bf16[2,3,144,128]{3,2,1,0:T(8,128)(2,1)S(1)}, u32[]{:S(2)}, u32[]{:S(2)}) collective-permute-start(bf16[2,3,144,128]{3,2,1,0:T(8,128)(2,1)S(1)} %get-tuple-element.95), channel_id=1, source_target_pairs={{0,1},{1,0},{2,3},{3,2},{4,5},{5,4},{6,7},{7,6},{8,9},{9,8},{10,11... | collective-permute-start | bytes 663560 | tf_op jit(solution)/shard_map/ppermute | solution.py:828
  29.7 36.5 %collective-permute-start.3 = (bf16[2,3,144,128]{3,2,1,0:T(8,128)(2,1)S(1)}, bf16[2,3,144,128]{3,2,1,0:T(8,128)(2,1)S(1)}, u32[]{:S(2)}, u32[]{:S(2)}) collective-permute-start(bf16[2,3,144,128]{3,2,1,0:T(8,128)(2,1)S(1)} %get-tuple-element.96), channel_id=1, source_target_pairs={{0,2},{1,3},{2,0},{3,1},{4,6},{5,7},{6,4},{7,5},{8,10},{9,11},{10,... | collective-permute-start | bytes 663560 | tf_op jit(solution)/shard_map/ppermute | solution.py:828
  31.2 3.7 %copy-start.30 = (bf16[2,3,144,128]{3,2,1,0:T(8,128)(2,1)}, bf16[2,3,144,128]{3,2,1,0:T(8,128)(2,1)S(1)}, u32[]{:S(2)}) copy-start(bf16[2,3,144,128]{3,2,1,0:T(8,128)(2,1)S(1)} %collective-permute-done.5.refs_1_) | copy-start | bytes 663556
  31.2 35.0 %collective-permute-start.4 = (bf16[2,3,144,128]{3,2,1,0:T(8,128)(2,1)S(1)}, bf16[2,3,144,128]{3,2,1,0:T(8,128)(2,1)S(1)}, u32[]{:S(2)}, u32[]{:S(2)}) collective-permute-start(bf16[2,3,144,128]{3,2,1,0:T(8,128)(2,1)S(1)} %get-tuple-element.97), channel_id=1, source_target_pairs={{0,3},{1,2},{2,1},{3,0},{4,7},{5,6},{6,5},{7,4},{8,11},{9,10},{10,... | collective-permute-start | bytes 663560 | tf_op jit(solution)/shard_map/ppermute | solution.py:828
  31.7 2.5 %copy-start.31 = (bf16[2,3,144,128]{3,2,1,0:T(8,128)(2,1)}, bf16[2,3,144,128]{3,2,1,0:T(8,128)(2,1)S(1)}, u32[]{:S(2)}) copy-start(bf16[2,3,144,128]{3,2,1,0:T(8,128)(2,1)S(1)} %collective-permute-done.6.refs_2_) | copy-start | bytes 663556
  34.2 0.7 copy-start.32
  62.7 39.8 %collective-permute-start.8 = (bf16[2,3,144,128]{3,2,1,0:T(8,128)(2,1)}, bf16[2,3,144,128]{3,2,1,0:T(8,128)(2,1)S(1)}, u32[]{:S(2)}, u32[]{:S(2)}) collective-permute-start(bf16[2,3,144,128]{3,2,1,0:T(8,128)(2,1)} %get-tuple-element.120), channel_id=1, source_target_pairs={{0,1},{1,0},{2,3},{3,2},{4,5},{5,4},{6,7},{7,6},{8,9},{9,8},{10,11... | collective-permute-start | bytes 663560 | tf_op jit(solution)/shard_map/ppermute | solution.py:828
  64.1 38.4 %collective-permute-start.9 = (bf16[2,3,144,128]{3,2,1,0:T(8,128)(2,1)}, bf16[2,3,144,128]{3,2,1,0:T(8,128)(2,1)S(1)}, u32[]{:S(2)}, u32[]{:S(2)}) collective-permute-start(bf16[2,3,144,128]{3,2,1,0:T(8,128)(2,1)} %get-tuple-element.121), channel_id=1, source_target_pairs={{0,2},{1,3},{2,0},{3,1},{4,6},{5,7},{6,4},{7,5},{8,10},{9,11},{10,... | collective-permute-start | bytes 663560 | tf_op jit(solution)/shard_map/ppermute | solution.py:828
  64.7 2.3 %copy-start.27 = (bf16[2,3,144,128]{3,2,1,0:T(8,128)(2,1)}, bf16[2,3,144,128]{3,2,1,0:T(8,128)(2,1)S(1)}, u32[]{:S(2)}) copy-start(bf16[2,3,144,128]{3,2,1,0:T(8,128)(2,1)S(1)} %collective-permute-done.2.refs_1_) | copy-start | bytes 663556
  64.7 37.8 %collective-permute-start.10 = (bf16[2,3,144,128]{3,2,1,0:T(8,128)(2,1)}, bf16[2,3,144,128]{3,2,1,0:T(8,128)(2,1)S(1)}, u32[]{:S(2)}, u32[]{:S(2)}) collective-permute-start(bf16[2,3,144,128]{3,2,1,0:T(8,128)(2,1)} %get-tuple-element.122), channel_id=1, source_target_pairs={{0,3},{1,2},{2,1},{3,0},{4,7},{5,6},{6,5},{7,4},{8,11},{9,10},{10,... | collective-permute-start | bytes 663560 | tf_op jit(solution)/shard_map/ppermute | solution.py:828
  66.2 0.7 copy-start.28
  66.3 0.7 copy-start.29
  67.0 36.1 %copy-start.3 = (bf16[2,3,144,128]{3,2,1,0:T(8,128)(2,1)S(1)}, bf16[2,3,144,128]{3,2,1,0:T(8,128)(2,1)}, u32[]{:S(2)}) copy-start(bf16[2,3,144,128]{3,2,1,0:T(8,128)(2,1)} %get-tuple-element.123.rest_2_) | copy-start | bytes 663556
  102.4 10.5 %copy-start.9 = (s32[2]{0:T(128)S(1)}, s32[2]{0:T(128)}, u32[]{:S(2)}) copy-start(s32[2]{0:T(128)} %offsets.9) | copy-start | bytes 28
  102.4 10.5 %copy-start.16 = (bf16[2,3,144,128]{3,2,1,0:T(8,128)(2,1)S(1)}, bf16[2,3,144,128]{3,2,1,0:T(8,128)(2,1)}, u32[]{:S(2)}) copy-start(bf16[2,3,144,128]{3,2,1,0:T(8,128)(2,1)} %get-tuple-element.127.refs_0_) | copy-start | bytes 663556
  102.4 10.5 %copy-start.17 = (bf16[2,3,144,128]{3,2,1,0:T(8,128)(2,1)S(1)}, bf16[2,3,144,128]{3,2,1,0:T(8,128)(2,1)}, u32[]{:S(2)}) copy-start(bf16[2,3,144,128]{3,2,1,0:T(8,128)(2,1)} %get-tuple-element.128.refs_1_) | copy-start | bytes 663556
  102.5 10.5 %copy-start.18 = (bf16[2,3,144,128]{3,2,1,0:T(8,128)(2,1)S(1)}, bf16[2,3,144,128]{3,2,1,0:T(8,128)(2,1)}, u32[]{:S(2)}) copy-start(bf16[2,3,144,128]{3,2,1,0:T(8,128)(2,1)} %get-tuple-element.129.refs_2_) | copy-start | bytes 663556
  102.5 10.5 %copy-start.19 = (bf16[2,3,144,128]{3,2,1,0:T(8,128)(2,1)S(1)}, bf16[2,3,144,128]{3,2,1,0:T(8,128)(2,1)}, u32[]{:S(2)}) copy-start(bf16[2,3,144,128]{3,2,1,0:T(8,128)(2,1)} %get-tuple-element.130.refs_3_) | copy-start | bytes 663556
  102.5 2.4 %collective-permute-start.16 = (bf16[4,656,128]{2,1,0:T(8,128)(2,1)}, bf16[4,656,128]{2,1,0:T(8,128)(2,1)S(1)}, u32[]{:S(2)}, u32[]{:S(2)}) collective-permute-start(bf16[4,656,128]{2,1,0:T(8,128)(2,1)} %get-tuple-element.137), channel_id=1, source_target_pairs={{0,4},{4,0},{8,12},{12,8},{16,20},{20,16},{24,28},{28,24},{1,5},{5... | collective-permute-start | bytes 2015240 | tf_op jit(solution)/shard_map/ppermute | solution.py:832
  102.6 10.3 %collective-permute-start.12 = (bf16[4,2,3,80,128]{4,3,2,1,0:T(8,128)(2,1)}, bf16[4,2,3,80,128]{4,3,2,1,0:T(8,128)(2,1)S(1)}, u32[]{:S(2)}, u32[]{:S(2)}) collective-permute-start(bf16[4,2,3,80,128]{4,3,2,1,0:T(8,128)(2,1)} %get-tuple-element.131), channel_id=1, source_target_pairs={{0,4},{4,8},{8,12},{12,16},{16,20},{20,24},{24,28},{28,0},{1,5},{5... | collective-permute-start | bytes 1474568 | tf_op jit(solution)/shard_map/ppermute | solution.py:1023
  103.2 16.6 %collective-permute-start.11 = (bf16[4,2,3,80,128]{4,3,2,1,0:T(8,128)(2,1)S(1)}, bf16[4,2,3,80,128]{4,3,2,1,0:T(8,128)(2,1)S(1)}, u32[]{:S(2)}, u32[]{:S(2)}) collective-permute-start(bf16[4,2,3,80,128]{4,3,2,1,0:T(8,128)(2,1)S(1)} %pad_maximum_fusion.1), channel_id=1, source_target_pairs={{0,4},{4,8},{8,12},{12,16},{16,20},{20,24},{24,28},{28,0},{1,5},{5... | collective-permute-start | bytes 1474568 | tf_op jit(solution)/shard_map/ppermute | solution.py:1023
  106.1 8.9 %collective-permute-start.17 = (bf16[656,128]{1,0:T(8,128)(2,1)S(1)}, bf16[656,128]{1,0:T(8,128)(2,1)S(1)}, u32[]{:S(2)}, u32[]{:S(2)}) collective-permute-start(bf16[656,128]{1,0:T(8,128)(2,1)S(1)} %get-tuple-element.157), channel_id=1, source_target_pairs={{0,1},{1,0},{2,3},{3,2},{4,5},{5,4},{6,7},{7,6},{8,9},{9,8},{10,11... | collective-permute-start | bytes 503816 | tf_op jit(solution)/shard_map/ppermute | solution.py:828
  107.5 9.4 %collective-permute-start.19 = (bf16[656,128]{1,0:T(8,128)(2,1)S(1)}, bf16[656,128]{1,0:T(8,128)(2,1)S(1)}, u32[]{:S(2)}, u32[]{:S(2)}) collective-permute-start(bf16[656,128]{1,0:T(8,128)(2,1)S(1)} %get-tuple-element.158), channel_id=1, source_target_pairs={{0,3},{1,2},{2,1},{3,0},{4,7},{5,6},{6,5},{7,4},{8,11},{9,10},{10,... | collective-permute-start | bytes 503816 | tf_op jit(solution)/shard_map/ppermute | solution.py:828
  108.2 16.2 %copy-start.14 = (s32[1,144]{1,0:T(1,128)S(1)}, s32[1,144]{1,0:T(1,128)}, u32[]{:S(2)}) copy-start(s32[1,144]{1,0:T(1,128)} %constant.34.rest_0_) | copy-start | bytes 1732
  108.2 16.2 %copy-start.15 = (s32[1,80]{1,0:T(1,128)S(1)}, s32[1,80]{1,0:T(1,128)}, u32[]{:S(2)}) copy-start(s32[1,80]{1,0:T(1,128)} %constant.35.rest_1_) | copy-start | bytes 964
  108.2 10.7 %collective-permute-start.18 = (bf16[656,128]{1,0:T(8,128)(2,1)S(1)}, bf16[656,128]{1,0:T(8,128)(2,1)S(1)}, u32[]{:S(2)}, u32[]{:S(2)}) collective-permute-start(bf16[656,128]{1,0:T(8,128)(2,1)S(1)} %get-tuple-element.159), channel_id=1, source_target_pairs={{0,2},{1,3},{2,0},{3,1},{4,6},{5,7},{6,4},{7,5},{8,10},{9,11},{10,... | collective-permute-start | bytes 503816 | tf_op jit(solution)/shard_map/ppermute | solution.py:828
  113.6 23.0 %collective-permute-start.13 = (bf16[2,3,144,128]{3,2,1,0:T(8,128)(2,1)S(1)}, bf16[2,3,144,128]{3,2,1,0:T(8,128)(2,1)S(1)}, u32[]{:S(2)}, u32[]{:S(2)}) collective-permute-start(bf16[2,3,144,128]{3,2,1,0:T(8,128)(2,1)S(1)} %get-tuple-element.133), channel_id=1, source_target_pairs={{0,1},{1,0},{2,3},{3,2},{4,5},{5,4},{6,7},{7,6},{8,9},{9,8},{10,11... | collective-permute-start | bytes 663560 | tf_op jit(solution)/shard_map/ppermute | solution.py:828
  115.0 22.5 %collective-permute-start.14 = (bf16[2,3,144,128]{3,2,1,0:T(8,128)(2,1)S(1)}, bf16[2,3,144,128]{3,2,1,0:T(8,128)(2,1)S(1)}, u32[]{:S(2)}, u32[]{:S(2)}) collective-permute-start(bf16[2,3,144,128]{3,2,1,0:T(8,128)(2,1)S(1)} %get-tuple-element.134), channel_id=1, source_target_pairs={{0,2},{1,3},{2,0},{3,1},{4,6},{5,7},{6,4},{7,5},{8,10},{9,11},{10,... | collective-permute-start | bytes 663560 | tf_op jit(solution)/shard_map/ppermute | solution.py:828
  119.9 8.4 %collective-permute-start.22 = (bf16[656,128]{1,0:T(8,128)(2,1)S(1)}, bf16[656,128]{1,0:T(8,128)(2,1)S(1)}, u32[]{:S(2)}, u32[]{:S(2)}) collective-permute-start(bf16[656,128]{1,0:T(8,128)(2,1)S(1)} %fusion.1), channel_id=1, source_target_pairs={{0,24},{4,28},{8,16},{12,20},{16,8},{20,12},{24,0},{28,4},{1,25},{... | collective-permute-start | bytes 503816 | tf_op jit(solution)/shard_map/ppermute | solution.py:832
  122.2 11.7 %collective-permute-start.21 = (bf16[656,128]{1,0:T(8,128)(2,1)S(1)}, bf16[656,128]{1,0:T(8,128)(2,1)S(1)}, u32[]{:S(2)}, u32[]{:S(2)}) collective-permute-start(bf16[656,128]{1,0:T(8,128)(2,1)S(1)} %fusion.1), channel_id=1, source_target_pairs={{0,16},{4,20},{8,24},{12,28},{16,0},{20,4},{24,8},{28,12},{1,17},{... | collective-permute-start | bytes 503816 | tf_op jit(solution)/shard_map/ppermute | solution.py:832
  122.2 11.7 %collective-permute-start.20 = (bf16[656,128]{1,0:T(8,128)(2,1)S(1)}, bf16[656,128]{1,0:T(8,128)(2,1)S(1)}, u32[]{:S(2)}, u32[]{:S(2)}) collective-permute-start(bf16[656,128]{1,0:T(8,128)(2,1)S(1)} %fusion.1), channel_id=1, source_target_pairs={{0,8},{4,12},{8,0},{12,4},{16,24},{20,28},{24,16},{28,20},{1,9},{5... | collective-permute-start | bytes 503816 | tf_op jit(solution)/shard_map/ppermute | solution.py:832
  128.3 9.2 %collective-permute-start.15 = (bf16[2,3,144,128]{3,2,1,0:T(8,128)(2,1)S(1)}, bf16[2,3,144,128]{3,2,1,0:T(8,128)(2,1)S(1)}, u32[]{:S(2)}, u32[]{:S(2)}) collective-permute-start(bf16[2,3,144,128]{3,2,1,0:T(8,128)(2,1)S(1)} %get-tuple-element.135), channel_id=1, source_target_pairs={{0,3},{1,2},{2,1},{3,0},{4,7},{5,6},{6,5},{7,4},{8,11},{9,10},{10,... | collective-permute-start | bytes 663560 | tf_op jit(solution)/shard_map/ppermute | solution.py:828
  134.0 7.6 %collective-permute-start.25 = (bf16[656,128]{1,0:T(8,128)(2,1)S(1)}, bf16[656,128]{1,0:T(8,128)(2,1)S(1)}, u32[]{:S(2)}, u32[]{:S(2)}) collective-permute-start(bf16[656,128]{1,0:T(8,128)(2,1)S(1)} %add_convert_fusion), channel_id=1, source_target_pairs={{0,3},{1,2},{2,1},{3,0},{4,7},{5,6},{6,5},{7,4},{8,11},{9,10},{10,... | collective-permute-start | bytes 503816 | tf_op jit(solution)/shard_map/ppermute | solution.py:828
  136.0 7.3 %collective-permute-start.24 = (bf16[656,128]{1,0:T(8,128)(2,1)S(1)}, bf16[656,128]{1,0:T(8,128)(2,1)S(1)}, u32[]{:S(2)}, u32[]{:S(2)}) collective-permute-start(bf16[656,128]{1,0:T(8,128)(2,1)S(1)} %add_convert_fusion), channel_id=1, source_target_pairs={{0,2},{1,3},{2,0},{3,1},{4,6},{5,7},{6,4},{7,5},{8,10},{9,11},{10,... | collective-permute-start | bytes 503816 | tf_op jit(solution)/shard_map/ppermute | solution.py:828
  136.6 6.7 %collective-permute-start.23 = (bf16[656,128]{1,0:T(8,128)(2,1)S(1)}, bf16[656,128]{1,0:T(8,128)(2,1)S(1)}, u32[]{:S(2)}, u32[]{:S(2)}) collective-permute-start(bf16[656,128]{1,0:T(8,128)(2,1)S(1)} %add_convert_fusion), channel_id=1, source_target_pairs={{0,1},{1,0},{2,3},{3,2},{4,5},{5,4},{6,7},{7,6},{8,9},{9,8},{10,11... | collective-permute-start | bytes 503816 | tf_op jit(solution)/shard_map/ppermute | solution.py:828
  137.6 8.0 %copy-start.12 = (bf16[128,128]{1,0:T(8,128)(2,1)S(1)}, bf16[128,128]{1,0:T(8,128)(2,1)}, u32[]{:S(2)}) copy-start(bf16[128,128]{1,0:T(8,128)(2,1)} %constant.29.clone.order) | copy-start | bytes 98308
  137.6 8.0 %copy-start.13 = (s32[6,192]{1,0:T(8,128)S(1)}, s32[6,192]{1,0:T(8,128)}, u32[]{:S(2)}) copy-start(s32[6,192]{1,0:T(8,128)} %constant.28.clone.lanes) | copy-start | bytes 13828
  143.4 2.2 %collective-permute-start.26 = (bf16[4,656,128]{2,1,0:T(8,128)(2,1)S(1)}, bf16[4,656,128]{2,1,0:T(8,128)(2,1)S(1)}, u32[]{:S(2)}, u32[]{:S(2)}) collective-permute-start(bf16[4,656,128]{2,1,0:T(8,128)(2,1)S(1)} %pad_maximum_fusion.own), channel_id=1, source_target_pairs={{0,4},{4,0},{8,12},{12,8},{16,20},{20,16},{24,28},{28,24},{1,5},{5... | collective-permute-start | bytes 2015240 | tf_op jit(solution)/shard_map/ppermute | solution.py:832

commit v4 on v3

--- a/solution.py
+++ b/solution.py
@@ -16,6 +16,9 @@
 HALO = TOK - HALO0
 GROUP = 8
 CHUNK = 2
+STOP = object()
+LAG_F = 0
+LAG_B = 0
 EPSILON = 1e-05
 NEGATIVE = -1000000000.0
 F32 = jnp.float32
@@ -219,6 +222,15 @@
             two[i - 1] = second(i - 1, one.pop(i - 1))
         if i >= 2:
             third(i - 2, two.pop(i - 2))
+        yield
+
+
+def interleave(programs, lag):
+    programs = [(i * lag, p) for i, p in enumerate(programs)]
+    at = 0
+    while programs:
+        programs = [(start, p) for start, p in programs if at < start or next(p, STOP) is not STOP]
+        at += 1
 
 
 def score(q, k, ones):
@@ -260,7 +272,7 @@
         values, center, rstd = got
         store(i, values, center * rstd, rstd)
 
-    pipelined(n, first, second, third)
+    yield from pipelined(n, first, second, third)
 
 
 def fold_rows(values):
@@ -275,7 +287,7 @@
 def wire_level(z, wire_s, k, l, b):
     half = z.d - LANES
     at = (l % 2) * half
-    rows = pl.ds(pl.multiple_of(b * TOK, 8), TOK)
+    rows = slice(b * TOK, (b + 1) * TOK)
     low, high = wire_s[k, l, rows, :], wire_s[k, z.l + l // 2, rows, :]
     return jnp.concatenate([low, high[:, at : at + half]], axis=1)
 
@@ -284,7 +296,7 @@
     for k in range(z.lev):
         parts = lane_parts(z, [level(k * z.l + l) for l in range(z.l)])
         for j, part in enumerate(parts):
-            wire_s[k, j, pl.ds(pl.multiple_of(b * TOK, 8), TOK), :] = part
+            wire_s[k, j, b * TOK : (b + 1) * TOK, :] = part
 
 
 def flush_wire(z, wire_s, refs):
@@ -334,7 +346,7 @@
             probs_at(i, t)[...] = got[t][0]
             store(i, t, outs[t])
 
-    pipelined(n, first, second, third)
+    yield from pipelined(n, first, second, third)
 
 
 def attention_back(n, qkv, grad, probs_at, store, ones, scales, scale):
@@ -365,14 +377,26 @@
         for t in range(2):
             store(i, t, outs[t])
 
-    pipelined(n, first, second, third)
+    yield from pipelined(n, first, second, third)
 
 
 def score_factor(z):
     return np.float32((z.d // z.heads) ** (-0.5) * np.log2(np.e))
 
 
+def of_band(b, refs):
+    return [ref.at[:, b : b + 1] for ref in refs]
+
+
 def forward_kernel(z, *refs):
+    wire_in, wire_out = refs[: z.lev], refs[z.lev + 16 : 2 * z.lev + 16]
+    wire_s = refs[2 * z.lev + 25]
+    load_wire(z, wire_in, wire_s)
+    interleave([forward_band(z, b, *refs) for b in range(z.nb)], LAG_F)
+    flush_wire(z, wire_s, wire_out)
+
+
+def forward_band(z, b, *refs):
     it = iter(refs)
     take = lambda n: [next(it) for _ in range(n)]
     wire_in = take(z.lev)
@@ -380,15 +404,11 @@
     gain1, shift1, gain2, shift2, gain3, shift3 = take(6)
     w_qkv1, wo1, w_qkv2, wo2, w_up, w_down_t = take(6)
     wire_out = take(z.lev)
-    norm1_ref, norm2_ref, norm3_ref, att_ref, co_ref, act_ref, slope_ref, probs_ref, probs2_ref = take(9)
-    wire_s, x_s, n_s, o_s, a_s, qkv_s, bias_s = take(7)
+    kept = of_band(b, take(9))
+    norm1_ref, norm2_ref, norm3_ref, att_ref, co_ref, act_ref, slope_ref, probs_ref, probs2_ref = kept
+    (wire_s,) = take(1)
+    x_s, n_s, o_s, a_s, qkv_s, bias_s = (ref.at[b] for ref in take(6))
     ones = head_masks(z)
-    b = pl.program_id(1)
-
-    @pl.when(b == 0)
-    def _():
-        load_wire(z, wire_in, wire_s)
-
     s = pl.program_id(0)
     token = lax.broadcasted_iota(jnp.int32, (TOK, 1), 0)
     cell = (token * 43) >> 8
@@ -396,7 +416,7 @@
     cell = cell + (lax.axis_index("lon") * z.cells + offsets[s])
     cell = jnp.where(cell >= z.cells * z.lon, cell - z.cells * z.lon, cell)
     valid = (row < sizes[s, 0]) & (cell < sizes[s, 1])
-    bias_s[...] = bias_ref[0] + jnp.where(valid, 0.0, NEGATIVE)
+    bias_s[...] = bias_ref[b] + jnp.where(valid, 0.0, NEGATIVE)
 
     def keep(ref, gain, shift):
         def store(lv, values, normed, rstd):
@@ -407,12 +427,12 @@
 
         return store
 
-    norm_levels(
+    yield from norm_levels(
         z.lt, lambda lv: wire_level(z, wire_s, lv // z.l, lv % z.l, b), keep(norm1_ref, gain1, shift1)
     )
     put_rows(z, qkv_s, nn(bf16_rows(z, n_s), w_qkv1[...]))
 
-    attention(
+    yield from attention(
         z.lt,
         lambda lv, j, t: qkv_s[lv, :, tile(j, t)],
         lambda t: bias_s[t],
@@ -425,10 +445,10 @@
     att_ref[0, 0] = att
     put_rows(z, o_s, nn(att, wo1[...]))
 
-    norm_levels(z.lt, lambda lv: x_s[lv] + o_s[lv], keep(norm2_ref, gain2, shift2))
+    yield from norm_levels(z.lt, lambda lv: x_s[lv] + o_s[lv], keep(norm2_ref, gain2, shift2))
     put_rows(z, qkv_s, nn(bf16_rows(z, n_s), w_qkv2[...]))
 
-    attention(
+    yield from attention(
         TOK // GROUP,
         lambda g, j, t: qkv_s[:, group(g), tile(j, t)].reshape(z.lt * GROUP, LANES),
         lambda t: column_mask[...],
@@ -441,7 +461,7 @@
     co_ref[0, 0] = co
     put_rows(z, o_s, nn(co, wo2[...]))
 
-    norm_levels(z.lt, lambda lv: x_s[lv] + o_s[lv], keep(norm3_ref, gain3, shift3))
+    yield from norm_levels(z.lt, lambda lv: x_s[lv] + o_s[lv], keep(norm3_ref, gain3, shift3))
 
     def up(i):
         return nn(some_rows(z, n_s, i), w_up[...])
@@ -458,17 +478,13 @@
         act_ref[0, 0, rows], slope_ref[0, 0, rows] = act, slope
         o_s[i * CHUNK : (i + 1) * CHUNK] = out.reshape(CHUNK, TOK, z.d)
 
-    pipelined(z.lt // CHUNK, up, gelu, down)
+    yield from pipelined(z.lt // CHUNK, up, gelu, down)
 
     store_wire_levels(z, wire_s, b, lambda lv: x_s[lv] + o_s[lv])
 
-    @pl.when(b == z.nb - 1)
-    def _():
-        flush_wire(z, wire_s, wire_out)
-
 
 def wire_specs(z):
-    return [pl.BlockSpec((1, z.nblk, z.ro, LANES), lambda s, b: (s, 0, 0, 0))] * z.lev
+    return [pl.BlockSpec((1, z.nblk, z.ro, LANES), lambda s: (s, 0, 0, 0))] * z.lev
 
 
 def wire_shapes(z):
@@ -476,11 +492,11 @@
 
 
 def unit_spec(shape):
-    return pl.BlockSpec((1, 1) + shape, lambda s, b: (s, b) + (0,) * len(shape))
+    return pl.BlockSpec((1,) + shape, lambda s: (s,) + (0,) * len(shape))
 
 
 def whole_spec(array):
-    return pl.BlockSpec(array.shape, lambda s, b: (0,) * array.ndim)
+    return pl.BlockSpec(array.shape, lambda s: (0,) * array.ndim)
 
 
 def residual_shapes(z):
@@ -499,26 +515,26 @@
 
 def forward(z, wire, offsets, sizes, bias, column_mask, norms, weights):
     res = residual_shapes(z)
-    rows3 = (z.lt, TOK, z.d)
+    rows3 = (z.nb, z.lt, TOK, z.d)
     out = pl.pallas_call(
         functools.partial(forward_kernel, z),
-        grid=(z.s, z.nb),
+        grid=(z.s,),
         in_specs=wire_specs(z)
         + [
             *in_smem(2),
-            pl.BlockSpec((1, 2, TOK, z.heads // 2 * TOK), lambda s, b: (b, 0, 0, 0)),
+            whole_spec(bias),
             whole_spec(column_mask),
         ]
         + [whole_spec(a) for a in norms]
         + [whole_spec(a) for a in weights],
-        out_specs=wire_specs(z) + [unit_spec(shape) for shape, _ in res],
+        out_specs=wire_specs(z) + [unit_spec((z.nb,) + shape) for shape, _ in res],
         out_shape=wire_shapes(z) + [jax.ShapeDtypeStruct((z.s, z.nb) + shape, t) for shape, t in res],
         scratch_shapes=[pltpu.VMEM((z.lev, z.nblk, z.ro, LANES), F32)]
         + [pltpu.VMEM(rows3, F32)] * 3
         + [
-            pltpu.VMEM((z.lt, TOK, 2 * LANES), F32),
-            pltpu.VMEM((z.lt, TOK, 6 * LANES), F32),
-            pltpu.VMEM((2, TOK, z.heads // 2 * TOK), F32),
+            pltpu.VMEM((z.nb, z.lt, TOK, 2 * LANES), F32),
+            pltpu.VMEM((z.nb, z.lt, TOK, 6 * LANES), F32),
+            pltpu.VMEM((z.nb, 2, TOK, z.heads // 2 * TOK), F32),
         ],
         compiler_params=pltpu.CompilerParams(vmem_limit_bytes=60 * 2**20),
         cost_estimate=cost(30),
@@ -580,30 +596,13 @@
     return pick
 
 
-def backward_kernel(z, *refs):
-    it = iter(refs)
-    take = lambda n: [next(it) for _ in range(n)]
-    wire_in = take(z.lev)
-    norm1_ref, norm2_ref, norm3_ref, att_ref, co_ref, act_ref, slope_ref, probs_ref, probs2_ref = take(9)
-    (pick_ref,) = take(1)
-    gain1, shift1, gain2, shift2, gain3, shift3 = take(6)
-    w_qkv1, wo1, w_qkv2, wo2, w_up, w_down_t = take(6)
-    wire_out = take(z.lev)
-    late_ref, mine_ref, other_ref = take(3)
-    wire_s, late_s, g_s, o_s, a_s, qkv_s, grad_s, gh_s, db_s, vec_s, sums_s = take(11)
-    grads = {name: ref for (name, _), ref in zip(grad_list(z), take(len(grad_list(z))))}
+def backward_band(z, b, kept, norms, weights, wire_s, own, db_s, vec_s, grads):
+    norm1_ref, norm2_ref, norm3_ref, att_ref, co_ref, act_ref, slope_ref, probs_ref, probs2_ref = kept
+    gain1, shift1, gain2, shift2, gain3, shift3 = norms
+    w_qkv1, wo1, w_qkv2, wo2, w_up, w_down_t = weights
+    g_s, o_s, a_s, qkv_s, grad_s, gh_s = own
     scale = np.float32((z.d // z.heads) ** (-0.5))
     ones, scales = head_masks(z), head_masks(z, scale)
-    s, b = pl.program_id(0), pl.program_id(1)
-
-    @pl.when((s == 0) & (b == 0))
-    def _():
-        for ref in list(grads.values()) + [db_s, vec_s]:
-            ref[...] = jnp.zeros_like(ref)
-
-    @pl.when(b == 0)
-    def _():
-        load_wire(z, wire_in, wire_s)
 
     for k in range(z.lev):
         got = [wire_level(z, wire_s, k, l, b) for l in range(z.l)]
@@ -626,12 +625,12 @@
         gh_s[i * CHUNK * TOK : (i + 1) * CHUNK * TOK] = grad
         o_s[i * CHUNK : (i + 1) * CHUNK] = out.reshape(CHUNK, TOK, z.d)
 
-    pipelined(z.lt // CHUNK, back_down, back_gelu, back_up)
+    yield from pipelined(z.lt // CHUNK, back_down, back_gelu, back_up)
     grads["down_t"][...] += tn(bf16_rows(z, g_s), act_ref[0, 0])
     grads["up"][...] += tn(normed_tokens(norm3_ref, gain3, shift3), gh_s[...])
 
     def norm_step(ref, gain, at, target):
-        sums = [vec_s[at], vec_s[at + 1]]
+        sums = [vec_s[b, at], vec_s[b, at + 1]]
 
         def first(lv):
             grad, normed, rstd = o_s[lv], ref[0, 0, lv, :, : z.d], ref[0, 0, lv, :, z.d : z.d + 1]
@@ -649,10 +648,10 @@
             old, normed, rstd, gained, one, two = got
             target[lv] = old + rstd * (gained - one - normed * two)
 
-        pipelined(z.lt, first, second, third)
-        vec_s[at], vec_s[at + 1] = sums
-
-    norm_step(norm3_ref, gain3, 4, g_s)
+        yield from pipelined(z.lt, first, second, third)
+        vec_s[b, at], vec_s[b, at + 1] = sums
+
+    yield from norm_step(norm3_ref, gain3, 4, g_s)
 
     branch = bf16_rows(z, g_s)
     grads["o2"][...] += tn(co_ref[0, 0], branch)
@@ -664,7 +663,7 @@
         for j in range(3):
             grad_s[:, group(g), tile(j, t)] = got[j].reshape(z.lt, GROUP, LANES)
 
-    attention_back(
+    yield from attention_back(
         TOK // GROUP,
         lambda g, j, t: qkv_s[:, group(g), tile(j, t)].reshape(z.lt * GROUP, LANES),
         lambda g, t: a_s[:, group(g), tile(0, t)].reshape(z.lt * GROUP, LANES),
@@ -681,7 +680,7 @@
         put_rows(z, o_s, nt(grad, w[...]))
 
     project_back(tokens, "qkv2", w_qkv2)
-    norm_step(norm2_ref, gain2, 2, g_s)
+    yield from norm_step(norm2_ref, gain2, 2, g_s)
 
     branch = bf16_rows(z, g_s)
     grads["o1"][...] += tn(att_ref[0, 0], branch)
@@ -694,7 +693,7 @@
             grad_s[lv, :, tile(j, t)] = got[j]
         db_s[b, t] += got[3].astype(F32)
 
-    attention_back(
+    yield from attention_back(
         z.lt,
         lambda lv, j, t: qkv_s[lv, :, tile(j, t)],
         lambda lv, t: a_s[lv, :, tile(0, t)],
@@ -705,19 +704,47 @@
         scale,
     )
     project_back(tokens, "qkv1", w_qkv1)
-    norm_step(norm1_ref, gain1, 0, g_s)
+    yield from norm_step(norm1_ref, gain1, 0, g_s)
 
     store_wire_levels(z, wire_s, b, lambda lv: g_s[lv])
 
-    @pl.when(b == z.nb - 1)
+
+def backward_kernel(z, *refs):
+    it = iter(refs)
+    take = lambda n: [next(it) for _ in range(n)]
+    wire_in = take(z.lev)
+    kept = take(9)
+    (pick_ref,) = take(1)
+    gain1, shift1, gain2, shift2, gain3, shift3 = take(6)
+    w_qkv1, wo1, w_qkv2, wo2, w_up, w_down_t = take(6)
+    wire_out = take(z.lev)
+    late_ref, mine_ref, other_ref = take(3)
+    wire_s, late_s, g_s, o_s, a_s, qkv_s, grad_s, gh_s, db_s, vec_s, sums_s = take(11)
+    grads = {name: ref for (name, _), ref in zip(grad_list(z), take(len(grad_list(z))))}
+    s = pl.program_id(0)
+
+    @pl.when(s == 0)
     def _():
-        flush_wire(z, wire_s, wire_out)
-        for band in range(z.nb):
-            rows = wire_s[:, :, band * TOK + HALO0 : (band + 1) * TOK, :]
-            late_s[:, :, band * HALO : (band + 1) * HALO, :] = rows
-        late_ref[:, 0] = late_s[...].astype(BF16)
-
-    @pl.when((s == z.s - 1) & (b == z.nb - 1))
+        for ref in list(grads.values()) + [db_s, vec_s]:
+            ref[...] = jnp.zeros_like(ref)
+
+    load_wire(z, wire_in, wire_s)
+    bands = []
+    for b in range(z.nb):
+        own = [ref.at[b] for ref in (g_s, o_s, a_s, qkv_s, grad_s, gh_s)]
+        norms = (gain1, shift1, gain2, shift2, gain3, shift3)
+        weights = (w_qkv1, wo1, w_qkv2, wo2, w_up, w_down_t)
+        bands.append(
+            backward_band(z, b, of_band(b, kept), norms, weights, wire_s, own, db_s, vec_s, grads)
+        )
+    interleave(bands, LAG_B)
+    flush_wire(z, wire_s, wire_out)
+    for band in range(z.nb):
+        rows = wire_s[:, :, band * TOK + HALO0 : (band + 1) * TOK, :]
+        late_s[:, :, band * HALO : (band + 1) * HALO, :] = rows
+    late_ref[:, 0] = late_s[...].astype(BF16)
+
+    @pl.when(s == z.s - 1)
     def _():
         p, core = lax.axis_index("lev"), lax.axis_index("lon") % 2
 
@@ -731,7 +758,7 @@
             sums_s[place(at // z.hb), start : start + 96, :] = block.astype(BF16)
         extra = z.hb * 96
         sums_s[:, extra:, :] = jnp.zeros_like(sums_s[:, extra:, :])
-        vectors = [jnp.sum(vec_s[i], axis=0, keepdims=True) for i in range(6)]
+        vectors = [jnp.sum(jnp.sum(vec_s[:, i], axis=0), axis=0, keepdims=True) for i in range(6)]
         vectors = jnp.concatenate(vectors + [jnp.zeros((UNIT - 6, z.d), F32)], axis=0)
         vectors = jnp.concatenate([vectors, jnp.zeros((UNIT, 2 * LANES - z.d), F32)], axis=1)
 
@@ -774,36 +801,36 @@
 
 def backward(z, wire, residuals, norms, weights):
     res = residual_shapes(z)
-    rows3 = (z.lt, TOK, z.d)
+    rows3 = (z.nb, z.lt, TOK, z.d)
     pick = jnp.asarray(bias_rows(z))
     half = (z.lev, z.pr, LANES)
     out = pl.pallas_call(
         functools.partial(backward_kernel, z),
         **dict(
-            grid=(z.s, z.nb),
+            grid=(z.s,),
             in_specs=[
                 spec
                 for spec in wire_specs(z)
-                + [unit_spec(shape) for shape, _ in res]
+                + [unit_spec((z.nb,) + shape) for shape, _ in res]
                 + [whole_spec(pick)]
                 + [whole_spec(a) for a in norms]
                 + [whole_spec(a) for a in weights]
             ],
             out_specs=[spec for spec in wire_specs(z)]
-            + [pl.BlockSpec((z.lev, 1, z.nblk, z.rh, LANES), lambda s, b: (0, s, 0, 0, 0))]
-            + [pl.BlockSpec(half, lambda s, b: (0, 0, 0))] * 2,
+            + [pl.BlockSpec((z.lev, 1, z.nblk, z.rh, LANES), lambda s: (0, s, 0, 0, 0))]
+            + [pl.BlockSpec(half, lambda s: (0, 0, 0))] * 2,
             scratch_shapes=[
                 pltpu.VMEM((z.lev, z.nblk, z.ro, LANES), F32),
                 pltpu.VMEM((z.lev, z.nblk, z.rh, LANES), F32),
             ]
             + [pltpu.VMEM(rows3, F32)] * 2
             + [
-                pltpu.VMEM((z.lt, TOK, 2 * LANES), F32),
-                pltpu.VMEM((z.lt, TOK, 6 * LANES), F32),
-                pltpu.VMEM((z.lt, TOK, 6 * LANES), F32),
-                pltpu.VMEM((z.n, z.ff), BF16),
+                pltpu.VMEM((z.nb, z.lt, TOK, 2 * LANES), F32),
+                pltpu.VMEM((z.nb, z.lt, TOK, 6 * LANES), F32),
+                pltpu.VMEM((z.nb, z.lt, TOK, 6 * LANES), F32),
+                pltpu.VMEM((z.nb, z.n, z.ff), BF16),
                 pltpu.VMEM((z.nb, 2, TOK, z.heads // 2 * TOK), F32),
-                pltpu.VMEM((6, 8, z.d), F32),
+                pltpu.VMEM((z.nb, 6, 8, z.d), F32),
                 pltpu.VMEM((z.np, z.pr, LANES), BF16),
             ]
             + [pltpu.VMEM(grad_buffer(z, *item), F32) for item in grad_list(z)],

time: 148 us -> 140 us (0.946)
  Pallas kernels: 77.8 us -> 70.2 us
    pallas_call x2, Pallas kernels: 63.2 us -> 55.5 us  [the longest x1 32.4 us: backward(): pl.pallas_call(functools.partial(backward_kernel, z), **dict(grid=(z.s,),...]
  transfers between devices with their start and end apart: 27 -> 27, of which waited for: 12 -> 13; matrix products, arithmetic and copies ran while one was open for 2% -> 2% of each run, Pallas kernels for 51% -> 48%
where the time goes in v4:
time: 140 us
  Pallas kernels  70.2 us (50%)
  starting transfers between devices  35.2 us (25%)
  waiting for transfers between devices  24.3 us (17%)
  local copies, waits for them, and re-layouts  6.62 us (5%)
  other arithmetic  2.49 us (2%)
    pallas_call x1, Pallas kernels, backward(): pl.pallas_call(functools.partial(backward_kernel, z), **dict(grid=(z.s,),...  32.4 us
    pallas_call x1, Pallas kernels, forward(): pl.pallas_call(functools.partial(forward_kernel, z), grid=(z.s,), in_spec...  23.1 us
    ppermute x18, starting transfers between devices, lev_swap(): return lax.ppermute(array, 'lev', [(i, i ^ k) for i in range(z.lev)])  22 us
    ppermute x4, starting transfers between devices, lon_shift(): lax.ppermute(array, 'lon', [(w, (w + distance) % z.lon) for w in range(z....  8.64 us
    ppermute x4, waiting for transfers between devices, lon_shift(): lax.ppermute(array, 'lon', [(w, (w + distance) % z.lon) for w in range(z....  8.35 us
    ppermute x18, waiting for transfers between devices, lev_swap(): return lax.ppermute(array, 'lev', [(i, i ^ k) for i in range(z.lev)])  8.35 us
    ppermute x5, waiting for transfers between devices, lon_swap(): return lax.ppermute(array, 'lon', [(i, i ^ k) for i in range(z.lon)])  7.56 us
    pallas_call x2, Pallas kernels, unpack(): pl.pallas_call(functools.partial(unpack_kernel, z, merged), in_specs=in_s...  6.01 us
  transfers between devices with their start and end apart: 27, of which 13 were waited for; matrix products, arithmetic and copies ran while one was open for 2% of the time, Pallas kernels for 48%

profile of v4, /device:TPU:0, one launch (start us, length us, event | category | flops | bytes accessed | tf_op | source)
XLA Modules:
  0.0 139.9 jit_solution(12698039824008426413)
XLA Ops:
  0.6 0.0 copy-start
  0.7 0.0 copy-start.11
  0.7 2.1 %slice.57 = bf16[2,2,6,48,192]{4,3,2,1,0:T(8,128)(2,1)} slice(bf16[2,2,12,48,192]{4,3,2,1,0:T(8,128)(2,1)} %bitcast.46), slice={[0:2], [0:2], [0:6], [0:48], [0:192]} | slice | bytes 884736 | tf_op jit(solution)/shard_map/slice | solution.py:1069
  2.8 4.5 %collective-permute-start = (bf16[2,2,6,48,192]{4,3,2,1,0:T(8,128)(2,1)}, bf16[2,2,6,48,192]{4,3,2,1,0:T(8,128)(2,1)S(1)}, u32[]{:S(2)}, u32[]{:S(2)}) collective-permute-start(bf16[2,2,6,48,192]{4,3,2,1,0:T(8,128)(2,1)} %slice.57), channel_id=1, source_target_pairs={{0,28},{4,0},{8,4},{12,8},{16,12},{20,16},{24,20},{28,24},{1,29},{... | collective-permute-start | bytes 1327112 | tf_op jit(solution)/shard_map/ppermute | solution.py:1050
  7.3 0.1 dynamic-slice_bitcast_fusion
  7.6 1.2 bias.1
  8.9 0.7 copy-done.21
  9.6 0.7 copy-done.22
  10.3 0.7 copy-done.26
  10.9 4.1 %collective-permute-done.halo_ref = bf16[2,2,6,48,192]{4,3,2,1,0:T(8,128)(2,1)S(1)} collective-permute-done((bf16[2,2,6,48,192]{4,3,2,1,0:T(8,128)(2,1)}, bf16[2,2,6,48,192]{4,3,2,1,0:T(8,128)(2,1)S(1)}, u32[]{:S(2)}, u32[]{:S(2)}) %collective-permute-start) | collective-permute-done | bytes 442400 | tf_op jit(solution)/shard_map/ppermute | solution.py:1050
  15.0 3.6 %collective-permute-start.1 = (bf16[2,2,6,48,192]{4,3,2,1,0:T(8,128)(2,1)S(1)}, bf16[2,2,6,48,192]{4,3,2,1,0:T(8,128)(2,1)S(1)}, u32[]{:S(2)}, u32[]{:S(2)}) collective-permute-start(bf16[2,2,6,48,192]{4,3,2,1,0:T(8,128)(2,1)S(1)} %slice.56), channel_id=1, source_target_pairs={{0,28},{4,0},{8,4},{12,8},{16,12},{20,16},{24,20},{28,24},{1,29},{... | collective-permute-start | bytes 1327112 | tf_op jit(solution)/shard_map/ppermute | solution.py:1050
  18.6 2.1 %pack.2 = (bf16[2,3,144,128]{3,2,1,0:T(8,128)(2,1)S(1)}, bf16[2,3,144,128]{3,2,1,0:T(8,128)(2,1)S(1)}, bf16[2,3,144,128]{3,2,1,0:T(8,128)(2,1)S(1)}, bf16[2,3,144,128]{3,2,1,0:T(8,128)(2,1)S(1)}) custom-call(s32[2]{0:T(128)S(1)} %copy-done.8, s32[144,1]{1,0:T(8,128)S(1)} %copy-done.10, bf16[2,2,12,48,192]{4,3,2,1,0:T(8,128)(2,1)S(1)} %bitcast.47, ...), custom_call_target="tpu_custom_call" | custom-call | flops 2000000000 | bytes 12000000 | tf_op jit(solution)/shard_map/pack/pallas_call | solution.py:118
  20.8 0.7 copy-done.24
  21.5 1.5 %collective-permute-start.5 = (bf16[2,3,144,128]{3,2,1,0:T(8,128)(2,1)S(1)}, bf16[2,3,144,128]{3,2,1,0:T(8,128)(2,1)S(1)}, u32[]{:S(2)}, u32[]{:S(2)}) collective-permute-start(bf16[2,3,144,128]{3,2,1,0:T(8,128)(2,1)S(1)} %get-tuple-element.90), channel_id=1, source_target_pairs={{0,1},{1,0},{2,3},{3,2},{4,5},{5,4},{6,7},{7,6},{8,9},{9,8},{10,11... | collective-permute-start | bytes 663560 | tf_op jit(solution)/shard_map/ppermute | solution.py:855
  22.9 1.5 %collective-permute-start.6 = (bf16[2,3,144,128]{3,2,1,0:T(8,128)(2,1)S(1)}, bf16[2,3,144,128]{3,2,1,0:T(8,128)(2,1)S(1)}, u32[]{:S(2)}, u32[]{:S(2)}) collective-permute-start(bf16[2,3,144,128]{3,2,1,0:T(8,128)(2,1)S(1)} %get-tuple-element.91), channel_id=1, source_target_pairs={{0,2},{1,3},{2,0},{3,1},{4,6},{5,7},{6,4},{7,5},{8,10},{9,11},{10,... | collective-permute-start | bytes 663560 | tf_op jit(solution)/shard_map/ppermute | solution.py:855
  24.5 0.5 collective-permute-start.7
  24.9 1.1 collective-permute-done.1.halo_ref
  26.0 2.1 %pack.3 = (bf16[2,3,144,128]{3,2,1,0:T(8,128)(2,1)S(1)}, bf16[2,3,144,128]{3,2,1,0:T(8,128)(2,1)S(1)}, bf16[2,3,144,128]{3,2,1,0:T(8,128)(2,1)S(1)}, bf16[2,3,144,128]{3,2,1,0:T(8,128)(2,1)S(1)}) custom-call(s32[2]{0:T(128)S(1)} %copy-done.8, s32[144,1]{1,0:T(8,128)S(1)} %copy-done.10, bf16[2,2,12,48,192]{4,3,2,1,0:T(8,128)(2,1)S(1)} %bitcast.49, ...), custom_call_target="tpu_custom_call" | custom-call | flops 2000000000 | bytes 12000000 | tf_op jit(solution)/shard_map/pack/pallas_call | solution.py:118
  28.1 1.6 %collective-permute-start.2 = (bf16[2,3,144,128]{3,2,1,0:T(8,128)(2,1)S(1)}, bf16[2,3,144,128]{3,2,1,0:T(8,128)(2,1)S(1)}, u32[]{:S(2)}, u32[]{:S(2)}) collective-permute-start(bf16[2,3,144,128]{3,2,1,0:T(8,128)(2,1)S(1)} %get-tuple-element.95), channel_id=1, source_target_pairs={{0,1},{1,0},{2,3},{3,2},{4,5},{5,4},{6,7},{7,6},{8,9},{9,8},{10,11... | collective-permute-start | bytes 663560 | tf_op jit(solution)/shard_map/ppermute | solution.py:855
  29.7 1.5 %collective-permute-start.3 = (bf16[2,3,144,128]{3,2,1,0:T(8,128)(2,1)S(1)}, bf16[2,3,144,128]{3,2,1,0:T(8,128)(2,1)S(1)}, u32[]{:S(2)}, u32[]{:S(2)}) collective-permute-start(bf16[2,3,144,128]{3,2,1,0:T(8,128)(2,1)S(1)} %get-tuple-element.96), channel_id=1, source_target_pairs={{0,2},{1,3},{2,0},{3,1},{4,6},{5,7},{6,4},{7,5},{8,10},{9,11},{10,... | collective-permute-start | bytes 663560 | tf_op jit(solution)/shard_map/ppermute | solution.py:855
  31.2 0.5 collective-permute-start.4
  31.7 2.5 %collective-permute-done.7.refs_3_ = bf16[2,3,144,128]{3,2,1,0:T(8,128)(2,1)S(1)} collective-permute-done((bf16[2,3,144,128]{3,2,1,0:T(8,128)(2,1)S(1)}, bf16[2,3,144,128]{3,2,1,0:T(8,128)(2,1)S(1)}, u32[]{:S(2)}, u32[]{:S(2)}) %collective-permute-start.7) | collective-permute-done | bytes 221216 | tf_op jit(solution)/shard_map/ppermute | solution.py:855
  34.2 0.7 copy-done.32
  34.9 23.1 %forward.1 = (bf16[2,3,144,128]{3,2,1,0:T(8,128)(2,1)}, bf16[2,3,144,128]{3,2,1,0:T(8,128)(2,1)}, bf16[2,3,144,128]{3,2,1,0:T(8,128)(2,1)}, bf16[2,3,144,128]{3,...) custom-call(bf16[2,3,144,128]{3,2,1,0:T(8,128)(2,1)} %copy-done.24, ...), custom_call_target="tpu_custom_call" | custom-call | flops 15000000512 | bytes 90000000 | tf_op jit(solution)/shard_map/forward/pallas_call | solution.py:519
  58.0 1.4 %collective-permute-start.8 = (bf16[2,3,144,128]{3,2,1,0:T(8,128)(2,1)}, bf16[2,3,144,128]{3,2,1,0:T(8,128)(2,1)S(1)}, u32[]{:S(2)}, u32[]{:S(2)}) collective-permute-start(bf16[2,3,144,128]{3,2,1,0:T(8,128)(2,1)} %get-tuple-element.120), channel_id=1, source_target_pairs={{0,1},{1,0},{2,3},{3,2},{4,5},{5,4},{6,7},{7,6},{8,9},{9,8},{10,11... | collective-permute-start | bytes 663560 | tf_op jit(solution)/shard_map/ppermute | solution.py:855
  59.5 0.6 collective-permute-start.9
  60.1 1.5 %collective-permute-start.10 = (bf16[2,3,144,128]{3,2,1,0:T(8,128)(2,1)}, bf16[2,3,144,128]{3,2,1,0:T(8,128)(2,1)S(1)}, u32[]{:S(2)}, u32[]{:S(2)}) collective-permute-start(bf16[2,3,144,128]{3,2,1,0:T(8,128)(2,1)} %get-tuple-element.122), channel_id=1, source_target_pairs={{0,3},{1,2},{2,1},{3,0},{4,7},{5,6},{6,5},{7,4},{8,11},{9,10},{10,... | collective-permute-start | bytes 663560 | tf_op jit(solution)/shard_map/ppermute | solution.py:855
  61.6 0.7 copy-done.28
  62.3 0.1 copy-done.29
  62.4 32.4 %backward.1 = (bf16[2,3,144,128]{3,2,1,0:T(8,128)(2,1)}, bf16[2,3,144,128]{3,2,1,0:T(8,128)(2,1)}, bf16[2,3,144,128]{3,2,1,0:T(8,128)(2,1)}, bf16[2,3,144,128]{3...) custom-call(bf16[2,3,144,128]{3,2,1,0:T(8,128)(2,1)} %copy-done.23, ...), custom_call_target="tpu_custom_call" | custom-call | flops 20000000000 | bytes 120000000 | tf_op jit(solution)/shard_map/backward/pallas_call | solution.py:807
  94.8 0.1 collective-permute-start.16
  94.9 0.5 collective-permute-start.12
  95.5 0.1 pad_maximum_fusion.1
  95.6 0.1 collective-permute-start.11
  95.7 1.6 %collective-permute-done.16 = bf16[4,656,128]{2,1,0:T(8,128)(2,1)S(1)} collective-permute-done((bf16[4,656,128]{2,1,0:T(8,128)(2,1)}, bf16[4,656,128]{2,1,0:T(8,128)(2,1)S(1)}, u32[]{:S(2)}, u32[]{:S(2)}) %collective-permute-start.16) | collective-permute-done | bytes 671776 | tf_op jit(solution)/shard_map/ppermute | solution.py:859
  97.2 1.2 fusion.3
  98.5 1.4 %collective-permute-start.17 = (bf16[656,128]{1,0:T(8,128)(2,1)S(1)}, bf16[656,128]{1,0:T(8,128)(2,1)S(1)}, u32[]{:S(2)}, u32[]{:S(2)}) collective-permute-start(bf16[656,128]{1,0:T(8,128)(2,1)S(1)} %get-tuple-element.157), channel_id=1, source_target_pairs={{0,1},{1,0},{2,3},{3,2},{4,5},{5,4},{6,7},{7,6},{8,9},{9,8},{10,11... | collective-permute-start | bytes 503816 | tf_op jit(solution)/shard_map/ppermute | solution.py:855
  99.9 0.6 collective-permute-start.19
  100.5 1.5 %collective-permute-start.18 = (bf16[656,128]{1,0:T(8,128)(2,1)S(1)}, bf16[656,128]{1,0:T(8,128)(2,1)S(1)}, u32[]{:S(2)}, u32[]{:S(2)}) collective-permute-start(bf16[656,128]{1,0:T(8,128)(2,1)S(1)} %get-tuple-element.159), channel_id=1, source_target_pairs={{0,2},{1,3},{2,0},{3,1},{4,6},{5,7},{6,4},{7,5},{8,10},{9,11},{10,... | collective-permute-start | bytes 503816 | tf_op jit(solution)/shard_map/ppermute | solution.py:855
  102.0 3.2 %collective-permute-done.12.refs_4_ = bf16[4,2,3,80,128]{4,3,2,1,0:T(8,128)(2,1)S(1)} collective-permute-done((bf16[4,2,3,80,128]{4,3,2,1,0:T(8,128)(2,1)}, bf16[4,2,3,80,128]{4,3,2,1,0:T(8,128)(2,1)S(1)}, u32[]{:S(2)}, u32[]{:S(2)}) %collective-permute-start.12) | collective-permute-done | bytes 491552 | tf_op jit(solution)/shard_map/ppermute | solution.py:1050
  105.3 0.7 merge.1
  106.0 1.4 %collective-permute-start.13 = (bf16[2,3,144,128]{3,2,1,0:T(8,128)(2,1)S(1)}, bf16[2,3,144,128]{3,2,1,0:T(8,128)(2,1)S(1)}, u32[]{:S(2)}, u32[]{:S(2)}) collective-permute-start(bf16[2,3,144,128]{3,2,1,0:T(8,128)(2,1)S(1)} %get-tuple-element.133), channel_id=1, source_target_pairs={{0,1},{1,0},{2,3},{3,2},{4,5},{5,4},{6,7},{7,6},{8,9},{9,8},{10,11... | collective-permute-start | bytes 663560 | tf_op jit(solution)/shard_map/ppermute | solution.py:855
  107.4 0.6 collective-permute-start.14
  108.0 1.3 collective-permute-done.19
  109.2 1.9 %collective-permute-done.18 = bf16[656,128]{1,0:T(8,128)(2,1)S(1)} collective-permute-done((bf16[656,128]{1,0:T(8,128)(2,1)S(1)}, bf16[656,128]{1,0:T(8,128)(2,1)S(1)}, u32[]{:S(2)}, u32[]{:S(2)}) %collective-permute-start.18) | collective-permute-done | bytes 167968 | tf_op jit(solution)/shard_map/ppermute | solution.py:855
  111.2 1.0 fusion.1
  112.2 2.1 %collective-permute-start.22 = (bf16[656,128]{1,0:T(8,128)(2,1)S(1)}, bf16[656,128]{1,0:T(8,128)(2,1)S(1)}, u32[]{:S(2)}, u32[]{:S(2)}) collective-permute-start(bf16[656,128]{1,0:T(8,128)(2,1)S(1)} %fusion.1), channel_id=1, source_target_pairs={{0,24},{4,28},{8,16},{12,20},{16,8},{20,12},{24,0},{28,4},{1,25},{... | collective-permute-start | bytes 503816 | tf_op jit(solution)/shard_map/ppermute | solution.py:859
  114.4 2.3 %collective-permute-start.20 = (bf16[656,128]{1,0:T(8,128)(2,1)S(1)}, bf16[656,128]{1,0:T(8,128)(2,1)S(1)}, u32[]{:S(2)}, u32[]{:S(2)}) collective-permute-start(bf16[656,128]{1,0:T(8,128)(2,1)S(1)} %fusion.1), channel_id=1, source_target_pairs={{0,8},{4,12},{8,0},{12,4},{16,24},{20,28},{24,16},{28,20},{1,9},{5... | collective-permute-start | bytes 503816 | tf_op jit(solution)/shard_map/ppermute | solution.py:859
  116.7 3.2 %unpack.2 = bf16[2,2,12,48,192]{4,3,2,1,0:T(8,128)(2,1)} custom-call(s32[2]{0:T(128)S(1)} %copy-done.9, s32[1,144]{1,0:T(1,128)S(1)} %copy-done.14, s32[1,80]{1,0:T(1,128)S(1)} %copy-done.15, bf16[2,3,144,128]{3,2,1,0:T(8,128)(2,1)S(1)} %copy-done.3, bf16[2,3,144,128]{3,2,1,0:T(8,128)(2,1)S(1)} %collective-permute-done.8.rest_3_, ...), custom_call_target="tpu_custom_call" | custom-call | flops 2000000000 | bytes 12000000 | tf_op jit(solution)/shard_map/unpack/pallas_call | solution.py:165
  119.9 0.8 collective-permute-done.22
  120.7 2.3 %collective-permute-start.15 = (bf16[2,3,144,128]{3,2,1,0:T(8,128)(2,1)S(1)}, bf16[2,3,144,128]{3,2,1,0:T(8,128)(2,1)S(1)}, u32[]{:S(2)}, u32[]{:S(2)}) collective-permute-start(bf16[2,3,144,128]{3,2,1,0:T(8,128)(2,1)S(1)} %get-tuple-element.135), channel_id=1, source_target_pairs={{0,3},{1,2},{2,1},{3,0},{4,7},{5,6},{6,5},{7,4},{8,11},{9,10},{10,... | collective-permute-start | bytes 663560 | tf_op jit(solution)/shard_map/ppermute | solution.py:855
  123.0 3.1 %collective-permute-done.21 = bf16[656,128]{1,0:T(8,128)(2,1)S(1)} collective-permute-done((bf16[656,128]{1,0:T(8,128)(2,1)S(1)}, bf16[656,128]{1,0:T(8,128)(2,1)S(1)}, u32[]{:S(2)}, u32[]{:S(2)}) %collective-permute-start.21) | collective-permute-done | bytes 167968 | tf_op jit(solution)/shard_map/ppermute | solution.py:859
  126.0 0.1 add_convert_fusion
  126.1 2.1 %collective-permute-start.25 = (bf16[656,128]{1,0:T(8,128)(2,1)S(1)}, bf16[656,128]{1,0:T(8,128)(2,1)S(1)}, u32[]{:S(2)}, u32[]{:S(2)}) collective-permute-start(bf16[656,128]{1,0:T(8,128)(2,1)S(1)} %add_convert_fusion), channel_id=1, source_target_pairs={{0,3},{1,2},{2,1},{3,0},{4,7},{5,6},{6,5},{7,4},{8,11},{9,10},{10,... | collective-permute-start | bytes 503816 | tf_op jit(solution)/shard_map/ppermute | solution.py:855
  128.2 0.8 collective-permute-start.24
  128.9 0.7 collective-permute-start.23
  129.7 2.8 %unpack.3 = bf16[2,2,12,48,192]{4,3,2,1,0:T(8,128)(2,1)} custom-call(s32[2]{0:T(128)S(1)} %copy-done.9, s32[1,144]{1,0:T(1,128)S(1)} %copy-done.14, bf16[2,3,144,128]{3,2,1,0:T(8,128)(2,1)S(1)} %get-tuple-element.132.rest_1_, bf16[2,3,144,128]{3,2,1,0:T(8,128)(2,1)S(1)} %collective-permute-done.13.rest_2_, ...), custom_call_target="tpu_custom_call" | custom-call | flops 2000000000 | bytes 12000000 | tf_op jit(solution)/shard_map/unpack/pallas_call | solution.py:165
  132.5 1.3 collective-permute-done.25
  133.9 1.0 collective-permute-done.24
  134.9 0.3 collective-permute-done.23
  135.2 0.1 pad_maximum_fusion.own
  135.3 0.1 collective-permute-start.26
  135.4 2.1 %collective-permute-done.26.other = bf16[4,656,128]{2,1,0:T(8,128)(2,1)S(1)} collective-permute-done((bf16[4,656,128]{2,1,0:T(8,128)(2,1)S(1)}, bf16[4,656,128]{2,1,0:T(8,128)(2,1)S(1)}, u32[]{:S(2)}, u32[]{:S(2)}) %collective-permute-start.26) | collective-permute-done | bytes 671776 | tf_op jit(solution)/shard_map/ppermute | solution.py:859
  137.5 2.5 %finish.1 = (f32[192,768]{1,0:T(8,128)}, f32[192,768]{1,0:T(8,128)}, f32[192,576]{1,0:T(8,128)}, f32[192,576]{1,0:T(8,128)}, f32[192,192]{1,0:T(8,128)}, /*index...) custom-call(s32[6,192]{1,0:T(8,128)S(1)} %copy-done.13, ...), custom_call_target="tpu_custom_call" | custom-call | flops 2000000000 | bytes 12000000 | tf_op jit(solution)/shard_map/finish/pallas_call | solution.py:965
  (79 shorter events, 0.3 us)
Async XLA Ops:
  0.6 6.6 %copy-start = (f32[8,6,6,6,23]{4,0,3,2,1:T(8,128)S(1)}, f32[8,6,6,6,23]{4,0,3,2,1:T(8,128)}, u32[]{:S(2)}) copy-start(f32[8,6,6,6,23]{4,0,3,2,1:T(8,128)} %param.35) | copy-start | bytes 476932
  0.7 6.9 %copy-start.11 = (f32[96,72]{1,0:T(8,128)S(1)}, f32[96,72]{1,0:T(8,128)}, u32[]{:S(2)}) copy-start(f32[96,72]{1,0:T(8,128)} %constant.24.clone.pick_ref.refs_13_) | copy-start | bytes 82948
  0.7 6.7 %copy-start.2 = (bf16[2,2,48,12,192]{4,2,3,1,0:T(8,128)(2,1)S(1)}, bf16[2,2,48,12,192]{4,2,3,1,0:T(8,128)(2,1)}, u32[]{:S(2)}) copy-start(bf16[2,2,48,12,192]{4,2,3,1,0:T(8,128)(2,1)} %param.28) | copy-start | bytes 2654212
  0.7 6.8 %copy-start.7 = (bf16[192,192]{1,0:T(8,128)(2,1)S(1)}, bf16[192,192]{1,0:T(8,128)(2,1)}, u32[]{:S(2)}) copy-start(bf16[192,192]{1,0:T(8,128)(2,1)} %out2.1) | copy-start | bytes 221188
  0.7 6.8 %copy-start.5 = (bf16[192,576]{1,0:T(8,128)(2,1)S(1)}, bf16[192,576]{1,0:T(8,128)(2,1)}, u32[]{:S(2)}) copy-start(bf16[192,576]{1,0:T(8,128)(2,1)} %qkv2.1) | copy-start | bytes 663556
  0.7 6.8 %copy-start.6 = (bf16[192,192]{1,0:T(8,128)(2,1)S(1)}, bf16[192,192]{1,0:T(8,128)(2,1)}, u32[]{:S(2)}) copy-start(bf16[192,192]{1,0:T(8,128)(2,1)} %out1.1) | copy-start | bytes 221188
  0.7 6.8 %copy-start.4 = (bf16[192,576]{1,0:T(8,128)(2,1)S(1)}, bf16[192,576]{1,0:T(8,128)(2,1)}, u32[]{:S(2)}) copy-start(bf16[192,576]{1,0:T(8,128)(2,1)} %qkv1.1) | copy-start | bytes 663556
  2.8 12.2 %collective-permute-start = (bf16[2,2,6,48,192]{4,3,2,1,0:T(8,128)(2,1)}, bf16[2,2,6,48,192]{4,3,2,1,0:T(8,128)(2,1)S(1)}, u32[]{:S(2)}, u32[]{:S(2)}) collective-permute-start(bf16[2,2,6,48,192]{4,3,2,1,0:T(8,128)(2,1)} %slice.57), channel_id=1, source_target_pairs={{0,28},{4,0},{8,4},{12,8},{16,12},{20,16},{24,20},{28,24},{1,29},{... | collective-permute-start | bytes 1327112 | tf_op jit(solution)/shard_map/ppermute | solution.py:1050
  7.6 11.0 %copy-start.1 = (bf16[2,2,48,12,192]{4,2,3,1,0:T(8,128)(2,1)S(1)}, bf16[2,2,48,12,192]{4,2,3,1,0:T(8,128)(2,1)}, u32[]{:S(2)}) copy-start(bf16[2,2,48,12,192]{4,2,3,1,0:T(8,128)(2,1)} %param.27) | copy-start | bytes 2654212
  7.6 11.0 %copy-start.8 = (s32[2]{0:T(128)S(1)}, s32[2]{0:T(128)}, u32[]{:S(2)}) copy-start(s32[2]{0:T(128)} %offsets.9) | copy-start | bytes 28
  7.6 11.0 %copy-start.10 = (s32[144,1]{1,0:T(8,128)S(1)}, s32[144,1]{1,0:T(8,128)}, u32[]{:S(2)}) copy-start(s32[144,1]{1,0:T(8,128)} %constant.36.base) | copy-start | bytes 1732
  8.8 0.7 copy-start.21
  9.6 0.7 copy-start.22
  10.3 0.7 copy-start.26
  10.9 9.8 %copy-start.20 = (bf16[192,768]{1,0:T(8,128)(2,1)}, bf16[192,768]{1,0:T(8,128)(2,1)S(1)}, u32[]{:S(2)}) copy-start(bf16[192,768]{1,0:T(8,128)(2,1)S(1)} %get-tuple-element.99.refs_14_.refs_20_) | copy-start | bytes 884740
  10.9 9.8 %copy-start.25 = (bf16[256,192]{1,0:T(8,128)(2,1)}, bf16[256,192]{1,0:T(8,128)(2,1)S(1)}, u32[]{:S(2)}) copy-start(bf16[256,192]{1,0:T(8,128)(2,1)S(1)} %get-tuple-element.100.refs_15_.refs_21_) | copy-start | bytes 294916
  15.0 11.0 %collective-permute-start.1 = (bf16[2,2,6,48,192]{4,3,2,1,0:T(8,128)(2,1)S(1)}, bf16[2,2,6,48,192]{4,3,2,1,0:T(8,128)(2,1)S(1)}, u32[]{:S(2)}, u32[]{:S(2)}) collective-permute-start(bf16[2,2,6,48,192]{4,3,2,1,0:T(8,128)(2,1)S(1)} %slice.56), channel_id=1, source_target_pairs={{0,28},{4,0},{8,4},{12,8},{16,12},{20,16},{24,20},{28,24},{1,29},{... | collective-permute-start | bytes 1327112 | tf_op jit(solution)/shard_map/ppermute | solution.py:1050
  20.8 0.7 copy-start.24
  21.5 9.8 %collective-permute-start.5 = (bf16[2,3,144,128]{3,2,1,0:T(8,128)(2,1)S(1)}, bf16[2,3,144,128]{3,2,1,0:T(8,128)(2,1)S(1)}, u32[]{:S(2)}, u32[]{:S(2)}) collective-permute-start(bf16[2,3,144,128]{3,2,1,0:T(8,128)(2,1)S(1)} %get-tuple-element.90), channel_id=1, source_target_pairs={{0,1},{1,0},{2,3},{3,2},{4,5},{5,4},{6,7},{7,6},{8,9},{9,8},{10,11... | collective-permute-start | bytes 663560 | tf_op jit(solution)/shard_map/ppermute | solution.py:855
  22.9 8.8 %collective-permute-start.6 = (bf16[2,3,144,128]{3,2,1,0:T(8,128)(2,1)S(1)}, bf16[2,3,144,128]{3,2,1,0:T(8,128)(2,1)S(1)}, u32[]{:S(2)}, u32[]{:S(2)}) collective-permute-start(bf16[2,3,144,128]{3,2,1,0:T(8,128)(2,1)S(1)} %get-tuple-element.91), channel_id=1, source_target_pairs={{0,2},{1,3},{2,0},{3,1},{4,6},{5,7},{6,4},{7,5},{8,10},{9,11},{10,... | collective-permute-start | bytes 663560 | tf_op jit(solution)/shard_map/ppermute | solution.py:855
  24.5 9.7 %collective-permute-start.7 = (bf16[2,3,144,128]{3,2,1,0:T(8,128)(2,1)S(1)}, bf16[2,3,144,128]{3,2,1,0:T(8,128)(2,1)S(1)}, u32[]{:S(2)}, u32[]{:S(2)}) collective-permute-start(bf16[2,3,144,128]{3,2,1,0:T(8,128)(2,1)S(1)} %get-tuple-element.92), channel_id=1, source_target_pairs={{0,3},{1,2},{2,1},{3,0},{4,7},{5,6},{6,5},{7,4},{8,11},{9,10},{10,... | collective-permute-start | bytes 663560 | tf_op jit(solution)/shard_map/ppermute | solution.py:855
  28.1 29.9 %copy-start.23 = (bf16[2,3,144,128]{3,2,1,0:T(8,128)(2,1)}, bf16[2,3,144,128]{3,2,1,0:T(8,128)(2,1)S(1)}, u32[]{:S(2)}) copy-start(bf16[2,3,144,128]{3,2,1,0:T(8,128)(2,1)S(1)} %get-tuple-element.94.refs_0_) | copy-start | bytes 663556
  28.1 31.9 %collective-permute-start.2 = (bf16[2,3,144,128]{3,2,1,0:T(8,128)(2,1)S(1)}, bf16[2,3,144,128]{3,2,1,0:T(8,128)(2,1)S(1)}, u32[]{:S(2)}, u32[]{:S(2)}) collective-permute-start(bf16[2,3,144,128]{3,2,1,0:T(8,128)(2,1)S(1)} %get-tuple-element.95), channel_id=1, source_target_pairs={{0,1},{1,0},{2,3},{3,2},{4,5},{5,4},{6,7},{7,6},{8,9},{9,8},{10,11... | collective-permute-start | bytes 663560 | tf_op jit(solution)/shard_map/ppermute | solution.py:855
  29.7 31.9 %collective-permute-start.3 = (bf16[2,3,144,128]{3,2,1,0:T(8,128)(2,1)S(1)}, bf16[2,3,144,128]{3,2,1,0:T(8,128)(2,1)S(1)}, u32[]{:S(2)}, u32[]{:S(2)}) collective-permute-start(bf16[2,3,144,128]{3,2,1,0:T(8,128)(2,1)S(1)} %get-tuple-element.96), channel_id=1, source_target_pairs={{0,2},{1,3},{2,0},{3,1},{4,6},{5,7},{6,4},{7,5},{8,10},{9,11},{10,... | collective-permute-start | bytes 663560 | tf_op jit(solution)/shard_map/ppermute | solution.py:855
  31.2 3.7 %copy-start.30 = (bf16[2,3,144,128]{3,2,1,0:T(8,128)(2,1)}, bf16[2,3,144,128]{3,2,1,0:T(8,128)(2,1)S(1)}, u32[]{:S(2)}) copy-start(bf16[2,3,144,128]{3,2,1,0:T(8,128)(2,1)S(1)} %collective-permute-done.5.refs_1_) | copy-start | bytes 663556
  31.2 30.4 %collective-permute-start.4 = (bf16[2,3,144,128]{3,2,1,0:T(8,128)(2,1)S(1)}, bf16[2,3,144,128]{3,2,1,0:T(8,128)(2,1)S(1)}, u32[]{:S(2)}, u32[]{:S(2)}) collective-permute-start(bf16[2,3,144,128]{3,2,1,0:T(8,128)(2,1)S(1)} %get-tuple-element.97), channel_id=1, source_target_pairs={{0,3},{1,2},{2,1},{3,0},{4,7},{5,6},{6,5},{7,4},{8,11},{9,10},{10,... | collective-permute-start | bytes 663560 | tf_op jit(solution)/shard_map/ppermute | solution.py:855
  31.7 2.5 %copy-start.31 = (bf16[2,3,144,128]{3,2,1,0:T(8,128)(2,1)}, bf16[2,3,144,128]{3,2,1,0:T(8,128)(2,1)S(1)}, u32[]{:S(2)}) copy-start(bf16[2,3,144,128]{3,2,1,0:T(8,128)(2,1)S(1)} %collective-permute-done.6.refs_2_) | copy-start | bytes 663556
  34.2 0.7 copy-start.32
  58.0 36.8 %collective-permute-start.8 = (bf16[2,3,144,128]{3,2,1,0:T(8,128)(2,1)}, bf16[2,3,144,128]{3,2,1,0:T(8,128)(2,1)S(1)}, u32[]{:S(2)}, u32[]{:S(2)}) collective-permute-start(bf16[2,3,144,128]{3,2,1,0:T(8,128)(2,1)} %get-tuple-element.120), channel_id=1, source_target_pairs={{0,1},{1,0},{2,3},{3,2},{4,5},{5,4},{6,7},{7,6},{8,9},{9,8},{10,11... | collective-permute-start | bytes 663560 | tf_op jit(solution)/shard_map/ppermute | solution.py:855
  59.5 35.4 %collective-permute-start.9 = (bf16[2,3,144,128]{3,2,1,0:T(8,128)(2,1)}, bf16[2,3,144,128]{3,2,1,0:T(8,128)(2,1)S(1)}, u32[]{:S(2)}, u32[]{:S(2)}) collective-permute-start(bf16[2,3,144,128]{3,2,1,0:T(8,128)(2,1)} %get-tuple-element.121), channel_id=1, source_target_pairs={{0,2},{1,3},{2,0},{3,1},{4,6},{5,7},{6,4},{7,5},{8,10},{9,11},{10,... | collective-permute-start | bytes 663560 | tf_op jit(solution)/shard_map/ppermute | solution.py:855
  60.1 2.3 %copy-start.27 = (bf16[2,3,144,128]{3,2,1,0:T(8,128)(2,1)}, bf16[2,3,144,128]{3,2,1,0:T(8,128)(2,1)S(1)}, u32[]{:S(2)}) copy-start(bf16[2,3,144,128]{3,2,1,0:T(8,128)(2,1)S(1)} %collective-permute-done.2.refs_1_) | copy-start | bytes 663556
  60.1 34.8 %collective-permute-start.10 = (bf16[2,3,144,128]{3,2,1,0:T(8,128)(2,1)}, bf16[2,3,144,128]{3,2,1,0:T(8,128)(2,1)S(1)}, u32[]{:S(2)}, u32[]{:S(2)}) collective-permute-start(bf16[2,3,144,128]{3,2,1,0:T(8,128)(2,1)} %get-tuple-element.122), channel_id=1, source_target_pairs={{0,3},{1,2},{2,1},{3,0},{4,7},{5,6},{6,5},{7,4},{8,11},{9,10},{10,... | collective-permute-start | bytes 663560 | tf_op jit(solution)/shard_map/ppermute | solution.py:855
  61.6 0.7 copy-start.28
  61.6 0.7 copy-start.29
  62.4 33.1 %copy-start.3 = (bf16[2,3,144,128]{3,2,1,0:T(8,128)(2,1)S(1)}, bf16[2,3,144,128]{3,2,1,0:T(8,128)(2,1)}, u32[]{:S(2)}) copy-start(bf16[2,3,144,128]{3,2,1,0:T(8,128)(2,1)} %get-tuple-element.123.rest_2_) | copy-start | bytes 663556
  94.8 10.5 %copy-start.9 = (s32[2]{0:T(128)S(1)}, s32[2]{0:T(128)}, u32[]{:S(2)}) copy-start(s32[2]{0:T(128)} %offsets.9) | copy-start | bytes 28
  94.8 10.5 %copy-start.16 = (bf16[2,3,144,128]{3,2,1,0:T(8,128)(2,1)S(1)}, bf16[2,3,144,128]{3,2,1,0:T(8,128)(2,1)}, u32[]{:S(2)}) copy-start(bf16[2,3,144,128]{3,2,1,0:T(8,128)(2,1)} %get-tuple-element.127.refs_0_) | copy-start | bytes 663556
  94.8 10.5 %copy-start.17 = (bf16[2,3,144,128]{3,2,1,0:T(8,128)(2,1)S(1)}, bf16[2,3,144,128]{3,2,1,0:T(8,128)(2,1)}, u32[]{:S(2)}) copy-start(bf16[2,3,144,128]{3,2,1,0:T(8,128)(2,1)} %get-tuple-element.128.refs_1_) | copy-start | bytes 663556
  94.8 10.5 %copy-start.18 = (bf16[2,3,144,128]{3,2,1,0:T(8,128)(2,1)S(1)}, bf16[2,3,144,128]{3,2,1,0:T(8,128)(2,1)}, u32[]{:S(2)}) copy-start(bf16[2,3,144,128]{3,2,1,0:T(8,128)(2,1)} %get-tuple-element.129.refs_2_) | copy-start | bytes 663556
  94.8 10.5 %copy-start.19 = (bf16[2,3,144,128]{3,2,1,0:T(8,128)(2,1)S(1)}, bf16[2,3,144,128]{3,2,1,0:T(8,128)(2,1)}, u32[]{:S(2)}) copy-start(bf16[2,3,144,128]{3,2,1,0:T(8,128)(2,1)} %get-tuple-element.130.refs_3_) | copy-start | bytes 663556
  94.8 2.4 %collective-permute-start.16 = (bf16[4,656,128]{2,1,0:T(8,128)(2,1)}, bf16[4,656,128]{2,1,0:T(8,128)(2,1)S(1)}, u32[]{:S(2)}, u32[]{:S(2)}) collective-permute-start(bf16[4,656,128]{2,1,0:T(8,128)(2,1)} %get-tuple-element.137), channel_id=1, source_target_pairs={{0,4},{4,0},{8,12},{12,8},{16,20},{20,16},{24,28},{28,24},{1,5},{5... | collective-permute-start | bytes 2015240 | tf_op jit(solution)/shard_map/ppermute | solution.py:859
  94.9 10.3 %collective-permute-start.12 = (bf16[4,2,3,80,128]{4,3,2,1,0:T(8,128)(2,1)}, bf16[4,2,3,80,128]{4,3,2,1,0:T(8,128)(2,1)S(1)}, u32[]{:S(2)}, u32[]{:S(2)}) collective-permute-start(bf16[4,2,3,80,128]{4,3,2,1,0:T(8,128)(2,1)} %get-tuple-element.131), channel_id=1, source_target_pairs={{0,4},{4,8},{8,12},{12,16},{16,20},{20,24},{24,28},{28,0},{1,5},{5... | collective-permute-start | bytes 1474568 | tf_op jit(solution)/shard_map/ppermute | solution.py:1050
  95.6 16.6 %collective-permute-start.11 = (bf16[4,2,3,80,128]{4,3,2,1,0:T(8,128)(2,1)S(1)}, bf16[4,2,3,80,128]{4,3,2,1,0:T(8,128)(2,1)S(1)}, u32[]{:S(2)}, u32[]{:S(2)}) collective-permute-start(bf16[4,2,3,80,128]{4,3,2,1,0:T(8,128)(2,1)S(1)} %pad_maximum_fusion.1), channel_id=1, source_target_pairs={{0,4},{4,8},{8,12},{12,16},{16,20},{20,24},{24,28},{28,0},{1,5},{5... | collective-permute-start | bytes 1474568 | tf_op jit(solution)/shard_map/ppermute | solution.py:1050
  98.5 8.9 %collective-permute-start.17 = (bf16[656,128]{1,0:T(8,128)(2,1)S(1)}, bf16[656,128]{1,0:T(8,128)(2,1)S(1)}, u32[]{:S(2)}, u32[]{:S(2)}) collective-permute-start(bf16[656,128]{1,0:T(8,128)(2,1)S(1)} %get-tuple-element.157), channel_id=1, source_target_pairs={{0,1},{1,0},{2,3},{3,2},{4,5},{5,4},{6,7},{7,6},{8,9},{9,8},{10,11... | collective-permute-start | bytes 503816 | tf_op jit(solution)/shard_map/ppermute | solution.py:855
  99.9 9.4 %collective-permute-start.19 = (bf16[656,128]{1,0:T(8,128)(2,1)S(1)}, bf16[656,128]{1,0:T(8,128)(2,1)S(1)}, u32[]{:S(2)}, u32[]{:S(2)}) collective-permute-start(bf16[656,128]{1,0:T(8,128)(2,1)S(1)} %get-tuple-element.158), channel_id=1, source_target_pairs={{0,3},{1,2},{2,1},{3,0},{4,7},{5,6},{6,5},{7,4},{8,11},{9,10},{10,... | collective-permute-start | bytes 503816 | tf_op jit(solution)/shard_map/ppermute | solution.py:855
  100.5 16.2 %copy-start.14 = (s32[1,144]{1,0:T(1,128)S(1)}, s32[1,144]{1,0:T(1,128)}, u32[]{:S(2)}) copy-start(s32[1,144]{1,0:T(1,128)} %constant.34.rest_0_) | copy-start | bytes 1732
  100.5 16.2 %copy-start.15 = (s32[1,80]{1,0:T(1,128)S(1)}, s32[1,80]{1,0:T(1,128)}, u32[]{:S(2)}) copy-start(s32[1,80]{1,0:T(1,128)} %constant.35.rest_1_) | copy-start | bytes 964
  100.5 10.7 %collective-permute-start.18 = (bf16[656,128]{1,0:T(8,128)(2,1)S(1)}, bf16[656,128]{1,0:T(8,128)(2,1)S(1)}, u32[]{:S(2)}, u32[]{:S(2)}) collective-permute-start(bf16[656,128]{1,0:T(8,128)(2,1)S(1)} %get-tuple-element.159), channel_id=1, source_target_pairs={{0,2},{1,3},{2,0},{3,1},{4,6},{5,7},{6,4},{7,5},{8,10},{9,11},{10,... | collective-permute-start | bytes 503816 | tf_op jit(solution)/shard_map/ppermute | solution.py:855
  106.0 23.0 %collective-permute-start.13 = (bf16[2,3,144,128]{3,2,1,0:T(8,128)(2,1)S(1)}, bf16[2,3,144,128]{3,2,1,0:T(8,128)(2,1)S(1)}, u32[]{:S(2)}, u32[]{:S(2)}) collective-permute-start(bf16[2,3,144,128]{3,2,1,0:T(8,128)(2,1)S(1)} %get-tuple-element.133), channel_id=1, source_target_pairs={{0,1},{1,0},{2,3},{3,2},{4,5},{5,4},{6,7},{7,6},{8,9},{9,8},{10,11... | collective-permute-start | bytes 663560 | tf_op jit(solution)/shard_map/ppermute | solution.py:855
  107.4 22.3 %collective-permute-start.14 = (bf16[2,3,144,128]{3,2,1,0:T(8,128)(2,1)S(1)}, bf16[2,3,144,128]{3,2,1,0:T(8,128)(2,1)S(1)}, u32[]{:S(2)}, u32[]{:S(2)}) collective-permute-start(bf16[2,3,144,128]{3,2,1,0:T(8,128)(2,1)S(1)} %get-tuple-element.134), channel_id=1, source_target_pairs={{0,2},{1,3},{2,0},{3,1},{4,6},{5,7},{6,4},{7,5},{8,10},{9,11},{10,... | collective-permute-start | bytes 663560 | tf_op jit(solution)/shard_map/ppermute | solution.py:855
  112.2 8.4 %collective-permute-start.22 = (bf16[656,128]{1,0:T(8,128)(2,1)S(1)}, bf16[656,128]{1,0:T(8,128)(2,1)S(1)}, u32[]{:S(2)}, u32[]{:S(2)}) collective-permute-start(bf16[656,128]{1,0:T(8,128)(2,1)S(1)} %fusion.1), channel_id=1, source_target_pairs={{0,24},{4,28},{8,16},{12,20},{16,8},{20,12},{24,0},{28,4},{1,25},{... | collective-permute-start | bytes 503816 | tf_op jit(solution)/shard_map/ppermute | solution.py:859
  114.4 11.7 %collective-permute-start.21 = (bf16[656,128]{1,0:T(8,128)(2,1)S(1)}, bf16[656,128]{1,0:T(8,128)(2,1)S(1)}, u32[]{:S(2)}, u32[]{:S(2)}) collective-permute-start(bf16[656,128]{1,0:T(8,128)(2,1)S(1)} %fusion.1), channel_id=1, source_target_pairs={{0,16},{4,20},{8,24},{12,28},{16,0},{20,4},{24,8},{28,12},{1,17},{... | collective-permute-start | bytes 503816 | tf_op jit(solution)/shard_map/ppermute | solution.py:859
  114.4 11.7 %collective-permute-start.20 = (bf16[656,128]{1,0:T(8,128)(2,1)S(1)}, bf16[656,128]{1,0:T(8,128)(2,1)S(1)}, u32[]{:S(2)}, u32[]{:S(2)}) collective-permute-start(bf16[656,128]{1,0:T(8,128)(2,1)S(1)} %fusion.1), channel_id=1, source_target_pairs={{0,8},{4,12},{8,0},{12,4},{16,24},{20,28},{24,16},{28,20},{1,9},{5... | collective-permute-start | bytes 503816 | tf_op jit(solution)/shard_map/ppermute | solution.py:859
  120.7 9.0 %collective-permute-start.15 = (bf16[2,3,144,128]{3,2,1,0:T(8,128)(2,1)S(1)}, bf16[2,3,144,128]{3,2,1,0:T(8,128)(2,1)S(1)}, u32[]{:S(2)}, u32[]{:S(2)}) collective-permute-start(bf16[2,3,144,128]{3,2,1,0:T(8,128)(2,1)S(1)} %get-tuple-element.135), channel_id=1, source_target_pairs={{0,3},{1,2},{2,1},{3,0},{4,7},{5,6},{6,5},{7,4},{8,11},{9,10},{10,... | collective-permute-start | bytes 663560 | tf_op jit(solution)/shard_map/ppermute | solution.py:855
  126.1 7.7 %collective-permute-start.25 = (bf16[656,128]{1,0:T(8,128)(2,1)S(1)}, bf16[656,128]{1,0:T(8,128)(2,1)S(1)}, u32[]{:S(2)}, u32[]{:S(2)}) collective-permute-start(bf16[656,128]{1,0:T(8,128)(2,1)S(1)} %add_convert_fusion), channel_id=1, source_target_pairs={{0,3},{1,2},{2,1},{3,0},{4,7},{5,6},{6,5},{7,4},{8,11},{9,10},{10,... | collective-permute-start | bytes 503816 | tf_op jit(solution)/shard_map/ppermute | solution.py:855
  128.2 6.7 %collective-permute-start.24 = (bf16[656,128]{1,0:T(8,128)(2,1)S(1)}, bf16[656,128]{1,0:T(8,128)(2,1)S(1)}, u32[]{:S(2)}, u32[]{:S(2)}) collective-permute-start(bf16[656,128]{1,0:T(8,128)(2,1)S(1)} %add_convert_fusion), channel_id=1, source_target_pairs={{0,2},{1,3},{2,0},{3,1},{4,6},{5,7},{6,4},{7,5},{8,10},{9,11},{10,... | collective-permute-start | bytes 503816 | tf_op jit(solution)/shard_map/ppermute | solution.py:855
  128.9 6.3 %collective-permute-start.23 = (bf16[656,128]{1,0:T(8,128)(2,1)S(1)}, bf16[656,128]{1,0:T(8,128)(2,1)S(1)}, u32[]{:S(2)}, u32[]{:S(2)}) collective-permute-start(bf16[656,128]{1,0:T(8,128)(2,1)S(1)} %add_convert_fusion), channel_id=1, source_target_pairs={{0,1},{1,0},{2,3},{3,2},{4,5},{5,4},{6,7},{7,6},{8,9},{9,8},{10,11... | collective-permute-start | bytes 503816 | tf_op jit(solution)/shard_map/ppermute | solution.py:855
  129.7 7.8 %copy-start.12 = (bf16[128,128]{1,0:T(8,128)(2,1)S(1)}, bf16[128,128]{1,0:T(8,128)(2,1)}, u32[]{:S(2)}) copy-start(bf16[128,128]{1,0:T(8,128)(2,1)} %constant.29.clone.order) | copy-start | bytes 98308
  129.7 7.8 %copy-start.13 = (s32[6,192]{1,0:T(8,128)S(1)}, s32[6,192]{1,0:T(8,128)}, u32[]{:S(2)}) copy-start(s32[6,192]{1,0:T(8,128)} %constant.28.clone.lanes) | copy-start | bytes 13828
  135.3 2.2 %collective-permute-start.26 = (bf16[4,656,128]{2,1,0:T(8,128)(2,1)S(1)}, bf16[4,656,128]{2,1,0:T(8,128)(2,1)S(1)}, u32[]{:S(2)}, u32[]{:S(2)}) collective-permute-start(bf16[4,656,128]{2,1,0:T(8,128)(2,1)S(1)} %pad_maximum_fusion.own), channel_id=1, source_target_pairs={{0,4},{4,0},{8,12},{12,8},{16,20},{20,16},{24,28},{28,24},{1,5},{5... | collective-permute-start | bytes 2015240 | tf_op jit(solution)/shard_map/ppermute | solution.py:859

commit v5 on v4

--- a/solution.py
+++ b/solution.py
@@ -15,9 +15,9 @@
 HALO0 = 32
 HALO = TOK - HALO0
 GROUP = 8
-CHUNK = 2
+CHUNK = 8
 STOP = object()
-LAG_F = 0
+LAG_F = 2
 LAG_B = 0
 EPSILON = 1e-05
 NEGATIVE = -1000000000.0
@@ -1070,8 +1070,9 @@
     raw = (qkv_window, out_window, qkv_column, out_column)
     bias, weights = bias_of(z, bias_table, p, raw)
     weights = weights + [w_up, w_down.T]
-    halo_x, bias = lax.optimization_barrier((halo_x, bias))
-    halo_c = lon_shift(z, tie(c[:, :, :half], halo_x), -1)
+    first_c = tie(c, bias)[:, :, :half]
+    halo_x, bias, first_c = lax.optimization_barrier((halo_x, bias, first_c))
+    halo_c = lon_shift(z, first_c, -1)
     wire_x = pack(z, x, halo_x, offsets)
     halo_c = tie(halo_c, *wire_x)
     wire_x = lev_exchange(z, wire_x)
@@ -1093,7 +1094,7 @@
     sums = sum_levels(z, sums)
     wire_g = lev_exchange(z, merge_cells(z, wire_g, late, offsets))
     result = unpack(z, wire_r, halo_r, offsets)
-    sums = sum_slabs(z, tie(sums, halo_r, late))
+    sums = sum_slabs(z, sums)
     sums = share_levels(z, tie(sums, result))
     input_grad = unpack(z, wire_g, None, offsets)
     own = jnp.stack(tie(sums, input_grad))

time: 140 us -> 136 us (0.971)
  local copies, waits for them, and re-layouts: 6.62 us -> 3.71 us
  Pallas kernels: 70.2 us -> 67.8 us
    unnamed x67, local copies, waits for them, and re-layouts: 4.35 us -> 2.29 us
    ppermute x4, waiting for transfers between devices: 8.35 us -> 10 us  [lon_shift(): lax.ppermute(array, 'lon', [(w, (w + distance) % z.lon) for w in range(z....]
where the time goes in v5:
time: 136 us
  Pallas kernels  67.8 us (50%)
  starting transfers between devices  35.5 us (26%)
  waiting for transfers between devices  25.6 us (19%)
  local copies, waits for them, and re-layouts  3.71 us (3%)
  other arithmetic  2.49 us (2%)
    pallas_call x1, Pallas kernels, backward(): pl.pallas_call(functools.partial(backward_kernel, z), **dict(grid=(z.s,),...  31.1 us
    ppermute x18, starting transfers between devices, lev_swap(): return lax.ppermute(array, 'lev', [(i, i ^ k) for i in range(z.lev)])  22 us
    pallas_call x1, Pallas kernels, forward(): pl.pallas_call(functools.partial(forward_kernel, z), grid=(z.s,), in_spec...  22 us
    ppermute x4, waiting for transfers between devices, lon_shift(): lax.ppermute(array, 'lon', [(w, (w + distance) % z.lon) for w in range(z....  10 us
    ppermute x4, starting transfers between devices, lon_shift(): lax.ppermute(array, 'lon', [(w, (w + distance) % z.lon) for w in range(z....  8.86 us
    ppermute x18, waiting for transfers between devices, lev_swap(): return lax.ppermute(array, 'lev', [(i, i ^ k) for i in range(z.lev)])  8.14 us
    ppermute x5, waiting for transfers between devices, lon_swap(): return lax.ppermute(array, 'lon', [(i, i ^ k) for i in range(z.lon)])  7.39 us
    pallas_call x2, Pallas kernels, unpack(): pl.pallas_call(functools.partial(unpack_kernel, z, merged), in_specs=in_s...  6.01 us
  transfers between devices with their start and end apart: 27, of which 13 were waited for; matrix products, arithmetic and copies ran while one was open for 2% of the time, Pallas kernels for 48%

profile of v5, /device:TPU:0, one launch (start us, length us, event | category | flops | bytes accessed | tf_op | source)
XLA Modules:
  0.0 136.2 jit_solution(8668936801452014361)
XLA Ops:
  0.6 0.0 copy-start
  0.7 0.0 copy-start.11
  0.7 1.2 slice.56
  1.9 4.5 %collective-permute-start = (bf16[2,2,6,48,192]{4,3,2,1,0:T(8,128)(2,1)S(1)}, bf16[2,2,6,48,192]{4,3,2,1,0:T(8,128)(2,1)S(1)}, u32[]{:S(2)}, u32[]{:S(2)}) collective-permute-start(bf16[2,2,6,48,192]{4,3,2,1,0:T(8,128)(2,1)S(1)} %slice.56), channel_id=1, source_target_pairs={{0,28},{4,0},{8,4},{12,8},{16,12},{20,16},{24,20},{28,24},{1,29},{... | collective-permute-start | bytes 1327112 | tf_op jit(solution)/shard_map/ppermute | solution.py:1050
  6.5 0.1 dynamic-slice_bitcast_fusion
  6.7 0.0 copy-start.8
  6.7 0.0 copy-start.10
  6.7 1.2 bias.1
  8.1 5.8 %collective-permute-done.halo_ref = bf16[2,2,6,48,192]{4,3,2,1,0:T(8,128)(2,1)S(1)} collective-permute-done((bf16[2,2,6,48,192]{4,3,2,1,0:T(8,128)(2,1)S(1)}, bf16[2,2,6,48,192]{4,3,2,1,0:T(8,128)(2,1)S(1)}, u32[]{:S(2)}, u32[]{:S(2)}) %collective-permute-start) | collective-permute-done | bytes 442400 | tf_op jit(solution)/shard_map/ppermute | solution.py:1050
  13.9 3.8 %collective-permute-start.1 = (bf16[2,2,6,48,192]{4,3,2,1,0:T(8,128)(2,1)S(1)}, bf16[2,2,6,48,192]{4,3,2,1,0:T(8,128)(2,1)S(1)}, u32[]{:S(2)}, u32[]{:S(2)}) collective-permute-start(bf16[2,2,6,48,192]{4,3,2,1,0:T(8,128)(2,1)S(1)} %slice.43), channel_id=1, source_target_pairs={{0,28},{4,0},{8,4},{12,8},{16,12},{20,16},{24,20},{28,24},{1,29},{... | collective-permute-start | bytes 1327112 | tf_op jit(solution)/shard_map/ppermute | solution.py:1050
  17.7 2.1 %pack.2 = (bf16[2,3,144,128]{3,2,1,0:T(8,128)(2,1)S(1)}, bf16[2,3,144,128]{3,2,1,0:T(8,128)(2,1)S(1)}, bf16[2,3,144,128]{3,2,1,0:T(8,128)(2,1)S(1)}, bf16[2,3,144,128]{3,2,1,0:T(8,128)(2,1)S(1)}) custom-call(s32[2]{0:T(128)S(1)} %copy-done.8, s32[144,1]{1,0:T(8,128)S(1)} %copy-done.10, bf16[2,2,12,48,192]{4,3,2,1,0:T(8,128)(2,1)S(1)} %bitcast.47, ...), custom_call_target="tpu_custom_call" | custom-call | flops 2000000000 | bytes 12000000 | tf_op jit(solution)/shard_map/pack/pallas_call | solution.py:118
  19.8 0.7 copy-done.24
  20.5 1.5 %collective-permute-start.5 = (bf16[2,3,144,128]{3,2,1,0:T(8,128)(2,1)S(1)}, bf16[2,3,144,128]{3,2,1,0:T(8,128)(2,1)S(1)}, u32[]{:S(2)}, u32[]{:S(2)}) collective-permute-start(bf16[2,3,144,128]{3,2,1,0:T(8,128)(2,1)S(1)} %get-tuple-element.91), channel_id=1, source_target_pairs={{0,1},{1,0},{2,3},{3,2},{4,5},{5,4},{6,7},{7,6},{8,9},{9,8},{10,11... | collective-permute-start | bytes 663560 | tf_op jit(solution)/shard_map/ppermute | solution.py:855
  22.0 1.5 %collective-permute-start.6 = (bf16[2,3,144,128]{3,2,1,0:T(8,128)(2,1)S(1)}, bf16[2,3,144,128]{3,2,1,0:T(8,128)(2,1)S(1)}, u32[]{:S(2)}, u32[]{:S(2)}) collective-permute-start(bf16[2,3,144,128]{3,2,1,0:T(8,128)(2,1)S(1)} %get-tuple-element.92), channel_id=1, source_target_pairs={{0,2},{1,3},{2,0},{3,1},{4,6},{5,7},{6,4},{7,5},{8,10},{9,11},{10,... | collective-permute-start | bytes 663560 | tf_op jit(solution)/shard_map/ppermute | solution.py:855
  23.5 0.5 collective-permute-start.7
  24.0 1.0 collective-permute-done.1.halo_ref
  25.0 2.1 %pack.3 = (bf16[2,3,144,128]{3,2,1,0:T(8,128)(2,1)S(1)}, bf16[2,3,144,128]{3,2,1,0:T(8,128)(2,1)S(1)}, bf16[2,3,144,128]{3,2,1,0:T(8,128)(2,1)S(1)}, bf16[2,3,144,128]{3,2,1,0:T(8,128)(2,1)S(1)}) custom-call(s32[2]{0:T(128)S(1)} %copy-done.8, s32[144,1]{1,0:T(8,128)S(1)} %copy-done.10, bf16[2,2,12,48,192]{4,3,2,1,0:T(8,128)(2,1)S(1)} %bitcast.49, ...), custom_call_target="tpu_custom_call" | custom-call | flops 2000000000 | bytes 12000000 | tf_op jit(solution)/shard_map/pack/pallas_call | solution.py:118
  27.2 1.6 %collective-permute-start.2 = (bf16[2,3,144,128]{3,2,1,0:T(8,128)(2,1)S(1)}, bf16[2,3,144,128]{3,2,1,0:T(8,128)(2,1)S(1)}, u32[]{:S(2)}, u32[]{:S(2)}) collective-permute-start(bf16[2,3,144,128]{3,2,1,0:T(8,128)(2,1)S(1)} %get-tuple-element.96), channel_id=1, source_target_pairs={{0,1},{1,0},{2,3},{3,2},{4,5},{5,4},{6,7},{7,6},{8,9},{9,8},{10,11... | collective-permute-start | bytes 663560 | tf_op jit(solution)/shard_map/ppermute | solution.py:855
  28.8 1.5 %collective-permute-start.3 = (bf16[2,3,144,128]{3,2,1,0:T(8,128)(2,1)S(1)}, bf16[2,3,144,128]{3,2,1,0:T(8,128)(2,1)S(1)}, u32[]{:S(2)}, u32[]{:S(2)}) collective-permute-start(bf16[2,3,144,128]{3,2,1,0:T(8,128)(2,1)S(1)} %get-tuple-element.97), channel_id=1, source_target_pairs={{0,2},{1,3},{2,0},{3,1},{4,6},{5,7},{6,4},{7,5},{8,10},{9,11},{10,... | collective-permute-start | bytes 663560 | tf_op jit(solution)/shard_map/ppermute | solution.py:855
  30.3 0.5 collective-permute-start.4
  30.8 2.1 %collective-permute-done.7.refs_3_ = bf16[2,3,144,128]{3,2,1,0:T(8,128)(2,1)S(1)} collective-permute-done((bf16[2,3,144,128]{3,2,1,0:T(8,128)(2,1)S(1)}, bf16[2,3,144,128]{3,2,1,0:T(8,128)(2,1)S(1)}, u32[]{:S(2)}, u32[]{:S(2)}) %collective-permute-start.7) | collective-permute-done | bytes 221216 | tf_op jit(solution)/shard_map/ppermute | solution.py:855
  32.9 0.7 copy-done.32
  33.6 22.0 %forward.1 = (bf16[2,3,144,128]{3,2,1,0:T(8,128)(2,1)}, bf16[2,3,144,128]{3,2,1,0:T(8,128)(2,1)}, bf16[2,3,144,128]{3,2,1,0:T(8,128)(2,1)}, bf16[2,3,144,128]{3,...) custom-call(bf16[2,3,144,128]{3,2,1,0:T(8,128)(2,1)} %copy-done.24, ...), custom_call_target="tpu_custom_call" | custom-call | flops 15000000512 | bytes 90000000 | tf_op jit(solution)/shard_map/forward/pallas_call | solution.py:519
  55.6 1.4 %collective-permute-start.8 = (bf16[2,3,144,128]{3,2,1,0:T(8,128)(2,1)}, bf16[2,3,144,128]{3,2,1,0:T(8,128)(2,1)S(1)}, u32[]{:S(2)}, u32[]{:S(2)}) collective-permute-start(bf16[2,3,144,128]{3,2,1,0:T(8,128)(2,1)} %get-tuple-element.121), channel_id=1, source_target_pairs={{0,1},{1,0},{2,3},{3,2},{4,5},{5,4},{6,7},{7,6},{8,9},{9,8},{10,11... | collective-permute-start | bytes 663560 | tf_op jit(solution)/shard_map/ppermute | solution.py:855
  57.0 0.6 collective-permute-start.9
  57.6 1.5 %collective-permute-start.10 = (bf16[2,3,144,128]{3,2,1,0:T(8,128)(2,1)}, bf16[2,3,144,128]{3,2,1,0:T(8,128)(2,1)S(1)}, u32[]{:S(2)}, u32[]{:S(2)}) collective-permute-start(bf16[2,3,144,128]{3,2,1,0:T(8,128)(2,1)} %get-tuple-element.123), channel_id=1, source_target_pairs={{0,3},{1,2},{2,1},{3,0},{4,7},{5,6},{6,5},{7,4},{8,11},{9,10},{10,... | collective-permute-start | bytes 663560 | tf_op jit(solution)/shard_map/ppermute | solution.py:855
  59.2 0.7 copy-done.28
  59.9 0.1 copy-done.29
  59.9 31.1 %backward.1 = (bf16[2,3,144,128]{3,2,1,0:T(8,128)(2,1)}, bf16[2,3,144,128]{3,2,1,0:T(8,128)(2,1)}, bf16[2,3,144,128]{3,2,1,0:T(8,128)(2,1)}, bf16[2,3,144,128]{3...) custom-call(bf16[2,3,144,128]{3,2,1,0:T(8,128)(2,1)} %copy-done.23, ...), custom_call_target="tpu_custom_call" | custom-call | flops 20000000000 | bytes 120000000 | tf_op jit(solution)/shard_map/backward/pallas_call | solution.py:807
  91.2 0.1 collective-permute-start.16
  91.2 0.5 collective-permute-start.12
  91.8 0.1 pad_maximum_fusion.1
  91.9 0.1 collective-permute-start.11
  92.0 1.6 %collective-permute-done.16 = bf16[4,656,128]{2,1,0:T(8,128)(2,1)S(1)} collective-permute-done((bf16[4,656,128]{2,1,0:T(8,128)(2,1)}, bf16[4,656,128]{2,1,0:T(8,128)(2,1)S(1)}, u32[]{:S(2)}, u32[]{:S(2)}) %collective-permute-start.16) | collective-permute-done | bytes 671776 | tf_op jit(solution)/shard_map/ppermute | solution.py:859
  93.6 1.2 fusion.3
  94.8 1.4 %collective-permute-start.17 = (bf16[656,128]{1,0:T(8,128)(2,1)S(1)}, bf16[656,128]{1,0:T(8,128)(2,1)S(1)}, u32[]{:S(2)}, u32[]{:S(2)}) collective-permute-start(bf16[656,128]{1,0:T(8,128)(2,1)S(1)} %get-tuple-element.157), channel_id=1, source_target_pairs={{0,1},{1,0},{2,3},{3,2},{4,5},{5,4},{6,7},{7,6},{8,9},{9,8},{10,11... | collective-permute-start | bytes 503816 | tf_op jit(solution)/shard_map/ppermute | solution.py:855
  96.2 0.6 collective-permute-start.19
  96.8 1.5 %collective-permute-start.18 = (bf16[656,128]{1,0:T(8,128)(2,1)S(1)}, bf16[656,128]{1,0:T(8,128)(2,1)S(1)}, u32[]{:S(2)}, u32[]{:S(2)}) collective-permute-start(bf16[656,128]{1,0:T(8,128)(2,1)S(1)} %get-tuple-element.159), channel_id=1, source_target_pairs={{0,2},{1,3},{2,0},{3,1},{4,6},{5,7},{6,4},{7,5},{8,10},{9,11},{10,... | collective-permute-start | bytes 503816 | tf_op jit(solution)/shard_map/ppermute | solution.py:855
  98.3 3.2 %collective-permute-done.12.refs_4_ = bf16[4,2,3,80,128]{4,3,2,1,0:T(8,128)(2,1)S(1)} collective-permute-done((bf16[4,2,3,80,128]{4,3,2,1,0:T(8,128)(2,1)}, bf16[4,2,3,80,128]{4,3,2,1,0:T(8,128)(2,1)S(1)}, u32[]{:S(2)}, u32[]{:S(2)}) %collective-permute-start.12) | collective-permute-done | bytes 491552 | tf_op jit(solution)/shard_map/ppermute | solution.py:1050
  101.6 0.7 merge.1
  102.3 1.4 %collective-permute-start.13 = (bf16[2,3,144,128]{3,2,1,0:T(8,128)(2,1)S(1)}, bf16[2,3,144,128]{3,2,1,0:T(8,128)(2,1)S(1)}, u32[]{:S(2)}, u32[]{:S(2)}) collective-permute-start(bf16[2,3,144,128]{3,2,1,0:T(8,128)(2,1)S(1)} %get-tuple-element.134), channel_id=1, source_target_pairs={{0,1},{1,0},{2,3},{3,2},{4,5},{5,4},{6,7},{7,6},{8,9},{9,8},{10,11... | collective-permute-start | bytes 663560 | tf_op jit(solution)/shard_map/ppermute | solution.py:855
  103.7 0.6 collective-permute-start.14
  104.3 1.3 collective-permute-done.19
  105.6 1.9 %collective-permute-done.18 = bf16[656,128]{1,0:T(8,128)(2,1)S(1)} collective-permute-done((bf16[656,128]{1,0:T(8,128)(2,1)S(1)}, bf16[656,128]{1,0:T(8,128)(2,1)S(1)}, u32[]{:S(2)}, u32[]{:S(2)}) %collective-permute-start.18) | collective-permute-done | bytes 167968 | tf_op jit(solution)/shard_map/ppermute | solution.py:855
  107.5 1.0 fusion.1
  108.5 2.0 %collective-permute-start.22 = (bf16[656,128]{1,0:T(8,128)(2,1)S(1)}, bf16[656,128]{1,0:T(8,128)(2,1)S(1)}, u32[]{:S(2)}, u32[]{:S(2)}) collective-permute-start(bf16[656,128]{1,0:T(8,128)(2,1)S(1)} %fusion.1), channel_id=1, source_target_pairs={{0,24},{4,28},{8,16},{12,20},{16,8},{20,12},{24,0},{28,4},{1,25},{... | collective-permute-start | bytes 503816 | tf_op jit(solution)/shard_map/ppermute | solution.py:859
  110.6 2.4 %collective-permute-start.20 = (bf16[656,128]{1,0:T(8,128)(2,1)S(1)}, bf16[656,128]{1,0:T(8,128)(2,1)S(1)}, u32[]{:S(2)}, u32[]{:S(2)}) collective-permute-start(bf16[656,128]{1,0:T(8,128)(2,1)S(1)} %fusion.1), channel_id=1, source_target_pairs={{0,8},{4,12},{8,0},{12,4},{16,24},{20,28},{24,16},{28,20},{1,9},{5... | collective-permute-start | bytes 503816 | tf_op jit(solution)/shard_map/ppermute | solution.py:859
  113.0 3.2 %unpack.2 = bf16[2,2,12,48,192]{4,3,2,1,0:T(8,128)(2,1)} custom-call(s32[2]{0:T(128)S(1)} %copy-done.9, s32[1,144]{1,0:T(1,128)S(1)} %copy-done.14, s32[1,80]{1,0:T(1,128)S(1)} %copy-done.15, bf16[2,3,144,128]{3,2,1,0:T(8,128)(2,1)S(1)} %copy-done.3, bf16[2,3,144,128]{3,2,1,0:T(8,128)(2,1)S(1)} %collective-permute-done.8.rest_3_, ...), custom_call_target="tpu_custom_call" | custom-call | flops 2000000000 | bytes 12000000 | tf_op jit(solution)/shard_map/unpack/pallas_call | solution.py:165
  116.2 0.8 collective-permute-done.22
  117.0 2.3 %collective-permute-start.15 = (bf16[2,3,144,128]{3,2,1,0:T(8,128)(2,1)S(1)}, bf16[2,3,144,128]{3,2,1,0:T(8,128)(2,1)S(1)}, u32[]{:S(2)}, u32[]{:S(2)}) collective-permute-start(bf16[2,3,144,128]{3,2,1,0:T(8,128)(2,1)S(1)} %get-tuple-element.136), channel_id=1, source_target_pairs={{0,3},{1,2},{2,1},{3,0},{4,7},{5,6},{6,5},{7,4},{8,11},{9,10},{10,... | collective-permute-start | bytes 663560 | tf_op jit(solution)/shard_map/ppermute | solution.py:855
  119.3 2.9 %collective-permute-done.21 = bf16[656,128]{1,0:T(8,128)(2,1)S(1)} collective-permute-done((bf16[656,128]{1,0:T(8,128)(2,1)S(1)}, bf16[656,128]{1,0:T(8,128)(2,1)S(1)}, u32[]{:S(2)}, u32[]{:S(2)}) %collective-permute-start.21) | collective-permute-done | bytes 167968 | tf_op jit(solution)/shard_map/ppermute | solution.py:859
  122.2 0.1 add_convert_fusion
  122.3 2.4 %collective-permute-start.25 = (bf16[656,128]{1,0:T(8,128)(2,1)S(1)}, bf16[656,128]{1,0:T(8,128)(2,1)S(1)}, u32[]{:S(2)}, u32[]{:S(2)}) collective-permute-start(bf16[656,128]{1,0:T(8,128)(2,1)S(1)} %add_convert_fusion), channel_id=1, source_target_pairs={{0,3},{1,2},{2,1},{3,0},{4,7},{5,6},{6,5},{7,4},{8,11},{9,10},{10,... | collective-permute-start | bytes 503816 | tf_op jit(solution)/shard_map/ppermute | solution.py:855
  124.6 0.6 collective-permute-start.24
  125.2 0.6 collective-permute-start.23
  125.8 0.0 copy-start.13
  125.8 2.8 %unpack.3 = bf16[2,2,12,48,192]{4,3,2,1,0:T(8,128)(2,1)} custom-call(s32[2]{0:T(128)S(1)} %copy-done.9, s32[1,144]{1,0:T(1,128)S(1)} %copy-done.14, bf16[2,3,144,128]{3,2,1,0:T(8,128)(2,1)S(1)} %get-tuple-element.133.rest_1_, bf16[2,3,144,128]{3,2,1,0:T(8,128)(2,1)S(1)} %collective-permute-done.13.rest_2_, ...), custom_call_target="tpu_custom_call" | custom-call | flops 2000000000 | bytes 12000000 | tf_op jit(solution)/shard_map/unpack/pallas_call | solution.py:165
  128.7 1.6 %collective-permute-done.25 = bf16[656,128]{1,0:T(8,128)(2,1)S(1)} collective-permute-done((bf16[656,128]{1,0:T(8,128)(2,1)S(1)}, bf16[656,128]{1,0:T(8,128)(2,1)S(1)}, u32[]{:S(2)}, u32[]{:S(2)}) %collective-permute-start.25) | collective-permute-done | bytes 167968 | tf_op jit(solution)/shard_map/ppermute | solution.py:855
  130.2 1.2 collective-permute-done.24
  131.4 0.1 collective-permute-done.23
  131.5 0.1 pad_maximum_fusion.own
  131.6 0.1 collective-permute-start.26
  131.7 2.1 %collective-permute-done.26.other = bf16[4,656,128]{2,1,0:T(8,128)(2,1)S(1)} collective-permute-done((bf16[4,656,128]{2,1,0:T(8,128)(2,1)S(1)}, bf16[4,656,128]{2,1,0:T(8,128)(2,1)S(1)}, u32[]{:S(2)}, u32[]{:S(2)}) %collective-permute-start.26) | collective-permute-done | bytes 671776 | tf_op jit(solution)/shard_map/ppermute | solution.py:859
  133.8 2.5 %finish.1 = (f32[192,768]{1,0:T(8,128)}, f32[192,768]{1,0:T(8,128)}, f32[192,576]{1,0:T(8,128)}, f32[192,576]{1,0:T(8,128)}, f32[192,192]{1,0:T(8,128)}, /*index...) custom-call(s32[6,192]{1,0:T(8,128)S(1)} %copy-done.13, ...), custom_call_target="tpu_custom_call" | custom-call | flops 2000000000 | bytes 12000000 | tf_op jit(solution)/shard_map/finish/pallas_call | solution.py:965
  (79 shorter events, 0.3 us)
Async XLA Ops:
  0.6 5.8 %copy-start = (f32[8,6,6,6,23]{4,0,3,2,1:T(8,128)S(1)}, f32[8,6,6,6,23]{4,0,3,2,1:T(8,128)}, u32[]{:S(2)}) copy-start(f32[8,6,6,6,23]{4,0,3,2,1:T(8,128)} %param.35) | copy-start | bytes 476932
  0.7 6.0 %copy-start.11 = (f32[96,72]{1,0:T(8,128)S(1)}, f32[96,72]{1,0:T(8,128)}, u32[]{:S(2)}) copy-start(f32[96,72]{1,0:T(8,128)} %constant.24.clone.pick_ref.refs_13_) | copy-start | bytes 82948
  0.7 6.0 %copy-start.7 = (bf16[192,192]{1,0:T(8,128)(2,1)S(1)}, bf16[192,192]{1,0:T(8,128)(2,1)}, u32[]{:S(2)}) copy-start(bf16[192,192]{1,0:T(8,128)(2,1)} %out2.1) | copy-start | bytes 221188
  0.7 6.0 %copy-start.5 = (bf16[192,576]{1,0:T(8,128)(2,1)S(1)}, bf16[192,576]{1,0:T(8,128)(2,1)}, u32[]{:S(2)}) copy-start(bf16[192,576]{1,0:T(8,128)(2,1)} %qkv2.1) | copy-start | bytes 663556
  0.7 6.0 %copy-start.6 = (bf16[192,192]{1,0:T(8,128)(2,1)S(1)}, bf16[192,192]{1,0:T(8,128)(2,1)}, u32[]{:S(2)}) copy-start(bf16[192,192]{1,0:T(8,128)(2,1)} %out1.1) | copy-start | bytes 221188
  0.7 6.0 %copy-start.4 = (bf16[192,576]{1,0:T(8,128)(2,1)S(1)}, bf16[192,576]{1,0:T(8,128)(2,1)}, u32[]{:S(2)}) copy-start(bf16[192,576]{1,0:T(8,128)(2,1)} %qkv1.1) | copy-start | bytes 663556
  1.9 11.9 %collective-permute-start = (bf16[2,2,6,48,192]{4,3,2,1,0:T(8,128)(2,1)S(1)}, bf16[2,2,6,48,192]{4,3,2,1,0:T(8,128)(2,1)S(1)}, u32[]{:S(2)}, u32[]{:S(2)}) collective-permute-start(bf16[2,2,6,48,192]{4,3,2,1,0:T(8,128)(2,1)S(1)} %slice.56), channel_id=1, source_target_pairs={{0,28},{4,0},{8,4},{12,8},{16,12},{20,16},{24,20},{28,24},{1,29},{... | collective-permute-start | bytes 1327112 | tf_op jit(solution)/shard_map/ppermute | solution.py:1050
  6.7 1.4 copy-start.2
  6.7 10.9 %copy-start.1 = (bf16[2,2,48,12,192]{4,2,3,1,0:T(8,128)(2,1)S(1)}, bf16[2,2,48,12,192]{4,2,3,1,0:T(8,128)(2,1)}, u32[]{:S(2)}) copy-start(bf16[2,2,48,12,192]{4,2,3,1,0:T(8,128)(2,1)} %param.27) | copy-start | bytes 2654212
  6.7 10.9 %copy-start.8 = (s32[2]{0:T(128)S(1)}, s32[2]{0:T(128)}, u32[]{:S(2)}) copy-start(s32[2]{0:T(128)} %offsets.9) | copy-start | bytes 28
  6.7 10.9 %copy-start.10 = (s32[144,1]{1,0:T(8,128)S(1)}, s32[144,1]{1,0:T(8,128)}, u32[]{:S(2)}) copy-start(s32[144,1]{1,0:T(8,128)} %constant.36.base) | copy-start | bytes 1732
  8.0 5.9 %copy-start.21 = (bf16[192,768]{1,0:T(8,128)(2,1)}, bf16[192,768]{1,0:T(8,128)(2,1)S(1)}, u32[]{:S(2)}) copy-start(bf16[192,768]{1,0:T(8,128)(2,1)S(1)} %get-tuple-element.102.refs_16_.refs_22_) | copy-start | bytes 884740
  8.0 5.9 %copy-start.22 = (f32[2,2,72,216]{3,2,1,0:T(8,128)}, f32[2,2,72,216]{3,2,1,0:T(8,128)S(1)}, u32[]{:S(2)}) copy-start(f32[2,2,72,216]{3,2,1,0:T(8,128)S(1)} %get-tuple-element.99.refs_6_) | copy-start | bytes 746500
  8.0 5.9 %copy-start.26 = (bf16[256,192]{1,0:T(8,128)(2,1)}, bf16[256,192]{1,0:T(8,128)(2,1)S(1)}, u32[]{:S(2)}) copy-start(bf16[256,192]{1,0:T(8,128)(2,1)S(1)} %get-tuple-element.103.refs_17_.refs_23_) | copy-start | bytes 294916
  8.0 11.8 %copy-start.20 = (bf16[192,768]{1,0:T(8,128)(2,1)}, bf16[192,768]{1,0:T(8,128)(2,1)S(1)}, u32[]{:S(2)}) copy-start(bf16[192,768]{1,0:T(8,128)(2,1)S(1)} %get-tuple-element.100.refs_14_.refs_20_) | copy-start | bytes 884740
  8.0 11.8 %copy-start.25 = (bf16[256,192]{1,0:T(8,128)(2,1)}, bf16[256,192]{1,0:T(8,128)(2,1)S(1)}, u32[]{:S(2)}) copy-start(bf16[256,192]{1,0:T(8,128)(2,1)S(1)} %get-tuple-element.101.refs_15_.refs_21_) | copy-start | bytes 294916
  13.9 11.2 %collective-permute-start.1 = (bf16[2,2,6,48,192]{4,3,2,1,0:T(8,128)(2,1)S(1)}, bf16[2,2,6,48,192]{4,3,2,1,0:T(8,128)(2,1)S(1)}, u32[]{:S(2)}, u32[]{:S(2)}) collective-permute-start(bf16[2,2,6,48,192]{4,3,2,1,0:T(8,128)(2,1)S(1)} %slice.43), channel_id=1, source_target_pairs={{0,28},{4,0},{8,4},{12,8},{16,12},{20,16},{24,20},{28,24},{1,29},{... | collective-permute-start | bytes 1327112 | tf_op jit(solution)/shard_map/ppermute | solution.py:1050
  19.8 0.7 copy-start.24
  20.5 9.8 %collective-permute-start.5 = (bf16[2,3,144,128]{3,2,1,0:T(8,128)(2,1)S(1)}, bf16[2,3,144,128]{3,2,1,0:T(8,128)(2,1)S(1)}, u32[]{:S(2)}, u32[]{:S(2)}) collective-permute-start(bf16[2,3,144,128]{3,2,1,0:T(8,128)(2,1)S(1)} %get-tuple-element.91), channel_id=1, source_target_pairs={{0,1},{1,0},{2,3},{3,2},{4,5},{5,4},{6,7},{7,6},{8,9},{9,8},{10,11... | collective-permute-start | bytes 663560 | tf_op jit(solution)/shard_map/ppermute | solution.py:855
  22.0 8.8 %collective-permute-start.6 = (bf16[2,3,144,128]{3,2,1,0:T(8,128)(2,1)S(1)}, bf16[2,3,144,128]{3,2,1,0:T(8,128)(2,1)S(1)}, u32[]{:S(2)}, u32[]{:S(2)}) collective-permute-start(bf16[2,3,144,128]{3,2,1,0:T(8,128)(2,1)S(1)} %get-tuple-element.92), channel_id=1, source_target_pairs={{0,2},{1,3},{2,0},{3,1},{4,6},{5,7},{6,4},{7,5},{8,10},{9,11},{10,... | collective-permute-start | bytes 663560 | tf_op jit(solution)/shard_map/ppermute | solution.py:855
  23.5 9.4 %collective-permute-start.7 = (bf16[2,3,144,128]{3,2,1,0:T(8,128)(2,1)S(1)}, bf16[2,3,144,128]{3,2,1,0:T(8,128)(2,1)S(1)}, u32[]{:S(2)}, u32[]{:S(2)}) collective-permute-start(bf16[2,3,144,128]{3,2,1,0:T(8,128)(2,1)S(1)} %get-tuple-element.93), channel_id=1, source_target_pairs={{0,3},{1,2},{2,1},{3,0},{4,7},{5,6},{6,5},{7,4},{8,11},{9,10},{10,... | collective-permute-start | bytes 663560 | tf_op jit(solution)/shard_map/ppermute | solution.py:855
  27.2 28.4 %copy-start.23 = (bf16[2,3,144,128]{3,2,1,0:T(8,128)(2,1)}, bf16[2,3,144,128]{3,2,1,0:T(8,128)(2,1)S(1)}, u32[]{:S(2)}) copy-start(bf16[2,3,144,128]{3,2,1,0:T(8,128)(2,1)S(1)} %get-tuple-element.95.refs_0_) | copy-start | bytes 663556
  27.2 30.4 %collective-permute-start.2 = (bf16[2,3,144,128]{3,2,1,0:T(8,128)(2,1)S(1)}, bf16[2,3,144,128]{3,2,1,0:T(8,128)(2,1)S(1)}, u32[]{:S(2)}, u32[]{:S(2)}) collective-permute-start(bf16[2,3,144,128]{3,2,1,0:T(8,128)(2,1)S(1)} %get-tuple-element.96), channel_id=1, source_target_pairs={{0,1},{1,0},{2,3},{3,2},{4,5},{5,4},{6,7},{7,6},{8,9},{9,8},{10,11... | collective-permute-start | bytes 663560 | tf_op jit(solution)/shard_map/ppermute | solution.py:855
  28.8 30.4 %collective-permute-start.3 = (bf16[2,3,144,128]{3,2,1,0:T(8,128)(2,1)S(1)}, bf16[2,3,144,128]{3,2,1,0:T(8,128)(2,1)S(1)}, u32[]{:S(2)}, u32[]{:S(2)}) collective-permute-start(bf16[2,3,144,128]{3,2,1,0:T(8,128)(2,1)S(1)} %get-tuple-element.97), channel_id=1, source_target_pairs={{0,2},{1,3},{2,0},{3,1},{4,6},{5,7},{6,4},{7,5},{8,10},{9,11},{10,... | collective-permute-start | bytes 663560 | tf_op jit(solution)/shard_map/ppermute | solution.py:855
  30.3 2.6 %copy-start.30 = (bf16[2,3,144,128]{3,2,1,0:T(8,128)(2,1)}, bf16[2,3,144,128]{3,2,1,0:T(8,128)(2,1)S(1)}, u32[]{:S(2)}) copy-start(bf16[2,3,144,128]{3,2,1,0:T(8,128)(2,1)S(1)} %collective-permute-done.5.refs_1_) | copy-start | bytes 663556
  30.3 28.9 %collective-permute-start.4 = (bf16[2,3,144,128]{3,2,1,0:T(8,128)(2,1)S(1)}, bf16[2,3,144,128]{3,2,1,0:T(8,128)(2,1)S(1)}, u32[]{:S(2)}, u32[]{:S(2)}) collective-permute-start(bf16[2,3,144,128]{3,2,1,0:T(8,128)(2,1)S(1)} %get-tuple-element.98), channel_id=1, source_target_pairs={{0,3},{1,2},{2,1},{3,0},{4,7},{5,6},{6,5},{7,4},{8,11},{9,10},{10,... | collective-permute-start | bytes 663560 | tf_op jit(solution)/shard_map/ppermute | solution.py:855
  30.8 2.1 %copy-start.31 = (bf16[2,3,144,128]{3,2,1,0:T(8,128)(2,1)}, bf16[2,3,144,128]{3,2,1,0:T(8,128)(2,1)S(1)}, u32[]{:S(2)}) copy-start(bf16[2,3,144,128]{3,2,1,0:T(8,128)(2,1)S(1)} %collective-permute-done.6.refs_2_) | copy-start | bytes 663556
  32.9 0.7 copy-start.32
  55.6 35.5 %collective-permute-start.8 = (bf16[2,3,144,128]{3,2,1,0:T(8,128)(2,1)}, bf16[2,3,144,128]{3,2,1,0:T(8,128)(2,1)S(1)}, u32[]{:S(2)}, u32[]{:S(2)}) collective-permute-start(bf16[2,3,144,128]{3,2,1,0:T(8,128)(2,1)} %get-tuple-element.121), channel_id=1, source_target_pairs={{0,1},{1,0},{2,3},{3,2},{4,5},{5,4},{6,7},{7,6},{8,9},{9,8},{10,11... | collective-permute-start | bytes 663560 | tf_op jit(solution)/shard_map/ppermute | solution.py:855
  57.0 34.1 %collective-permute-start.9 = (bf16[2,3,144,128]{3,2,1,0:T(8,128)(2,1)}, bf16[2,3,144,128]{3,2,1,0:T(8,128)(2,1)S(1)}, u32[]{:S(2)}, u32[]{:S(2)}) collective-permute-start(bf16[2,3,144,128]{3,2,1,0:T(8,128)(2,1)} %get-tuple-element.122), channel_id=1, source_target_pairs={{0,2},{1,3},{2,0},{3,1},{4,6},{5,7},{6,4},{7,5},{8,10},{9,11},{10,... | collective-permute-start | bytes 663560 | tf_op jit(solution)/shard_map/ppermute | solution.py:855
  57.6 2.3 %copy-start.27 = (bf16[2,3,144,128]{3,2,1,0:T(8,128)(2,1)}, bf16[2,3,144,128]{3,2,1,0:T(8,128)(2,1)S(1)}, u32[]{:S(2)}) copy-start(bf16[2,3,144,128]{3,2,1,0:T(8,128)(2,1)S(1)} %collective-permute-done.2.refs_1_) | copy-start | bytes 663556
  57.6 33.5 %collective-permute-start.10 = (bf16[2,3,144,128]{3,2,1,0:T(8,128)(2,1)}, bf16[2,3,144,128]{3,2,1,0:T(8,128)(2,1)S(1)}, u32[]{:S(2)}, u32[]{:S(2)}) collective-permute-start(bf16[2,3,144,128]{3,2,1,0:T(8,128)(2,1)} %get-tuple-element.123), channel_id=1, source_target_pairs={{0,3},{1,2},{2,1},{3,0},{4,7},{5,6},{6,5},{7,4},{8,11},{9,10},{10,... | collective-permute-start | bytes 663560 | tf_op jit(solution)/shard_map/ppermute | solution.py:855
  59.2 0.7 copy-start.28
  59.2 0.7 copy-start.29
  59.9 31.9 %copy-start.3 = (bf16[2,3,144,128]{3,2,1,0:T(8,128)(2,1)S(1)}, bf16[2,3,144,128]{3,2,1,0:T(8,128)(2,1)}, u32[]{:S(2)}) copy-start(bf16[2,3,144,128]{3,2,1,0:T(8,128)(2,1)} %get-tuple-element.124.rest_2_) | copy-start | bytes 663556
  91.1 10.5 %copy-start.9 = (s32[2]{0:T(128)S(1)}, s32[2]{0:T(128)}, u32[]{:S(2)}) copy-start(s32[2]{0:T(128)} %offsets.9) | copy-start | bytes 28
  91.1 10.5 %copy-start.16 = (bf16[2,3,144,128]{3,2,1,0:T(8,128)(2,1)S(1)}, bf16[2,3,144,128]{3,2,1,0:T(8,128)(2,1)}, u32[]{:S(2)}) copy-start(bf16[2,3,144,128]{3,2,1,0:T(8,128)(2,1)} %get-tuple-element.128.refs_0_) | copy-start | bytes 663556
  91.1 10.5 %copy-start.17 = (bf16[2,3,144,128]{3,2,1,0:T(8,128)(2,1)S(1)}, bf16[2,3,144,128]{3,2,1,0:T(8,128)(2,1)}, u32[]{:S(2)}) copy-start(bf16[2,3,144,128]{3,2,1,0:T(8,128)(2,1)} %get-tuple-element.129.refs_1_) | copy-start | bytes 663556
  91.1 10.5 %copy-start.18 = (bf16[2,3,144,128]{3,2,1,0:T(8,128)(2,1)S(1)}, bf16[2,3,144,128]{3,2,1,0:T(8,128)(2,1)}, u32[]{:S(2)}) copy-start(bf16[2,3,144,128]{3,2,1,0:T(8,128)(2,1)} %get-tuple-element.130.refs_2_) | copy-start | bytes 663556
  91.1 10.5 %copy-start.19 = (bf16[2,3,144,128]{3,2,1,0:T(8,128)(2,1)S(1)}, bf16[2,3,144,128]{3,2,1,0:T(8,128)(2,1)}, u32[]{:S(2)}) copy-start(bf16[2,3,144,128]{3,2,1,0:T(8,128)(2,1)} %get-tuple-element.131.refs_3_) | copy-start | bytes 663556
  91.2 2.4 %collective-permute-start.16 = (bf16[4,656,128]{2,1,0:T(8,128)(2,1)}, bf16[4,656,128]{2,1,0:T(8,128)(2,1)S(1)}, u32[]{:S(2)}, u32[]{:S(2)}) collective-permute-start(bf16[4,656,128]{2,1,0:T(8,128)(2,1)} %get-tuple-element.138), channel_id=1, source_target_pairs={{0,4},{4,0},{8,12},{12,8},{16,20},{20,16},{24,28},{28,24},{1,5},{5... | collective-permute-start | bytes 2015240 | tf_op jit(solution)/shard_map/ppermute | solution.py:859
  91.2 10.3 %collective-permute-start.12 = (bf16[4,2,3,80,128]{4,3,2,1,0:T(8,128)(2,1)}, bf16[4,2,3,80,128]{4,3,2,1,0:T(8,128)(2,1)S(1)}, u32[]{:S(2)}, u32[]{:S(2)}) collective-permute-start(bf16[4,2,3,80,128]{4,3,2,1,0:T(8,128)(2,1)} %get-tuple-element.132), channel_id=1, source_target_pairs={{0,4},{4,8},{8,12},{12,16},{16,20},{20,24},{24,28},{28,0},{1,5},{5... | collective-permute-start | bytes 1474568 | tf_op jit(solution)/shard_map/ppermute | solution.py:1050
  91.9 18.7 %collective-permute-start.11 = (bf16[4,2,3,80,128]{4,3,2,1,0:T(8,128)(2,1)S(1)}, bf16[4,2,3,80,128]{4,3,2,1,0:T(8,128)(2,1)S(1)}, u32[]{:S(2)}, u32[]{:S(2)}) collective-permute-start(bf16[4,2,3,80,128]{4,3,2,1,0:T(8,128)(2,1)S(1)} %pad_maximum_fusion.1), channel_id=1, source_target_pairs={{0,4},{4,8},{8,12},{12,16},{16,20},{20,24},{24,28},{28,0},{1,5},{5... | collective-permute-start | bytes 1474568 | tf_op jit(solution)/shard_map/ppermute | solution.py:1050
  94.8 8.9 %collective-permute-start.17 = (bf16[656,128]{1,0:T(8,128)(2,1)S(1)}, bf16[656,128]{1,0:T(8,128)(2,1)S(1)}, u32[]{:S(2)}, u32[]{:S(2)}) collective-permute-start(bf16[656,128]{1,0:T(8,128)(2,1)S(1)} %get-tuple-element.157), channel_id=1, source_target_pairs={{0,1},{1,0},{2,3},{3,2},{4,5},{5,4},{6,7},{7,6},{8,9},{9,8},{10,11... | collective-permute-start | bytes 503816 | tf_op jit(solution)/shard_map/ppermute | solution.py:855
  96.2 9.4 %collective-permute-start.19 = (bf16[656,128]{1,0:T(8,128)(2,1)S(1)}, bf16[656,128]{1,0:T(8,128)(2,1)S(1)}, u32[]{:S(2)}, u32[]{:S(2)}) collective-permute-start(bf16[656,128]{1,0:T(8,128)(2,1)S(1)} %get-tuple-element.158), channel_id=1, source_target_pairs={{0,3},{1,2},{2,1},{3,0},{4,7},{5,6},{6,5},{7,4},{8,11},{9,10},{10,... | collective-permute-start | bytes 503816 | tf_op jit(solution)/shard_map/ppermute | solution.py:855
  96.8 16.2 %copy-start.14 = (s32[1,144]{1,0:T(1,128)S(1)}, s32[1,144]{1,0:T(1,128)}, u32[]{:S(2)}) copy-start(s32[1,144]{1,0:T(1,128)} %constant.34.rest_0_) | copy-start | bytes 1732
  96.8 16.2 %copy-start.15 = (s32[1,80]{1,0:T(1,128)S(1)}, s32[1,80]{1,0:T(1,128)}, u32[]{:S(2)}) copy-start(s32[1,80]{1,0:T(1,128)} %constant.35.rest_1_) | copy-start | bytes 964
  96.8 10.7 %collective-permute-start.18 = (bf16[656,128]{1,0:T(8,128)(2,1)S(1)}, bf16[656,128]{1,0:T(8,128)(2,1)S(1)}, u32[]{:S(2)}, u32[]{:S(2)}) collective-permute-start(bf16[656,128]{1,0:T(8,128)(2,1)S(1)} %get-tuple-element.159), channel_id=1, source_target_pairs={{0,2},{1,3},{2,0},{3,1},{4,6},{5,7},{6,4},{7,5},{8,10},{9,11},{10,... | collective-permute-start | bytes 503816 | tf_op jit(solution)/shard_map/ppermute | solution.py:855
  102.3 23.0 %collective-permute-start.13 = (bf16[2,3,144,128]{3,2,1,0:T(8,128)(2,1)S(1)}, bf16[2,3,144,128]{3,2,1,0:T(8,128)(2,1)S(1)}, u32[]{:S(2)}, u32[]{:S(2)}) collective-permute-start(bf16[2,3,144,128]{3,2,1,0:T(8,128)(2,1)S(1)} %get-tuple-element.134), channel_id=1, source_target_pairs={{0,1},{1,0},{2,3},{3,2},{4,5},{5,4},{6,7},{7,6},{8,9},{9,8},{10,11... | collective-permute-start | bytes 663560 | tf_op jit(solution)/shard_map/ppermute | solution.py:855
  103.7 22.1 %collective-permute-start.14 = (bf16[2,3,144,128]{3,2,1,0:T(8,128)(2,1)S(1)}, bf16[2,3,144,128]{3,2,1,0:T(8,128)(2,1)S(1)}, u32[]{:S(2)}, u32[]{:S(2)}) collective-permute-start(bf16[2,3,144,128]{3,2,1,0:T(8,128)(2,1)S(1)} %get-tuple-element.135), channel_id=1, source_target_pairs={{0,2},{1,3},{2,0},{3,1},{4,6},{5,7},{6,4},{7,5},{8,10},{9,11},{10,... | collective-permute-start | bytes 663560 | tf_op jit(solution)/shard_map/ppermute | solution.py:855
  108.5 8.4 %collective-permute-start.22 = (bf16[656,128]{1,0:T(8,128)(2,1)S(1)}, bf16[656,128]{1,0:T(8,128)(2,1)S(1)}, u32[]{:S(2)}, u32[]{:S(2)}) collective-permute-start(bf16[656,128]{1,0:T(8,128)(2,1)S(1)} %fusion.1), channel_id=1, source_target_pairs={{0,24},{4,28},{8,16},{12,20},{16,8},{20,12},{24,0},{28,4},{1,25},{... | collective-permute-start | bytes 503816 | tf_op jit(solution)/shard_map/ppermute | solution.py:859
  110.6 11.6 %collective-permute-start.21 = (bf16[656,128]{1,0:T(8,128)(2,1)S(1)}, bf16[656,128]{1,0:T(8,128)(2,1)S(1)}, u32[]{:S(2)}, u32[]{:S(2)}) collective-permute-start(bf16[656,128]{1,0:T(8,128)(2,1)S(1)} %fusion.1), channel_id=1, source_target_pairs={{0,16},{4,20},{8,24},{12,28},{16,0},{20,4},{24,8},{28,12},{1,17},{... | collective-permute-start | bytes 503816 | tf_op jit(solution)/shard_map/ppermute | solution.py:859
  110.6 11.6 %collective-permute-start.20 = (bf16[656,128]{1,0:T(8,128)(2,1)S(1)}, bf16[656,128]{1,0:T(8,128)(2,1)S(1)}, u32[]{:S(2)}, u32[]{:S(2)}) collective-permute-start(bf16[656,128]{1,0:T(8,128)(2,1)S(1)} %fusion.1), channel_id=1, source_target_pairs={{0,8},{4,12},{8,0},{12,4},{16,24},{20,28},{24,16},{28,20},{1,9},{5... | collective-permute-start | bytes 503816 | tf_op jit(solution)/shard_map/ppermute | solution.py:859
  117.0 8.9 %collective-permute-start.15 = (bf16[2,3,144,128]{3,2,1,0:T(8,128)(2,1)S(1)}, bf16[2,3,144,128]{3,2,1,0:T(8,128)(2,1)S(1)}, u32[]{:S(2)}, u32[]{:S(2)}) collective-permute-start(bf16[2,3,144,128]{3,2,1,0:T(8,128)(2,1)S(1)} %get-tuple-element.136), channel_id=1, source_target_pairs={{0,3},{1,2},{2,1},{3,0},{4,7},{5,6},{6,5},{7,4},{8,11},{9,10},{10,... | collective-permute-start | bytes 663560 | tf_op jit(solution)/shard_map/ppermute | solution.py:855
  122.3 8.0 %collective-permute-start.25 = (bf16[656,128]{1,0:T(8,128)(2,1)S(1)}, bf16[656,128]{1,0:T(8,128)(2,1)S(1)}, u32[]{:S(2)}, u32[]{:S(2)}) collective-permute-start(bf16[656,128]{1,0:T(8,128)(2,1)S(1)} %add_convert_fusion), channel_id=1, source_target_pairs={{0,3},{1,2},{2,1},{3,0},{4,7},{5,6},{6,5},{7,4},{8,11},{9,10},{10,... | collective-permute-start | bytes 503816 | tf_op jit(solution)/shard_map/ppermute | solution.py:855
  124.6 6.8 %collective-permute-start.24 = (bf16[656,128]{1,0:T(8,128)(2,1)S(1)}, bf16[656,128]{1,0:T(8,128)(2,1)S(1)}, u32[]{:S(2)}, u32[]{:S(2)}) collective-permute-start(bf16[656,128]{1,0:T(8,128)(2,1)S(1)} %add_convert_fusion), channel_id=1, source_target_pairs={{0,2},{1,3},{2,0},{3,1},{4,6},{5,7},{6,4},{7,5},{8,10},{9,11},{10,... | collective-permute-start | bytes 503816 | tf_op jit(solution)/shard_map/ppermute | solution.py:855
  125.2 6.2 %collective-permute-start.23 = (bf16[656,128]{1,0:T(8,128)(2,1)S(1)}, bf16[656,128]{1,0:T(8,128)(2,1)S(1)}, u32[]{:S(2)}, u32[]{:S(2)}) collective-permute-start(bf16[656,128]{1,0:T(8,128)(2,1)S(1)} %add_convert_fusion), channel_id=1, source_target_pairs={{0,1},{1,0},{2,3},{3,2},{4,5},{5,4},{6,7},{7,6},{8,9},{9,8},{10,11... | collective-permute-start | bytes 503816 | tf_op jit(solution)/shard_map/ppermute | solution.py:855
  125.8 7.9 %copy-start.12 = (bf16[128,128]{1,0:T(8,128)(2,1)S(1)}, bf16[128,128]{1,0:T(8,128)(2,1)}, u32[]{:S(2)}) copy-start(bf16[128,128]{1,0:T(8,128)(2,1)} %constant.29.clone.order) | copy-start | bytes 98308
  125.8 7.9 %copy-start.13 = (s32[6,192]{1,0:T(8,128)S(1)}, s32[6,192]{1,0:T(8,128)}, u32[]{:S(2)}) copy-start(s32[6,192]{1,0:T(8,128)} %constant.28.clone.lanes) | copy-start | bytes 13828
  131.6 2.2 %collective-permute-start.26 = (bf16[4,656,128]{2,1,0:T(8,128)(2,1)S(1)}, bf16[4,656,128]{2,1,0:T(8,128)(2,1)S(1)}, u32[]{:S(2)}, u32[]{:S(2)}) collective-permute-start(bf16[4,656,128]{2,1,0:T(8,128)(2,1)S(1)} %pad_maximum_fusion.own), channel_id=1, source_target_pairs={{0,4},{4,0},{8,12},{12,8},{16,20},{20,16},{24,28},{28,24},{1,5},{5... | collective-permute-start | bytes 2015240 | tf_op jit(solution)/shard_map/ppermute | solution.py:859
